TPU v7x, 32 devices: a whole 2x2x4 slice. The times are simulated.
32 devices in a mesh: seq: 8 (over y, x, core), rows: 4 (over z).
Axes of the slice: x: 2, y: 2, z: 4, core: 2. Of those that a mesh axis runs over, the one named last changes fastest.
Arguments:
- source: bfloat16 [2, 4, 1024, 1024], P(None, 'rows', 'seq'), may hold values from -6 to 6
- target: bfloat16 [2, 4, 1024, 1024], P(None, 'rows', 'seq'), may hold values from -6 to 6
- source_segments: int32 [2, 4, 1024], P(None, 'rows'), may hold values from 0 to 2, as said below
- target_segments: int32 [2, 4, 1024], P(None, 'rows'), may hold values from 0 to 2, as said below
- cotangent: bfloat16 [2, 4, 1024, 1024], P(None, 'rows', 'seq'), may hold values from -6 to 6
- encoder_qkv: bfloat16 [3, 1024, 1024], P(None, None, ('seq', 'rows')), may hold values from -0.1875 to 0.1875
- encoder_output: bfloat16 [1024, 1024], P(None, ('seq', 'rows')), may hold values from -1.5 to 1.5
- encoder_prefix: bfloat16 [2, 30, 1024], P(None, None, ('seq', 'rows')), may hold values from -4 to 4
- encoder_expand: bfloat16 [1024, 4096], P(None, ('seq', 'rows')), may hold values from -0.1875 to 0.1875
- encoder_contract: bfloat16 [4096, 1024], P(None, ('seq', 'rows')), may hold values from -0.09375 to 0.09375
- encoder_down: bfloat16 [1024, 512], P(None, ('seq', 'rows')), may hold values from -0.1875 to 0.1875
- encoder_up: bfloat16 [512, 1024], P(None, ('seq', 'rows')), may hold values from -0.0625 to 0.0625
- encoder_norms: bfloat16 [2, 2, 1024], P(None, None, ('seq', 'rows')), may hold values from -0.9 to 1.3
- decoder_qkv: bfloat16 [3, 1024, 1024], P(None, None, ('seq', 'rows')), may hold values from -0.1875 to 0.1875
- decoder_output: bfloat16 [1024, 1024], P(None, ('seq', 'rows')), may hold values from -1.5 to 1.5
- decoder_prefix: bfloat16 [2, 30, 1024], P(None, None, ('seq', 'rows')), may hold values from -4 to 4
- cross_query: bfloat16 [1024, 1024], P(None, ('seq', 'rows')), may hold values from -0.1875 to 0.1875
- cross_kv: bfloat16 [2, 1024, 1024], P(None, None, ('seq', 'rows')), may hold values from -0.1875 to 0.1875
- cross_output: bfloat16 [1024, 1024], P(None, ('seq', 'rows')), may hold values from -1.5 to 1.5
- cross_prefix: bfloat16 [2, 30, 1024], P(None, None, ('seq', 'rows')), may hold values from -4 to 4
- decoder_expand: bfloat16 [1024, 4096], P(None, ('seq', 'rows')), may hold values from -0.1875 to 0.1875
- decoder_contract: bfloat16 [4096, 1024], P(None, ('seq', 'rows')), may hold values from -0.09375 to 0.09375
- decoder_down: bfloat16 [1024, 512], P(None, ('seq', 'rows')), may hold values from -0.1875 to 0.1875
- decoder_up: bfloat16 [512, 1024], P(None, ('seq', 'rows')), may hold values from -0.0625 to 0.0625
- decoder_norms: bfloat16 [3, 2, 1024], P(None, None, ('seq', 'rows')), may hold values from -0.9 to 1.3
Outputs:
- result: bfloat16 [2, 4, 1024, 1024], P(None, 'rows', 'seq')
- source_grad: float32 [2, 4, 1024, 1024], P(None, 'rows', 'seq')
- target_grad: float32 [2, 4, 1024, 1024], P(None, 'rows', 'seq')
- encoder_qkv_grad: float32 [3, 1024, 1024], P(None, None, ('seq', 'rows'))
- encoder_output_grad: float32 [1024, 1024], P(None, ('seq', 'rows'))
- encoder_prefix_grad: float32 [2, 30, 1024], P(None, None, ('seq', 'rows'))
- encoder_expand_grad: float32 [1024, 4096], P(None, ('seq', 'rows'))
- encoder_contract_grad: float32 [4096, 1024], P(None, ('seq', 'rows'))
- encoder_down_grad: float32 [1024, 512], P(None, ('seq', 'rows'))
- encoder_up_grad: float32 [512, 1024], P(None, ('seq', 'rows'))
- encoder_norms_grad: float32 [2, 2, 1024], P(None, None, ('seq', 'rows'))
- decoder_qkv_grad: float32 [3, 1024, 1024], P(None, None, ('seq', 'rows'))
- decoder_output_grad: float32 [1024, 1024], P(None, ('seq', 'rows'))
- decoder_prefix_grad: float32 [2, 30, 1024], P(None, None, ('seq', 'rows'))
- cross_query_grad: float32 [1024, 1024], P(None, ('seq', 'rows'))
- cross_kv_grad: float32 [2, 1024, 1024], P(None, None, ('seq', 'rows'))
- cross_output_grad: float32 [1024, 1024], P(None, ('seq', 'rows'))
- cross_prefix_grad: float32 [2, 30, 1024], P(None, None, ('seq', 'rows'))
- decoder_expand_grad: float32 [1024, 4096], P(None, ('seq', 'rows'))
- decoder_contract_grad: float32 [4096, 1024], P(None, ('seq', 'rows'))
- decoder_down_grad: float32 [1024, 512], P(None, ('seq', 'rows'))
- decoder_up_grad: float32 [512, 1024], P(None, ('seq', 'rows'))
- decoder_norms_grad: float32 [3, 2, 1024], P(None, None, ('seq', 'rows'))
Inputs may be any that keep to these rules, and one draw needn't show every extreme that they name: `source_segments`: ids never fall along a row; id 1 begins within the first 64 positions and ends within the last 64; ids 0 and 2 each cover at least one position. `target_segments`: ids never fall along a row; id 1 begins within the first 64 positions and ends within the last 64; ids 0 and 2 each cover at least one position.
All inputs are finite; a program needn't handle non-finite values.
Results may differ from a plain program's by a relative error of at most 0.024.
Values may be sent and summed in bfloat16 or wider, within the bound.
A program may use at most 448 MiB of HBM per device.

v0:
```python
import jax
import jax.numpy as jnp
from jax import lax
from jax.sharding import PartitionSpec as P

HEADS = 16
HEAD_DIM = 64


epsilon = 1e-05
masked = -1e30
adapter_scale = 4.0


def project(inputs, weight):
    return jnp.einsum("bsd,de->bse", inputs, weight, preferred_element_type=jnp.float32)


def project_back(upstream, weight):
    return jnp.einsum("bse,de->bsd", upstream, weight, preferred_element_type=jnp.float32)


def outer_sum(inputs, upstream):
    return jnp.einsum("bsd,bse->de", inputs, upstream, preferred_element_type=jnp.float32)


def layer_norm(tensor, gains, shifts):
    average = jnp.mean(tensor, axis=-1, keepdims=True)
    centered = tensor - average
    spread = jnp.mean(centered * centered, axis=-1, keepdims=True)
    return centered * lax.rsqrt(spread + epsilon) * gains + shifts


def norm_back(upstream, tensor, scales, index):
    _, pullback = jax.vjp(layer_norm, tensor, scales[index, 0], scales[index, 1])
    return pullback(upstream)


def gelu_exact(tensor):
    return jax.nn.gelu(tensor, approximate=False)


def split_heads(tensor):
    return tensor.reshape(tensor.shape[:-1] + (HEADS, HEAD_DIM))


def attention_scores(queries, keys_full, prefix_keys, allowed):
    scaling = HEAD_DIM ** (-0.5)
    heads_query = split_heads(queries)
    main_scores = (
        jnp.einsum(
            "bqhd,bkhd->bhqk",
            heads_query,
            split_heads(keys_full),
            preferred_element_type=jnp.float32,
        )
        * scaling
    )
    main_scores = jnp.where(allowed[:, None], main_scores, masked)
    extra_scores = (
        jnp.einsum(
            "bqhd,phd->bhqp",
            heads_query,
            split_heads(prefix_keys),
            preferred_element_type=jnp.float32,
        )
        * scaling
    )
    return (main_scores, extra_scores)


def attend_forward(inputs, memory, w_query, w_key, w_value, w_output, prefix, allowed):
    queries = project(inputs, w_query).astype(jnp.bfloat16)
    keys_local = project(memory, w_key).astype(jnp.bfloat16)
    values_local = project(memory, w_value).astype(jnp.bfloat16)
    keys_full, values_full = (
        lax.all_gather(keys_local, "seq", axis=1, tiled=True),
        lax.all_gather(values_local, "seq", axis=1, tiled=True),
    )
    main_scores, extra_scores = attention_scores(queries, keys_full, prefix[0], allowed)
    peaks = jnp.maximum(jnp.max(main_scores, axis=-1), jnp.max(extra_scores, axis=-1))
    totals = jnp.sum(jnp.exp(main_scores - peaks[..., None]), axis=-1) + jnp.sum(
        jnp.exp(extra_scores - peaks[..., None]), axis=-1
    )
    log_total = peaks + jnp.log(totals)
    main_weights = jnp.exp(main_scores - log_total[..., None]).astype(jnp.bfloat16)
    extra_weights = jnp.exp(extra_scores - log_total[..., None]).astype(jnp.bfloat16)
    context = jnp.einsum(
        "bhqk,bkhd->bqhd",
        main_weights,
        split_heads(values_full),
        preferred_element_type=jnp.float32,
    )
    context = context + jnp.einsum(
        "bhqp,phd->bqhd", extra_weights, split_heads(prefix[1]), preferred_element_type=jnp.float32
    )
    context = context.reshape(inputs.shape[0], inputs.shape[1], -1).astype(jnp.bfloat16)
    output = project(context, w_output)
    return (output, (inputs, memory, queries, keys_local, values_local, None, context, log_total))


def attend_backward(grad_out, saved, w_query, w_key, w_value, w_output, prefix, allowed):
    inputs, memory, queries, keys_local, values_local, stored, context, log_total = saved
    grad_low = grad_out.astype(jnp.bfloat16)
    output_grad = outer_sum(context, grad_low)
    context_grad = split_heads(project_back(grad_low, w_output).astype(jnp.bfloat16))
    keys_full, values_full = (
        lax.all_gather(keys_local, "seq", axis=1, tiled=True),
        lax.all_gather(values_local, "seq", axis=1, tiled=True),
    )
    main_scores, extra_scores = attention_scores(queries, keys_full, prefix[0], allowed)
    main_probs = jnp.exp(main_scores - log_total[..., None])
    extra_probs = jnp.exp(extra_scores - log_total[..., None])
    main_dots = jnp.einsum(
        "bqhd,bkhd->bhqk",
        context_grad,
        split_heads(values_full),
        preferred_element_type=jnp.float32,
    )
    extra_dots = jnp.einsum(
        "bqhd,phd->bhqp", context_grad, split_heads(prefix[1]), preferred_element_type=jnp.float32
    )
    centre = jnp.sum(main_probs * main_dots, axis=-1) + jnp.sum(extra_probs * extra_dots, axis=-1)
    main_slope = (main_probs * (main_dots - centre[..., None])).astype(jnp.bfloat16)
    extra_slope = (extra_probs * (extra_dots - centre[..., None])).astype(jnp.bfloat16)
    scaling = HEAD_DIM ** (-0.5)
    heads_query = split_heads(queries)
    query_grad = jnp.einsum(
        "bhqk,bkhd->bqhd", main_slope, split_heads(keys_full), preferred_element_type=jnp.float32
    )
    query_grad = query_grad + jnp.einsum(
        "bhqp,phd->bqhd", extra_slope, split_heads(prefix[0]), preferred_element_type=jnp.float32
    )
    query_grad = (query_grad * scaling).reshape(queries.shape).astype(jnp.bfloat16)
    prefix_key = (
        jnp.einsum("bhqp,bqhd->phd", extra_slope, heads_query, preferred_element_type=jnp.float32)
        * scaling
    )
    prefix_value = jnp.einsum(
        "bhqp,bqhd->phd",
        extra_probs.astype(jnp.bfloat16),
        context_grad,
        preferred_element_type=jnp.float32,
    )
    key_terms = (
        jnp.einsum("bhqk,bqhd->bkhd", main_slope, heads_query, preferred_element_type=jnp.float32)
        * scaling
    )
    value_terms = jnp.einsum(
        "bhqk,bqhd->bkhd",
        main_probs.astype(jnp.bfloat16),
        context_grad,
        preferred_element_type=jnp.float32,
    )
    key_sums, value_sums = (
        lax.psum_scatter(
            key_terms.reshape(keys_full.shape).astype(jnp.bfloat16),
            "seq",
            scatter_dimension=1,
            tiled=True,
        ).astype(jnp.float32),
        lax.psum_scatter(
            value_terms.reshape(values_full.shape).astype(jnp.bfloat16),
            "seq",
            scatter_dimension=1,
            tiled=True,
        ).astype(jnp.float32),
    )
    key_grad = key_sums.astype(jnp.bfloat16)
    value_grad = value_sums.astype(jnp.bfloat16)
    query_weight = outer_sum(inputs, query_grad)
    key_weight = outer_sum(memory, key_grad)
    value_weight = outer_sum(memory, value_grad)
    input_grad = project_back(query_grad, w_query)
    memory_grad = project_back(key_grad, w_key) + project_back(value_grad, w_value)
    prefix_grad = jnp.stack(
        [prefix_key.reshape(prefix.shape[1], -1), prefix_value.reshape(prefix.shape[1], -1)]
    )
    return (
        (query_weight, key_weight, value_weight, output_grad, prefix_grad),
        input_grad,
        memory_grad,
    )


def ffn_forward(inputs, w_expand, w_contract, w_down, w_up):
    expanded = project(inputs, w_expand)
    hidden = gelu_exact(expanded).astype(jnp.bfloat16)
    reduced = project(inputs, w_down)
    adapted = gelu_exact(reduced).astype(jnp.bfloat16)
    output = project(hidden, w_contract) + adapter_scale * project(adapted, w_up)
    return (output, (inputs, expanded, reduced))


def ffn_backward(grad_out, saved, w_expand, w_contract, w_down, w_up):
    inputs, expanded, reduced = saved
    grad_low = grad_out.astype(jnp.bfloat16)
    hidden = gelu_exact(expanded).astype(jnp.bfloat16)
    adapted = gelu_exact(reduced).astype(jnp.bfloat16)
    contract_grad = outer_sum(hidden, grad_low)
    up_grad = adapter_scale * outer_sum(adapted, grad_low)
    _, hidden_pull = jax.vjp(gelu_exact, expanded)
    expand_in = hidden_pull(project_back(grad_low, w_contract))[0].astype(jnp.bfloat16)
    _, adapt_pull = jax.vjp(gelu_exact, reduced)
    down_in = adapt_pull(adapter_scale * project_back(grad_low, w_up))[0].astype(jnp.bfloat16)
    expand_grad = outer_sum(inputs, expand_in)
    down_grad = outer_sum(inputs, down_in)
    input_grad = project_back(expand_in, w_expand) + project_back(down_in, w_down)
    return ((expand_grad, contract_grad, down_grad, up_grad), input_grad)


def local(
    source,
    target,
    source_segments,
    target_segments,
    cotangent,
    encoder_qkv,
    encoder_output,
    encoder_prefix,
    encoder_expand,
    encoder_contract,
    encoder_down,
    encoder_up,
    encoder_norms,
    decoder_qkv,
    decoder_output,
    decoder_prefix,
    cross_query,
    cross_kv,
    cross_output,
    cross_prefix,
    decoder_expand,
    decoder_contract,
    decoder_down,
    decoder_up,
    decoder_norms,
):
    (
        encoder_qkv,
        encoder_output,
        encoder_prefix,
        encoder_expand,
        encoder_contract,
        encoder_down,
        encoder_up,
        encoder_norms,
        decoder_qkv,
        decoder_output,
        decoder_prefix,
        cross_query,
        cross_kv,
        cross_output,
        cross_prefix,
        decoder_expand,
        decoder_contract,
        decoder_down,
        decoder_up,
        decoder_norms,
    ) = (
        lax.all_gather(encoder_qkv, ("seq", "rows"), axis=2, tiled=True),
        lax.all_gather(encoder_output, ("seq", "rows"), axis=1, tiled=True),
        lax.all_gather(encoder_prefix, ("seq", "rows"), axis=2, tiled=True),
        lax.all_gather(encoder_expand, ("seq", "rows"), axis=1, tiled=True),
        lax.all_gather(encoder_contract, ("seq", "rows"), axis=1, tiled=True),
        lax.all_gather(encoder_down, ("seq", "rows"), axis=1, tiled=True),
        lax.all_gather(encoder_up, ("seq", "rows"), axis=1, tiled=True),
        lax.all_gather(encoder_norms, ("seq", "rows"), axis=2, tiled=True),
        lax.all_gather(decoder_qkv, ("seq", "rows"), axis=2, tiled=True),
        lax.all_gather(decoder_output, ("seq", "rows"), axis=1, tiled=True),
        lax.all_gather(decoder_prefix, ("seq", "rows"), axis=2, tiled=True),
        lax.all_gather(cross_query, ("seq", "rows"), axis=1, tiled=True),
        lax.all_gather(cross_kv, ("seq", "rows"), axis=2, tiled=True),
        lax.all_gather(cross_output, ("seq", "rows"), axis=1, tiled=True),
        lax.all_gather(cross_prefix, ("seq", "rows"), axis=2, tiled=True),
        lax.all_gather(decoder_expand, ("seq", "rows"), axis=1, tiled=True),
        lax.all_gather(decoder_contract, ("seq", "rows"), axis=1, tiled=True),
        lax.all_gather(decoder_down, ("seq", "rows"), axis=1, tiled=True),
        lax.all_gather(decoder_up, ("seq", "rows"), axis=1, tiled=True),
        lax.all_gather(decoder_norms, ("seq", "rows"), axis=2, tiled=True),
    )
    encoder_scales = encoder_norms.astype(jnp.float32)
    decoder_scales = decoder_norms.astype(jnp.float32)
    micro_count = source.shape[0]
    batch_rows = source.shape[1]
    block_size = source.shape[2]
    width = source.shape[3]
    full_length = source_segments.shape[2]
    stacked = micro_count * batch_rows
    source_rows = source.reshape(stacked, block_size, width)
    target_rows = target.reshape(stacked, block_size, width)
    upstream = cotangent.reshape(stacked, block_size, width).astype(jnp.float32)
    source_ids = source_segments.reshape(stacked, full_length)
    target_ids = target_segments.reshape(stacked, full_length)
    offset = lax.axis_index("seq") * block_size
    query_places = offset + jnp.arange(block_size, dtype=jnp.int32)
    key_places = jnp.arange(full_length, dtype=jnp.int32)
    causal = key_places[None, :] <= query_places[:, None]
    source_here = lax.dynamic_slice_in_dim(source_ids, offset, block_size, 1)
    target_here = lax.dynamic_slice_in_dim(target_ids, offset, block_size, 1)
    encoder_mask = source_here[:, :, None] == source_ids[:, None, :]
    decoder_mask = (target_here[:, :, None] == target_ids[:, None, :]) & causal[None]
    cross_mask = target_here[:, :, None] == source_ids[:, None, :]
    attended, encoder_saved = attend_forward(
        source_rows,
        source_rows,
        encoder_qkv[0],
        encoder_qkv[1],
        encoder_qkv[2],
        encoder_output,
        encoder_prefix,
        encoder_mask,
    )
    resid_one = source_rows.astype(jnp.float32) + attended
    middle = layer_norm(resid_one, encoder_scales[0, 0], encoder_scales[0, 1])
    branch, encoder_ffn_saved = ffn_forward(
        middle.astype(jnp.bfloat16), encoder_expand, encoder_contract, encoder_down, encoder_up
    )
    resid_two = middle + branch
    memory = layer_norm(resid_two, encoder_scales[1, 0], encoder_scales[1, 1])
    memory_low = memory.astype(jnp.bfloat16)
    attended, decoder_saved = attend_forward(
        target_rows,
        target_rows,
        decoder_qkv[0],
        decoder_qkv[1],
        decoder_qkv[2],
        decoder_output,
        decoder_prefix,
        decoder_mask,
    )
    resid_three = target_rows.astype(jnp.float32) + attended
    first_rows = layer_norm(resid_three, decoder_scales[0, 0], decoder_scales[0, 1])
    crossed, cross_saved = attend_forward(
        first_rows.astype(jnp.bfloat16),
        memory_low,
        cross_query,
        cross_kv[0],
        cross_kv[1],
        cross_output,
        cross_prefix,
        cross_mask,
    )
    resid_four = first_rows + crossed
    second_rows = layer_norm(resid_four, decoder_scales[1, 0], decoder_scales[1, 1])
    branch, decoder_ffn_saved = ffn_forward(
        second_rows.astype(jnp.bfloat16), decoder_expand, decoder_contract, decoder_down, decoder_up
    )
    resid_five = second_rows + branch
    final_rows = layer_norm(resid_five, decoder_scales[2, 0], decoder_scales[2, 1])
    third_in, gain_three, shift_three = norm_back(upstream, resid_five, decoder_scales, 2)
    decoder_ffn_grads, from_ffn = ffn_backward(
        third_in, decoder_ffn_saved, decoder_expand, decoder_contract, decoder_down, decoder_up
    )
    second_in, gain_two, shift_two = norm_back(third_in + from_ffn, resid_four, decoder_scales, 1)
    cross_grads, from_cross, memory_grad = attend_backward(
        second_in,
        cross_saved,
        cross_query,
        cross_kv[0],
        cross_kv[1],
        cross_output,
        cross_prefix,
        cross_mask,
    )
    first_in, gain_one, shift_one = norm_back(
        second_in + from_cross, resid_three, decoder_scales, 0
    )
    decoder_self, from_query, from_keys = attend_backward(
        first_in,
        decoder_saved,
        decoder_qkv[0],
        decoder_qkv[1],
        decoder_qkv[2],
        decoder_output,
        decoder_prefix,
        decoder_mask,
    )
    target_grad = first_in + from_query + from_keys
    memory_in, encoder_gain_two, encoder_shift_two = norm_back(
        memory_grad, resid_two, encoder_scales, 1
    )
    encoder_ffn_grads, from_ffn = ffn_backward(
        memory_in, encoder_ffn_saved, encoder_expand, encoder_contract, encoder_down, encoder_up
    )
    middle_in, encoder_gain_one, encoder_shift_one = norm_back(
        memory_in + from_ffn, resid_one, encoder_scales, 0
    )
    encoder_self, from_query, from_keys = attend_backward(
        middle_in,
        encoder_saved,
        encoder_qkv[0],
        encoder_qkv[1],
        encoder_qkv[2],
        encoder_output,
        encoder_prefix,
        encoder_mask,
    )
    source_grad = middle_in + from_query + from_keys
    gradients = (
        jnp.stack([encoder_self[0], encoder_self[1], encoder_self[2]]),
        encoder_self[3],
        encoder_self[4],
        encoder_ffn_grads[0],
        encoder_ffn_grads[1],
        encoder_ffn_grads[2],
        encoder_ffn_grads[3],
        jnp.stack(
            [
                jnp.stack([encoder_gain_one, encoder_shift_one]),
                jnp.stack([encoder_gain_two, encoder_shift_two]),
            ]
        ),
        jnp.stack([decoder_self[0], decoder_self[1], decoder_self[2]]),
        decoder_self[3],
        decoder_self[4],
        cross_grads[0],
        jnp.stack([cross_grads[1], cross_grads[2]]),
        cross_grads[3],
        cross_grads[4],
        decoder_ffn_grads[0],
        decoder_ffn_grads[1],
        decoder_ffn_grads[2],
        decoder_ffn_grads[3],
        jnp.stack(
            [
                jnp.stack([gain_one, shift_one]),
                jnp.stack([gain_two, shift_two]),
                jnp.stack([gain_three, shift_three]),
            ]
        ),
    )
    reduced = (
        lax.psum_scatter(gradients[0], ("seq", "rows"), scatter_dimension=2, tiled=True),
        lax.psum_scatter(gradients[1], ("seq", "rows"), scatter_dimension=1, tiled=True),
        lax.psum_scatter(gradients[2], ("seq", "rows"), scatter_dimension=2, tiled=True),
        lax.psum_scatter(gradients[3], ("seq", "rows"), scatter_dimension=1, tiled=True),
        lax.psum_scatter(gradients[4], ("seq", "rows"), scatter_dimension=1, tiled=True),
        lax.psum_scatter(gradients[5], ("seq", "rows"), scatter_dimension=1, tiled=True),
        lax.psum_scatter(gradients[6], ("seq", "rows"), scatter_dimension=1, tiled=True),
        lax.psum_scatter(gradients[7], ("seq", "rows"), scatter_dimension=2, tiled=True),
        lax.psum_scatter(gradients[8], ("seq", "rows"), scatter_dimension=2, tiled=True),
        lax.psum_scatter(gradients[9], ("seq", "rows"), scatter_dimension=1, tiled=True),
        lax.psum_scatter(gradients[10], ("seq", "rows"), scatter_dimension=2, tiled=True),
        lax.psum_scatter(gradients[11], ("seq", "rows"), scatter_dimension=1, tiled=True),
        lax.psum_scatter(gradients[12], ("seq", "rows"), scatter_dimension=2, tiled=True),
        lax.psum_scatter(gradients[13], ("seq", "rows"), scatter_dimension=1, tiled=True),
        lax.psum_scatter(gradients[14], ("seq", "rows"), scatter_dimension=2, tiled=True),
        lax.psum_scatter(gradients[15], ("seq", "rows"), scatter_dimension=1, tiled=True),
        lax.psum_scatter(gradients[16], ("seq", "rows"), scatter_dimension=1, tiled=True),
        lax.psum_scatter(gradients[17], ("seq", "rows"), scatter_dimension=1, tiled=True),
        lax.psum_scatter(gradients[18], ("seq", "rows"), scatter_dimension=1, tiled=True),
        lax.psum_scatter(gradients[19], ("seq", "rows"), scatter_dimension=2, tiled=True),
    )
    shape_out = (micro_count, batch_rows, block_size, width)
    return (
        final_rows.astype(jnp.bfloat16).reshape(shape_out),
        source_grad.reshape(shape_out),
        target_grad.reshape(shape_out),
        reduced[0],
        reduced[1],
        reduced[2],
        reduced[3],
        reduced[4],
        reduced[5],
        reduced[6],
        reduced[7],
        reduced[8],
        reduced[9],
        reduced[10],
        reduced[11],
        reduced[12],
        reduced[13],
        reduced[14],
        reduced[15],
        reduced[16],
        reduced[17],
        reduced[18],
        reduced[19],
    )


def solution(mesh):
    in_specs = (
        P(None, "rows", "seq", None),
        P(None, "rows", "seq", None),
        P(None, "rows", None),
        P(None, "rows", None),
        P(None, "rows", "seq", None),
        P(None, None, ("seq", "rows")),
        P(None, ("seq", "rows")),
        P(None, None, ("seq", "rows")),
        P(None, ("seq", "rows")),
        P(None, ("seq", "rows")),
        P(None, ("seq", "rows")),
        P(None, ("seq", "rows")),
        P(None, None, ("seq", "rows")),
        P(None, None, ("seq", "rows")),
        P(None, ("seq", "rows")),
        P(None, None, ("seq", "rows")),
        P(None, ("seq", "rows")),
        P(None, None, ("seq", "rows")),
        P(None, ("seq", "rows")),
        P(None, None, ("seq", "rows")),
        P(None, ("seq", "rows")),
        P(None, ("seq", "rows")),
        P(None, ("seq", "rows")),
        P(None, ("seq", "rows")),
        P(None, None, ("seq", "rows")),
    )
    out_specs = (
        P(None, "rows", "seq", None),
        P(None, "rows", "seq", None),
        P(None, "rows", "seq", None),
        P(None, None, ("seq", "rows")),
        P(None, ("seq", "rows")),
        P(None, None, ("seq", "rows")),
        P(None, ("seq", "rows")),
        P(None, ("seq", "rows")),
        P(None, ("seq", "rows")),
        P(None, ("seq", "rows")),
        P(None, None, ("seq", "rows")),
        P(None, None, ("seq", "rows")),
        P(None, ("seq", "rows")),
        P(None, None, ("seq", "rows")),
        P(None, ("seq", "rows")),
        P(None, None, ("seq", "rows")),
        P(None, ("seq", "rows")),
        P(None, None, ("seq", "rows")),
        P(None, ("seq", "rows")),
        P(None, ("seq", "rows")),
        P(None, ("seq", "rows")),
        P(None, ("seq", "rows")),
        P(None, None, ("seq", "rows")),
    )
    return jax.shard_map(local, mesh=mesh, in_specs=in_specs, out_specs=out_specs, check_vma=False)
```

profile of v0, /device:TPU:0, one launch (start us, length us, event | category | flops | bytes accessed | tf_op | source)
XLA Modules:
  0.0 5662.0 jit_solution(18073061559360769543)
XLA Ops:
  10.5 72.5 %all-gather.30.cloned.1.call-done = bf16[3,1024,1024]{1,2,0:T(8,128)(2,1)} async-done(((bf16[3,1024,32]{1,2,0:T(8,128)(2,1)}), bf16[3,1024,1024]{1,2,0:T(8,128)(2,1)}) %all-gather.30.cloned.1.call-update) | async-done | bytes 6291472 | tf_op jit(solution)/shard_map/all_gather | solution.py:261
  93.0 61.1 %all-gather.22.cloned.1.call-done = bf16[3,1024,1024]{1,2,0:T(8,128)(2,1)} async-done(((bf16[3,1024,32]{1,2,0:T(8,128)(2,1)}), bf16[3,1024,1024]{1,2,0:T(8,128)(2,1)}) %all-gather.22.cloned.1.call-update) | async-done | bytes 6291472 | tf_op jit(solution)/shard_map/all_gather | solution.py:269
  162.3 72.7 %all_gather.93 = bf16[2,30,1024]{1,0,2:T(2,128)(2,1)S(1)} all-gather(bf16[2,30,32]{1,0,2:T(2,128)(2,1)S(1)} %copy.484), channel_id=1, replica_groups=mesh['seq'=8,'rows'=4] {'seq','rows'}, dimensions={2}, use_global_device_ids=true | all-gather | bytes 126720 | tf_op jit(solution)/shard_map/all_gather | solution.py:263
  237.4 68.6 %all_gather.95 = bf16[2,2,1024]{1,0,2:T(2,128)(2,1)S(1)} all-gather(bf16[2,2,32]{1,0,2:T(2,128)(2,1)S(1)} %copy.496), channel_id=1, replica_groups=mesh['seq'=8,'rows'=4] {'seq','rows'}, dimensions={2}, use_global_device_ids=true | all-gather | bytes 8448 | tf_op jit(solution)/shard_map/all_gather | solution.py:268
  417.9 89.3 %all-gather.38.cloned.1.call-done = bf16[1024,4096]{1,0:T(8,128)(2,1)} async-done(((bf16[1024,128]{1,0:T(8,128)(2,1)}), bf16[1024,4096]{1,0:T(8,128)(2,1)}) %all-gather.38.cloned.1.call-update) | async-done | bytes 8388624 | tf_op jit(solution)/shard_map/all_gather | solution.py:264
  527.2 58.6 %all-gather.40.cloned.1.call-done = bf16[4096,1024]{0,1:T(8,128)(2,1)} async-done(((bf16[4096,32]{0,1:T(8,128)(2,1)}), bf16[4096,1024]{0,1:T(8,128)(2,1)}) %all-gather.40.cloned.1.call-update) | async-done | bytes 8388624 | tf_op jit(solution)/shard_map/all_gather | solution.py:265
  660.0 71.8 %all_gather.87 = bf16[2,30,1024]{1,0,2:T(2,128)(2,1)S(1)} all-gather(bf16[2,30,32]{1,0,2:T(2,128)(2,1)S(1)} %copy.465), channel_id=1, replica_groups=mesh['seq'=8,'rows'=4] {'seq','rows'}, dimensions={2}, use_global_device_ids=true | all-gather | bytes 126720 | tf_op jit(solution)/shard_map/all_gather | solution.py:271
  733.6 69.9 %all_gather.89 = bf16[3,2,1024]{0,1,2:T(2,128)(2,1)S(1)} all-gather(bf16[3,2,32]{0,1,2:T(2,128)(2,1)S(1)} %copy.477), channel_id=1, replica_groups=mesh['seq'=8,'rows'=4] {'seq','rows'}, dimensions={2}, use_global_device_ids=true | all-gather | bytes 12672 | tf_op jit(solution)/shard_map/all_gather | solution.py:280
  821.8 69.9 %all_gather.104 = bf16[2,30,1024]{1,0,2:T(2,128)(2,1)S(1)} all-gather(bf16[2,30,32]{1,0,2:T(2,128)(2,1)S(1)} %copy.503), channel_id=1, replica_groups=mesh['seq'=8,'rows'=4] {'seq','rows'}, dimensions={2}, use_global_device_ids=true | all-gather | bytes 126720 | tf_op jit(solution)/shard_map/all_gather | solution.py:275
  980.3 88.1 %all-gather.56.cloned.1.call-done = bf16[1024,4096]{1,0:T(8,128)(2,1)} async-done(((bf16[1024,128]{1,0:T(8,128)(2,1)}), bf16[1024,4096]{1,0:T(8,128)(2,1)}) %all-gather.56.cloned.1.call-update) | async-done | bytes 8388624 | tf_op jit(solution)/shard_map/all_gather | solution.py:276
  1128.3 74.3 %all-gather.58.cloned.1.call-done = bf16[4096,1024]{0,1:T(8,128)(2,1)} async-done(((bf16[4096,32]{0,1:T(8,128)(2,1)}), bf16[4096,1024]{0,1:T(8,128)(2,1)}) %all-gather.58.cloned.1.call-update) | async-done | bytes 8388624 | tf_op jit(solution)/shard_map/all_gather | solution.py:277
  1209.9 48.0 all-gather.62.cloned.1.call-done
  1716.5 63.1 %reduce-scatter.92.cloned.1.call-done = f32[32,6]{1,0:T(8,128)} async-done(((f32[1024,6]{1,0:T(8,128)}), f32[32,6]{1,0:T(8,128)}) %reduce-scatter.92.cloned.1.call-update) | async-done | bytes 784
  1781.1 131.6 %reduce-scatter.90.cloned.1.call-done = f32[32,60]{1,0:T(8,128)} async-done(((f32[1024,60]{1,0:T(8,128)}), f32[32,60]{1,0:T(8,128)}) %reduce-scatter.90.cloned.1.call-update) | async-done | bytes 7696
  1914.2 131.1 %reduce-scatter.88.cloned.1.call-done = f32[32,60]{1,0:T(8,128)} async-done(((f32[1024,60]{1,0:T(8,128)}), f32[32,60]{1,0:T(8,128)}) %reduce-scatter.88.cloned.1.call-update) | async-done | bytes 7696
  2056.0 122.4 %reduce-scatter.86.cloned.1.call-done = f32[32,4]{1,0:T(8,128)} async-done(((f32[1024,4]{1,0:T(8,128)}), f32[32,4]{1,0:T(8,128)}) %reduce-scatter.86.cloned.1.call-update) | async-done | bytes 528
  2179.8 131.5 %reduce-scatter.84.cloned.1.call-done = f32[32,60]{1,0:T(8,128)} async-done(((f32[1024,60]{1,0:T(8,128)}), f32[32,60]{1,0:T(8,128)}) %reduce-scatter.84.cloned.1.call-update) | async-done | bytes 7696
  2312.9 180.2 %all-reduce.3.cloned.1.call-done = f32[2,1024,1024]{1,0,2:T(2,128)} async-done(((f32[2,1024,1024]{1,0,2:T(2,128)}), f32[2,1024,1024]{1,0,2:T(2,128)}) %all-reduce.3.cloned.1.call-update) | async-done | bytes 8388624
  2500.5 133.8 %reduce-scatter.74.cloned.1.call-done = f32[512,32]{0,1:T(8,128)} async-done(((f32[512,1024]{0,1:T(8,128)}), f32[512,32]{0,1:T(8,128)}) %reduce-scatter.74.cloned.1.call-update) | async-done | bytes 65552 | tf_op jit(solution)/shard_map/reduce_scatter | solution.py:452
  2634.3 139.1 %reduce-scatter.72.cloned.1.call-done = f32[1024,16]{0,1:T(8,128)} async-done(((f32[1024,512]{0,1:T(8,128)}), f32[1024,16]{0,1:T(8,128)}) %reduce-scatter.72.cloned.1.call-update) | async-done | bytes 65552 | tf_op jit(solution)/shard_map/reduce_scatter | solution.py:451
  2773.5 148.8 %reduce-scatter.66.cloned.1.call-done = f32[1024,32]{0,1:T(8,128)} async-done(((f32[1024,1024]{0,1:T(8,128)}), f32[1024,32]{0,1:T(8,128)}) %reduce-scatter.66.cloned.1.call-update) | async-done | bytes 131088 | tf_op jit(solution)/shard_map/reduce_scatter | solution.py:447
  2922.3 149.0 %reduce-scatter.64.cloned.1.call-done = f32[1024,32]{0,1:T(8,128)} async-done(((f32[1024,1024]{0,1:T(8,128)}), f32[1024,32]{0,1:T(8,128)}) %reduce-scatter.64.cloned.1.call-update) | async-done | bytes 131088 | tf_op jit(solution)/shard_map/reduce_scatter | solution.py:445
  3071.3 148.9 %reduce-scatter.62.cloned.1.call-done = f32[1024,32]{0,1:T(8,128)} async-done(((f32[1024,1024]{0,1:T(8,128)}), f32[1024,32]{0,1:T(8,128)}) %reduce-scatter.62.cloned.1.call-update) | async-done | bytes 131088 | tf_op jit(solution)/shard_map/reduce_scatter | solution.py:443
  3220.2 139.8 %reduce-scatter.58.cloned.1.call-done = f32[512,32]{0,1:T(8,128)} async-done(((f32[512,1024]{0,1:T(8,128)}), f32[512,32]{0,1:T(8,128)}) %reduce-scatter.58.cloned.1.call-update) | async-done | bytes 65552 | tf_op jit(solution)/shard_map/reduce_scatter | solution.py:440
  3360.0 139.2 %reduce-scatter.56.cloned.1.call-done = f32[1024,16]{0,1:T(8,128)} async-done(((f32[1024,512]{0,1:T(8,128)}), f32[1024,16]{0,1:T(8,128)}) %reduce-scatter.56.cloned.1.call-update) | async-done | bytes 65552 | tf_op jit(solution)/shard_map/reduce_scatter | solution.py:439
  3499.2 148.9 %reduce-scatter.50.cloned.1.call-done = f32[1024,32]{0,1:T(8,128)} async-done(((f32[1024,1024]{0,1:T(8,128)}), f32[1024,32]{0,1:T(8,128)}) %reduce-scatter.50.cloned.1.call-update) | async-done | bytes 131088 | tf_op jit(solution)/shard_map/reduce_scatter | solution.py:435
  3648.1 274.4 %reduce-scatter.60.cloned.1.call-done = f32[3,1024,32]{1,2,0:T(8,128)} async-done(((f32[3,1024,1024]{1,2,0:T(8,128)}), f32[3,1024,32]{1,2,0:T(8,128)}) %reduce-scatter.60.cloned.1.call-update) | async-done | bytes 393232 | tf_op jit(solution)/shard_map/reduce_scatter | solution.py:442
  3922.5 364.6 %reduce-scatter.70.cloned.1.call-done = f32[4096,32]{0,1:T(8,128)} async-done(((f32[4096,1024]{0,1:T(8,128)}), f32[4096,32]{0,1:T(8,128)}) %reduce-scatter.70.cloned.1.call-update) | async-done | bytes 524304 | tf_op jit(solution)/shard_map/reduce_scatter | solution.py:450
  4287.1 365.1 %reduce-scatter.68.cloned.1.call-done = f32[1024,128]{1,0:T(8,128)} async-done(((f32[1024,4096]{1,0:T(8,128)}), f32[1024,128]{1,0:T(8,128)}) %reduce-scatter.68.cloned.1.call-update) | async-done | bytes 524304 | tf_op jit(solution)/shard_map/reduce_scatter | solution.py:449
  4652.2 273.5 %reduce-scatter.48.cloned.1.call-done = f32[3,1024,32]{1,2,0:T(8,128)} async-done(((f32[3,1024,1024]{1,2,0:T(8,128)}), f32[3,1024,32]{1,2,0:T(8,128)}) %reduce-scatter.48.cloned.1.call-update) | async-done | bytes 393232 | tf_op jit(solution)/shard_map/reduce_scatter | solution.py:434
  4925.7 364.6 %reduce-scatter.54.cloned.1.call-done = f32[4096,32]{0,1:T(8,128)} async-done(((f32[4096,1024]{0,1:T(8,128)}), f32[4096,32]{0,1:T(8,128)}) %reduce-scatter.54.cloned.1.call-update) | async-done | bytes 524304 | tf_op jit(solution)/shard_map/reduce_scatter | solution.py:438
  5290.3 365.0 %reduce-scatter.52.cloned.1.call-done = f32[1024,128]{1,0:T(8,128)} async-done(((f32[1024,4096]{1,0:T(8,128)}), f32[1024,128]{1,0:T(8,128)}) %reduce-scatter.52.cloned.1.call-update) | async-done | bytes 524304 | tf_op jit(solution)/shard_map/reduce_scatter | solution.py:437
  (782 shorter events, 884.8 us)
Async XLA Ops:
  90.9 416.4 %all-gather.38.cloned.1.call-start = ((), (), s32[]{:S(2)}) async-start(), calls=%async_computation.33 | async-start | bytes 8650752 | tf_op jit(solution)/shard_map/all_gather | solution.py:264
  91.6 494.1 %all-gather.40.cloned.1.call-start = ((), (), s32[]{:S(2)}) async-start(), calls=%async_computation.34 | async-start | bytes 8650752 | tf_op jit(solution)/shard_map/all_gather | solution.py:265
  92.4 548.6 %all-gather.44.cloned.1.call-start = ((), (), s32[]{:S(2)}) async-start(), calls=%async_computation.36 | async-start | bytes 1081344 | tf_op jit(solution)/shard_map/all_gather | solution.py:267
  93.0 804.7 %all-gather.26.cloned.1.call-start = ((), (), s32[]{:S(2)}) async-start(), calls=%async_computation.27 | async-start | bytes 4718592 | tf_op jit(solution)/shard_map/all_gather | solution.py:77
  157.3 757.7 %all-gather.24.cloned.1.call-start = ((), (), s32[]{:S(2)}) async-start(), calls=%async_computation.26 | async-start | bytes 4718592 | tf_op jit(solution)/shard_map/all_gather | solution.py:78
  160.5 770.3 %all-gather.28.cloned.1.call-start = ((), (), s32[]{:S(2)}) async-start(), calls=%async_computation.28 | async-start | bytes 2162688 | tf_op jit(solution)/shard_map/all_gather | solution.py:270
  161.3 772.5 %all-gather.50.cloned.1.call-start = ((), (), s32[]{:S(2)}) async-start(), calls=%async_computation.39 | async-start | bytes 2162688 | tf_op jit(solution)/shard_map/all_gather | solution.py:272
  161.9 774.9 %all-gather.52.cloned.1.call-start = ((), (), s32[]{:S(2)}) async-start(), calls=%async_computation.40 | async-start | bytes 4718592 | tf_op jit(solution)/shard_map/all_gather | solution.py:77
  657.2 411.3 %all-gather.56.cloned.1.call-start = ((), (), s32[]{:S(2)}) async-start(), calls=%async_computation.42 | async-start | bytes 8650752 | tf_op jit(solution)/shard_map/all_gather | solution.py:276
  657.8 465.6 %all-gather.60.cloned.1.call-start = ((), (), s32[]{:S(2)}) async-start(), calls=%async_computation.44 | async-start | bytes 1081344 | tf_op jit(solution)/shard_map/all_gather | solution.py:278
  658.5 544.1 %all-gather.58.cloned.1.call-start = ((), (), s32[]{:S(2)}) async-start(), calls=%async_computation.43 | async-start | bytes 8650752 | tf_op jit(solution)/shard_map/all_gather | solution.py:277
  659.1 598.8 %all-gather.62.cloned.1.call-start = ((), (), s32[]{:S(2)}) async-start(), calls=%async_computation.45 | async-start | bytes 1081344 | tf_op jit(solution)/shard_map/all_gather | solution.py:279
  659.8 767.3 %reduce-scatter.44.cloned.1.call-start = ((), (), s32[]{:S(2)}) async-start(), calls=%async_computation.46 | async-start | bytes 4718592 | tf_op jit(solution)/shard_map/reduce_scatter | solution.py:156
  1543.7 369.0 %reduce-scatter.90.cloned.1.call-start = ((), (), s32[]{:S(2)}) async-start(), calls=%async_computation.69 | async-start | bytes 540672
  1549.6 495.7 %reduce-scatter.88.cloned.1.call-start = ((), (), s32[]{:S(2)}) async-start(), calls=%async_computation.68 | async-start | bytes 540672
  1558.7 619.6 %reduce-scatter.86.cloned.1.call-start = ((), (), s32[]{:S(2)}) async-start(), calls=%async_computation.67 | async-start | bytes 540672
  1565.5 745.8 %reduce-scatter.84.cloned.1.call-start = ((), (), s32[]{:S(2)}) async-start(), calls=%async_computation.66 | async-start | bytes 540672
  1567.6 925.5 %all-reduce.3.cloned.1.call-start = ((), (), s32[]{:S(2)}) async-start(), calls=%async_computation.71 | async-start | bytes 16777216
  1587.9 1046.4 %reduce-scatter.74.cloned.1.call-start = ((), (), s32[]{:S(2)}) async-start(), calls=%async_computation.61 | async-start | bytes 2162688 | tf_op jit(solution)/shard_map/reduce_scatter | solution.py:452
  1590.9 1182.6 %reduce-scatter.72.cloned.1.call-start = ((), (), s32[]{:S(2)}) async-start(), calls=%async_computation.60 | async-start | bytes 2162688 | tf_op jit(solution)/shard_map/reduce_scatter | solution.py:451
  1592.8 1329.4 %reduce-scatter.66.cloned.1.call-start = ((), (), s32[]{:S(2)}) async-start(), calls=%async_computation.57 | async-start | bytes 4325376 | tf_op jit(solution)/shard_map/reduce_scatter | solution.py:447
  1596.9 1474.4 %reduce-scatter.64.cloned.1.call-start = ((), (), s32[]{:S(2)}) async-start(), calls=%async_computation.56 | async-start | bytes 4325376 | tf_op jit(solution)/shard_map/reduce_scatter | solution.py:445
  1600.3 1619.9 %reduce-scatter.62.cloned.1.call-start = ((), (), s32[]{:S(2)}) async-start(), calls=%async_computation.55 | async-start | bytes 4325376 | tf_op jit(solution)/shard_map/reduce_scatter | solution.py:443
  1603.2 1756.8 %reduce-scatter.58.cloned.1.call-start = ((), (), s32[]{:S(2)}) async-start(), calls=%async_computation.53 | async-start | bytes 2162688 | tf_op jit(solution)/shard_map/reduce_scatter | solution.py:440
  1605.1 1894.1 %reduce-scatter.56.cloned.1.call-start = ((), (), s32[]{:S(2)}) async-start(), calls=%async_computation.52 | async-start | bytes 2162688 | tf_op jit(solution)/shard_map/reduce_scatter | solution.py:439
  1608.1 2040.0 %reduce-scatter.50.cloned.1.call-start = ((), (), s32[]{:S(2)}) async-start(), calls=%async_computation.49 | async-start | bytes 4325376 | tf_op jit(solution)/shard_map/reduce_scatter | solution.py:435
  1611.1 2311.4 %reduce-scatter.60.cloned.1.call-start = ((), (), s32[]{:S(2)}) async-start(), calls=%async_computation.54 | async-start | bytes 12976128 | tf_op jit(solution)/shard_map/reduce_scatter | solution.py:442
  1639.8 2647.3 %reduce-scatter.70.cloned.1.call-start = ((), (), s32[]{:S(2)}) async-start(), calls=%async_computation.59 | async-start | bytes 17301504 | tf_op jit(solution)/shard_map/reduce_scatter | solution.py:450
  1650.7 3001.5 %reduce-scatter.68.cloned.1.call-start = ((), (), s32[]{:S(2)}) async-start(), calls=%async_computation.58 | async-start | bytes 17301504 | tf_op jit(solution)/shard_map/reduce_scatter | solution.py:449
  1661.5 3264.2 %reduce-scatter.48.cloned.1.call-start = ((), (), s32[]{:S(2)}) async-start(), calls=%async_computation.48 | async-start | bytes 12976128 | tf_op jit(solution)/shard_map/reduce_scatter | solution.py:434
  1690.6 3599.7 %reduce-scatter.54.cloned.1.call-start = ((), (), s32[]{:S(2)}) async-start(), calls=%async_computation.51 | async-start | bytes 17301504 | tf_op jit(solution)/shard_map/reduce_scatter | solution.py:438
  1701.4 3953.9 %reduce-scatter.52.cloned.1.call-start = ((), (), s32[]{:S(2)}) async-start(), calls=%async_computation.50 | async-start | bytes 17301504 | tf_op jit(solution)/shard_map/reduce_scatter | solution.py:437
  (210 other events, 10695.0 us)
Sparse Core Ops, SparseCore 0:
  11.0 71.9 all-gather.29
  86.0 68.1 all-gather.21
  157.7 62.3 all-gather.45
  301.0 56.3 all-gather.35
  360.4 52.6 all-gather.41
  415.9 91.2 all-gather.37
  510.2 75.5 all-gather.39
  722.0 57.0 all-gather.27
  781.9 55.3 all-gather.49
  918.1 56.4 all-gather.53
  977.3 91.0 all-gather.55
  1126.2 76.3 all-gather.57
  1645.2 134.4 reduce-scatter.91
  1782.0 130.7 reduce-scatter.89
  1914.8 130.4 reduce-scatter.87
  2047.6 130.6 reduce-scatter.85
  2180.6 130.7 reduce-scatter.83
  2317.8 175.2 all-reduce.2
  2496.0 138.2 reduce-scatter.73
  2637.2 136.2 reduce-scatter.71
  2776.3 145.9 reduce-scatter.65
  2925.1 146.1 reduce-scatter.63
  3074.2 145.9 reduce-scatter.61
  3223.0 136.9 reduce-scatter.57
  3362.8 136.3 reduce-scatter.55
  3502.1 145.8 reduce-scatter.49
  3651.1 271.4 reduce-scatter.59
  3925.3 361.6 reduce-scatter.69
  4290.0 362.1 reduce-scatter.67
  4655.0 270.6 reduce-scatter.47
  4928.6 361.6 reduce-scatter.53
  5293.1 362.1 reduce-scatter.51
  (15 shorter events, 683.1 us)
where the time goes:
time: 5670 us; the launch traced here: 5660 us
  waiting for transfers between devices  4520 us (80%)
  matrix products  363 us (6%)
  blocking collectives  353 us (6%)
  local copies, waits for them, and re-layouts  298 us (5%)
  other arithmetic  107 us (2%)
    unnamed x57, waiting for transfers between devices  769 us
    reduce_scatter x1, waiting for transfers between devices, local(): lax.psum_scatter(gradients[15], ('seq', 'rows'), scatter_dimension=1, til...  365 us
    reduce_scatter x1, waiting for transfers between devices, local(): lax.psum_scatter(gradients[3], ('seq', 'rows'), scatter_dimension=1, tile...  365 us
    reduce_scatter x1, waiting for transfers between devices, local(): lax.psum_scatter(gradients[16], ('seq', 'rows'), scatter_dimension=1, til...  365 us
    reduce_scatter x1, waiting for transfers between devices, local(): lax.psum_scatter(gradients[4], ('seq', 'rows'), scatter_dimension=1, tile...  365 us
    reduce_scatter x1, waiting for transfers between devices, local(): lax.psum_scatter(gradients[8], ('seq', 'rows'), scatter_dimension=2, tile...  274 us
    reduce_scatter x1, waiting for transfers between devices, local(): lax.psum_scatter(gradients[0], ('seq', 'rows'), scatter_dimension=2, tile...  274 us
    unnamed x437, local copies, waits for them, and re-layouts  164 us
  transfers between devices with their start and end apart: 47, of which 31 were waited for; matrix products, arithmetic and copies ran while one was open for 12% of the time, Pallas kernels for 0%

commit v1 on v0

v1 whole, which is shorter than its diff:
```python
import functools

import jax
import jax.numpy as jnp
from jax import lax
from jax.experimental import pallas as pl
from jax.experimental.pallas import tpu as pltpu
from jax.sharding import PartitionSpec as P

HEADS = 16
HEAD_DIM = 64
EPSILON = 1e-05
MASKED = -1e30
ADAPTER_SCALE = 4.0
SCALING = HEAD_DIM ** (-0.5)
PAD_PREFIX = 32
QUERY_BLOCK = 256

low = jnp.bfloat16
wide = jnp.float32


def dot(left, right, left_axis, right_axis):
    return lax.dot_general(
        left, right, (((left_axis,), (right_axis,)), ((), ())), preferred_element_type=wide
    )


def bit_list(count):
    bits = []
    value = 1
    while value < count:
        bits.append(value)
        value *= 2
    return bits


def swap_pairs(count, bit):
    return [(index, index ^ bit) for index in range(count)]


class Plane:
    def __init__(self, seq, block):
        self.seq = seq
        self.block = block
        bits = bit_list(seq)
        self.axes = bits[:1] + bits[1:][::-1]
        self.depth = len(bits)

    def order(self, micro):
        others = self.axes[1:]
        if micro % 2:
            others = others[::-1]
        return others + self.axes[:1]

    def gather(self, rows, micro):
        width = rows.shape[-1]
        value = rows.reshape((1,) * self.depth + rows.shape)
        for bit in self.order(micro):
            other = lax.ppermute(value, "seq", swap_pairs(self.seq, bit))
            value = jnp.concatenate([value, other], axis=self.axes.index(bit))
        return value.reshape(-1, width)

    def scatter(self, terms, micro):
        half = terms[0][0].shape[0] // 2
        width = terms[0][1].shape[1 - terms[0][2]]

        def part(start):
            total = None
            for left, right, axis in terms:
                value = dot(lax.slice_in_dim(left, start, start + half, axis=0), right, 1, axis)
                total = value if total is None else total + value
            return total

        order = self.order(micro)[::-1]
        sent = lax.ppermute(part(half).astype(low), "seq", swap_pairs(self.seq, order[0]))
        value = part(0) + sent.astype(wide)
        value = value.reshape((2,) * (self.depth - 1) + (self.block, width))
        for bit in order[1:]:
            axis = self.axes.index(bit) - 1
            keep = lax.slice_in_dim(value, 0, 1, axis=axis)
            send = lax.slice_in_dim(value, 1, 2, axis=axis).astype(low)
            sent = lax.ppermute(send, "seq", swap_pairs(self.seq, bit))
            value = keep + sent.astype(wide)
        return value.reshape(self.block, width)

    def relative(self, places, me):
        value = places.reshape((2,) * self.depth + (self.block,))
        for axis in range(self.depth):
            bit = 1 << (self.depth - 1 - axis)
            value = jnp.where((me & bit) != 0, jnp.flip(value, axis), value)
        value = jnp.moveaxis(value, self.depth - 1, 0)
        return value.reshape(-1)


def small_gather(value, axes):
    value = value[None]
    for name, count in axes[::-1]:
        me = lax.axis_index(name)
        for bit in bit_list(count):
            other = lax.ppermute(value, name, swap_pairs(count, bit))
            flip = (me & bit) != 0
            value = jnp.where(
                flip, jnp.concatenate([other, value]), jnp.concatenate([value, other])
            )
    return value


def small_scatter(value, axes):
    for name, count in axes:
        me = lax.axis_index(name)
        for bit in bit_list(count)[::-1]:
            half = value.shape[0] // 2
            flip = (me & bit) != 0
            lower, upper = value[:half], value[half:]
            sent = lax.ppermute(jnp.where(flip, lower, upper), name, swap_pairs(count, bit))
            value = jnp.where(flip, upper, lower) + sent
    return value[0]


def masked_scores(keys, queries, key_ids, query_ids, key_places, query_places, causal):
    scores = dot(keys, queries, 1, 1)
    allowed = key_ids == query_ids
    if causal:
        allowed = allowed & (key_places <= query_places)
    return jnp.where(allowed, scores, MASKED)


def prefix_scores(keys, queries, count):
    scores = dot(keys, queries, 1, 1)
    rows = lax.broadcasted_iota(jnp.int32, scores.shape, 0)
    return jnp.where(rows < count, scores, MASKED)


def attend_kernel(
    heads, offsets, count, causal, q_ref, kv_ref, prefix_ref, kid_ref, qid_ref, kpos_ref, qpos_ref,
    context_ref, logs_ref,
):
    q_at, k_at, v_at = offsets
    step = pl.program_id(0)
    block = context_ref.shape[0]
    rows = pl.ds(pl.multiple_of(step * block, block), block)
    for head in range(heads):
        lanes = slice(head * HEAD_DIM, (head + 1) * HEAD_DIM)
        at = head * HEAD_DIM
        queries = q_ref[rows, q_at + at : q_at + at + HEAD_DIM] * jnp.asarray(SCALING, low)
        keys = kv_ref[:, k_at + at : k_at + at + HEAD_DIM]
        values = kv_ref[:, v_at + at : v_at + at + HEAD_DIM]
        scores = masked_scores(
            keys, queries, kid_ref[...], qid_ref[...], kpos_ref[...], qpos_ref[...], causal
        )
        extra = prefix_scores(prefix_ref[0, :, lanes], queries, count)
        peak = jnp.maximum(
            jnp.max(scores, axis=0, keepdims=True), jnp.max(extra, axis=0, keepdims=True)
        )
        scores = jnp.exp(scores - peak)
        extra = jnp.exp(extra - peak)
        total = jnp.sum(scores, axis=0, keepdims=True) + jnp.sum(extra, axis=0, keepdims=True)
        context = dot(values, scores.astype(low), 0, 0)
        context = context + dot(prefix_ref[1, :, lanes], extra.astype(low), 0, 0)
        context = context / total
        context_ref[:, lanes] = context.T.astype(low)
        logs_ref[head : head + 1, :] = peak + jnp.log(total)


def attend_back_kernel(
    heads, offsets, count, causal, q_ref, kv_ref, prefix_ref, kid_ref, qid_ref, kpos_ref, qpos_ref,
    logs_ref, up_ref, grad_ref, prefix_grad_ref, k_sum, v_sum,
):
    q_at, k_at, v_at = offsets
    step = pl.program_id(0)
    width = heads * HEAD_DIM
    block = up_ref.shape[0]
    rows = pl.ds(pl.multiple_of(step * block, block), block)

    @pl.when(step == 0)
    def _():
        k_sum[...] = jnp.zeros_like(k_sum)
        v_sum[...] = jnp.zeros_like(v_sum)
        prefix_grad_ref[...] = jnp.zeros_like(prefix_grad_ref)

    for head in range(heads):
        lanes = slice(head * HEAD_DIM, (head + 1) * HEAD_DIM)
        at = head * HEAD_DIM
        queries = q_ref[rows, q_at + at : q_at + at + HEAD_DIM] * jnp.asarray(SCALING, low)
        keys = kv_ref[:, k_at + at : k_at + at + HEAD_DIM]
        values = kv_ref[:, v_at + at : v_at + at + HEAD_DIM]
        logs = logs_ref[head : head + 1, :]
        scores = masked_scores(
            keys, queries, kid_ref[...], qid_ref[...], kpos_ref[...], qpos_ref[...], causal
        )
        weights = jnp.exp(scores - logs)
        extra = jnp.exp(prefix_scores(prefix_ref[0, :, lanes], queries, count) - logs)
        up = up_ref[:, lanes]
        dots = dot(values, up, 1, 1)
        extra_dots = dot(prefix_ref[1, :, lanes], up, 1, 1)
        centre = jnp.sum(weights * dots, axis=0, keepdims=True) + jnp.sum(
            extra * extra_dots, axis=0, keepdims=True
        )
        slope = (weights * (dots - centre)).astype(low)
        extra_slope = (extra * (extra_dots - centre)).astype(low)
        query_grad = dot(keys, slope, 0, 0) + dot(prefix_ref[0, :, lanes], extra_slope, 0, 0)
        grad_ref[rows, lanes] = (query_grad * SCALING).T.astype(low)
        k_sum[:, lanes] += dot(slope, queries, 1, 0)
        v_sum[:, lanes] += dot(weights.astype(low), up, 1, 0)
        prefix_grad_ref[0, :, lanes] += dot(extra_slope, queries, 1, 0)
        prefix_grad_ref[1, :, lanes] += dot(extra.astype(low), up, 1, 0)

    @pl.when(step == pl.num_programs(0) - 1)
    def _():
        grad_ref[:, width : 2 * width] = k_sum[...].astype(low)
        grad_ref[:, 2 * width : 3 * width] = v_sum[...].astype(low)


def whole_spec(array):
    rank = len(array.shape)
    return pl.BlockSpec(array.shape, lambda step: (0,) * rank)


def attend_forward(queries, keyvalues, offsets, prefix, count, ids, causal):
    key_ids, query_ids, key_places, query_places = ids
    length = queries.shape[0]
    width = prefix.shape[2]
    heads = width // HEAD_DIM
    block = min(QUERY_BLOCK, length)
    row_spec = pl.BlockSpec((1, block), lambda step: (0, step))
    pairs = length * (keyvalues.shape[0] + PAD_PREFIX) * heads
    return pl.pallas_call(
        functools.partial(attend_kernel, heads, offsets, count, causal),
        grid=(length // block,),
        out_shape=(
            jax.ShapeDtypeStruct((length, width), low),
            jax.ShapeDtypeStruct((heads, length), wide),
        ),
        in_specs=[
            whole_spec(queries),
            whole_spec(keyvalues),
            whole_spec(prefix),
            whole_spec(key_ids),
            row_spec,
            whole_spec(key_places),
            row_spec,
        ],
        out_specs=(
            pl.BlockSpec((block, width), lambda step: (step, 0)),
            pl.BlockSpec((heads, block), lambda step: (0, step)),
        ),
        compiler_params=pltpu.CompilerParams(vmem_limit_bytes=40 * 1024 * 1024),
        cost_estimate=pl.CostEstimate(
            flops=pairs * HEAD_DIM * 4 * 4, bytes_accessed=4 * 2 * length * width, transcendentals=pairs
        ),
    )(queries, keyvalues, prefix, key_ids, query_ids, key_places, query_places)


def attend_backward(queries, keyvalues, offsets, prefix, count, ids, causal, logs, upstream):
    key_ids, query_ids, key_places, query_places = ids
    length = queries.shape[0]
    width = prefix.shape[2]
    heads = width // HEAD_DIM
    block = min(QUERY_BLOCK, length)
    row_spec = pl.BlockSpec((1, block), lambda step: (0, step))
    pairs = length * (keyvalues.shape[0] + PAD_PREFIX) * heads
    return pl.pallas_call(
        functools.partial(attend_back_kernel, heads, offsets, count, causal),
        grid=(length // block,),
        out_shape=(
            jax.ShapeDtypeStruct((length, 3 * width), low),
            jax.ShapeDtypeStruct((2, PAD_PREFIX, width), wide),
        ),
        in_specs=[
            whole_spec(queries),
            whole_spec(keyvalues),
            whole_spec(prefix),
            whole_spec(key_ids),
            row_spec,
            whole_spec(key_places),
            row_spec,
            pl.BlockSpec((heads, block), lambda step: (0, step)),
            pl.BlockSpec((block, width), lambda step: (step, 0)),
        ],
        out_specs=(
            pl.BlockSpec((length, 3 * width), lambda step: (0, 0)),
            pl.BlockSpec((2, PAD_PREFIX, width), lambda step: (0, 0, 0)),
        ),
        scratch_shapes=[
            pltpu.VMEM((length, width), wide),
            pltpu.VMEM((length, width), wide),
        ],
        compiler_params=pltpu.CompilerParams(vmem_limit_bytes=40 * 1024 * 1024),
        cost_estimate=pl.CostEstimate(
            flops=pairs * HEAD_DIM * 10 * 4, bytes_accessed=8 * 2 * length * width, transcendentals=pairs
        ),
    )(queries, keyvalues, prefix, key_ids, query_ids, key_places, query_places, logs, upstream)


def normalized(tensor):
    average = jnp.mean(tensor, axis=-1, keepdims=True)
    centered = tensor - average
    spread = jnp.mean(centered * centered, axis=-1, keepdims=True)
    inverse = lax.rsqrt(spread + EPSILON)
    return centered * inverse, inverse


def layer_norm(tensor, scales):
    return normalized(tensor)[0] * scales[0] + scales[1]


def norm_back(upstream, tensor, scales):
    unit, inverse = normalized(tensor)
    slope = upstream * scales[0]
    grad = inverse * (
        slope
        - jnp.mean(slope, axis=-1, keepdims=True)
        - unit * jnp.mean(slope * unit, axis=-1, keepdims=True)
    )
    return grad, jnp.stack([jnp.sum(upstream * unit, axis=0), jnp.sum(upstream, axis=0)])


def gelu_exact(tensor):
    return jax.nn.gelu(tensor, approximate=False)


def gelu_slope(tensor):
    _, pullback = jax.vjp(gelu_exact, tensor)
    return pullback(jnp.ones_like(tensor))[0]


def outer_sum(lefts, rights):
    total = None
    for left, right in zip(lefts, rights):
        value = dot(left, right, 0, 0)
        total = value if total is None else total + value
    return total


def local(
    seq, ranks,
    source, target, source_segments, target_segments, cotangent,
    encoder_qkv, encoder_output, encoder_prefix, encoder_expand, encoder_contract, encoder_down,
    encoder_up, encoder_norms, decoder_qkv, decoder_output, decoder_prefix, cross_query, cross_kv,
    cross_output, cross_prefix, decoder_expand, decoder_contract, decoder_down, decoder_up,
    decoder_norms,
):
    micro_count, batch_rows, block, width = source.shape
    length = source_segments.shape[2]
    me = lax.axis_index("seq")
    plane = Plane(seq, block)
    stacked = micro_count * batch_rows
    every = range(stacked)
    head_width = width // seq
    slice_cols = encoder_output.shape[1]
    count = encoder_prefix.shape[1]
    hidden = encoder_contract.shape[0] // seq
    adapt = encoder_up.shape[0] // seq
    both = hidden + adapt

    sources = [row for row in source.reshape(stacked, block, width)]
    targets = [row for row in target.reshape(stacked, block, width)]
    upstreams = [row for row in cotangent.reshape(stacked, block, width)]

    places = plane.relative(jnp.arange(length, dtype=jnp.int32), me)
    place_pair = (places[:, None], places[None, :])
    source_ids = [plane.relative(row, me) for row in source_segments.reshape(stacked, length)]
    target_ids = [plane.relative(row, me) for row in target_segments.reshape(stacked, length)]

    def id_set(keys, queries):
        return (keys[:, None], queries[None, :]) + place_pair

    encoder_ids = [id_set(source_ids[m], source_ids[m]) for m in every]
    decoder_ids = [id_set(target_ids[m], target_ids[m]) for m in every]
    cross_ids = [id_set(source_ids[m], target_ids[m]) for m in every]

    def columns(weight):
        return jnp.swapaxes(weight, -1, -2)

    def gather_rows(value):
        return lax.all_gather(value, "rows", axis=0, tiled=False)

    def stack_columns(pieces):
        gathered = gather_rows(jnp.concatenate(pieces, axis=0))
        outs = []
        start = 0
        for piece in pieces:
            size = piece.shape[0]
            outs.append(gathered[:, start : start + size])
            start += size
        return outs

    def flat_columns(gathered, parts):
        value = gathered.reshape(ranks, parts, slice_cols, width)
        return jnp.swapaxes(value, 0, 1).reshape(parts * ranks * slice_cols, width)

    def split_rows(weight):
        value = columns(weight)
        return value.reshape(slice_cols, seq, -1)

    def exchange(value):
        return lax.all_to_all(value, "seq", 1, 1, tiled=False)

    row_pieces = jnp.concatenate(
        [
            split_rows(encoder_output),
            split_rows(decoder_output),
            split_rows(cross_output),
            split_rows(encoder_contract),
            split_rows(encoder_up) * jnp.asarray(ADAPTER_SCALE, low),
            split_rows(decoder_contract),
            split_rows(decoder_up) * jnp.asarray(ADAPTER_SCALE, low),
        ],
        axis=2,
    )
    row_pieces = lax.all_to_all(row_pieces, "seq", 1, 0, tiled=False).reshape(
        seq, slice_cols, -1
    )

    def row_weight(start, size):
        gathered = gather_rows(row_pieces[:, :, start : start + size])
        return jnp.swapaxes(gathered, 0, 1).reshape(width, size)

    qkv_parts = gather_rows(
        jnp.concatenate(
            [
                columns(encoder_qkv).reshape(-1, width),
                columns(decoder_qkv).reshape(-1, width),
            ]
        )
    )
    encoder_in = flat_columns(qkv_parts[:, : 3 * slice_cols], 3)
    decoder_in = flat_columns(qkv_parts[:, 3 * slice_cols :], 3)
    outputs_low = row_weight(0, 3 * head_width)
    encoder_out = outputs_low[:, :head_width]
    decoder_out = outputs_low[:, head_width : 2 * head_width]
    cross_out = outputs_low[:, 2 * head_width :]

    def ffn_in(expand, down):
        gathered = gather_rows(jnp.concatenate([columns(expand), columns(down)]))
        cut = expand.shape[1]
        return jnp.concatenate(
            [gathered[:, :cut].reshape(-1, width), gathered[:, cut:].reshape(-1, width)]
        )

    encoder_one = ffn_in(encoder_expand, encoder_down)
    encoder_two = row_weight(3 * head_width, both)
    cross_parts = gather_rows(
        jnp.concatenate([columns(cross_query), columns(cross_kv).reshape(-1, width)])
    )
    cross_in = flat_columns(cross_parts, 3)
    cross_q_in, cross_kv_in = cross_in[:head_width], cross_in[head_width:]
    decoder_one = ffn_in(decoder_expand, decoder_down)
    decoder_two = row_weight(3 * head_width + both, both)

    prefixes = small_gather(
        jnp.concatenate([encoder_prefix, decoder_prefix, cross_prefix]), [("rows", ranks)]
    )
    prefixes = jnp.moveaxis(prefixes, 0, 2).reshape(6, count, head_width)
    prefixes = jnp.pad(prefixes, ((0, 0), (0, PAD_PREFIX - count), (0, 0)))
    encoder_pre, decoder_pre, cross_pre = prefixes[0:2], prefixes[2:4], prefixes[4:6]

    norm_axes = [("seq", seq), ("rows", ranks)]
    scales = small_gather(
        jnp.concatenate([encoder_norms, decoder_norms]), norm_axes
    )
    scales = jnp.moveaxis(scales, 0, 2).reshape(-1, 2, width).astype(wide)
    norm_count = encoder_norms.shape[0]

    self_offsets = (0, head_width, 2 * head_width)
    cross_offsets = (0, 0, head_width)

    def ffn_forward(rows, weight_one):
        before = dot(rows, weight_one, 1, 1)
        return before, gelu_exact(before).astype(low)

    source_all = [plane.gather(sources[m], m) for m in every]
    target_all = [plane.gather(targets[m], m) for m in every]
    encoder_qkvs = [dot(source_all[m], encoder_in, 1, 1).astype(low) for m in every]
    decoder_qkvs = [dot(target_all[m], decoder_in, 1, 1).astype(low) for m in every]
    encoder_ctx, encoder_logs, resid_one, middle, middle_all = [], [], [], [], []
    decoder_ctx, decoder_logs, resid_three, first, first_all = [], [], [], [], []
    for m in every:
        context, logs = attend_forward(
            encoder_qkvs[m], encoder_qkvs[m], self_offsets, encoder_pre, count, encoder_ids[m], False
        )
        encoder_ctx.append(context)
        encoder_logs.append(logs)
        attended = plane.scatter([(context, encoder_out, 1)], m)
        resid_one.append(sources[m].astype(wide) + attended)
        middle.append(layer_norm(resid_one[m], scales[0]))
        middle_all.append(plane.gather(middle[m].astype(low), m))
    for m in every:
        context, logs = attend_forward(
            decoder_qkvs[m], decoder_qkvs[m], self_offsets, decoder_pre, count, decoder_ids[m], True
        )
        decoder_ctx.append(context)
        decoder_logs.append(logs)
        attended = plane.scatter([(context, decoder_out, 1)], m)
        resid_three.append(targets[m].astype(wide) + attended)
        first.append(layer_norm(resid_three[m], scales[norm_count]))
        first_all.append(plane.gather(first[m].astype(low), m))
    encoder_before, encoder_hidden, resid_two, memory_all = [], [], [], []
    for m in every:
        before, after = ffn_forward(middle_all[m], encoder_one)
        encoder_before.append(before)
        encoder_hidden.append(after)
        branch = plane.scatter([(after, encoder_two, 1)], m)
        resid_two.append(middle[m] + branch)
        memory = layer_norm(resid_two[m], scales[1])
        memory_all.append(plane.gather(memory.astype(low), m))
    cross_q = [dot(first_all[m], cross_q_in, 1, 1).astype(low) for m in every]
    cross_kvs = [dot(memory_all[m], cross_kv_in, 1, 1).astype(low) for m in every]
    cross_ctx, cross_logs, resid_four, second, second_all = [], [], [], [], []
    for m in every:
        context, logs = attend_forward(
            cross_q[m], cross_kvs[m], cross_offsets, cross_pre, count, cross_ids[m], False
        )
        cross_ctx.append(context)
        cross_logs.append(logs)
        crossed = plane.scatter([(context, cross_out, 1)], m)
        resid_four.append(first[m] + crossed)
        second.append(layer_norm(resid_four[m], scales[norm_count + 1]))
        second_all.append(plane.gather(second[m].astype(low), m))
    decoder_before, decoder_hidden, resid_five, results = [], [], [], []
    for m in every:
        before, after = ffn_forward(second_all[m], decoder_one)
        decoder_before.append(before)
        decoder_hidden.append(after)
        branch = plane.scatter([(after, decoder_two, 1)], m)
        resid_five.append(second[m] + branch)
        results.append(layer_norm(resid_five[m], scales[norm_count + 2]).astype(low))

    def scatter_ranks(value):
        return lax.psum_scatter(value.astype(low), "rows", scatter_dimension=0, tiled=False)

    def reduce_columns(grad, parts):
        value = grad.reshape(parts, ranks, slice_cols, width)
        return scatter_ranks(jnp.swapaxes(value, 0, 1))

    def reduce_rows(grad):
        value = grad.reshape(seq, ranks, slice_cols, -1)
        return scatter_ranks(jnp.swapaxes(value, 0, 1))

    def reduce_ffn_in(grad):
        value = jnp.concatenate(
            [grad[:hidden].reshape(ranks, -1, width), grad[hidden:].reshape(ranks, -1, width)],
            axis=1,
        )
        return scatter_ranks(value)

    def ffn_backward(low_all, befores, weight_one, weight_two, m):
        slope = dot(low_all, weight_two, 1, 0) * gelu_slope(befores[m])
        slope = slope.astype(low)
        return slope, plane.scatter([(slope, weight_one, 0)], m)

    norm_grads = {}

    def norm_step(index, upstream_rows, residuals):
        grads, sums = [], None
        for m in every:
            grad, pair = norm_back(upstream_rows[m], residuals[m], scales[index])
            grads.append(grad)
            sums = pair if sums is None else sums + pair
        norm_grads[index] = sums
        return grads

    third_in = norm_step(norm_count + 2, [u.astype(wide) for u in upstreams], resid_five)
    third_all = [plane.gather(third_in[m].astype(low), m) for m in every]
    slopes, second_up = [], []
    for m in every:
        slope, from_ffn = ffn_backward(third_all[m], decoder_before, decoder_one, decoder_two, m)
        slopes.append(slope)
        second_up.append(third_in[m] + from_ffn)
    decoder_two_grad = reduce_rows(outer_sum(third_all, decoder_hidden))
    decoder_one_grad = reduce_ffn_in(outer_sum(slopes, second_all))

    second_in = norm_step(norm_count + 1, second_up, resid_four)
    second_low = [plane.gather(second_in[m].astype(low), m) for m in every]
    cross_grads, cross_pre_grad, first_up, memory_up = [], None, [], []
    for m in every:
        context_grad = dot(second_low[m], cross_out, 1, 0).astype(low)
        grads, pre = attend_backward(
            cross_q[m], cross_kvs[m], cross_offsets, cross_pre, count, cross_ids[m], False,
            cross_logs[m], context_grad,
        )
        cross_grads.append(grads)
        cross_pre_grad = pre if cross_pre_grad is None else cross_pre_grad + pre
        memory_up.append(plane.scatter([(grads[:, head_width:], cross_kv_in, 0)], m))
        first_up.append(
            second_in[m] + plane.scatter([(grads[:, :head_width], cross_q_in, 0)], m)
        )
    cross_out_grad = reduce_rows(outer_sum(second_low, cross_ctx))
    cross_in_grad = reduce_columns(
        jnp.concatenate(
            [
                outer_sum([g[:, :head_width] for g in cross_grads], first_all),
                outer_sum([g[:, head_width:] for g in cross_grads], memory_all),
            ]
        ),
        3,
    )

    memory_in = norm_step(1, memory_up, resid_two)
    first_in = norm_step(norm_count, first_up, resid_three)
    memory_low = [plane.gather(memory_in[m].astype(low), m) for m in every]
    first_low = [plane.gather(first_in[m].astype(low), m) for m in every]

    slopes, middle_up = [], []
    for m in every:
        slope, from_ffn = ffn_backward(memory_low[m], encoder_before, encoder_one, encoder_two, m)
        slopes.append(slope)
        middle_up.append(memory_in[m] + from_ffn)
    encoder_two_grad = reduce_rows(outer_sum(memory_low, encoder_hidden))
    encoder_one_grad = reduce_ffn_in(outer_sum(slopes, middle_all))

    def self_backward(low_all, out_weight, in_weight, qkvs, prefix, ids, causal, logs, rows_in):
        grads_all, prefix_sum, totals = [], None, []
        for m in every:
            context_grad = dot(low_all[m], out_weight, 1, 0).astype(low)
            grads, pre = attend_backward(
                qkvs[m], qkvs[m], self_offsets, prefix, count, ids[m], causal, logs[m], context_grad
            )
            grads_all.append(grads)
            prefix_sum = pre if prefix_sum is None else prefix_sum + pre
            totals.append(rows_in[m] + plane.scatter([(grads, in_weight, 0)], m))
        return grads_all, prefix_sum, totals

    decoder_grads, decoder_pre_grad, target_grads = self_backward(
        first_low, decoder_out, decoder_in, decoder_qkvs, decoder_pre, decoder_ids, True,
        decoder_logs, first_in,
    )
    decoder_out_grad = reduce_rows(outer_sum(first_low, decoder_ctx))
    decoder_in_grad = reduce_columns(outer_sum(decoder_grads, target_all), 3)

    middle_in = norm_step(0, middle_up, resid_one)
    middle_low = [plane.gather(middle_in[m].astype(low), m) for m in every]
    encoder_grads, encoder_pre_grad, source_grads = self_backward(
        middle_low, encoder_out, encoder_in, encoder_qkvs, encoder_pre, encoder_ids, False,
        encoder_logs, middle_in,
    )
    encoder_out_grad = reduce_rows(outer_sum(middle_low, encoder_ctx))
    encoder_in_grad = reduce_columns(outer_sum(encoder_grads, source_all), 3)

    def give_back(pieces):
        value = jnp.concatenate(pieces, axis=2)
        return lax.all_to_all(value, "seq", 0, 1, tiled=False)

    decoder_rows = give_back([decoder_two_grad, cross_out_grad, decoder_out_grad])
    encoder_rows = give_back([encoder_two_grad, encoder_out_grad])

    def row_grad(value, start, size, scale=None):
        piece = value[:, :, start : start + size].astype(wide)
        if scale is not None:
            piece = piece * scale
        return piece.reshape(slice_cols, -1).T

    def column_grad(value):
        return jnp.swapaxes(value.astype(wide), -1, -2)

    prefix_total = jnp.concatenate([encoder_pre_grad, decoder_pre_grad, cross_pre_grad])[:, :count]
    prefix_total = jnp.moveaxis(prefix_total.reshape(6, count, ranks, slice_cols), 2, 0)
    prefix_total = small_scatter(prefix_total, [("rows", ranks)])
    norm_total = jnp.stack([norm_grads[index] for index in sorted(norm_grads)])
    norm_total = jnp.moveaxis(norm_total.reshape(-1, 2, seq * ranks, slice_cols), 2, 0)
    norm_total = small_scatter(norm_total, norm_axes)

    cut = encoder_expand.shape[1]
    shape_out = source.shape
    return (
        jnp.stack(results).reshape(shape_out),
        jnp.stack(source_grads).reshape(shape_out),
        jnp.stack(target_grads).reshape(shape_out),
        column_grad(encoder_in_grad),
        row_grad(encoder_rows, both, head_width),
        prefix_total[0:2],
        column_grad(encoder_one_grad[:cut]),
        row_grad(encoder_rows, 0, hidden),
        column_grad(encoder_one_grad[cut:]),
        row_grad(encoder_rows, hidden, adapt, ADAPTER_SCALE),
        norm_total[:norm_count],
        column_grad(decoder_in_grad),
        row_grad(decoder_rows, both + head_width, head_width),
        prefix_total[2:4],
        column_grad(cross_in_grad[0]),
        column_grad(cross_in_grad[1:]),
        row_grad(decoder_rows, both, head_width),
        prefix_total[4:6],
        column_grad(decoder_one_grad[:cut]),
        row_grad(decoder_rows, 0, hidden),
        column_grad(decoder_one_grad[cut:]),
        row_grad(decoder_rows, hidden, adapt, ADAPTER_SCALE),
        norm_total[norm_count:],
    )


def solution(mesh):
    rows = P(None, "rows", "seq", None)
    ids = P(None, "rows", None)
    flat = P(None, ("seq", "rows"))
    deep = P(None, None, ("seq", "rows"))
    weights = (
        deep, flat, deep, flat, flat, flat, flat, deep, deep, flat, deep, flat, deep, flat, deep,
        flat, flat, flat, flat, deep,
    )
    body = functools.partial(local, mesh.shape["seq"], mesh.shape["rows"])
    return jax.shard_map(
        body,
        mesh=mesh,
        in_specs=(rows, rows, ids, ids, rows) + weights,
        out_specs=(rows, rows, rows) + weights,
        check_vma=False,
    )
```

time: 5670 us -> 1100 us (0.19)
  waiting for transfers between devices: 4520 us -> 370 us
  blocking collectives: 353 us -> 35.6 us
  matrix products: 363 us -> 134 us
  local copies, waits for them, and re-layouts: 298 us -> 119 us
  starting transfers between devices: 3.63 us -> 140 us
  Pallas kernels: 0 us -> 103 us
  other arithmetic: 107 us -> 169 us
    reduce_scatter x16 -> x8, waiting for transfers between devices: 3150 us -> 9.03 us  [scatter_ranks(): lax.psum_scatter(value.astype(low), 'rows', scatter_dimension=0, tiled=Fa...]
    unnamed x57 -> x15, waiting for transfers between devices: 769 us -> 0.23 us
    all_gather x21 -> x5, waiting for transfers between devices: 595 us -> 22.2 us  [gather_rows(): return lax.all_gather(value, 'rows', axis=0, tiled=False)]
    ppermute x0 -> x146, waiting for transfers between devices: none -> 337 us  [the longest x66 158 us: gather(): other = lax.ppermute(value, 'seq', swap_pairs(self.seq, bit))]
    all_gather x5 -> x2, blocking collectives: 353 us -> 35.6 us  [gather_rows(): return lax.all_gather(value, 'rows', axis=0, tiled=False)]
    dot_general x96 -> x88, matrix products: 363 us -> 134 us  [dot(): lax.dot_general(left, right, (((left_axis,), (right_axis,)), ((), ())), p...]
    unnamed x437 -> x786, local copies, waits for them, and re-layouts: 164 us -> 36.5 us
    ppermute x0 -> x146, starting transfers between devices: none -> 127 us  [the longest x66 54.9 us: gather(): other = lax.ppermute(value, 'seq', swap_pairs(self.seq, bit))]
  transfers between devices with their start and end apart: 47 -> 163, of which waited for: 31 -> 77; matrix products, arithmetic and copies ran while one was open for 12% -> 34% of each run, Pallas kernels for 0% -> 9%
where the time goes in v1:
time: 1100 us; the launch traced here: 1090 us
  waiting for transfers between devices  370 us (34%)
  other arithmetic  169 us (15%)
  starting transfers between devices  140 us (13%)
  matrix products  134 us (12%)
  local copies, waits for them, and re-layouts  119 us (11%)
  Pallas kernels  103 us (9%)
  blocking collectives  35.6 us (3%)
  between operations  21.2 us (2%)
    ppermute x66, waiting for transfers between devices, gather(): other = lax.ppermute(value, 'seq', swap_pairs(self.seq, bit))  158 us
    ppermute x44, waiting for transfers between devices, scatter(): sent = lax.ppermute(send, 'seq', swap_pairs(self.seq, bit))  150 us
    dot_general x88, matrix products, dot(): lax.dot_general(left, right, (((left_axis,), (right_axis,)), ((), ())), p...  134 us
    concatenate x66, other arithmetic, gather(): value = jnp.concatenate([value, other], axis=self.axes.index(bit))  66.1 us
    pallas_call x6, Pallas kernels, attend_backward(): pl.pallas_call(functools.partial(attend_back_kernel, heads, offsets, coun...  58.2 us
    ppermute x66, starting transfers between devices, gather(): other = lax.ppermute(value, 'seq', swap_pairs(self.seq, bit))  54.9 us
    ppermute x44, starting transfers between devices, scatter(): sent = lax.ppermute(send, 'seq', swap_pairs(self.seq, bit))  50.9 us
    pallas_call x6, Pallas kernels, attend_forward(): pl.pallas_call(functools.partial(attend_kernel, heads, offsets, count, ca...  44.7 us
  transfers between devices with their start and end apart: 163, of which 77 were waited for; matrix products, arithmetic and copies ran while one was open for 34% of the time, Pallas kernels for 9%

profile of v1, /device:TPU:0, one launch (start us, length us, event | category | flops | bytes accessed | tf_op | source)
XLA Modules:
  0.0 1091.8 jit_solution(17680804987242091845)
XLA Ops:
  83.7 17.9 %all-gather.1 = bf16[32,32,384]{2,1,0:T(8,128)(2,1)S(1)} all-gather(bf16[8,32,384]{2,1,0:T(8,128)(2,1)S(1)} %slice.1020), channel_id=3, replica_groups=mesh['seq'=8,'rows'=4] {'rows'}, dimensions={0}, use_global_device_ids=true | all-gather | bytes 983040 | tf_op jit(solution)/shard_map/all_gather | solution.py:377
  120.1 7.5 shard_map.420
  129.5 7.3 shard_map.417
  139.9 7.4 shard_map.419
  149.8 7.8 shard_map.416
  160.8 11.3 %collective-permute-done.53 = bf16[1,2,128,1024]{3,2,1,0:T(8,128)(2,1)S(1)} collective-permute-done((bf16[1,2,128,1024]{3,2,1,0:T(8,128)(2,1)S(1)}, bf16[1,2,128,1024]{3,2,1,0:T(8,128)(2,1)S(1)}, u32[]{:S(2)}, u32[]{:S(2)}) %collective-permute-start.53) | collective-permute-done | bytes 524320 | tf_op jit(solution)/shard_map/ppermute | solution.py:83
  219.6 11.4 %collective-permute-done.23 = bf16[1,2,1,128,1024]{4,3,2,1,0:T(8,128)(2,1)S(1)} collective-permute-done((bf16[1,2,1,128,1024]{4,3,2,1,0:T(8,128)(2,1)S(1)}, bf16[1,2,1,128,1024]{4,3,2,1,0:T(8,128)(2,1)S(1)}, u32[]{:S(2)}, u32[]{:S(2)}) %collective-permute-start.23) | collective-permute-done | bytes 524320 | tf_op jit(solution)/shard_map/ppermute | solution.py:60
  233.7 9.0 multiply_convert_fusion.5
  245.4 9.1 multiply_convert_fusion.7
  304.0 17.7 %all-gather.2 = bf16[384,1024]{1,0:T(8,128)(2,1)S(1)} all-gather(bf16[96,1024]{1,0:T(8,128)(2,1)S(1)} %pad_maximum_fusion.74), channel_id=4, replica_groups=mesh['seq'=8,'rows'=4] {'rows'}, dimensions={0}, use_global_device_ids=true | all-gather | bytes 983040 | tf_op jit(solution)/shard_map/all_gather | solution.py:377
  325.7 7.3 collective-permute-done.29
  335.5 7.5 shard_map.421
  357.6 10.7 collective-permute-done.65
  396.3 12.2 %collective-permute-done.68 = bf16[1,1,2,128,1024]{4,3,2,1,0:T(8,128)(2,1)S(1)} collective-permute-done((bf16[1,1,2,128,1024]{4,3,2,1,0:T(8,128)(2,1)S(1)}, bf16[1,1,2,128,1024]{4,3,2,1,0:T(8,128)(2,1)S(1)}, u32[]{:S(2)}, u32[]{:S(2)}) %collective-permute-start.68) | collective-permute-done | bytes 524320 | tf_op jit(solution)/shard_map/ppermute | solution.py:60
  417.9 22.2 %all-gather.21.cloned.1.call-done = bf16[32,32,576]{2,1,0:T(8,128)(2,1)} async-done(((bf16[8,32,576]{2,1,0:T(8,128)(2,1)}), bf16[32,32,576]{2,1,0:T(8,128)(2,1)}) %all-gather.21.cloned.1.call-update) | async-done | bytes 1179664 | tf_op jit(solution)/shard_map/all_gather | solution.py:377
  466.4 10.0 collective-permute-done.71
  499.6 12.1 %collective-permute-done.98 = bf16[1,1,2,128,1024]{4,3,2,1,0:T(8,128)(2,1)S(1)} collective-permute-done((bf16[1,1,2,128,1024]{4,3,2,1,0:T(8,128)(2,1)S(1)}, bf16[1,1,2,128,1024]{4,3,2,1,0:T(8,128)(2,1)S(1)}, u32[]{:S(2)}, u32[]{:S(2)}) %collective-permute-start.98) | collective-permute-done | bytes 524320 | tf_op jit(solution)/shard_map/ppermute | solution.py:60
  516.1 10.2 collective-permute-done.74
  539.1 10.1 collective-permute-done.101
  573.3 10.2 collective-permute-done.80
  588.0 9.8 shard_map.422
  599.9 12.9 %collective-permute-done.104 = bf16[1,1,2,128,1024]{4,3,2,1,0:T(8,128)(2,1)S(1)} collective-permute-done((bf16[1,1,2,128,1024]{4,3,2,1,0:T(8,128)(2,1)S(1)}, bf16[1,1,2,128,1024]{4,3,2,1,0:T(8,128)(2,1)S(1)}, u32[]{:S(2)}, u32[]{:S(2)}) %collective-permute-start.104) | collective-permute-done | bytes 524320 | tf_op jit(solution)/shard_map/ppermute | solution.py:60
  618.9 10.0 collective-permute-done.83
  651.8 9.6 shard_map.424
  677.7 10.2 collective-permute-done.107
  731.9 7.8 collective-permute-done.134
  746.6 10.3 collective-permute-done.125
  764.5 9.8 shard_map.427
  779.3 9.9 shard_map.426
  889.9 9.7 shard_map.423
  1007.4 9.5 shard_map.425
  1059.1 10.5 collective-permute-done.119
  (1593 shorter events, 731.9 us)
Async XLA Ops:
  7.3 109.4 %all-gather.13.cloned.1.call-start = ((), (), s32[]{:S(2)}) async-start(), calls=%async_computation.19 | async-start | bytes 1966080 | tf_op jit(solution)/shard_map/all_gather | solution.py:377
  10.3 42.3 %collective-permute-start.49 = (bf16[1,1,1,128,1024]{4,3,2,1,0:T(8,128)(2,1)S(1)}, bf16[1,1,1,128,1024]{4,3,2,1,0:T(8,128)(2,1)}, u32[]{:S(2)}, u32[]{:S(2)}) collective-permute-start(bf16[1,1,1,128,1024]{4,3,2,1,0:T(8,128)(2,1)S(1)} %get-tuple-element.322), channel_id=1, source_target_pairs={{0,8},{4,12},{8,0},{12,4},{16,24},{20,28},{24,16},{28,20},{1,9},{5... | collective-permute-start | bytes 786440 | tf_op jit(solution)/shard_map/ppermute | solution.py:60
  13.4 27.5 %collective-permute-start.3 = (bf16[1,6,30,32]{3,1,2,0:T(8,128)(2,1)S(1)}, bf16[1,6,30,32]{3,1,2,0:T(8,128)(2,1)}, u32[]{:S(2)}, u32[]{:S(2)}) collective-permute-start(bf16[1,6,30,32]{3,1,2,0:T(8,128)(2,1)S(1)} %maximum_bitcast_fusion.5), channel_id=1, source_target_pairs={{0,1},{1,0},{2,3},{3,2},{4,5},{5,4},{6,7},{7,6},{8,9},{9,8},{10,11... | collective-permute-start | bytes 34568 | tf_op jit(solution)/shard_map/ppermute | solution.py:101
  17.2 57.6 %all-to-all-start = ((bf16[1,32,8,1536]{3,1,0,2:T(8,128)(2,1)}), bf16[1,32,8,1536]{3,1,0,2:T(8,128)(2,1)}, u32[]{:S(2)}, u32[]{:S(2)}) async-start(bf16[1,32,8,1536]{3,1,0,2:T(8,128)(2,1)} %copy.318), calls=%async_computation | async-start | bytes 1572864 | tf_op jit(solution)/shard_map/all_to_all | solution.py:412
  21.6 188.4 %all-gather.15.cloned.1.call-start = ((), (), s32[]{:S(2)}) async-start(), calls=%async_computation.20 | async-start | bytes 1474560 | tf_op jit(solution)/shard_map/all_gather | solution.py:377
  21.6 34.3 %collective-permute-start.16 = (bf16[1,1,1,128,1024]{4,3,2,1,0:T(8,128)(2,1)S(1)}, bf16[1,1,1,128,1024]{4,3,2,1,0:T(8,128)(2,1)}, u32[]{:S(2)}, u32[]{:S(2)}) collective-permute-start(bf16[1,1,1,128,1024]{4,3,2,1,0:T(8,128)(2,1)S(1)} %get-tuple-element.321), channel_id=1, source_target_pairs={{0,16},{4,20},{8,24},{12,28},{16,0},{20,4},{24,8},{28,12},{1,17},{... | collective-permute-start | bytes 786440 | tf_op jit(solution)/shard_map/ppermute | solution.py:60
  24.7 34.1 %collective-permute-start.40 = (bf16[1,1,1,128,1024]{4,3,2,1,0:T(8,128)(2,1)}, bf16[1,1,1,128,1024]{4,3,2,1,0:T(8,128)(2,1)}, u32[]{:S(2)}, u32[]{:S(2)}) collective-permute-start(bf16[1,1,1,128,1024]{4,3,2,1,0:T(8,128)(2,1)} %get-tuple-element.326), channel_id=1, source_target_pairs={{0,8},{4,12},{8,0},{12,4},{16,24},{20,28},{24,16},{28,20},{1,9},{5... | collective-permute-start | bytes 786440 | tf_op jit(solution)/shard_map/ppermute | solution.py:60
  27.1 186.7 %all-gather.17.cloned.1.call-start = ((), (), s32[]{:S(2)}) async-start(), calls=%async_computation.21 | async-start | bytes 1638400 | tf_op jit(solution)/shard_map/all_gather | solution.py:377
  71.8 32.9 %collective-permute-start.51 = (bf16[1,2,2,128,1024]{4,3,2,1,0:T(8,128)(2,1)}, bf16[1,2,2,128,1024]{4,3,2,1,0:T(8,128)(2,1)}, u32[]{:S(2)}, u32[]{:S(2)}) collective-permute-start(bf16[1,2,2,128,1024]{4,3,2,1,0:T(8,128)(2,1)} %pad_maximum_fusion.34), channel_id=1, source_target_pairs={{0,4},{4,0},{8,12},{12,8},{16,20},{20,16},{24,28},{28,24},{1,5},{5... | collective-permute-start | bytes 3145736 | tf_op jit(solution)/shard_map/ppermute | solution.py:60
  74.8 32.9 %collective-permute-start.18 = (bf16[1,2,2,128,1024]{4,3,2,1,0:T(8,128)(2,1)}, bf16[1,2,2,128,1024]{4,3,2,1,0:T(8,128)(2,1)}, u32[]{:S(2)}, u32[]{:S(2)}) collective-permute-start(bf16[1,2,2,128,1024]{4,3,2,1,0:T(8,128)(2,1)} %pad_maximum_fusion.28), channel_id=1, source_target_pairs={{0,4},{4,0},{8,12},{12,8},{16,20},{20,16},{24,28},{28,24},{1,5},{5... | collective-permute-start | bytes 3145736 | tf_op jit(solution)/shard_map/ppermute | solution.py:60
  80.7 29.9 %collective-permute-start.42 = (bf16[1,2,2,128,1024]{4,3,2,1,0:T(8,128)(2,1)}, bf16[1,2,2,128,1024]{4,3,2,1,0:T(8,128)(2,1)}, u32[]{:S(2)}, u32[]{:S(2)}) collective-permute-start(bf16[1,2,2,128,1024]{4,3,2,1,0:T(8,128)(2,1)} %pad_maximum_fusion.32), channel_id=1, source_target_pairs={{0,4},{4,0},{8,12},{12,8},{16,20},{20,16},{24,28},{28,24},{1,5},{5... | collective-permute-start | bytes 3145736 | tf_op jit(solution)/shard_map/ppermute | solution.py:60
  83.6 30.2 %collective-permute-start.2 = (bf16[1,2,2,128,1024]{4,3,2,1,0:T(8,128)(2,1)}, bf16[1,2,2,128,1024]{4,3,2,1,0:T(8,128)(2,1)}, u32[]{:S(2)}, u32[]{:S(2)}) collective-permute-start(bf16[1,2,2,128,1024]{4,3,2,1,0:T(8,128)(2,1)} %pad_maximum_fusion.26), channel_id=1, source_target_pairs={{0,4},{4,0},{8,12},{12,8},{16,20},{20,16},{24,28},{28,24},{1,5},{5... | collective-permute-start | bytes 3145736 | tf_op jit(solution)/shard_map/ppermute | solution.py:60
  104.6 309.3 %all-gather.19.cloned.1.call-start = ((), (), s32[]{:S(2)}) async-start(), calls=%async_computation.22 | async-start | bytes 1474560 | tf_op jit(solution)/shard_map/all_gather | solution.py:377
  128.1 29.5 %collective-permute-start.52 = (bf16[512,1024]{1,0:T(8,128)(2,1)S(1)}, bf16[512,1024]{1,0:T(8,128)(2,1)S(1)}, u32[]{:S(2)}, u32[]{:S(2)}) collective-permute-start(bf16[512,1024]{1,0:T(8,128)(2,1)S(1)} %convolution_convert_fusion.3), channel_id=1, source_target_pairs={{0,4},{4,0},{8,12},{12,8},{16,20},{20,16},{24,28},{28,24},{1,5},{5... | collective-permute-start | bytes 3145736 | tf_op jit(solution)/shard_map/ppermute | solution.py:76
  294.2 29.2 %collective-permute-start.48 = (bf16[1,2,2,128,1024]{4,3,2,1,0:T(8,128)(2,1)S(1)}, bf16[1,2,2,128,1024]{4,3,2,1,0:T(8,128)(2,1)S(1)}, u32[]{:S(2)}, u32[]{:S(2)}) collective-permute-start(bf16[1,2,2,128,1024]{4,3,2,1,0:T(8,128)(2,1)S(1)} %pad_maximum_fusion.33), channel_id=1, source_target_pairs={{0,4},{4,0},{8,12},{12,8},{16,20},{20,16},{24,28},{28,24},{1,5},{5... | collective-permute-start | bytes 3145736 | tf_op jit(solution)/shard_map/ppermute | solution.py:60
  377.5 62.5 %all-gather.21.cloned.1.call-start = ((), (), s32[]{:S(2)}) async-start(), calls=%async_computation.23 | async-start | bytes 1638400 | tf_op jit(solution)/shard_map/all_gather | solution.py:377
  387.6 440.9 %reduce-scatter.25.cloned.1.call-start = ((), (), s32[]{:S(2)}) async-start(), calls=%async_computation.18 | async-start | bytes 1474560 | tf_op jit(solution)/shard_map/reduce_scatter | solution.py:531
  410.7 32.2 %collective-permute-start.69 = (bf16[1,2,2,128,1024]{4,3,2,1,0:T(8,128)(2,1)}, bf16[1,2,2,128,1024]{4,3,2,1,0:T(8,128)(2,1)}, u32[]{:S(2)}, u32[]{:S(2)}) collective-permute-start(bf16[1,2,2,128,1024]{4,3,2,1,0:T(8,128)(2,1)} %pad_maximum_fusion.37), channel_id=1, source_target_pairs={{0,4},{4,0},{8,12},{12,8},{16,20},{20,16},{24,28},{28,24},{1,5},{5... | collective-permute-start | bytes 3145736 | tf_op jit(solution)/shard_map/ppermute | solution.py:60
  412.8 28.8 %collective-permute-start.35 = (bf16[1,2,1,128,1024]{4,3,2,1,0:T(8,128)(2,1)}, bf16[1,2,1,128,1024]{4,3,2,1,0:T(8,128)(2,1)}, u32[]{:S(2)}, u32[]{:S(2)}) collective-permute-start(bf16[1,2,1,128,1024]{4,3,2,1,0:T(8,128)(2,1)} %pad_maximum_fusion.54), channel_id=1, source_target_pairs={{0,8},{4,12},{8,0},{12,4},{16,24},{20,28},{24,16},{28,20},{1,9},{5... | collective-permute-start | bytes 1572872 | tf_op jit(solution)/shard_map/ppermute | solution.py:60
  633.3 213.0 %reduce-scatter.23.cloned.1.call-start = ((), (), s32[]{:S(2)}) async-start(), calls=%async_computation.17 | async-start | bytes 983040 | tf_op jit(solution)/shard_map/reduce_scatter | solution.py:531
  746.6 195.2 %reduce-scatter.17.cloned.1.call-start = ((), (), s32[]{:S(2)}) async-start(), calls=%async_computation.14 | async-start | bytes 983040 | tf_op jit(solution)/shard_map/reduce_scatter | solution.py:531
  760.5 39.7 %collective-permute-start.111 = (bf16[1,2,2,128,1024]{4,3,2,1,0:T(8,128)(2,1)}, bf16[1,2,2,128,1024]{4,3,2,1,0:T(8,128)(2,1)}, u32[]{:S(2)}, u32[]{:S(2)}) collective-permute-start(bf16[1,2,2,128,1024]{4,3,2,1,0:T(8,128)(2,1)} %pad_maximum_fusion.44), channel_id=1, source_target_pairs={{0,4},{4,0},{8,12},{12,8},{16,20},{20,16},{24,28},{28,24},{1,5},{5... | collective-permute-start | bytes 3145736 | tf_op jit(solution)/shard_map/ppermute | solution.py:60
  791.2 188.4 %all-reduce.6.cloned.1.call-start = ((), (), s32[]{:S(2)}) async-start(), calls=%async_computation.24 | async-start | bytes 5242880
  809.5 171.8 %reduce-scatter.19.cloned.1.call-start = ((), (), s32[]{:S(2)}) async-start(), calls=%async_computation.15 | async-start | bytes 327680 | tf_op jit(solution)/shard_map/reduce_scatter | solution.py:531
  845.4 135.9 %reduce-scatter.21.cloned.1.call-start = ((), (), s32[]{:S(2)}) async-start(), calls=%async_computation.16 | async-start | bytes 327680 | tf_op jit(solution)/shard_map/reduce_scatter | solution.py:531
  872.3 30.8 %collective-permute-start.112 = (bf16[512,1024]{1,0:T(8,128)(2,1)}, bf16[512,1024]{1,0:T(8,128)(2,1)}, u32[]{:S(2)}, u32[]{:S(2)}) collective-permute-start(bf16[512,1024]{1,0:T(8,128)(2,1)} %convolution_convert_fusion.11), channel_id=1, source_target_pairs={{0,4},{4,0},{8,12},{12,8},{16,20},{20,16},{24,28},{28,24},{1,5},{5... | collective-permute-start | bytes 3145736 | tf_op jit(solution)/shard_map/ppermute | solution.py:76
  886.7 103.2 %reduce-scatter.15.cloned.1.call-start = ((), (), s32[]{:S(2)}) async-start(), calls=%async_computation.13 | async-start | bytes 1474560 | tf_op jit(solution)/shard_map/reduce_scatter | solution.py:531
  928.7 30.1 %collective-permute-start.129 = (bf16[1,1,128,1024]{3,2,1,0:T(8,128)(2,1)}, bf16[1,1,128,1024]{3,2,1,0:T(8,128)(2,1)}, u32[]{:S(2)}, u32[]{:S(2)}) collective-permute-start(bf16[1,1,128,1024]{3,2,1,0:T(8,128)(2,1)} %slice.1633), channel_id=1, source_target_pairs={{0,16},{4,20},{8,24},{12,28},{16,0},{20,4},{24,8},{28,12},{1,17},{... | collective-permute-start | bytes 786440 | tf_op jit(solution)/shard_map/ppermute | solution.py:83
  936.7 28.0 %collective-permute-start.138 = (bf16[1,1,128,1024]{3,2,1,0:T(8,128)(2,1)}, bf16[1,1,128,1024]{3,2,1,0:T(8,128)(2,1)}, u32[]{:S(2)}, u32[]{:S(2)}) collective-permute-start(bf16[1,1,128,1024]{3,2,1,0:T(8,128)(2,1)} %slice.1631), channel_id=1, source_target_pairs={{0,8},{4,12},{8,0},{12,4},{16,24},{20,28},{24,16},{28,20},{1,9},{5... | collective-permute-start | bytes 786440 | tf_op jit(solution)/shard_map/ppermute | solution.py:83
  940.9 27.9 %collective-permute-start.96 = (bf16[1,1,128,1024]{3,2,1,0:T(8,128)(2,1)}, bf16[1,1,128,1024]{3,2,1,0:T(8,128)(2,1)}, u32[]{:S(2)}, u32[]{:S(2)}) collective-permute-start(bf16[1,1,128,1024]{3,2,1,0:T(8,128)(2,1)} %slice.1639), channel_id=1, source_target_pairs={{0,16},{4,20},{8,24},{12,28},{16,0},{20,4},{24,8},{28,12},{1,17},{... | collective-permute-start | bytes 786440 | tf_op jit(solution)/shard_map/ppermute | solution.py:83
  987.2 58.2 %reduce-scatter.13.cloned.1.call-start = ((), (), s32[]{:S(2)}) async-start(), calls=%async_computation.12 | async-start | bytes 327680 | tf_op jit(solution)/shard_map/reduce_scatter | solution.py:531
  1025.5 52.6 %reduce-scatter.11.cloned.1.call-start = ((), (), s32[]{:S(2)}) async-start(), calls=%async_computation.11 | async-start | bytes 983040 | tf_op jit(solution)/shard_map/reduce_scatter | solution.py:531
  (526 other events, 8972.3 us)
Sparse Core Ops, SparseCore 0:
  10.3 40.0 all-gather.12
  52.5 29.8 all-gather.14
  104.8 31.0 all-gather.16
  377.7 29.0 all-gather.18
  408.2 31.7 all-gather.20
  633.4 27.4 reduce-scatter.24
  746.7 21.5 reduce-scatter.22
  791.3 21.3 reduce-scatter.16
  815.1 103.7 all-reduce.5
  921.0 18.6 reduce-scatter.18
  942.1 17.8 reduce-scatter.20
  962.1 27.6 reduce-scatter.14
  1025.6 19.7 reduce-scatter.12
  1047.7 21.3 reduce-scatter.10

commit v2 on v1

--- a/solution.py
+++ b/solution.py
@@ -4,6 +4,7 @@
 import jax.numpy as jnp
 from jax import lax
 from jax.experimental import pallas as pl
+from jax.experimental.layout import Layout, with_layout_constraint
 from jax.experimental.pallas import tpu as pltpu
 from jax.sharding import PartitionSpec as P
 
@@ -15,6 +16,11 @@
 SCALING = HEAD_DIM ** (-0.5)
 PAD_PREFIX = 32
 QUERY_BLOCK = 256
+CHUNK = 256
+LANES = 128
+VMEM_LIMIT = 56 * 1024 * 1024
+HALF_ROOT = 0.7071067811865476
+DENSITY = 0.3989422804014327
 
 low = jnp.bfloat16
 wide = jnp.float32
@@ -313,16 +319,471 @@
         - jnp.mean(slope, axis=-1, keepdims=True)
         - unit * jnp.mean(slope * unit, axis=-1, keepdims=True)
     )
-    return grad, jnp.stack([jnp.sum(upstream * unit, axis=0), jnp.sum(upstream, axis=0)])
+    return (
+        grad,
+        jnp.sum(upstream * unit, axis=0, keepdims=True),
+        jnp.sum(upstream, axis=0, keepdims=True),
+    )
 
 
 def gelu_exact(tensor):
-    return jax.nn.gelu(tensor, approximate=False)
+    return tensor * (0.5 + 0.5 * lax.erf(tensor * HALF_ROOT))
 
 
 def gelu_slope(tensor):
-    _, pullback = jax.vjp(gelu_exact, tensor)
-    return pullback(jnp.ones_like(tensor))[0]
+    density = jnp.exp(-0.5 * tensor * tensor) * DENSITY
+    return 0.5 + 0.5 * lax.erf(tensor * HALF_ROOT) + tensor * density
+
+
+class Links:
+    def __init__(self, seq):
+        self.seq = seq
+        self.far = [bit for bit in bit_list(seq) if bit > 1]
+        self.orders = [self.far, self.far[::-1]]
+        self.half = seq // 2
+        self.me = lax.axis_index("seq")
+
+    def place(self, mask):
+        return (mask & 1) * self.half + (mask >> 1)
+
+    def device(self, bit):
+        return {"seq": jnp.bitwise_xor(self.me, bit)}
+
+    def enter(self):
+        barrier = pltpu.get_barrier_semaphore()
+        bits = bit_list(self.seq)
+        for bit in bits:
+            pl.semaphore_signal(
+                barrier, inc=1, device_id=self.device(bit), device_id_type=pl.DeviceIdType.MESH
+            )
+        pl.semaphore_wait(barrier, len(bits))
+
+    def copy(self, source, target, send_sem, recv_sem, bit):
+        return pltpu.make_async_remote_copy(
+            src_ref=source,
+            dst_ref=target,
+            send_sem=send_sem,
+            recv_sem=recv_sem,
+            device_id=self.device(bit),
+            device_id_type=pl.DeviceIdType.MESH,
+        )
+
+
+def span(bits):
+    masks = [0]
+    for bit in bits:
+        masks = masks + [mask | bit for mask in masks]
+    return masks
+
+
+class Gather:
+    def __init__(self, links, own_ref, all_ref, sends, recvs, local_sem):
+        self.links, self.own, self.all = links, own_ref, all_ref
+        self.sends, self.recvs, self.local = sends, recvs, local_sem
+        self.rows = own_ref.shape[1]
+        self.cut = self.rows // 2
+
+    def at(self, micro, mask, part):
+        start = self.links.place(mask) * self.rows + part * self.cut
+        return self.all.at[micro, start : start + self.cut]
+
+    def piece(self, micro, mask, part):
+        if mask & 1:
+            return 1
+        seen = 0
+        for bit in self.links.orders[part]:
+            if mask & bit:
+                seen = bit
+        return seen
+
+    def send(self, micro, mask, part, bit):
+        there = mask ^ bit
+        source = self.at(micro, mask, part)
+        if mask == 0:
+            source = self.own.at[micro, part * self.cut : (part + 1) * self.cut]
+        self.links.copy(
+            source,
+            self.at(micro, there, part),
+            self.sends.at[micro, self.links.place(there), part],
+            self.recvs.at[micro, self.links.place(there), part],
+            bit,
+        ).start()
+
+    def descriptor(self, micro, mask, part):
+        bit = self.piece(micro, mask, part)
+        source = self.at(micro, mask ^ bit, part)
+        if mask ^ bit == 0:
+            source = self.own.at[micro, part * self.cut : (part + 1) * self.cut]
+        place = self.links.place(mask)
+        return self.links.copy(
+            source,
+            self.at(micro, mask, part),
+            self.sends.at[micro, place, part],
+            self.recvs.at[micro, place, part],
+            bit,
+        )
+
+    def keep_own(self, micro):
+        return pltpu.make_async_copy(
+            self.own.at[micro], self.all.at[micro, 0 : self.rows], self.local.at[micro]
+        )
+
+    def start(self, micro):
+        for part in range(2):
+            self.send(micro, 0, part, self.links.orders[part][0])
+        for part in range(2):
+            self.send(micro, 0, part, 1)
+        self.keep_own(micro).start()
+
+    def advance(self, micro, phase):
+        count = len(self.links.far)
+        for part in range(2):
+            order = self.links.orders[part]
+            fresh = [mask | order[phase] for mask in span(order[:phase])]
+            for mask in fresh:
+                self.descriptor(micro, mask, part).wait_recv()
+            if phase + 1 < count:
+                for mask in span(order[: phase + 1]):
+                    self.send(micro, mask, part, order[phase + 1])
+            for mask in fresh:
+                self.send(micro, mask, part, 1)
+
+    def phases(self):
+        return len(self.links.far)
+
+    def near(self, micro):
+        for part in range(2):
+            for mask in span(self.links.far):
+                self.descriptor(micro, mask | 1, part).wait_recv()
+        self.keep_own(micro).wait()
+
+    def drain(self, micro):
+        for part in range(2):
+            for mask in range(1, self.links.seq):
+                self.descriptor(micro, mask, part).wait_send()
+
+
+class Scatter:
+    def __init__(self, links, rows, sum_ref, near_send, near_recv, far_send, far_recv, sems):
+        self.links, self.rows, self.cut = links, rows, rows // 2
+        self.sum, self.near_send, self.near_recv = sum_ref, near_send, near_recv
+        self.far_send, self.far_recv = far_send, far_recv
+        self.near_sems, self.far_sems = sems
+
+    def near_copy(self, micro, index):
+        view = slice(index * self.rows, (index + 1) * self.rows)
+        return self.links.copy(
+            self.near_send.at[micro, view],
+            self.near_recv.at[micro, view],
+            self.near_sems.at[0, micro, index],
+            self.near_sems.at[1, micro, index],
+            1,
+        )
+
+    def start(self, micro, indexes):
+        for index in indexes:
+            self.near_copy(micro, index).start()
+
+    def far_view(self, index, part):
+        start = index * self.rows + part * self.cut
+        return slice(start, start + self.cut)
+
+    def bit_of(self, index, part):
+        last = 0
+        for bit in self.links.orders[part]:
+            if (index * 2) & bit:
+                last = bit
+        return last
+
+    def far_copy(self, micro, index, part):
+        view = self.far_view(index, part)
+        return self.links.copy(
+            self.far_send.at[micro, view],
+            self.far_recv.at[micro, view],
+            self.far_sems.at[0, micro, index, part],
+            self.far_sems.at[1, micro, index, part],
+            self.bit_of(index, part),
+        )
+
+    def send_far(self, micro, index, part, value):
+        self.far_send[micro, self.far_view(index, part)] = value.astype(low)
+        self.far_copy(micro, index, part).start()
+
+    def near_sum(self, micro):
+        count = len(self.links.far)
+        first = {}
+        for part in range(2):
+            bit = self.links.orders[part][count - 1]
+            first[part] = [mask | bit for mask in span(self.links.orders[part][: count - 1])]
+        ordered = sorted(range(self.links.half), key=lambda index: index == 0)
+        for index in ordered:
+            self.near_copy(micro, index).wait_recv()
+            for part in range(2):
+                view = self.far_view(index, part)
+                value = self.sum[micro, view] + self.near_recv[micro, view].astype(wide)
+                if index * 2 in first[part]:
+                    self.send_far(micro, index, part, value)
+                else:
+                    self.sum[micro, view] = value
+
+    def far_sum(self, micro, phase):
+        count = len(self.links.far)
+        for part in range(2):
+            order = self.links.orders[part]
+            bit = order[count - 1 - phase]
+            remain = span(order[: count - 1 - phase])
+            following = order[count - 2 - phase] if phase + 1 < count else 0
+            for mask in sorted(remain, key=lambda mask: (mask & following) == 0):
+                index, came = mask // 2, (mask | bit) // 2
+                self.far_copy(micro, came, part).wait_recv()
+                view = self.far_view(index, part)
+                value = self.sum[micro, view] + self.far_recv[
+                    micro, self.far_view(came, part)
+                ].astype(wide)
+                if mask & following:
+                    self.send_far(micro, index, part, value)
+                else:
+                    self.sum[micro, view] = value
+
+    def total(self, micro):
+        return self.sum[micro, 0 : self.rows]
+
+    def phases(self):
+        return len(self.links.far)
+
+    def drain(self, micro):
+        for index in range(self.links.half):
+            self.near_copy(micro, index).wait_send()
+        for part in range(2):
+            for index in range(1, self.links.half):
+                self.far_copy(micro, index, part).wait_send()
+
+
+def gather_scratch(seq, micros):
+    return [
+        pltpu.SemaphoreType.DMA((micros, seq, 2)),
+        pltpu.SemaphoreType.DMA((micros, seq, 2)),
+        pltpu.SemaphoreType.DMA((micros,)),
+    ]
+
+
+def scatter_scratch(seq, micros, rows, width):
+    half = seq // 2
+    part = pltpu.VMEM((micros, half * rows, width), low)
+    return [
+        pltpu.VMEM((micros, half * rows, width), wide),
+        part,
+        part,
+        part,
+        part,
+        pltpu.SemaphoreType.DMA((2, micros, half)),
+        pltpu.SemaphoreType.DMA((2, micros, half, 2)),
+    ]
+
+
+def merged(first, second):
+    steps = []
+    for index in range(max(len(first), len(second))):
+        steps += first[index : index + 1] + second[index : index + 1]
+    return steps
+
+
+def run_stage(micros, arrive, compute, leave):
+    for step in arrive(0):
+        step()
+    for micro in range(micros):
+        other = (leave(micro - 1) if micro > 0 else []) + (
+            arrive(micro + 1) if micro + 1 < micros else []
+        )
+        for step in merged(compute(micro), other):
+            step()
+    for step in leave(micros - 1):
+        step()
+
+
+def arrive_steps(gathers, micro):
+    steps = []
+    for gather in gathers:
+        for phase in range(gather.phases()):
+            steps.append(functools.partial(gather.advance, micro, phase))
+    return steps + [functools.partial(gather.near, micro) for gather in gathers]
+
+
+def leave_steps(scatters, finish, micro):
+    steps = [functools.partial(scatter.near_sum, micro) for scatter in scatters]
+    for phase in range(scatters[0].phases()):
+        for scatter in scatters:
+            steps.append(functools.partial(scatter.far_sum, micro, phase))
+    return steps + [functools.partial(finish, micro)]
+
+
+def half_steps(scatter, micro, length, chunk):
+    half = length // 2
+    size = min(CHUNK, half)
+
+    def odd():
+        def body(index, carry):
+            start = pl.multiple_of(half + index * size, size)
+            place = pl.ds(pl.multiple_of(index * size, size), size)
+            scatter.near_send[micro, place] = chunk(start, size).astype(low)
+            return carry
+
+        lax.fori_loop(0, half // size, body, 0)
+        scatter.start(micro, range(scatter.links.half))
+
+    def even():
+        def body(index, carry):
+            start = pl.multiple_of(index * size, size)
+            scatter.sum[micro, pl.ds(start, size)] = chunk(start, size)
+            return carry
+
+        lax.fori_loop(0, half // size, body, 0)
+
+    return [odd, even]
+
+
+def ffn_kernel(
+    seq, own_ref, resid_ref, one_ref, two_ref, pair_ref, all_ref, before_ref, hidden_ref, sum_ref,
+    norm_ref, *scratch,
+):
+    links = Links(seq)
+    micros, rows, _ = own_ref.shape
+    length = all_ref.shape[1]
+    gather = Gather(links, own_ref, all_ref, *scratch[:3])
+    scatter = Scatter(links, rows, *scratch[3:8], scratch[8:])
+    links.enter()
+    for micro in range(micros):
+        gather.start(micro)
+
+    def compute(micro):
+        def chunk(start, size):
+            place = pl.ds(start, size)
+            before = dot(all_ref[micro, place], one_ref[...], 1, 1)
+            before_ref[micro, place] = before
+            after = gelu_exact(before).astype(low)
+            hidden_ref[micro, place] = after
+            return dot(after, two_ref[...], 1, 1)
+
+        return half_steps(scatter, micro, length, chunk)
+
+    def finish(micro):
+        total = resid_ref[micro] + scatter.total(micro)
+        sum_ref[micro] = total
+        norm_ref[micro] = layer_norm(total, (pair_ref[0:1], pair_ref[1:2]))
+
+    run_stage(
+        micros,
+        functools.partial(arrive_steps, [gather]),
+        compute,
+        functools.partial(leave_steps, [scatter], finish),
+    )
+    for micro in range(micros):
+        gather.drain(micro)
+        scatter.drain(micro)
+
+
+def stage_call(kernel, name_id, outs, scratch, args, flops):
+    return pl.pallas_call(
+        kernel,
+        out_shape=outs,
+        in_specs=[pl.BlockSpec(memory_space=pltpu.VMEM)] * len(args),
+        out_specs=tuple(pl.BlockSpec(memory_space=pltpu.VMEM) for _ in outs),
+        scratch_shapes=scratch,
+        compiler_params=pltpu.CompilerParams(
+            collective_id=name_id, has_side_effects=True, vmem_limit_bytes=VMEM_LIMIT
+        ),
+        cost_estimate=pl.CostEstimate(flops=flops, bytes_accessed=1 << 24, transcendentals=0),
+    )(*args)
+
+
+def ffn_stage(seq, name_id, own, resid, one, two, pair):
+    micros, rows, width = own.shape
+    hidden = one.shape[0]
+    length = rows * seq
+    outs = (
+        jax.ShapeDtypeStruct((micros, length, width), low),
+        jax.ShapeDtypeStruct((micros, length, hidden), wide),
+        jax.ShapeDtypeStruct((micros, length, hidden), low),
+        jax.ShapeDtypeStruct((micros, rows, width), wide),
+        jax.ShapeDtypeStruct((micros, rows, width), wide),
+    )
+    scratch = gather_scratch(seq, micros) + scatter_scratch(seq, micros, rows, width)
+    return stage_call(
+        functools.partial(ffn_kernel, seq), name_id, outs, scratch,
+        (own, resid, one, two, pair), 4 * micros * length * width * hidden,
+    )
+
+
+def prologue(micro, up_ref, resid_ref, pair_ref, own_ref, kept_ref, pair_grad_ref):
+    gains = (pair_ref[0:1], pair_ref[1:2])
+    grad, gain_grad, shift_grad = norm_back(up_ref[micro].astype(wide), resid_ref[micro], gains)
+    kept_ref[micro] = grad
+    own_ref[micro] = grad.astype(low)
+    if micro == 0:
+        pair_grad_ref[0:1] = gain_grad
+        pair_grad_ref[1:2] = shift_grad
+    else:
+        pair_grad_ref[0:1] += gain_grad
+        pair_grad_ref[1:2] += shift_grad
+
+
+def ffn_back_kernel(
+    seq, up_ref, resid_ref, pair_ref, before_ref, one_ref, two_ref, all_ref, slope_ref, out_ref,
+    pair_grad_ref, own_ref, kept_ref, *scratch,
+):
+    links = Links(seq)
+    micros, rows, _ = own_ref.shape
+    length = all_ref.shape[1]
+    gather = Gather(links, own_ref, all_ref, *scratch[:3])
+    scatter = Scatter(links, rows, *scratch[3:8], scratch[8:])
+    links.enter()
+    for micro in range(micros):
+        prologue(micro, up_ref, resid_ref, pair_ref, own_ref, kept_ref, pair_grad_ref)
+        gather.start(micro)
+
+    def compute(micro):
+        def chunk(start, size):
+            place = pl.ds(start, size)
+            slope = dot(all_ref[micro, place], two_ref[...], 1, 0)
+            slope = (slope * gelu_slope(before_ref[micro, place])).astype(low)
+            slope_ref[micro, place] = slope
+            return dot(slope, one_ref[...], 1, 0)
+
+        return half_steps(scatter, micro, length, chunk)
+
+    def finish(micro):
+        out_ref[micro] = kept_ref[micro] + scatter.total(micro)
+
+    run_stage(
+        micros,
+        functools.partial(arrive_steps, [gather]),
+        compute,
+        functools.partial(leave_steps, [scatter], finish),
+    )
+    for micro in range(micros):
+        gather.drain(micro)
+        scatter.drain(micro)
+
+
+def ffn_back_stage(seq, name_id, up, resid, pair, before, one, two):
+    micros, rows, width = up.shape
+    hidden = one.shape[0]
+    length = rows * seq
+    outs = (
+        jax.ShapeDtypeStruct((micros, length, width), low),
+        jax.ShapeDtypeStruct((micros, length, hidden), low),
+        jax.ShapeDtypeStruct((micros, rows, width), wide),
+        jax.ShapeDtypeStruct((2, width), wide),
+    )
+    scratch = (
+        [pltpu.VMEM((micros, rows, width), low), pltpu.VMEM((micros, rows, width), wide)]
+        + gather_scratch(seq, micros)
+        + scatter_scratch(seq, micros, rows, width)
+    )
+    return stage_call(
+        functools.partial(ffn_back_kernel, seq), name_id, outs, scratch,
+        (up, resid, pair, before, one, two), 4 * micros * length * width * hidden,
+    )
 
 
 def outer_sum(lefts, rights):
@@ -353,10 +814,10 @@
     hidden = encoder_contract.shape[0] // seq
     adapt = encoder_up.shape[0] // seq
     both = hidden + adapt
+    padded = (both + LANES - 1) // LANES * LANES
 
     sources = [row for row in source.reshape(stacked, block, width)]
     targets = [row for row in target.reshape(stacked, block, width)]
-    upstreams = [row for row in cotangent.reshape(stacked, block, width)]
 
     places = plane.relative(jnp.arange(length, dtype=jnp.int32), me)
     place_pair = (places[:, None], places[None, :])
@@ -397,21 +858,19 @@
     def exchange(value):
         return lax.all_to_all(value, "seq", 1, 1, tiled=False)
 
+    def ffn_rows(contract, up):
+        pieces = [split_rows(contract), split_rows(up) * jnp.asarray(ADAPTER_SCALE, low)]
+        if padded > both:
+            pieces.append(jnp.zeros((slice_cols, seq, padded - both), low))
+        return pieces
+
     row_pieces = jnp.concatenate(
-        [
-            split_rows(encoder_output),
-            split_rows(decoder_output),
-            split_rows(cross_output),
-            split_rows(encoder_contract),
-            split_rows(encoder_up) * jnp.asarray(ADAPTER_SCALE, low),
-            split_rows(decoder_contract),
-            split_rows(decoder_up) * jnp.asarray(ADAPTER_SCALE, low),
-        ],
+        [split_rows(encoder_output), split_rows(decoder_output), split_rows(cross_output)]
+        + ffn_rows(encoder_contract, encoder_up)
+        + ffn_rows(decoder_contract, decoder_up),
         axis=2,
     )
-    row_pieces = lax.all_to_all(row_pieces, "seq", 1, 0, tiled=False).reshape(
-        seq, slice_cols, -1
-    )
+    row_pieces = lax.all_to_all(row_pieces, "seq", 1, 0, tiled=False).reshape(seq, slice_cols, -1)
 
     def row_weight(start, size):
         gathered = gather_rows(row_pieces[:, :, start : start + size])
@@ -427,27 +886,37 @@
     )
     encoder_in = flat_columns(qkv_parts[:, : 3 * slice_cols], 3)
     decoder_in = flat_columns(qkv_parts[:, 3 * slice_cols :], 3)
-    outputs_low = row_weight(0, 3 * head_width)
-    encoder_out = outputs_low[:, :head_width]
-    decoder_out = outputs_low[:, head_width : 2 * head_width]
-    cross_out = outputs_low[:, 2 * head_width :]
-
-    def ffn_in(expand, down):
-        gathered = gather_rows(jnp.concatenate([columns(expand), columns(down)]))
-        cut = expand.shape[1]
-        return jnp.concatenate(
-            [gathered[:, :cut].reshape(-1, width), gathered[:, cut:].reshape(-1, width)]
-        )
-
-    encoder_one = ffn_in(encoder_expand, encoder_down)
-    encoder_two = row_weight(3 * head_width, both)
-    cross_parts = gather_rows(
-        jnp.concatenate([columns(cross_query), columns(cross_kv).reshape(-1, width)])
-    )
-    cross_in = flat_columns(cross_parts, 3)
+    first_rows = row_weight(0, 3 * head_width + padded)
+    encoder_out = first_rows[:, :head_width]
+    decoder_out = first_rows[:, head_width : 2 * head_width]
+    cross_out = first_rows[:, 2 * head_width : 3 * head_width]
+    encoder_two = first_rows[:, 3 * head_width :]
+    cut = encoder_expand.shape[1]
+
+    def ffn_in(gathered):
+        pieces = [gathered[:, :cut].reshape(-1, width), gathered[:, cut:].reshape(-1, width)]
+        if padded > both:
+            pieces.append(jnp.zeros((padded - both, width), low))
+        return jnp.concatenate(pieces)
+
+    second_parts = gather_rows(
+        jnp.concatenate(
+            [
+                columns(encoder_expand),
+                columns(encoder_down),
+                columns(cross_query),
+                columns(cross_kv).reshape(-1, width),
+            ]
+        )
+    )
+    ffn_cut = cut + encoder_down.shape[1]
+    encoder_one = ffn_in(second_parts[:, :ffn_cut])
+    cross_in = flat_columns(second_parts[:, ffn_cut:], 3)
     cross_q_in, cross_kv_in = cross_in[:head_width], cross_in[head_width:]
-    decoder_one = ffn_in(decoder_expand, decoder_down)
-    decoder_two = row_weight(3 * head_width + both, both)
+    decoder_one = ffn_in(
+        gather_rows(jnp.concatenate([columns(decoder_expand), columns(decoder_down)]))
+    )
+    decoder_two = row_weight(3 * head_width + padded, padded)
 
     prefixes = small_gather(
         jnp.concatenate([encoder_prefix, decoder_prefix, cross_prefix]), [("rows", ranks)]
@@ -465,16 +934,12 @@
 
     self_offsets = (0, head_width, 2 * head_width)
     cross_offsets = (0, 0, head_width)
-
-    def ffn_forward(rows, weight_one):
-        before = dot(rows, weight_one, 1, 1)
-        return before, gelu_exact(before).astype(low)
 
     source_all = [plane.gather(sources[m], m) for m in every]
     target_all = [plane.gather(targets[m], m) for m in every]
     encoder_qkvs = [dot(source_all[m], encoder_in, 1, 1).astype(low) for m in every]
     decoder_qkvs = [dot(target_all[m], decoder_in, 1, 1).astype(low) for m in every]
-    encoder_ctx, encoder_logs, resid_one, middle, middle_all = [], [], [], [], []
+    encoder_ctx, encoder_logs, resid_one, middle = [], [], [], []
     decoder_ctx, decoder_logs, resid_three, first, first_all = [], [], [], [], []
     for m in every:
         context, logs = attend_forward(
@@ -485,7 +950,6 @@
         attended = plane.scatter([(context, encoder_out, 1)], m)
         resid_one.append(sources[m].astype(wide) + attended)
         middle.append(layer_norm(resid_one[m], scales[0]))
-        middle_all.append(plane.gather(middle[m].astype(low), m))
     for m in every:
         context, logs = attend_forward(
             decoder_qkvs[m], decoder_qkvs[m], self_offsets, decoder_pre, count, decoder_ids[m], True
@@ -496,18 +960,15 @@
         resid_three.append(targets[m].astype(wide) + attended)
         first.append(layer_norm(resid_three[m], scales[norm_count]))
         first_all.append(plane.gather(first[m].astype(low), m))
-    encoder_before, encoder_hidden, resid_two, memory_all = [], [], [], []
-    for m in every:
-        before, after = ffn_forward(middle_all[m], encoder_one)
-        encoder_before.append(before)
-        encoder_hidden.append(after)
-        branch = plane.scatter([(after, encoder_two, 1)], m)
-        resid_two.append(middle[m] + branch)
-        memory = layer_norm(resid_two[m], scales[1])
-        memory_all.append(plane.gather(memory.astype(low), m))
+    middle_low = jnp.stack(middle).astype(low)
+    middle_all, encoder_before, encoder_hidden, resid_two, memory = ffn_stage(
+        seq, 1, middle_low, jnp.stack(middle), encoder_one, encoder_two, scales[1]
+    )
+    memory_low = memory.astype(low)
+    memory_all = [plane.gather(memory_low[m], m) for m in every]
     cross_q = [dot(first_all[m], cross_q_in, 1, 1).astype(low) for m in every]
     cross_kvs = [dot(memory_all[m], cross_kv_in, 1, 1).astype(low) for m in every]
-    cross_ctx, cross_logs, resid_four, second, second_all = [], [], [], [], []
+    cross_ctx, cross_logs, resid_four, second = [], [], [], []
     for m in every:
         context, logs = attend_forward(
             cross_q[m], cross_kvs[m], cross_offsets, cross_pre, count, cross_ids[m], False
@@ -517,18 +978,15 @@
         crossed = plane.scatter([(context, cross_out, 1)], m)
         resid_four.append(first[m] + crossed)
         second.append(layer_norm(resid_four[m], scales[norm_count + 1]))
-        second_all.append(plane.gather(second[m].astype(low), m))
-    decoder_before, decoder_hidden, resid_five, results = [], [], [], []
-    for m in every:
-        before, after = ffn_forward(second_all[m], decoder_one)
-        decoder_before.append(before)
-        decoder_hidden.append(after)
-        branch = plane.scatter([(after, decoder_two, 1)], m)
-        resid_five.append(second[m] + branch)
-        results.append(layer_norm(resid_five[m], scales[norm_count + 2]).astype(low))
+    second_low = jnp.stack(second).astype(low)
+    second_all, decoder_before, decoder_hidden, resid_five, third = ffn_stage(
+        seq, 2, second_low, jnp.stack(second), decoder_one, decoder_two, scales[norm_count + 2]
+    )
+    result = third.astype(low)
 
     def scatter_ranks(value):
-        return lax.psum_scatter(value.astype(low), "rows", scatter_dimension=0, tiled=False)
+        value = with_layout_constraint(value.astype(low), Layout(tuple(range(value.ndim))))
+        return lax.psum_scatter(value, "rows", scatter_dimension=0, tiled=False)
 
     def reduce_columns(grad, parts):
         value = grad.reshape(parts, ranks, slice_cols, width)
@@ -540,36 +998,42 @@
 
     def reduce_ffn_in(grad):
         value = jnp.concatenate(
-            [grad[:hidden].reshape(ranks, -1, width), grad[hidden:].reshape(ranks, -1, width)],
+            [
+                grad[:hidden].reshape(ranks, -1, width),
+                grad[hidden:both].reshape(ranks, -1, width),
+            ],
             axis=1,
         )
         return scatter_ranks(value)
 
-    def ffn_backward(low_all, befores, weight_one, weight_two, m):
-        slope = dot(low_all, weight_two, 1, 0) * gelu_slope(befores[m])
-        slope = slope.astype(low)
-        return slope, plane.scatter([(slope, weight_one, 0)], m)
+    def flat(value):
+        return value.reshape(-1, value.shape[-1])
 
     norm_grads = {}
 
     def norm_step(index, upstream_rows, residuals):
-        grads, sums = [], None
+        grads, gain_sum, shift_sum = [], 0.0, 0.0
         for m in every:
-            grad, pair = norm_back(upstream_rows[m], residuals[m], scales[index])
+            grad, gain_grad, shift_grad = norm_back(upstream_rows[m], residuals[m], scales[index])
             grads.append(grad)
-            sums = pair if sums is None else sums + pair
-        norm_grads[index] = sums
+            gain_sum = gain_sum + gain_grad
+            shift_sum = shift_sum + shift_grad
+        norm_grads[index] = (gain_sum, shift_sum)
         return grads
 
-    third_in = norm_step(norm_count + 2, [u.astype(wide) for u in upstreams], resid_five)
-    third_all = [plane.gather(third_in[m].astype(low), m) for m in every]
-    slopes, second_up = [], []
-    for m in every:
-        slope, from_ffn = ffn_backward(third_all[m], decoder_before, decoder_one, decoder_two, m)
-        slopes.append(slope)
-        second_up.append(third_in[m] + from_ffn)
-    decoder_two_grad = reduce_rows(outer_sum(third_all, decoder_hidden))
-    decoder_one_grad = reduce_ffn_in(outer_sum(slopes, second_all))
+    def ffn_back(name_id, index, up, resid, before, hidden_low, rows_all, one, two):
+        up_all, slope, out, pair = ffn_back_stage(
+            seq, name_id, up, resid, scales[index], before, one, two
+        )
+        norm_grads[index] = (pair[0:1], pair[1:2])
+        two_grad = reduce_rows(dot(flat(up_all), flat(hidden_low), 0, 0))
+        one_grad = reduce_ffn_in(dot(flat(slope), flat(rows_all), 0, 0))
+        return out, one_grad, two_grad
+
+    second_up, decoder_one_grad, decoder_two_grad = ffn_back(
+        3, norm_count + 2, cotangent.reshape(stacked, block, width), resid_five, decoder_before,
+        decoder_hidden, second_all, decoder_one, decoder_two,
+    )
 
     second_in = norm_step(norm_count + 1, second_up, resid_four)
     second_low = [plane.gather(second_in[m].astype(low), m) for m in every]
@@ -597,18 +1061,12 @@
         3,
     )
 
-    memory_in = norm_step(1, memory_up, resid_two)
+    middle_up, encoder_one_grad, encoder_two_grad = ffn_back(
+        4, 1, jnp.stack(memory_up), resid_two, encoder_before, encoder_hidden, middle_all,
+        encoder_one, encoder_two,
+    )
     first_in = norm_step(norm_count, first_up, resid_three)
-    memory_low = [plane.gather(memory_in[m].astype(low), m) for m in every]
     first_low = [plane.gather(first_in[m].astype(low), m) for m in every]
-
-    slopes, middle_up = [], []
-    for m in every:
-        slope, from_ffn = ffn_backward(memory_low[m], encoder_before, encoder_one, encoder_two, m)
-        slopes.append(slope)
-        middle_up.append(memory_in[m] + from_ffn)
-    encoder_two_grad = reduce_rows(outer_sum(memory_low, encoder_hidden))
-    encoder_one_grad = reduce_ffn_in(outer_sum(slopes, middle_all))
 
     def self_backward(low_all, out_weight, in_weight, qkvs, prefix, ids, causal, logs, rows_in):
         grads_all, prefix_sum, totals = [], None, []
@@ -657,18 +1115,19 @@
     prefix_total = jnp.concatenate([encoder_pre_grad, decoder_pre_grad, cross_pre_grad])[:, :count]
     prefix_total = jnp.moveaxis(prefix_total.reshape(6, count, ranks, slice_cols), 2, 0)
     prefix_total = small_scatter(prefix_total, [("rows", ranks)])
-    norm_total = jnp.stack([norm_grads[index] for index in sorted(norm_grads)])
+    norm_rows = [row for index in sorted(norm_grads) for row in norm_grads[index]]
+    which = lax.broadcasted_iota(jnp.int32, (len(norm_rows), width), 0)
+    norm_total = sum(jnp.where(which == k, row, 0.0) for k, row in enumerate(norm_rows))
     norm_total = jnp.moveaxis(norm_total.reshape(-1, 2, seq * ranks, slice_cols), 2, 0)
     norm_total = small_scatter(norm_total, norm_axes)
 
-    cut = encoder_expand.shape[1]
     shape_out = source.shape
     return (
-        jnp.stack(results).reshape(shape_out),
+        result.reshape(shape_out),
         jnp.stack(source_grads).reshape(shape_out),
         jnp.stack(target_grads).reshape(shape_out),
         column_grad(encoder_in_grad),
-        row_grad(encoder_rows, both, head_width),
+        row_grad(encoder_rows, padded, head_width),
         prefix_total[0:2],
         column_grad(encoder_one_grad[:cut]),
         row_grad(encoder_rows, 0, hidden),
@@ -676,11 +1135,11 @@
         row_grad(encoder_rows, hidden, adapt, ADAPTER_SCALE),
         norm_total[:norm_count],
         column_grad(decoder_in_grad),
-        row_grad(decoder_rows, both + head_width, head_width),
+        row_grad(decoder_rows, padded + head_width, head_width),
         prefix_total[2:4],
         column_grad(cross_in_grad[0]),
         column_grad(cross_in_grad[1:]),
-        row_grad(decoder_rows, both, head_width),
+        row_grad(decoder_rows, padded, head_width),
         prefix_total[4:6],
         column_grad(decoder_one_grad[:cut]),
         row_grad(decoder_rows, 0, hidden),

time: 1100 us -> 1030 us (0.936)
  Pallas kernels: 103 us -> 348 us
  waiting for transfers between devices: 370 us -> 219 us
  other arithmetic: 169 us -> 117 us
  starting transfers between devices: 140 us -> 89 us
  matrix products: 134 us -> 107 us
  local copies, waits for them, and re-layouts: 119 us -> 101 us
  blocking collectives: 35.6 us -> 18.4 us
    pallas_call x0 -> x4, Pallas kernels: none -> 245 us  [stage_call(): pl.pallas_call(kernel, out_shape=outs, in_specs=[pl.BlockSpec(memory_spac...]
    ppermute x44 -> x28, waiting for transfers between devices: 150 us -> 63.2 us  [scatter(): sent = lax.ppermute(send, 'seq', swap_pairs(self.seq, bit))]
    ppermute x66 -> x42, waiting for transfers between devices: 158 us -> 82.7 us  [gather(): other = lax.ppermute(value, 'seq', swap_pairs(self.seq, bit))]
    all_gather x2 -> x0, blocking collectives: 35.6 us -> none  [gather_rows(): return lax.all_gather(value, 'rows', axis=0, tiled=False)]
    concatenate x66 -> x42, other arithmetic: 66.1 us -> 36.6 us  [gather(): value = jnp.concatenate([value, other], axis=self.axes.index(bit))]
    another operation x21 -> x2, local copies, waits for them, and re-layouts: 26.6 us -> 0.02 us  [the longest x20 25.5 us: norm_back(): jnp.stack([jnp.sum(upstream * unit, axis=0), jnp.sum(upstream, axis=0)])]
    dot_general x88 -> x60, matrix products: 134 us -> 107 us  [dot(): lax.dot_general(left, right, (((left_axis,), (right_axis,)), ((), ())), p...]
    ppermute x66 -> x42, starting transfers between devices: 54.9 us -> 31.8 us  [gather(): other = lax.ppermute(value, 'seq', swap_pairs(self.seq, bit))]
  transfers between devices with their start and end apart: 163 -> 115, of which waited for: 77 -> 42; matrix products, arithmetic and copies ran while one was open for 34% -> 28% of each run, Pallas kernels for 9% -> 22%
where the time goes in v2:
time: 1030 us; the launch traced here: 1020 us
  Pallas kernels  348 us (34%)
  waiting for transfers between devices  219 us (21%)
  other arithmetic  117 us (11%)
  matrix products  107 us (10%)
  local copies, waits for them, and re-layouts  101 us (10%)
  starting transfers between devices  89 us (9%)
  between operations  19.3 us (2%)
  blocking collectives  18.4 us (2%)
    pallas_call x4, Pallas kernels, stage_call(): pl.pallas_call(kernel, out_shape=outs, in_specs=[pl.BlockSpec(memory_spac...  245 us
    dot_general x60, matrix products, dot(): lax.dot_general(left, right, (((left_axis,), (right_axis,)), ((), ())), p...  107 us
    ppermute x42, waiting for transfers between devices, gather(): other = lax.ppermute(value, 'seq', swap_pairs(self.seq, bit))  82.7 us
    ppermute x28, waiting for transfers between devices, scatter(): sent = lax.ppermute(send, 'seq', swap_pairs(self.seq, bit))  63.2 us
    pallas_call x6, Pallas kernels, attend_backward(): pl.pallas_call(functools.partial(attend_back_kernel, heads, offsets, coun...  58.2 us
    pallas_call x6, Pallas kernels, attend_forward(): pl.pallas_call(functools.partial(attend_kernel, heads, offsets, count, ca...  44.6 us
    concatenate x42, other arithmetic, gather(): value = jnp.concatenate([value, other], axis=self.axes.index(bit))  36.6 us
    ppermute x28, starting transfers between devices, scatter(): sent = lax.ppermute(send, 'seq', swap_pairs(self.seq, bit))  34 us
  transfers between devices with their start and end apart: 115, of which 42 were waited for; matrix products, arithmetic and copies ran while one was open for 28% of the time, Pallas kernels for 22%

profile of v2, /device:TPU:0, one launch (start us, length us, event | category | flops | bytes accessed | tf_op | source)
XLA Modules:
  0.0 1018.5 jit_solution(16516547554501300569)
XLA Ops:
  15.2 18.4 %all_to_all.45 = bf16[1,32,8,1664]{3,1,0,2:T(8,128)(2,1)S(1)} all-to-all(bf16[1,32,8,1664]{3,1,0,2:T(8,128)(2,1)S(1)} %copy.292), channel_id=1, replica_groups=mesh['seq'=8,'rows'=4] {'seq'}, dimensions={2} | all-to-all | bytes 1703936 | tf_op jit(solution)/shard_map/all_to_all | solution.py:873
  57.1 10.9 %collective-permute-done.11 = bf16[8,5,2,32]{3,2,1,0:T(2,128)(2,1)S(1)} collective-permute-done((bf16[8,5,2,32]{3,2,1,0:T(2,128)(2,1)S(1)}, bf16[8,5,2,32]{3,2,1,0:T(2,128)(2,1)S(1)}, u32[]{:S(2)}, u32[]{:S(2)}) %collective-permute-start.11) | collective-permute-done | bytes 5152 | tf_op jit(solution)/shard_map/ppermute | solution.py:107
  90.2 7.9 collective-permute-done.4
  118.0 7.6 shard_map.416
  126.9 7.4 shard_map.421
  135.6 7.3 shard_map.417
  148.8 7.7 shard_map.418
  166.4 13.0 %all-gather.15.cloned.1.call-done = bf16[960,1024]{1,0:T(8,128)(2,1)} async-done(((bf16[240,1024]{1,0:T(8,128)(2,1)}), bf16[960,1024]{1,0:T(8,128)(2,1)}) %all-gather.15.cloned.1.call-update) | async-done | bytes 1966096 | tf_op jit(solution)/shard_map/all_gather | solution.py:838
  193.7 7.1 collective-permute-done.6
  205.0 7.0 collective-permute-done.20
  231.9 61.6 %shard_map.419 = (bf16[2,1024,1024]{2,1,0:T(8,128)(2,1)}, f32[2,1024,640]{2,1,0:T(8,128)}, bf16[2,1024,640]{2,1,0:T(8,128)(2,1)}, f32[2,128,1024]{2,1,0:T(8,128)}, f32[2,128,1024]{2,1,0:T(8,128)}) custom-call(bf16[2,128,1024]{2,1,0:T(8,128)(2,1)} %fusion.207.own_ref, f32[2,128,1024]{2,1,0:T(8,128)} %pad_maximum_fusion.20.resid_ref, ...), custom_call_target="tpu_custom_call" | custom-call | flops 5368709120 | bytes 16777216 | tf_op jit(solution)/shard_map/pallas_call | solution.py:686
  310.1 11.0 %collective-permute-done.29 = bf16[1,2,1,128,1024]{4,3,2,1,0:T(8,128)(2,1)S(1)} collective-permute-done((bf16[1,2,1,128,1024]{4,3,2,1,0:T(8,128)(2,1)S(1)}, bf16[1,2,1,128,1024]{4,3,2,1,0:T(8,128)(2,1)S(1)}, u32[]{:S(2)}, u32[]{:S(2)}) %collective-permute-start.29) | collective-permute-done | bytes 524320 | tf_op jit(solution)/shard_map/ppermute | solution.py:66
  330.6 9.8 collective-permute-done.41
  350.4 7.3 shard_map.420
  362.6 7.3 shard_map.422
  379.3 10.3 %collective-permute-done.32 = bf16[2,1,128,1024]{3,2,1,0:T(8,128)(2,1)S(1)} collective-permute-done((bf16[2,1,128,1024]{3,2,1,0:T(8,128)(2,1)S(1)}, bf16[2,1,128,1024]{3,2,1,0:T(8,128)(2,1)S(1)}, u32[]{:S(2)}, u32[]{:S(2)}) %collective-permute-start.32) | collective-permute-done | bytes 524320 | tf_op jit(solution)/shard_map/ppermute | solution.py:89
  395.9 8.3 all-gather.19.cloned.1.call-done
  412.6 63.1 %shard_map.423 = (bf16[2,1024,1024]{2,1,0:T(8,128)(2,1)}, f32[2,1024,640]{2,1,0:T(8,128)}, bf16[2,1024,640]{2,1,0:T(8,128)(2,1)}, f32[2,128,1024]{2,1,0:T(8,128)}, f32[2,128,1024]{2,1,0:T(8,128)}) custom-call(bf16[2,128,1024]{2,1,0:T(8,128)(2,1)} %fusion.206.own_ref, f32[2,128,1024]{2,1,0:T(8,128)} %pad_maximum_fusion.25.resid_ref, ...), custom_call_target="tpu_custom_call" | custom-call | flops 5368709120 | bytes 16777216 | tf_op jit(solution)/shard_map/pallas_call | solution.py:686
  475.7 60.9 %shard_map.424 = (bf16[2,1024,1024]{2,1,0:T(8,128)(2,1)}, bf16[2,1024,640]{2,1,0:T(8,128)(2,1)}, f32[2,128,1024]{2,1,0:T(8,128)}, f32[2,1024]{1,0:T(2,128)}) custom-call(bf16[2,128,1024]{2,1,0:T(8,128)(2,1)} %bitcast.976, f32[2,128,1024]{2,1,0:T(8,128)} %get-tuple-element.74.resid_ref, f32[2,1024]{1,0:T(2,128)} %squeeze.54.pair_ref, ...), custom_call_target="tpu_custom_call" | custom-call | flops 5368709120 | bytes 16777216 | tf_op jit(solution)/shard_map/pallas_call | solution.py:686
  583.7 9.7 shard_map.426
  594.8 9.5 shard_map.425
  620.1 7.6 fusion.10
  639.8 7.1 collective-permute-done.53
  649.0 8.8 collective-permute-done.74
  671.2 59.7 %shard_map.427 = (bf16[2,1024,1024]{2,1,0:T(8,128)(2,1)}, bf16[2,1024,640]{2,1,0:T(8,128)(2,1)}, f32[2,128,1024]{2,1,0:T(8,128)}, f32[2,1024]{1,0:T(2,128)}) custom-call(f32[2,128,1024]{2,1,0:T(8,128)} %pad_maximum_fusion.28.up_ref, f32[2,128,1024]{2,1,0:T(8,128)} %get-tuple-element.80.resid_ref, f32[2,1024]{1,0:T(2,128)} %squeeze.53.pair_ref, ...), custom_call_target="tpu_custom_call" | custom-call | flops 5368709120 | bytes 16777216 | tf_op jit(solution)/shard_map/pallas_call | solution.py:686
  748.3 8.4 collective-permute-done.77
  812.0 7.5 fusion.13
  824.8 9.5 shard_map.428
  836.1 9.5 shard_map.429
  854.9 9.8 shard_map.430
  864.8 10.2 shard_map.431
  883.8 18.7 %collective-permute-done.91 = f32[2,6,30,32]{3,1,2,0:T(8,128)} collective-permute-done((f32[2,6,30,32]{3,1,2,0:T(8,128)S(1)}, f32[2,6,30,32]{3,1,2,0:T(8,128)}, u32[]{:S(2)}, u32[]{:S(2)}) %collective-permute-start.91) | collective-permute-done | bytes 46112 | tf_op jit(solution)/shard_map/ppermute | solution.py:122
  (1135 shorter events, 489.3 us)
Async XLA Ops:
  7.2 105.8 %all-gather.11.cloned.1.call-start = ((), (), s32[]{:S(2)}) async-start(), calls=%async_computation.23 | async-start | bytes 1966080 | tf_op jit(solution)/shard_map/all_gather | solution.py:838
  9.1 136.0 %all-gather.13.cloned.1.call-start = ((), (), s32[]{:S(2)}) async-start(), calls=%async_computation.24 | async-start | bytes 2621440 | tf_op jit(solution)/shard_map/all_gather | solution.py:838
  35.3 127.8 %all-gather.17.cloned.1.call-start = ((), (), s32[]{:S(2)}) async-start(), calls=%async_computation.26 | async-start | bytes 1474560 | tf_op jit(solution)/shard_map/all_gather | solution.py:838
  36.3 143.0 %all-gather.15.cloned.1.call-start = ((), (), s32[]{:S(2)}) async-start(), calls=%async_computation.25 | async-start | bytes 2457600 | tf_op jit(solution)/shard_map/all_gather | solution.py:838
  38.2 37.0 %collective-permute-start.3 = (bf16[1,6,30,32]{3,1,2,0:T(8,128)(2,1)S(1)}, bf16[1,6,30,32]{3,1,2,0:T(8,128)(2,1)}, u32[]{:S(2)}, u32[]{:S(2)}) collective-permute-start(bf16[1,6,30,32]{3,1,2,0:T(8,128)(2,1)S(1)} %maximum_bitcast_fusion.4), channel_id=1, source_target_pairs={{0,1},{1,0},{2,3},{3,2},{4,5},{5,4},{6,7},{7,6},{8,9},{9,8},{10,11... | collective-permute-start | bytes 34568 | tf_op jit(solution)/shard_map/ppermute | solution.py:107
  42.5 361.7 %all-gather.19.cloned.1.call-start = ((), (), s32[]{:S(2)}) async-start(), calls=%async_computation.27 | async-start | bytes 1638400 | tf_op jit(solution)/shard_map/all_gather | solution.py:838
  73.0 28.3 %collective-permute-start.2 = (bf16[1,2,2,128,1024]{4,3,2,1,0:T(8,128)(2,1)}, bf16[1,2,2,128,1024]{4,3,2,1,0:T(8,128)(2,1)}, u32[]{:S(2)}, u32[]{:S(2)}) collective-permute-start(bf16[1,2,2,128,1024]{4,3,2,1,0:T(8,128)(2,1)} %pad_maximum_fusion.16), channel_id=1, source_target_pairs={{0,4},{4,0},{8,12},{12,8},{16,20},{20,16},{24,28},{28,24},{1,5},{5... | collective-permute-start | bytes 3145736 | tf_op jit(solution)/shard_map/ppermute | solution.py:66
  75.2 29.2 %collective-permute-start.36 = (bf16[1,2,2,128,1024]{4,3,2,1,0:T(8,128)(2,1)}, bf16[1,2,2,128,1024]{4,3,2,1,0:T(8,128)(2,1)}, u32[]{:S(2)}, u32[]{:S(2)}) collective-permute-start(bf16[1,2,2,128,1024]{4,3,2,1,0:T(8,128)(2,1)} %pad_maximum_fusion.22), channel_id=1, source_target_pairs={{0,4},{4,0},{8,12},{12,8},{16,20},{20,16},{24,28},{28,24},{1,5},{5... | collective-permute-start | bytes 3145736 | tf_op jit(solution)/shard_map/ppermute | solution.py:66
  148.7 33.0 %collective-permute-start.37 = (bf16[512,1024]{1,0:T(8,128)(2,1)}, bf16[512,1024]{1,0:T(8,128)(2,1)}, u32[]{:S(2)}, u32[]{:S(2)}) collective-permute-start(bf16[512,1024]{1,0:T(8,128)(2,1)} %convolution_convert_fusion.3), channel_id=1, source_target_pairs={{0,4},{4,0},{8,12},{12,8},{16,20},{20,16},{24,28},{28,24},{1,5},{5... | collective-permute-start | bytes 3145736 | tf_op jit(solution)/shard_map/ppermute | solution.py:82
  157.9 25.6 %collective-permute-start.5 = (bf16[512,1024]{1,0:T(8,128)(2,1)}, bf16[512,1024]{1,0:T(8,128)(2,1)}, u32[]{:S(2)}, u32[]{:S(2)}) collective-permute-start(bf16[512,1024]{1,0:T(8,128)(2,1)} %convolution_convert_fusion.7), channel_id=1, source_target_pairs={{0,4},{4,0},{8,12},{12,8},{16,20},{20,16},{24,28},{28,24},{1,5},{5... | collective-permute-start | bytes 3145736 | tf_op jit(solution)/shard_map/ppermute | solution.py:82
  159.8 27.6 %collective-permute-start.25 = (bf16[512,1024]{1,0:T(8,128)(2,1)}, bf16[512,1024]{1,0:T(8,128)(2,1)}, u32[]{:S(2)}, u32[]{:S(2)}) collective-permute-start(bf16[512,1024]{1,0:T(8,128)(2,1)} %convolution_convert_fusion.5), channel_id=1, source_target_pairs={{0,4},{4,0},{8,12},{12,8},{16,20},{20,16},{24,28},{28,24},{1,5},{5... | collective-permute-start | bytes 3145736 | tf_op jit(solution)/shard_map/ppermute | solution.py:82
  161.3 29.4 %collective-permute-start.19 = (bf16[512,1024]{1,0:T(8,128)(2,1)}, bf16[512,1024]{1,0:T(8,128)(2,1)}, u32[]{:S(2)}, u32[]{:S(2)}) collective-permute-start(bf16[512,1024]{1,0:T(8,128)(2,1)} %convolution_convert_fusion.6), channel_id=1, source_target_pairs={{0,4},{4,0},{8,12},{12,8},{16,20},{20,16},{24,28},{28,24},{1,5},{5... | collective-permute-start | bytes 3145736 | tf_op jit(solution)/shard_map/ppermute | solution.py:82
  230.4 64.5 %collective-permute-start.13 = (bf16[1,1,1,128,1024]{4,3,2,1,0:T(8,128)(2,1)S(1)}, bf16[1,1,1,128,1024]{4,3,2,1,0:T(8,128)(2,1)S(1)}, u32[]{:S(2)}, u32[]{:S(2)}) collective-permute-start(bf16[1,1,1,128,1024]{4,3,2,1,0:T(8,128)(2,1)S(1)} %get-tuple-element.260), channel_id=1, source_target_pairs={{0,16},{4,20},{8,24},{12,28},{16,0},{20,4},{24,8},{28,12},{1,17},{... | collective-permute-start | bytes 786440 | tf_op jit(solution)/shard_map/ppermute | solution.py:66
  310.0 37.5 %collective-permute-start.15 = (bf16[1,2,2,128,1024]{4,3,2,1,0:T(8,128)(2,1)S(1)}, bf16[1,2,2,128,1024]{4,3,2,1,0:T(8,128)(2,1)S(1)}, u32[]{:S(2)}, u32[]{:S(2)}) collective-permute-start(bf16[1,2,2,128,1024]{4,3,2,1,0:T(8,128)(2,1)S(1)} %pad_maximum_fusion.17), channel_id=1, source_target_pairs={{0,4},{4,0},{8,12},{12,8},{16,20},{20,16},{24,28},{28,24},{1,5},{5... | collective-permute-start | bytes 3145736 | tf_op jit(solution)/shard_map/ppermute | solution.py:66
  321.3 26.5 %collective-permute-start.30 = (bf16[1,2,2,128,1024]{4,3,2,1,0:T(8,128)(2,1)S(1)}, bf16[1,2,2,128,1024]{4,3,2,1,0:T(8,128)(2,1)S(1)}, u32[]{:S(2)}, u32[]{:S(2)}) collective-permute-start(bf16[1,2,2,128,1024]{4,3,2,1,0:T(8,128)(2,1)S(1)} %pad_maximum_fusion.21), channel_id=1, source_target_pairs={{0,4},{4,0},{8,12},{12,8},{16,20},{20,16},{24,28},{28,24},{1,5},{5... | collective-permute-start | bytes 3145736 | tf_op jit(solution)/shard_map/ppermute | solution.py:66
  373.1 416.1 %reduce-scatter.29.cloned.1.call-start = ((), (), s32[]{:S(2)}) async-start(), calls=%async_computation.22 | async-start | bytes 1474560 | tf_op jit(solution)/shard_map/reduce_scatter | solution.py:989
  576.5 216.1 %reduce-scatter.27.cloned.1.call-start = ((), (), s32[]{:S(2)}) async-start(), calls=%async_computation.21 | async-start | bytes 983040 | tf_op jit(solution)/shard_map/reduce_scatter | solution.py:989
  609.3 300.7 %reduce-scatter.23.cloned.1.call-start = ((), (), s32[]{:S(2)}) async-start(), calls=%async_computation.19 | async-start | bytes 327680 | tf_op jit(solution)/shard_map/reduce_scatter | solution.py:989
  619.8 290.2 %reduce-scatter.21.cloned.1.call-start = ((), (), s32[]{:S(2)}) async-start(), calls=%async_computation.18 | async-start | bytes 1638400 | tf_op jit(solution)/shard_map/reduce_scatter | solution.py:989
  627.7 282.3 %reduce-scatter.25.cloned.1.call-start = ((), (), s32[]{:S(2)}) async-start(), calls=%async_computation.20 | async-start | bytes 327680 | tf_op jit(solution)/shard_map/reduce_scatter | solution.py:989
  658.7 74.8 %collective-permute-start.75 = (bf16[1,1,128,1024]{3,2,1,0:T(8,128)(2,1)}, bf16[1,1,128,1024]{3,2,1,0:T(8,128)(2,1)S(1)}, u32[]{:S(2)}, u32[]{:S(2)}) collective-permute-start(bf16[1,1,128,1024]{3,2,1,0:T(8,128)(2,1)} %slice.1276), channel_id=1, source_target_pairs={{0,16},{4,20},{8,24},{12,28},{16,0},{20,4},{24,8},{28,12},{1,17},{... | collective-permute-start | bytes 786440 | tf_op jit(solution)/shard_map/ppermute | solution.py:89
  664.0 69.5 %collective-permute-start.84 = (bf16[1,1,128,1024]{3,2,1,0:T(8,128)(2,1)S(1)}, bf16[1,1,128,1024]{3,2,1,0:T(8,128)(2,1)S(1)}, u32[]{:S(2)}, u32[]{:S(2)}) collective-permute-start(bf16[1,1,128,1024]{3,2,1,0:T(8,128)(2,1)S(1)} %slice.1274), channel_id=1, source_target_pairs={{0,8},{4,12},{8,0},{12,4},{16,24},{20,28},{24,16},{28,20},{1,9},{5... | collective-permute-start | bytes 786440 | tf_op jit(solution)/shard_map/ppermute | solution.py:89
  774.4 141.6 %reduce-scatter.17.cloned.1.call-start = ((), (), s32[]{:S(2)}) async-start(), calls=%async_computation.16 | async-start | bytes 1474560 | tf_op jit(solution)/shard_map/reduce_scatter | solution.py:989
  781.9 139.3 %reduce-scatter.15.cloned.1.call-start = ((), (), s32[]{:S(2)}) async-start(), calls=%async_computation.15 | async-start | bytes 327680 | tf_op jit(solution)/shard_map/reduce_scatter | solution.py:989
  812.0 109.3 %reduce-scatter.13.cloned.1.call-start = ((), (), s32[]{:S(2)}) async-start(), calls=%async_computation.14 | async-start | bytes 1638400 | tf_op jit(solution)/shard_map/reduce_scatter | solution.py:989
  819.6 164.7 %reduce-scatter.11.cloned.1.call-start = ((), (), s32[]{:S(2)}) async-start(), calls=%async_computation.13 | async-start | bytes 983040 | tf_op jit(solution)/shard_map/reduce_scatter | solution.py:989
  836.0 104.5 %collective-permute-start.64 = (bf16[512,1024]{1,0:T(8,128)(2,1)}, bf16[512,1024]{1,0:T(8,128)(2,1)}, u32[]{:S(2)}, u32[]{:S(2)}) collective-permute-start(bf16[512,1024]{1,0:T(8,128)(2,1)} %convolution_convert_fusion.11), channel_id=1, source_target_pairs={{0,4},{4,0},{8,12},{12,8},{16,20},{20,16},{24,28},{28,24},{1,5},{5... | collective-permute-start | bytes 3145736 | tf_op jit(solution)/shard_map/ppermute | solution.py:82
  851.0 91.5 %collective-permute-start.70 = (bf16[512,1024]{1,0:T(8,128)(2,1)}, bf16[512,1024]{1,0:T(8,128)(2,1)}, u32[]{:S(2)}, u32[]{:S(2)}) collective-permute-start(bf16[512,1024]{1,0:T(8,128)(2,1)} %convolution_convert_fusion.10), channel_id=1, source_target_pairs={{0,4},{4,0},{8,12},{12,8},{16,20},{20,16},{24,28},{28,24},{1,5},{5... | collective-permute-start | bytes 3145736 | tf_op jit(solution)/shard_map/ppermute | solution.py:82
  877.8 114.1 %reduce-scatter.19.cloned.1.call-start = ((), (), s32[]{:S(2)}) async-start(), calls=%async_computation.17 | async-start | bytes 983040 | tf_op jit(solution)/shard_map/reduce_scatter | solution.py:989
  883.7 70.4 %collective-permute-start.79 = (bf16[512,1024]{1,0:T(8,128)(2,1)}, bf16[512,1024]{1,0:T(8,128)(2,1)}, u32[]{:S(2)}, u32[]{:S(2)}) collective-permute-start(bf16[512,1024]{1,0:T(8,128)(2,1)} %convolution_convert_fusion.9), channel_id=1, source_target_pairs={{0,4},{4,0},{8,12},{12,8},{16,20},{20,16},{24,28},{28,24},{1,5},{5... | collective-permute-start | bytes 3145736 | tf_op jit(solution)/shard_map/ppermute | solution.py:82
  906.2 39.0 %collective-permute-start.88 = (bf16[512,1024]{1,0:T(8,128)(2,1)}, bf16[512,1024]{1,0:T(8,128)(2,1)}, u32[]{:S(2)}, u32[]{:S(2)}) collective-permute-start(bf16[512,1024]{1,0:T(8,128)(2,1)} %convolution_convert_fusion.8), channel_id=1, source_target_pairs={{0,4},{4,0},{8,12},{12,8},{16,20},{20,16},{24,28},{28,24},{1,5},{5... | collective-permute-start | bytes 3145736 | tf_op jit(solution)/shard_map/ppermute | solution.py:82
  925.0 33.9 %all-to-all-start.1 = ((bf16[8,32,1,768]{3,1,2,0:T(8,128)(2,1)}), bf16[8,32,1,768]{3,1,2,0:T(8,128)(2,1)S(1)}, u32[]{:S(2)}, u32[]{:S(2)}) async-start(bf16[8,32,1,768]{3,1,2,0:T(8,128)(2,1)} %maximum_bitcast_fusion.3), calls=%async_computation.4 | async-start | bytes 786432 | tf_op jit(solution)/shard_map/all_to_all | solution.py:1101
  (345 other events, 5921.4 us)
Sparse Core Ops, SparseCore 0:
  10.2 40.1 all-gather.10
  52.5 51.0 all-gather.12
  105.8 29.1 all-gather.16
  136.4 42.8 all-gather.14
  373.2 30.8 all-gather.18
  576.6 26.8 reduce-scatter.28
  609.4 21.0 reduce-scatter.26
  632.7 18.8 reduce-scatter.22
  654.0 29.5 reduce-scatter.20
  774.6 16.8 reduce-scatter.24
  793.8 27.4 reduce-scatter.16
  824.0 18.3 reduce-scatter.14
  844.8 29.4 reduce-scatter.12
  877.9 26.2 reduce-scatter.10
  906.5 24.7 reduce-scatter.18

commit v3 on v2

v3 whole, which is shorter than its diff:
```python
import functools

import jax
import jax.numpy as jnp
from jax import lax
from jax.experimental import pallas as pl
from jax.experimental.layout import Layout, with_layout_constraint
from jax.experimental.pallas import tpu as pltpu
from jax.sharding import PartitionSpec as P

HEADS = 16
HEAD_DIM = 64
EPSILON = 1e-05
MASKED = -1e30
ADAPTER_SCALE = 4.0
SCALING = HEAD_DIM ** (-0.5)
PAD_PREFIX = 32
CHUNK = 256
LANES = 128
VMEM_LIMIT = 60 * 1024 * 1024
HALF_ROOT = 0.7071067811865476
DENSITY = 0.3989422804014327

low = jnp.bfloat16
wide = jnp.float32


def dot(left, right, left_axis, right_axis):
    return lax.dot_general(
        left, right, (((left_axis,), (right_axis,)), ((), ())), preferred_element_type=wide
    )


def bit_list(count):
    bits = []
    value = 1
    while value < count:
        bits.append(value)
        value *= 2
    return bits


def swap_pairs(count, bit):
    return [(index, index ^ bit) for index in range(count)]


def relative(places, seq, me):
    depth = len(bit_list(seq))
    value = places.reshape((2,) * depth + (-1,))
    for axis in range(depth):
        bit = 1 << (depth - 1 - axis)
        value = jnp.where((me & bit) != 0, jnp.flip(value, axis), value)
    return jnp.moveaxis(value, depth - 1, 0).reshape(-1)


def small_gather(value, axes):
    value = value[None]
    for name, count in axes[::-1]:
        me = lax.axis_index(name)
        for bit in bit_list(count):
            other = lax.ppermute(value, name, swap_pairs(count, bit))
            flip = (me & bit) != 0
            value = jnp.where(
                flip, jnp.concatenate([other, value]), jnp.concatenate([value, other])
            )
    return value


def small_scatter(value, axes):
    for name, count in axes:
        me = lax.axis_index(name)
        for bit in bit_list(count)[::-1]:
            half = value.shape[0] // 2
            flip = (me & bit) != 0
            lower, upper = value[:half], value[half:]
            sent = lax.ppermute(jnp.where(flip, lower, upper), name, swap_pairs(count, bit))
            value = jnp.where(flip, upper, lower) + sent
    return value[0]


def normalized(tensor):
    average = jnp.mean(tensor, axis=-1, keepdims=True)
    centered = tensor - average
    spread = jnp.mean(centered * centered, axis=-1, keepdims=True)
    inverse = lax.rsqrt(spread + EPSILON)
    return centered * inverse, inverse


def layer_norm(tensor, scales):
    return normalized(tensor)[0] * scales[0] + scales[1]


def norm_back(upstream, tensor, scales):
    unit, inverse = normalized(tensor)
    slope = upstream * scales[0]
    grad = inverse * (
        slope
        - jnp.mean(slope, axis=-1, keepdims=True)
        - unit * jnp.mean(slope * unit, axis=-1, keepdims=True)
    )
    return (
        grad,
        jnp.sum(upstream * unit, axis=0, keepdims=True),
        jnp.sum(upstream, axis=0, keepdims=True),
    )


def gelu_exact(tensor):
    return tensor * (0.5 + 0.5 * lax.erf(tensor * HALF_ROOT))


def gelu_slope(tensor):
    density = jnp.exp(-0.5 * tensor * tensor) * DENSITY
    return 0.5 + 0.5 * lax.erf(tensor * HALF_ROOT) + tensor * density


class Links:
    def __init__(self, seq):
        self.seq = seq
        self.far = [bit for bit in bit_list(seq) if bit > 1]
        self.orders = [self.far, self.far[::-1]]
        self.half = seq // 2
        self.me = lax.axis_index("seq")

    def place(self, mask):
        return (mask & 1) * self.half + (mask >> 1)

    def device(self, bit):
        return {"seq": jnp.bitwise_xor(self.me, bit)}

    def enter(self):
        barrier = pltpu.get_barrier_semaphore()
        bits = bit_list(self.seq)
        for bit in bits:
            pl.semaphore_signal(
                barrier, inc=1, device_id=self.device(bit), device_id_type=pl.DeviceIdType.MESH
            )
        pl.semaphore_wait(barrier, len(bits))

    def copy(self, source, target, send_sem, recv_sem, bit):
        return pltpu.make_async_remote_copy(
            src_ref=source,
            dst_ref=target,
            send_sem=send_sem,
            recv_sem=recv_sem,
            device_id=self.device(bit),
            device_id_type=pl.DeviceIdType.MESH,
        )


def span(bits):
    masks = [0]
    for bit in bits:
        masks = masks + [mask | bit for mask in masks]
    return masks


class Gather:
    def __init__(self, links, own_ref, all_ref, sends, recvs, local_sem):
        self.links, self.own, self.all = links, own_ref, all_ref
        self.sends, self.recvs, self.local = sends, recvs, local_sem
        self.rows = own_ref.shape[1]
        self.cut = self.rows // 2

    def at(self, micro, mask, part):
        start = self.links.place(mask) * self.rows + part * self.cut
        return self.all.at[micro, start : start + self.cut]

    def piece(self, micro, mask, part):
        if mask & 1:
            return 1
        seen = 0
        for bit in self.links.orders[part]:
            if mask & bit:
                seen = bit
        return seen

    def send(self, micro, mask, part, bit):
        there = mask ^ bit
        source = self.at(micro, mask, part)
        if mask == 0:
            source = self.own.at[micro, part * self.cut : (part + 1) * self.cut]
        self.links.copy(
            source,
            self.at(micro, there, part),
            self.sends.at[micro, self.links.place(there), part],
            self.recvs.at[micro, self.links.place(there), part],
            bit,
        ).start()

    def descriptor(self, micro, mask, part):
        bit = self.piece(micro, mask, part)
        source = self.at(micro, mask ^ bit, part)
        if mask ^ bit == 0:
            source = self.own.at[micro, part * self.cut : (part + 1) * self.cut]
        place = self.links.place(mask)
        return self.links.copy(
            source,
            self.at(micro, mask, part),
            self.sends.at[micro, place, part],
            self.recvs.at[micro, place, part],
            bit,
        )

    def keep_own(self, micro):
        return pltpu.make_async_copy(
            self.own.at[micro], self.all.at[micro, 0 : self.rows], self.local.at[micro]
        )

    def start(self, micro):
        for part in range(2):
            self.send(micro, 0, part, self.links.orders[part][0])
        for part in range(2):
            self.send(micro, 0, part, 1)
        self.keep_own(micro).start()

    def advance(self, micro, phase):
        count = len(self.links.far)
        for part in range(2):
            order = self.links.orders[part]
            fresh = [mask | order[phase] for mask in span(order[:phase])]
            for mask in fresh:
                self.descriptor(micro, mask, part).wait_recv()
            if phase + 1 < count:
                for mask in span(order[: phase + 1]):
                    self.send(micro, mask, part, order[phase + 1])
            for mask in fresh:
                self.send(micro, mask, part, 1)

    def phases(self):
        return len(self.links.far)

    def near(self, micro):
        for part in range(2):
            for mask in span(self.links.far):
                self.descriptor(micro, mask | 1, part).wait_recv()
        self.keep_own(micro).wait()

    def drain(self, micro):
        for part in range(2):
            for mask in range(1, self.links.seq):
                self.descriptor(micro, mask, part).wait_send()


class Scatter:
    def __init__(self, links, rows, sum_ref, near_send, near_recv, far_send, far_recv, sems):
        self.links, self.rows, self.cut = links, rows, rows // 2
        self.sum, self.near_send, self.near_recv = sum_ref, near_send, near_recv
        self.far_send, self.far_recv = far_send, far_recv
        self.near_sems, self.far_sems = sems

    def near_copy(self, micro, index):
        view = slice(index * self.rows, (index + 1) * self.rows)
        return self.links.copy(
            self.near_send.at[micro, view],
            self.near_recv.at[micro, view],
            self.near_sems.at[0, micro, index],
            self.near_sems.at[1, micro, index],
            1,
        )

    def start(self, micro, indexes):
        for index in indexes:
            self.near_copy(micro, index).start()

    def far_view(self, index, part):
        start = index * self.rows + part * self.cut
        return slice(start, start + self.cut)

    def bit_of(self, index, part):
        last = 0
        for bit in self.links.orders[part]:
            if (index * 2) & bit:
                last = bit
        return last

    def far_copy(self, micro, index, part):
        view = self.far_view(index, part)
        return self.links.copy(
            self.far_send.at[micro, view],
            self.far_recv.at[micro, view],
            self.far_sems.at[0, micro, index, part],
            self.far_sems.at[1, micro, index, part],
            self.bit_of(index, part),
        )

    def send_far(self, micro, index, part, value):
        self.far_send[micro, self.far_view(index, part)] = value.astype(low)
        self.far_copy(micro, index, part).start()

    def near_sum(self, micro):
        count = len(self.links.far)
        first = {}
        for part in range(2):
            bit = self.links.orders[part][count - 1]
            first[part] = [mask | bit for mask in span(self.links.orders[part][: count - 1])]
        ordered = sorted(range(self.links.half), key=lambda index: index == 0)
        for index in ordered:
            self.near_copy(micro, index).wait_recv()
            for part in range(2):
                view = self.far_view(index, part)
                value = self.sum[micro, view] + self.near_recv[micro, view].astype(wide)
                if index * 2 in first[part]:
                    self.send_far(micro, index, part, value)
                else:
                    self.sum[micro, view] = value

    def far_sum(self, micro, phase):
        count = len(self.links.far)
        for part in range(2):
            order = self.links.orders[part]
            bit = order[count - 1 - phase]
            remain = span(order[: count - 1 - phase])
            following = order[count - 2 - phase] if phase + 1 < count else 0
            for mask in sorted(remain, key=lambda mask: (mask & following) == 0):
                index, came = mask // 2, (mask | bit) // 2
                self.far_copy(micro, came, part).wait_recv()
                view = self.far_view(index, part)
                value = self.sum[micro, view] + self.far_recv[
                    micro, self.far_view(came, part)
                ].astype(wide)
                if mask & following:
                    self.send_far(micro, index, part, value)
                else:
                    self.sum[micro, view] = value

    def total(self, micro):
        return self.sum[micro, 0 : self.rows]

    def phases(self):
        return len(self.links.far)

    def drain(self, micro):
        for index in range(self.links.half):
            self.near_copy(micro, index).wait_send()
        for part in range(2):
            for index in range(1, self.links.half):
                self.far_copy(micro, index, part).wait_send()


def gather_scratch(seq, micros):
    return [
        pltpu.SemaphoreType.DMA((micros, seq, 2)),
        pltpu.SemaphoreType.DMA((micros, seq, 2)),
        pltpu.SemaphoreType.DMA((micros,)),
    ]


def scatter_scratch(seq, micros, rows, width):
    half = seq // 2
    part = pltpu.VMEM((micros, half * rows, width), low)
    return [
        pltpu.VMEM((micros, half * rows, width), wide),
        part,
        part,
        part,
        part,
        pltpu.SemaphoreType.DMA((2, micros, half)),
        pltpu.SemaphoreType.DMA((2, micros, half, 2)),
    ]


def merged(first, second):
    steps = []
    for index in range(max(len(first), len(second))):
        steps += first[index : index + 1] + second[index : index + 1]
    return steps


def run_stage(micros, arrive, compute, leave):
    for step in arrive(0):
        step()
    for micro in range(micros):
        other = (leave(micro - 1) if micro > 0 else []) + (
            arrive(micro + 1) if micro + 1 < micros else []
        )
        for step in merged(compute(micro), other):
            step()
    for step in leave(micros - 1):
        step()


def arrive_steps(gathers, micro):
    steps = []
    for gather in gathers:
        for phase in range(gather.phases()):
            steps.append(functools.partial(gather.advance, micro, phase))
    return steps + [functools.partial(gather.near, micro) for gather in gathers]


def leave_steps(scatters, finish, micro):
    steps = [functools.partial(scatter.near_sum, micro) for scatter in scatters]
    for phase in range(scatters[0].phases()):
        for scatter in scatters:
            steps.append(functools.partial(scatter.far_sum, micro, phase))
    return steps + [functools.partial(finish, micro)]


def half_steps(scatter, micro, length, chunk):
    half = length // 2
    size = min(CHUNK, half)

    def odd():
        def body(index, carry):
            start = pl.multiple_of(half + index * size, size)
            place = pl.ds(pl.multiple_of(index * size, size), size)
            scatter.near_send[micro, place] = chunk(start, size).astype(low)
            return carry

        lax.fori_loop(0, half // size, body, 0)
        scatter.start(micro, range(scatter.links.half))

    def even():
        def body(index, carry):
            start = pl.multiple_of(index * size, size)
            scatter.sum[micro, pl.ds(start, size)] = chunk(start, size)
            return carry

        lax.fori_loop(0, half // size, body, 0)

    return [odd, even]


def ffn_kernel(
    seq, own_ref, resid_ref, one_ref, two_ref, pair_ref, all_ref, before_ref, hidden_ref, sum_ref,
    norm_ref, *scratch,
):
    links = Links(seq)
    micros, rows, _ = own_ref.shape
    length = all_ref.shape[1]
    gather = Gather(links, own_ref, all_ref, *scratch[:3])
    scatter = Scatter(links, rows, *scratch[3:8], scratch[8:])
    links.enter()
    for micro in range(micros):
        gather.start(micro)

    def compute(micro):
        def chunk(start, size):
            place = pl.ds(start, size)
            before = dot(all_ref[micro, place], one_ref[...], 1, 1)
            before_ref[micro, place] = before
            after = gelu_exact(before).astype(low)
            hidden_ref[micro, place] = after
            return dot(after, two_ref[...], 1, 1)

        return half_steps(scatter, micro, length, chunk)

    def finish(micro):
        total = resid_ref[micro] + scatter.total(micro)
        sum_ref[micro] = total
        norm_ref[micro] = layer_norm(total, (pair_ref[0:1], pair_ref[1:2]))

    run_stage(
        micros,
        functools.partial(arrive_steps, [gather]),
        compute,
        functools.partial(leave_steps, [scatter], finish),
    )
    for micro in range(micros):
        gather.drain(micro)
        scatter.drain(micro)


def stage_call(kernel, name_id, outs, scratch, args, micros):
    return pl.pallas_call(
        kernel,
        out_shape=outs,
        in_specs=[pl.BlockSpec(memory_space=pltpu.VMEM)] * len(args),
        out_specs=tuple(pl.BlockSpec(memory_space=pltpu.VMEM) for _ in outs),
        scratch_shapes=scratch,
        compiler_params=pltpu.CompilerParams(
            collective_id=name_id, has_side_effects=True, vmem_limit_bytes=VMEM_LIMIT
        ),
        cost_estimate=pl.CostEstimate(
            flops=micros * 2_500_000_000, bytes_accessed=1 << 24, transcendentals=0
        ),
    )(*args)


def ffn_stage(seq, name_id, own, resid, one, two, pair):
    micros, rows, width = own.shape
    hidden = one.shape[0]
    length = rows * seq
    outs = (
        jax.ShapeDtypeStruct((micros, length, width), low),
        jax.ShapeDtypeStruct((micros, length, hidden), wide),
        jax.ShapeDtypeStruct((micros, length, hidden), low),
        jax.ShapeDtypeStruct((micros, rows, width), wide),
        jax.ShapeDtypeStruct((micros, rows, width), wide),
    )
    scratch = gather_scratch(seq, micros) + scatter_scratch(seq, micros, rows, width)
    return stage_call(
        functools.partial(ffn_kernel, seq), name_id, outs, scratch,
        (own, resid, one, two, pair), 60,
    )


def prologue(micro, up_ref, resid_ref, pair_ref, own_ref, kept_ref, pair_grad_ref):
    gains = (pair_ref[0:1], pair_ref[1:2])
    grad, gain_grad, shift_grad = norm_back(up_ref[micro].astype(wide), resid_ref[micro], gains)
    kept_ref[micro] = grad
    own_ref[micro] = grad.astype(low)
    if micro == 0:
        pair_grad_ref[0:1] = gain_grad
        pair_grad_ref[1:2] = shift_grad
    else:
        pair_grad_ref[0:1] += gain_grad
        pair_grad_ref[1:2] += shift_grad


def ffn_back_kernel(
    seq, up_ref, resid_ref, pair_ref, before_ref, one_ref, two_ref, all_ref, slope_ref, out_ref,
    pair_grad_ref, own_ref, kept_ref, *scratch,
):
    links = Links(seq)
    micros, rows, _ = own_ref.shape
    length = all_ref.shape[1]
    gather = Gather(links, own_ref, all_ref, *scratch[:3])
    scatter = Scatter(links, rows, *scratch[3:8], scratch[8:])
    links.enter()
    for micro in range(micros):
        prologue(micro, up_ref, resid_ref, pair_ref, own_ref, kept_ref, pair_grad_ref)
        gather.start(micro)

    def compute(micro):
        def chunk(start, size):
            place = pl.ds(start, size)
            slope = dot(all_ref[micro, place], two_ref[...], 1, 0)
            slope = (slope * gelu_slope(before_ref[micro, place])).astype(low)
            slope_ref[micro, place] = slope
            return dot(slope, one_ref[...], 1, 0)

        return half_steps(scatter, micro, length, chunk)

    def finish(micro):
        out_ref[micro] = kept_ref[micro] + scatter.total(micro)

    run_stage(
        micros,
        functools.partial(arrive_steps, [gather]),
        compute,
        functools.partial(leave_steps, [scatter], finish),
    )
    for micro in range(micros):
        gather.drain(micro)
        scatter.drain(micro)


def ffn_back_stage(seq, name_id, up, resid, pair, before, one, two):
    micros, rows, width = up.shape
    hidden = one.shape[0]
    length = rows * seq
    outs = (
        jax.ShapeDtypeStruct((micros, length, width), low),
        jax.ShapeDtypeStruct((micros, length, hidden), low),
        jax.ShapeDtypeStruct((micros, rows, width), wide),
        jax.ShapeDtypeStruct((2, width), wide),
    )
    scratch = (
        [pltpu.VMEM((micros, rows, width), low), pltpu.VMEM((micros, rows, width), wide)]
        + gather_scratch(seq, micros)
        + scatter_scratch(seq, micros, rows, width)
    )
    return stage_call(
        functools.partial(ffn_back_kernel, seq), name_id, outs, scratch,
        (up, resid, pair, before, one, two), 60,
    )


class Task:
    def __init__(self, begin, arrive, compute, leave, drain):
        self.begin, self.arrive, self.compute = begin, arrive, compute
        self.leave, self.drain = leave, drain


def spread(first, second):
    steps, done = [], 0
    for index, step in enumerate(first):
        steps.append(step)
        upto = len(second) * (index + 1) // len(first)
        steps += second[done:upto]
        done = upto
    return steps + second[done:]


def run_tasks(tasks):
    for task in tasks[:2]:
        task.begin()
    for step in tasks[0].arrive:
        step()
    for index, task in enumerate(tasks):
        other = []
        if index > 0:
            other += tasks[index - 1].leave
        if index + 1 < len(tasks):
            other += tasks[index + 1].arrive
        if index + 2 < len(tasks):
            other.append(tasks[index + 2].begin)
        for step in spread(task.compute, other):
            step()
    for step in tasks[-1].leave:
        step()
    for task in tasks:
        task.drain()


def make_task(micro, gathers, scatters, compute, finish, before=None):
    def begin():
        if before is not None:
            before(micro)
        for gather in gathers:
            gather.start(micro)

    def drain():
        for item in gathers + scatters:
            item.drain(micro)

    arrive = arrive_steps(gathers, micro)
    leave = leave_steps(scatters, finish, micro) if scatters else []
    return Task(begin, arrive, compute(micro), leave, drain)


def gather_kernel(seq, count, *refs):
    links = Links(seq)
    owns, alls, scratch = refs[:count], refs[count : 2 * count], refs[2 * count :]
    gathers = [
        Gather(links, owns[k], alls[k], *scratch[3 * k : 3 * k + 3]) for k in range(count)
    ]
    links.enter()
    tasks = []
    for gather in gathers:
        for micro in range(owns[0].shape[0]):
            tasks.append(make_task(micro, [gather], [], lambda micro: [], None))
    for task in tasks:
        task.begin()
    for phase in range(len(tasks[0].arrive)):
        for task in tasks:
            task.arrive[phase]()
    for task in tasks:
        task.drain()


def gather_stage(seq, name_id, owns):
    micros, rows, width = owns[0].shape
    outs = tuple(jax.ShapeDtypeStruct((micros, seq * rows, width), low) for _ in owns)
    scratch = gather_scratch(seq, micros) * len(owns)
    return stage_call(
        functools.partial(gather_kernel, seq, len(owns)), name_id, outs, scratch, owns, 45
    )


class Attention:
    def __init__(self, q_ref, kv_ref, offsets, prefix_ref, ids, count, causal):
        self.q, self.kv, self.offsets, self.prefix = q_ref, kv_ref, offsets, prefix_ref
        self.key_ids, self.query_ids, self.key_places, self.query_places = ids
        self.count, self.causal = count, causal
        self.heads = prefix_ref.shape[2] // HEAD_DIM

    def load(self, micro, head, place):
        q_at, k_at, v_at = (at + head * HEAD_DIM for at in self.offsets)
        queries = self.q[micro, place, q_at : q_at + HEAD_DIM] * jnp.asarray(SCALING, low)
        keys = self.kv[micro, :, k_at : k_at + HEAD_DIM]
        values = self.kv[micro, :, v_at : v_at + HEAD_DIM]
        return queries, keys, values

    def scores(self, micro, keys, queries, lanes, place):
        scores = dot(keys, queries, 1, 1)
        allowed = self.key_ids[micro] == self.query_ids[micro, :, place]
        if self.causal:
            allowed = allowed & (self.key_places[...] <= self.query_places[:, place])
        scores = jnp.where(allowed, scores, MASKED)
        extra = dot(self.prefix[0, :, lanes], queries, 1, 1)
        rows = lax.broadcasted_iota(jnp.int32, extra.shape, 0)
        return scores, jnp.where(rows < self.count, extra, MASKED)

    def forward(self, micro, start, size, context_ref, logs_ref):
        place = pl.ds(start, size)
        for head in range(self.heads):
            lanes = slice(head * HEAD_DIM, (head + 1) * HEAD_DIM)
            queries, keys, values = self.load(micro, head, place)
            scores, extra = self.scores(micro, keys, queries, lanes, place)
            peak = jnp.maximum(
                jnp.max(scores, axis=0, keepdims=True), jnp.max(extra, axis=0, keepdims=True)
            )
            scores = jnp.exp(scores - peak)
            extra = jnp.exp(extra - peak)
            total = jnp.sum(scores, axis=0, keepdims=True) + jnp.sum(extra, axis=0, keepdims=True)
            context = dot(values, scores.astype(low), 0, 0)
            context = context + dot(self.prefix[1, :, lanes], extra.astype(low), 0, 0)
            context_ref[micro, place, lanes] = (context / total).T.astype(low)
            logs_ref[micro, head : head + 1, place] = peak + jnp.log(total)

    def backward(self, micro, start, size, up_ref, logs_ref, grad_ref, k_sum, v_sum, pre_ref):
        place = pl.ds(start, size)
        for head in range(self.heads):
            lanes = slice(head * HEAD_DIM, (head + 1) * HEAD_DIM)
            queries, keys, values = self.load(micro, head, place)
            scores, extra = self.scores(micro, keys, queries, lanes, place)
            logs = logs_ref[micro, head : head + 1, place]
            weights = jnp.exp(scores - logs)
            extra = jnp.exp(extra - logs)
            up = up_ref[:, lanes]
            dots = dot(values, up, 1, 1)
            extra_dots = dot(self.prefix[1, :, lanes], up, 1, 1)
            centre = jnp.sum(weights * dots, axis=0, keepdims=True) + jnp.sum(
                extra * extra_dots, axis=0, keepdims=True
            )
            slope = (weights * (dots - centre)).astype(low)
            extra_slope = (extra * (extra_dots - centre)).astype(low)
            query_grad = dot(keys, slope, 0, 0) + dot(self.prefix[0, :, lanes], extra_slope, 0, 0)
            grad_ref[micro, place, lanes] = (query_grad * SCALING).T.astype(low)
            k_sum[:, lanes] += dot(slope, queries, 1, 0)
            v_sum[:, lanes] += dot(weights.astype(low), up, 1, 0)
            pre_ref[0, :, lanes] += dot(extra_slope, queries, 1, 0)
            pre_ref[1, :, lanes] += dot(extra.astype(low), up, 1, 0)


def loop(first, count, size, body):
    def step(index, carry):
        body(pl.multiple_of(first + index * size, size), index)
        return carry

    lax.fori_loop(0, count, step, 0)


def project_steps(micro, rows_ref, weight_ref, out_ref):
    length = rows_ref.shape[1]
    size = min(CHUNK, length)

    def body(start, index):
        place = pl.ds(start, size)
        out_ref[micro, place] = dot(rows_ref[micro, place], weight_ref[...], 1, 1).astype(low)

    return [lambda: loop(0, length // size, size, body)]


def self_kernel(seq, count, *refs):
    kinds = 2
    scratch = refs[-kinds * 7 :]
    refs = refs[: -kinds * 7]
    places = refs[:2]
    links = Links(seq)
    links.enter()
    tasks = []
    for kind in range(kinds):
        (all_ref, own_ref, in_ref, out_ref, prefix_ref, kid_ref, qid_ref, pair_ref) = refs[
            2 + 8 * kind : 10 + 8 * kind
        ]
        (qkv_ref, context_ref, logs_ref, sum_ref, norm_ref, low_ref) = refs[
            2 + 8 * kinds + 6 * kind : 8 + 8 * kinds + 6 * kind
        ]
        micros, rows, _ = own_ref.shape
        length = all_ref.shape[1]
        head_width = prefix_ref.shape[2]
        piece = scratch[7 * kind : 7 * kind + 7]
        scatter = Scatter(links, rows, *piece[:5], piece[5:])
        ids = (kid_ref, qid_ref) + tuple(places)
        attention = Attention(
            qkv_ref, qkv_ref, (0, head_width, 2 * head_width), prefix_ref, ids, count, kind == 1
        )

        def compute(
            micro, attention=attention, context_ref=context_ref, logs_ref=logs_ref,
            out_ref=out_ref, all_ref=all_ref, in_ref=in_ref, qkv_ref=qkv_ref, scatter=scatter,
        ):
            def chunk(start, size):
                attention.forward(micro, start, size, context_ref, logs_ref)
                return dot(context_ref[micro, pl.ds(start, size)], out_ref[...], 1, 1)

            return project_steps(micro, all_ref, in_ref, qkv_ref) + half_steps(
                scatter, micro, length, chunk
            )

        def finish(
            micro, own_ref=own_ref, scatter=scatter, sum_ref=sum_ref, norm_ref=norm_ref,
            low_ref=low_ref, pair_ref=pair_ref,
        ):
            total = own_ref[micro].astype(wide) + scatter.total(micro)
            sum_ref[micro] = total
            value = layer_norm(total, (pair_ref[0:1], pair_ref[1:2]))
            norm_ref[micro] = value
            low_ref[micro] = value.astype(low)

        for micro in range(micros):
            tasks.append(make_task(micro, [], [scatter], compute, finish))
    run_tasks(tasks)


def self_stage(seq, name_id, count, places, sides):
    micros, rows, width = sides[0][1].shape
    length = rows * seq
    head_width = sides[0][4].shape[2]
    heads = head_width // HEAD_DIM
    side_outs = (
        jax.ShapeDtypeStruct((micros, length, 3 * head_width), low),
        jax.ShapeDtypeStruct((micros, length, head_width), low),
        jax.ShapeDtypeStruct((micros, heads, length), wide),
        jax.ShapeDtypeStruct((micros, rows, width), wide),
        jax.ShapeDtypeStruct((micros, rows, width), wide),
        jax.ShapeDtypeStruct((micros, rows, width), low),
    )
    scratch = scatter_scratch(seq, micros, rows, width) * 2
    args = tuple(places) + sides[0] + sides[1]
    outs = stage_call(
        functools.partial(self_kernel, seq, count), name_id, side_outs * 2, scratch, args, 75
    )
    return outs[:6], outs[6:]


def cross_kernel(
    seq, count, kpos_ref, qpos_ref, first_ref, first_low_ref, memory_ref, q_in_ref, kv_in_ref,
    out_ref, prefix_ref, kid_ref, qid_ref, pair_ref, first_all, memory_all, q_ref, kv_ref,
    context_ref, logs_ref, sum_ref, norm_ref, low_ref, *scratch,
):
    links = Links(seq)
    micros, rows, _ = first_ref.shape
    length = first_all.shape[1]
    head_width = prefix_ref.shape[2]
    gathers = [
        Gather(links, memory_ref, memory_all, *scratch[:3]),
        Gather(links, first_low_ref, first_all, *scratch[3:6]),
    ]
    scatter = Scatter(links, rows, *scratch[6:11], scratch[11:])
    ids = (kid_ref, qid_ref, kpos_ref, qpos_ref)
    attention = Attention(q_ref, kv_ref, (0, 0, head_width), prefix_ref, ids, count, False)
    links.enter()

    def compute(micro):
        def chunk(start, size):
            attention.forward(micro, start, size, context_ref, logs_ref)
            return dot(context_ref[micro, pl.ds(start, size)], out_ref[...], 1, 1)

        return (
            project_steps(micro, memory_all, kv_in_ref, kv_ref)
            + project_steps(micro, first_all, q_in_ref, q_ref)
            + half_steps(scatter, micro, length, chunk)
        )

    def finish(micro):
        total = first_ref[micro] + scatter.total(micro)
        sum_ref[micro] = total
        value = layer_norm(total, (pair_ref[0:1], pair_ref[1:2]))
        norm_ref[micro] = value
        low_ref[micro] = value.astype(low)

    run_tasks(
        [make_task(micro, gathers, [scatter], compute, finish) for micro in range(micros)]
    )


def cross_stage(seq, name_id, count, places, args):
    micros, rows, width = args[0].shape
    length = rows * seq
    head_width = args[6].shape[2]
    heads = head_width // HEAD_DIM
    whole = jax.ShapeDtypeStruct((micros, length, width), low)
    outs = (
        whole,
        whole,
        jax.ShapeDtypeStruct((micros, length, head_width), low),
        jax.ShapeDtypeStruct((micros, length, 2 * head_width), low),
        jax.ShapeDtypeStruct((micros, length, head_width), low),
        jax.ShapeDtypeStruct((micros, heads, length), wide),
        jax.ShapeDtypeStruct((micros, rows, width), wide),
        jax.ShapeDtypeStruct((micros, rows, width), wide),
        jax.ShapeDtypeStruct((micros, rows, width), low),
    )
    scratch = gather_scratch(seq, micros) * 2 + scatter_scratch(seq, micros, rows, width)
    return stage_call(
        functools.partial(cross_kernel, seq, count), name_id, outs, scratch,
        tuple(places) + args, 85,
    )


def attend_back_steps(
    attention, micro, length, up_all, out_ref, logs_ref, grad_ref, k_sum, v_sum, pre_ref, up_ref,
    emit=None,
):
    head_width = up_ref.shape[1]
    half = length // 2
    size = min(CHUNK, half)

    def run(first, zero):
        if zero:
            k_sum[...] = jnp.zeros_like(k_sum)
            v_sum[...] = jnp.zeros_like(v_sum)
            if micro == 0:
                pre_ref[...] = jnp.zeros_like(pre_ref)

        def body(start, index):
            place = pl.ds(start, size)
            up_ref[...] = dot(up_all[micro, place], out_ref[...], 1, 0).astype(low)
            attention.backward(
                micro, start, size, up_ref, logs_ref, grad_ref, k_sum, v_sum, pre_ref
            )
            if emit is not None:
                emit(start, index, size)

        loop(first, half // size, size, body)

    def keys():
        grad_ref[micro, :, head_width : 2 * head_width] = k_sum[...].astype(low)
        grad_ref[micro, :, 2 * head_width : 3 * head_width] = v_sum[...].astype(low)

    return [lambda: run(half, True), lambda: run(0, False), keys]


def cross_back_kernel(
    seq, count, kpos_ref, qpos_ref, up_ref, resid_ref, pair_ref, q_ref, kv_ref, logs_ref, q_in_ref,
    kv_in_ref, out_ref, prefix_ref, kid_ref, qid_ref, up_all, grad_ref, pre_ref, first_out,
    memory_out, pair_grad_ref, own_ref, kept_ref, k_sum, v_sum, up_chunk, *scratch,
):
    links = Links(seq)
    micros, rows, _ = own_ref.shape
    length = up_all.shape[1]
    head_width = prefix_ref.shape[2]
    gather = Gather(links, own_ref, up_all, *scratch[:3])
    first_sum = Scatter(links, rows, *scratch[3:8], scratch[8:10])
    memory_sum = Scatter(links, rows, *scratch[10:15], scratch[15:17])
    ids = (kid_ref, qid_ref, kpos_ref, qpos_ref)
    attention = Attention(q_ref, kv_ref, (0, 0, head_width), prefix_ref, ids, count, False)
    links.enter()

    def before(micro):
        prologue(micro, up_ref, resid_ref, pair_ref, own_ref, kept_ref, pair_grad_ref)

    def compute(micro):
        def first_chunk(start, size):
            return dot(
                grad_ref[micro, pl.ds(start, size), 0:head_width], q_in_ref[...], 1, 0
            )

        def memory_chunk(start, size):
            return dot(
                grad_ref[micro, pl.ds(start, size), head_width : 3 * head_width],
                kv_in_ref[...],
                1,
                0,
            )

        attend = attend_back_steps(
            attention, micro, length, up_all, out_ref, logs_ref, grad_ref, k_sum, v_sum, pre_ref,
            up_chunk,
        )
        sums = half_steps(first_sum, micro, length, first_chunk)
        return (
            [attend[0], sums[0], attend[1], sums[1], attend[2]]
            + half_steps(memory_sum, micro, length, memory_chunk)
        )

    def finish(micro):
        first_out[micro] = kept_ref[micro] + first_sum.total(micro)
        memory_out[micro] = memory_sum.total(micro)

    run_tasks(
        [
            make_task(micro, [gather], [first_sum, memory_sum], compute, finish, before)
            for micro in range(micros)
        ]
    )


def cross_back_stage(seq, name_id, count, places, args):
    micros, rows, width = args[0].shape
    length = rows * seq
    head_width = args[9].shape[2]
    own = jax.ShapeDtypeStruct((micros, rows, width), wide)
    outs = (
        jax.ShapeDtypeStruct((micros, length, width), low),
        jax.ShapeDtypeStruct((micros, length, 3 * head_width), low),
        jax.ShapeDtypeStruct((2, PAD_PREFIX, head_width), wide),
        own,
        own,
        jax.ShapeDtypeStruct((2, width), wide),
    )
    scratch = (
        back_scratch(micros, rows, width)
        + sum_scratch(length, head_width)
        + gather_scratch(seq, micros)
        + scatter_scratch(seq, micros, rows, width) * 2
    )
    return stage_call(
        functools.partial(cross_back_kernel, seq, count), name_id, outs, scratch,
        tuple(places) + args, 85,
    )


def back_scratch(micros, rows, width):
    return [pltpu.VMEM((micros, rows, width), low), pltpu.VMEM((micros, rows, width), wide)]


def sum_scratch(length, head_width):
    return [
        pltpu.VMEM((length, head_width), wide),
        pltpu.VMEM((length, head_width), wide),
        pltpu.VMEM((min(CHUNK, length // 2), head_width), low),
    ]


def self_back_kernel(seq, count, causals, *refs):
    kinds = len(causals)
    size = 2 + 3 + 7
    scratch = refs[-(3 + kinds * size) :]
    refs = refs[: -(3 + kinds * size)]
    k_sum, v_sum, up_chunk = scratch[:3]
    places = refs[:2]
    links = Links(seq)
    links.enter()
    tasks = []
    for kind in range(kinds):
        (
            up_ref, resid_ref, pair_ref, qkv_ref, logs_ref, in_ref, out_ref, prefix_ref, kid_ref,
            qid_ref,
        ) = refs[2 + 10 * kind : 12 + 10 * kind]
        up_all, grad_ref, pre_ref, grad_out, pair_grad_ref = refs[
            2 + 10 * kinds + 5 * kind : 7 + 10 * kinds + 5 * kind
        ]
        piece = scratch[3 + size * kind : 3 + size * kind + size]
        own_ref, kept_ref = piece[:2]
        micros, rows, _ = own_ref.shape
        length = up_all.shape[1]
        head_width = prefix_ref.shape[2]
        gather = Gather(links, own_ref, up_all, *piece[2:5])
        scatter = Scatter(links, rows, *piece[5:10], piece[10:12])
        ids = (kid_ref, qid_ref) + tuple(places)
        attention = Attention(
            qkv_ref, qkv_ref, (0, head_width, 2 * head_width), prefix_ref, ids, count, causals[kind]
        )

        def before(
            micro, args=(up_ref, resid_ref, pair_ref, own_ref, kept_ref, pair_grad_ref)
        ):
            prologue(micro, *args)

        def compute(
            micro, attention=attention, up_all=up_all, out_ref=out_ref, logs_ref=logs_ref,
            grad_ref=grad_ref, pre_ref=pre_ref, in_ref=in_ref, scatter=scatter,
        ):
            def chunk(start, size):
                return dot(grad_ref[micro, pl.ds(start, size)], in_ref[...], 1, 0)

            return attend_back_steps(
                attention, micro, length, up_all, out_ref, logs_ref, grad_ref, k_sum, v_sum,
                pre_ref, up_chunk,
            ) + half_steps(scatter, micro, length, chunk)

        def finish(micro, grad_out=grad_out, kept_ref=kept_ref, scatter=scatter):
            grad_out[micro] = kept_ref[micro] + scatter.total(micro)

        for micro in range(micros):
            tasks.append(make_task(micro, [gather], [scatter], compute, finish, before))
    run_tasks(tasks)


def self_back_stage(seq, name_id, count, places, causal, side):
    micros, rows, width = side[0].shape
    length = rows * seq
    head_width = side[7].shape[2]
    outs = (
        jax.ShapeDtypeStruct((micros, length, width), low),
        jax.ShapeDtypeStruct((micros, length, 3 * head_width), low),
        jax.ShapeDtypeStruct((2, PAD_PREFIX, head_width), wide),
        jax.ShapeDtypeStruct((micros, rows, width), wide),
        jax.ShapeDtypeStruct((2, width), wide),
    )
    scratch = sum_scratch(length, head_width) + (
        back_scratch(micros, rows, width)
        + gather_scratch(seq, micros)
        + scatter_scratch(seq, micros, rows, width)
    )
    return stage_call(
        functools.partial(self_back_kernel, seq, count, (causal,)), name_id, outs, scratch,
        tuple(places) + side, 75,
    )


def local(
    seq, ranks,
    source, target, source_segments, target_segments, cotangent,
    encoder_qkv, encoder_output, encoder_prefix, encoder_expand, encoder_contract, encoder_down,
    encoder_up, encoder_norms, decoder_qkv, decoder_output, decoder_prefix, cross_query, cross_kv,
    cross_output, cross_prefix, decoder_expand, decoder_contract, decoder_down, decoder_up,
    decoder_norms,
):
    micro_count, batch_rows, block, width = source.shape
    length = source_segments.shape[2]
    me = lax.axis_index("seq")
    stacked = micro_count * batch_rows
    head_width = width // seq
    slice_cols = encoder_output.shape[1]
    count = encoder_prefix.shape[1]
    hidden = encoder_contract.shape[0] // seq
    adapt = encoder_up.shape[0] // seq
    both = hidden + adapt
    padded = (both + LANES - 1) // LANES * LANES

    sources = source.reshape(stacked, block, width)
    targets = target.reshape(stacked, block, width)

    order = relative(jnp.arange(length, dtype=jnp.int32), seq, me)
    places = (order[:, None], order[None, :])

    def relative_ids(ids):
        rows = [relative(row, seq, me) for row in ids.reshape(stacked, length)]
        value = jnp.stack(rows)
        return value[:, :, None], value[:, None, :]

    source_keys, source_queries = relative_ids(source_segments)
    target_keys, target_queries = relative_ids(target_segments)

    def columns(weight):
        return jnp.swapaxes(weight, -1, -2)

    def gather_rows(value):
        return lax.all_gather(value, "rows", axis=0, tiled=False)

    def stack_columns(pieces):
        gathered = gather_rows(jnp.concatenate(pieces, axis=0))
        outs = []
        start = 0
        for piece in pieces:
            size = piece.shape[0]
            outs.append(gathered[:, start : start + size])
            start += size
        return outs

    def flat_columns(gathered, parts):
        value = gathered.reshape(ranks, parts, slice_cols, width)
        return jnp.swapaxes(value, 0, 1).reshape(parts * ranks * slice_cols, width)

    def split_rows(weight):
        value = columns(weight)
        return value.reshape(slice_cols, seq, -1)

    def exchange(value):
        return lax.all_to_all(value, "seq", 1, 1, tiled=False)

    def ffn_rows(contract, up):
        pieces = [split_rows(contract), split_rows(up) * jnp.asarray(ADAPTER_SCALE, low)]
        if padded > both:
            pieces.append(jnp.zeros((slice_cols, seq, padded - both), low))
        return pieces

    row_pieces = jnp.concatenate(
        [split_rows(encoder_output), split_rows(decoder_output), split_rows(cross_output)]
        + ffn_rows(encoder_contract, encoder_up)
        + ffn_rows(decoder_contract, decoder_up),
        axis=2,
    )
    row_pieces = lax.all_to_all(row_pieces, "seq", 1, 0, tiled=False).reshape(seq, slice_cols, -1)

    qkv_parts = gather_rows(
        jnp.concatenate(
            [
                columns(encoder_qkv).reshape(-1, width),
                columns(decoder_qkv).reshape(-1, width),
            ]
        )
    )
    lead = 512 if 3 * head_width < 512 else 3 * head_width
    front = gather_rows(row_pieces[:, :, :lead])
    late = [
        jnp.concatenate(
            [
                columns(encoder_expand),
                columns(encoder_down),
                columns(cross_query),
                columns(cross_kv).reshape(-1, width),
            ]
        ),
        row_pieces[:, :, lead : 3 * head_width + padded],
        jnp.concatenate([columns(decoder_expand), columns(decoder_down)]),
        row_pieces[:, :, 3 * head_width + padded :],
    ]
    source_all, target_all = gather_stage(seq, 1, (sources, targets))
    source_all, qkv_parts, front, late = lax.optimization_barrier(
        (source_all, qkv_parts, front, late)
    )
    encoder_in = flat_columns(qkv_parts[:, : 3 * slice_cols], 3)
    decoder_in = flat_columns(qkv_parts[:, 3 * slice_cols :], 3)
    front_rows = jnp.swapaxes(front[..., : 3 * head_width], 0, 1).reshape(width, -1)
    encoder_out = front_rows[:, :head_width]
    decoder_out = front_rows[:, head_width : 2 * head_width]
    cross_out = front_rows[:, 2 * head_width :]
    cut = encoder_expand.shape[1]

    def ffn_in(gathered):
        pieces = [gathered[:, :cut].reshape(-1, width), gathered[:, cut:].reshape(-1, width)]
        if padded > both:
            pieces.append(jnp.zeros((padded - both, width), low))
        return jnp.concatenate(pieces)

    def row_order(gathered):
        return jnp.swapaxes(gathered, 0, 1).reshape(width, -1)

    second_parts = gather_rows(late[0])
    rest = gather_rows(late[1])
    prefixes = small_gather(
        jnp.concatenate([encoder_prefix, decoder_prefix, cross_prefix]), [("rows", ranks)]
    )
    prefixes = jnp.moveaxis(prefixes, 0, 2).reshape(6, count, head_width)
    prefixes = jnp.pad(prefixes, ((0, 0), (0, PAD_PREFIX - count), (0, 0)))
    encoder_pre, decoder_pre, cross_pre = prefixes[0:2], prefixes[2:4], prefixes[4:6]

    norm_axes = [("seq", seq), ("rows", ranks)]
    scales = small_gather(
        jnp.concatenate([encoder_norms, decoder_norms]), norm_axes
    )
    scales = jnp.moveaxis(scales, 0, 2).reshape(-1, 2, width).astype(wide)
    norm_count = encoder_norms.shape[0]

    encoder_side, decoder_side = self_stage(
        seq, 2, count, places,
        (
            (
                source_all, sources, encoder_in, encoder_out, encoder_pre, source_keys,
                source_queries, scales[0],
            ),
            (
                target_all, targets, decoder_in, decoder_out, decoder_pre, target_keys,
                target_queries, scales[norm_count],
            ),
        ),
    )
    encoder_qkvs, encoder_ctx, encoder_logs, resid_one, middle, middle_low = encoder_side
    middle_low, second_parts, rest, last = lax.optimization_barrier(
        (middle_low, second_parts, rest, late[2:])
    )
    encoder_two = row_order(jnp.concatenate([front[..., 3 * head_width :], rest], axis=3))
    ffn_cut = cut + encoder_down.shape[1]
    encoder_one = ffn_in(second_parts[:, :ffn_cut])
    cross_in = flat_columns(second_parts[:, ffn_cut:], 3)
    cross_q_in, cross_kv_in = cross_in[:head_width], cross_in[head_width:]
    decoder_one = ffn_in(gather_rows(last[0]))
    decoder_two = row_order(gather_rows(last[1]))

    decoder_qkvs, decoder_ctx, decoder_logs, resid_three, first, first_low = decoder_side
    middle_all, encoder_before, encoder_hidden, resid_two, memory = ffn_stage(
        seq, 3, middle_low, middle, encoder_one, encoder_two, scales[1]
    )
    (
        first_all, memory_all, cross_q, cross_kvs, cross_ctx, cross_logs, resid_four, second,
        second_low,
    ) = cross_stage(
        seq, 4, count, places,
        (
            first, first_low, memory.astype(low), cross_q_in, cross_kv_in, cross_out, cross_pre,
            source_keys, target_queries, scales[norm_count + 1],
        ),
    )
    second_all, decoder_before, decoder_hidden, resid_five, third = ffn_stage(
        seq, 5, second_low, second, decoder_one, decoder_two, scales[norm_count + 2]
    )
    result = third.astype(low)

    def scatter_ranks(value):
        return lax.psum_scatter(value, "rows", scatter_dimension=0, tiled=False)

    def laid(value):
        return with_layout_constraint(value.astype(low), Layout(tuple(range(value.ndim))))

    def column_terms(grad, parts):
        value = grad.reshape(parts, ranks, slice_cols, width)
        return laid(jnp.swapaxes(value, 0, 1))

    def row_terms(grad):
        value = grad.astype(low).T.reshape(seq, ranks, slice_cols, -1)
        return laid(jnp.swapaxes(value, 0, 1))

    def ffn_in_terms(grad):
        return laid(
            jnp.concatenate(
                [
                    grad[:hidden].reshape(ranks, -1, width),
                    grad[hidden:both].reshape(ranks, -1, width),
                ],
                axis=1,
            )
        )

    def flat(value):
        return value.reshape(-1, value.shape[-1])

    norm_grads = {}

    def ffn_back(name_id, index, up, resid, before, hidden_low, rows_all, one, two):
        up_all, slope, out, pair = ffn_back_stage(
            seq, name_id, up, resid, scales[index], before, one, two
        )
        norm_grads[index] = (pair[0:1], pair[1:2])
        two_terms = row_terms(dot(flat(hidden_low), flat(up_all), 0, 0))
        one_terms = ffn_in_terms(dot(flat(slope), flat(rows_all), 0, 0))
        return out, one_terms, two_terms

    def hold(value, terms, sums):
        value, terms, sums = lax.optimization_barrier((value, terms, sums))
        return value, [scatter_ranks(term) for term in terms], sums

    second_up, one_terms, two_terms = ffn_back(
        6, norm_count + 2, cotangent.reshape(stacked, block, width), resid_five, decoder_before,
        decoder_hidden, second_all, decoder_one, decoder_two,
    )
    second_up, ffn_sums, _ = hold(second_up, [two_terms, one_terms], [])

    def keep_pair(index, pair):
        norm_grads[index] = (pair[0:1], pair[1:2])

    second_grad_all, cross_grads, cross_pre_grad, first_up, memory_up, pair = cross_back_stage(
        seq, 7, count, places,
        (
            second_up, resid_four, scales[norm_count + 1], cross_q, cross_kvs, cross_logs,
            cross_q_in, cross_kv_in, cross_out, cross_pre, source_keys, target_queries,
        ),
    )
    keep_pair(norm_count + 1, pair)
    cross_terms = [
        row_terms(dot(flat(cross_ctx), flat(second_grad_all), 0, 0)),
        column_terms(
            jnp.concatenate(
                [
                    dot(flat(cross_grads[:, :, :head_width]), flat(first_all), 0, 0),
                    dot(flat(cross_grads[:, :, head_width:]), flat(memory_all), 0, 0),
                ]
            ),
            3,
        ),
    ]
    first_up, cross_sums, ffn_sums = hold(first_up, cross_terms, ffn_sums)
    decoder_two_grad, decoder_one_grad = ffn_sums

    def self_back(name_id, index, causal, side, context, rows_all, sums):
        grad_all, grads, pre_grad, out, pair = self_back_stage(
            seq, name_id, count, places, causal, side
        )
        grad_all, grads, pre_grad, out, pair, sums = lax.optimization_barrier(
            (grad_all, grads, pre_grad, out, pair, sums)
        )
        keep_pair(index, pair)
        return (
            out,
            pre_grad,
            sums,
            [
                row_terms(dot(flat(context), flat(grad_all), 0, 0)),
                column_terms(dot(flat(grads), flat(rows_all), 0, 0), 3),
            ],
        )

    target_grad, decoder_pre_grad, cross_sums, self_terms = self_back(
        9, norm_count, True,
        (
            first_up, resid_three, scales[norm_count], decoder_qkvs, decoder_logs, decoder_in,
            decoder_out, decoder_pre, target_keys, target_queries,
        ),
        decoder_ctx, target_all, cross_sums,
    )
    memory_up, self_sums, _ = hold(memory_up, self_terms, [])
    cross_out_grad, cross_in_grad = cross_sums

    middle_up, one_terms, two_terms = ffn_back(
        8, 1, memory_up, resid_two, encoder_before, encoder_hidden, middle_all,
        encoder_one, encoder_two,
    )
    middle_up, ffn_sums, self_sums = hold(middle_up, [two_terms, one_terms], self_sums)
    decoder_out_grad, decoder_in_grad = self_sums

    def give_back(pieces):
        value = jnp.concatenate(pieces, axis=2) if len(pieces) > 1 else pieces[0]
        return lax.all_to_all(value, "seq", 0, 1, tiled=False)

    decoder_rows = give_back([decoder_two_grad, cross_out_grad, decoder_out_grad])

    source_grad, encoder_pre_grad, ffn_sums, self_terms = self_back(
        10, 0, False,
        (
            middle_up, resid_one, scales[0], encoder_qkvs, encoder_logs, encoder_in,
            encoder_out, encoder_pre, source_keys, source_queries,
        ),
        encoder_ctx, source_all, ffn_sums,
    )
    source_grad, self_sums, _ = hold(source_grad, self_terms, [])
    encoder_two_grad, encoder_one_grad = ffn_sums
    encoder_out_grad, encoder_in_grad = self_sums
    encoder_rows = give_back([encoder_two_grad])
    encoder_out_rows = give_back([encoder_out_grad])

    def row_grad(value, start, size, scale=None):
        piece = value[:, :, start : start + size].astype(wide)
        if scale is not None:
            piece = piece * scale
        return piece.reshape(slice_cols, -1).T

    def column_grad(value):
        return jnp.swapaxes(value.astype(wide), -1, -2)

    prefix_total = jnp.concatenate([encoder_pre_grad, decoder_pre_grad, cross_pre_grad])[:, :count]
    prefix_total = jnp.moveaxis(prefix_total.reshape(6, count, ranks, slice_cols), 2, 0)
    prefix_total = small_scatter(prefix_total, [("rows", ranks)])
    norm_rows = [row for index in sorted(norm_grads) for row in norm_grads[index]]
    which = lax.broadcasted_iota(jnp.int32, (len(norm_rows), width), 0)
    norm_total = sum(jnp.where(which == k, row, 0.0) for k, row in enumerate(norm_rows))
    norm_total = jnp.moveaxis(norm_total.reshape(-1, 2, seq * ranks, slice_cols), 2, 0)
    norm_total = small_scatter(norm_total, norm_axes)

    shape_out = source.shape
    return (
        result.reshape(shape_out),
        source_grad.reshape(shape_out),
        target_grad.reshape(shape_out),
        column_grad(encoder_in_grad),
        row_grad(encoder_out_rows, 0, head_width),
        prefix_total[0:2],
        column_grad(encoder_one_grad[:cut]),
        row_grad(encoder_rows, 0, hidden),
        column_grad(encoder_one_grad[cut:]),
        row_grad(encoder_rows, hidden, adapt, ADAPTER_SCALE),
        norm_total[:norm_count],
        column_grad(decoder_in_grad),
        row_grad(decoder_rows, padded + head_width, head_width),
        prefix_total[2:4],
        column_grad(cross_in_grad[0]),
        column_grad(cross_in_grad[1:]),
        row_grad(decoder_rows, padded, head_width),
        prefix_total[4:6],
        column_grad(decoder_one_grad[:cut]),
        row_grad(decoder_rows, 0, hidden),
        column_grad(decoder_one_grad[cut:]),
        row_grad(decoder_rows, hidden, adapt, ADAPTER_SCALE),
        norm_total[norm_count:],
    )


def solution(mesh):
    rows = P(None, "rows", "seq", None)
    ids = P(None, "rows", None)
    flat = P(None, ("seq", "rows"))
    deep = P(None, None, ("seq", "rows"))
    weights = (
        deep, flat, deep, flat, flat, flat, flat, deep, deep, flat, deep, flat, deep, flat, deep,
        flat, flat, flat, flat, deep,
    )
    body = functools.partial(local, mesh.shape["seq"], mesh.shape["rows"])
    return jax.shard_map(
        body,
        mesh=mesh,
        in_specs=(rows, rows, ids, ids, rows) + weights,
        out_specs=(rows, rows, rows) + weights,
        check_vma=False,
    )
```

time: 1030 us -> 960 us (0.932)
  Pallas kernels: 348 us -> 699 us
  waiting for transfers between devices: 219 us -> 65.5 us
  other arithmetic: 117 us -> 24.7 us
  starting transfers between devices: 89 us -> 23.2 us
  matrix products: 107 us -> 41.9 us
  local copies, waits for them, and re-layouts: 101 us -> 59.6 us
    pallas_call x4 -> x10, Pallas kernels: 245 us -> 699 us  [stage_call(): pl.pallas_call(kernel, out_shape=outs, in_specs=[pl.BlockSpec(memory_spac...]
    ppermute x84 -> x0, waiting for transfers between devices: 146 us -> none  [the longest x42 82.7 us: gather(): other = lax.ppermute(value, 'seq', swap_pairs(self.seq, bit))]
    pallas_call x12 -> x0, Pallas kernels: 103 us -> none  [the longest x6 58.2 us: attend_backward(): pl.pallas_call(functools.partial(attend_back_kernel, heads, offsets, coun...]
    ppermute x84 -> x0, starting transfers between devices: 68.4 us -> none  [the longest x28 34 us: scatter(): sent = lax.ppermute(send, 'seq', swap_pairs(self.seq, bit))]
    dot_general x60 -> x11, matrix products: 107 us -> 41.9 us  [dot(): lax.dot_general(left, right, (((left_axis,), (right_axis,)), ((), ())), p...]
    concatenate x45 -> x3, other arithmetic: 40.3 us -> 2.31 us  [the longest x2 2.25 us: ffn_in_terms(): jnp.concatenate([grad[:hidden].reshape(ranks, -1, width), grad[hidden:bot...]
    unnamed x521 -> x154, local copies, waits for them, and re-layouts: 24.5 us -> 11.3 us
    slice x50 -> x19, local copies, waits for them, and re-layouts: 17.6 us -> 4.64 us  [the longest x1 0.97 us: local(): front[..., 3 * head_width:]]
  transfers between devices with their start and end apart: 115 -> 33, of which waited for: 42 -> 13; matrix products, arithmetic and copies ran while one was open for 28% -> 9% of each run, Pallas kernels for 22% -> 61%
where the time goes in v3:
time: 960 us; the launch traced here: 948 us
  Pallas kernels  699 us (73%)
  waiting for transfers between devices  65.5 us (7%)
  local copies, waits for them, and re-layouts  59.6 us (6%)
  matrix products  41.9 us (4%)
  other arithmetic  24.7 us (3%)
  starting transfers between devices  23.2 us (2%)
  blocking collectives  18.4 us (2%)
  between operations  15.9 us (2%)
    pallas_call x10, Pallas kernels, stage_call(): pl.pallas_call(kernel, out_shape=outs, in_specs=[pl.BlockSpec(memory_spac...  699 us
    dot_general x11, matrix products, dot(): lax.dot_general(left, right, (((left_axis,), (right_axis,)), ((), ())), p...  41.9 us
    all_gather x6, waiting for transfers between devices, gather_rows(): return lax.all_gather(value, 'rows', axis=0, tiled=False)  25.6 us
    ppermute x7, waiting for transfers between devices, small_scatter(): lax.ppermute(jnp.where(flip, lower, upper), name, swap_pairs(count, bit))  20.7 us
  transfers between devices with their start and end apart: 33, of which 13 were waited for; matrix products, arithmetic and copies ran while one was open for 9% of the time, Pallas kernels for 61%

profile of v3, /device:TPU:0, one launch (start us, length us, event | category | flops | bytes accessed | tf_op | source)
XLA Modules:
  0.0 948.0 jit_solution(9707659544852353623)
XLA Ops:
  14.2 18.4 %all_to_all.54 = bf16[1,32,8,1664]{3,1,0,2:T(8,128)(2,1)S(1)} all-to-all(bf16[1,32,8,1664]{3,1,0,2:T(8,128)(2,1)S(1)} %copy.297), channel_id=1, replica_groups=mesh['seq'=8,'rows'=4] {'seq'}, dimensions={2} | all-to-all | bytes 1703936 | tf_op jit(solution)/shard_map/all_to_all | solution.py:1150
  37.2 42.9 %shard_map.416 = (bf16[2,1024,1024]{2,1,0:T(8,128)(2,1)}, bf16[2,1024,1024]{2,1,0:T(8,128)(2,1)}) custom-call(bf16[2,128,1024]{2,1,0:T(8,128)(2,1)} %bitcast.435, bf16[2,128,1024]{2,1,0:T(8,128)(2,1)} %bitcast.437), custom_call_target="tpu_custom_call" | custom-call | flops 112499998720 | bytes 16777216 | tf_op jit(solution)/shard_map/pallas_call | solution.py:465
  94.1 5.8 all-gather.13.cloned.1.call-done
  106.4 3.2 collective-permute-done.1
  114.1 78.6 %shard_map.417 = (bf16[2,1024,384]{2,1,0:T(8,128)(2,1)}, bf16[2,1024,128]{2,1,0:T(8,128)(2,1)}, f32[2,2,1024]{2,1,0:T(2,128)}, f32[2,128,1024]{2,1,0:T(8,128)}, ...) custom-call(s32[1024,1]{1,0:T(8,128)} %copy.321.refs_0_.kpos_ref, ...), custom_call_target="tpu_custom_call" | custom-call | flops 187500003328 | bytes 16777216 | tf_op jit(solution)/shard_map/pallas_call | solution.py:465
  202.7 19.7 %all-gather.21.cloned.1.call-done = bf16[576,1024]{1,0:T(8,128)(2,1)} async-done(((bf16[144,1024]{1,0:T(8,128)(2,1)}), bf16[576,1024]{1,0:T(8,128)(2,1)}) %all-gather.21.cloned.1.call-update) | async-done | bytes 1179664 | tf_op jit(solution)/shard_map/all_gather | solution.py:1115
  226.6 62.3 %shard_map.418 = (bf16[2,1024,1024]{2,1,0:T(8,128)(2,1)}, f32[2,1024,640]{2,1,0:T(8,128)}, bf16[2,1024,640]{2,1,0:T(8,128)(2,1)}, f32[2,128,1024]{2,1,0:T(8,128)}, f32[2,128,1024]{2,1,0:T(8,128)}) custom-call(bf16[2,128,1024]{2,1,0:T(8,128)(2,1)} %get-tuple-element.137.own_ref, f32[2,128,1024]{2,1,0:T(8,128)} %get-tuple-element.138.resid_ref, ...), custom_call_target="tpu_custom_call" | custom-call | flops 149999992832 | bytes 16777216 | tf_op jit(solution)/shard_map/pallas_call | solution.py:465
  291.0 85.8 %shard_map.419 = (bf16[2,1024,1024]{2,1,0:T(8,128)(2,1)}, bf16[2,1024,1024]{2,1,0:T(8,128)(2,1)}, bf16[2,1024,128]{2,1,0:T(8,128)(2,1)}, bf16[2,1024,256]{2,1,0:...) custom-call(s32[1024,1]{1,0:T(8,128)} %copy.321.refs_0_.kpos_ref, ...), custom_call_target="tpu_custom_call" | custom-call | flops 212500004864 | bytes 16777216 | tf_op jit(solution)/shard_map/pallas_call | solution.py:465
  379.3 62.8 %shard_map.420 = (bf16[2,1024,1024]{2,1,0:T(8,128)(2,1)}, f32[2,1024,640]{2,1,0:T(8,128)}, bf16[2,1024,640]{2,1,0:T(8,128)(2,1)}, f32[2,128,1024]{2,1,0:T(8,128)}, f32[2,128,1024]{2,1,0:T(8,128)}) custom-call(bf16[2,128,1024]{2,1,0:T(8,128)(2,1)} %get-tuple-element.142.own_ref, f32[2,128,1024]{2,1,0:T(8,128)} %get-tuple-element.143.resid_ref, ...), custom_call_target="tpu_custom_call" | custom-call | flops 149999992832 | bytes 16777216 | tf_op jit(solution)/shard_map/pallas_call | solution.py:465
  442.2 61.4 %shard_map.421 = (bf16[2,1024,1024]{2,1,0:T(8,128)(2,1)}, bf16[2,1024,640]{2,1,0:T(8,128)(2,1)}, f32[2,128,1024]{2,1,0:T(8,128)}, f32[2,1024]{1,0:T(2,128)}) custom-call(bf16[2,128,1024]{2,1,0:T(8,128)(2,1)} %bitcast.439, f32[2,128,1024]{2,1,0:T(8,128)} %get-tuple-element.147.resid_ref, f32[2,1024]{1,0:T(2,128)} %squeeze.38.pair_ref, ...), custom_call_target="tpu_custom_call" | custom-call | flops 149999992832 | bytes 16777216 | tf_op jit(solution)/shard_map/pallas_call | solution.py:465
  503.6 6.0 bitcast_convert_fusion.2
  509.7 3.6 bitcast_convert_fusion.3
  517.0 87.6 %shard_map.422 = (bf16[2,1024,1024]{2,1,0:T(8,128)(2,1)}, bf16[2,1024,384]{2,1,0:T(8,128)(2,1)}, f32[2,32,128]{2,1,0:T(8,128)}, f32[2,128,1024]{2,1,0:T(8,128)},...) custom-call(s32[1024,1]{1,0:T(8,128)} %copy.321.refs_0_.kpos_ref, s32[1,1024]{1,0:T(1,128)} %bitcast.424, ...), custom_call_target="tpu_custom_call" | custom-call | flops 212500004864 | bytes 16777216 | tf_op jit(solution)/shard_map/pallas_call | solution.py:465
  604.7 3.6 fusion.17
  614.3 77.6 %shard_map.423 = (bf16[2,1024,1024]{2,1,0:T(8,128)(2,1)}, bf16[2,1024,384]{2,1,0:T(8,128)(2,1)}, f32[2,32,128]{2,1,0:T(8,128)}, f32[2,128,1024]{2,1,0:T(8,128)}, f32[2,1024]{1,0:T(2,128)}) custom-call(s32[1024,1]{1,0:T(8,128)} %copy.321.refs_0_.kpos_ref, s32[1,1024]{1,0:T(1,128)} %bitcast.425, f32[2,128,1024]{2,1,0:T(8,128)} %get-tuple-element.168.refs_2_, ...), custom_call_target="tpu_custom_call" | custom-call | flops 187500003328 | bytes 16777216 | tf_op jit(solution)/shard_map/pallas_call | solution.py:465
  692.0 3.6 fusion.19
  697.1 4.9 fusion.13
  702.6 60.7 %shard_map.424 = (bf16[2,1024,1024]{2,1,0:T(8,128)(2,1)}, bf16[2,1024,640]{2,1,0:T(8,128)(2,1)}, f32[2,128,1024]{2,1,0:T(8,128)}, f32[2,1024]{1,0:T(2,128)}) custom-call(f32[2,128,1024]{2,1,0:T(8,128)} %get-tuple-element.182.up_ref, f32[2,128,1024]{2,1,0:T(8,128)} %get-tuple-element.183.resid_ref, f32[2,1024]{1,0:T(2,128)} %squeeze.36.pair_ref, ...), custom_call_target="tpu_custom_call" | custom-call | flops 149999992832 | bytes 16777216 | tf_op jit(solution)/shard_map/pallas_call | solution.py:465
  763.3 6.0 bitcast_convert_fusion
  769.4 3.6 bitcast_convert_fusion.1
  789.1 4.1 all-to-all-start.3
  793.9 79.2 %shard_map.425 = (bf16[2,1024,1024]{2,1,0:T(8,128)(2,1)}, bf16[2,1024,384]{2,1,0:T(8,128)(2,1)}, f32[2,32,128]{2,1,0:T(8,128)}, f32[2,128,1024]{2,1,0:T(8,128)}, f32[2,1024]{1,0:T(2,128)}) custom-call(s32[1024,1]{1,0:T(8,128)} %copy.321.refs_0_.kpos_ref, s32[1,1024]{1,0:T(1,128)} %bitcast.426, f32[2,128,1024]{2,1,0:T(8,128)} %get-tuple-element.192.refs_2_, ...), custom_call_target="tpu_custom_call" | custom-call | flops 187500003328 | bytes 16777216 | tf_op jit(solution)/shard_map/pallas_call | solution.py:465
  883.0 4.9 fusion.10
  887.9 3.6 fusion.20
  893.1 3.3 collective-permute-done.10
  898.0 4.8 collective-permute-done.12
  904.8 3.4 all-to-all-start.2
  909.4 7.4 collective-permute-done.7
  917.6 4.3 collective-permute-done.8
  922.7 3.6 all-to-all-start.1
  927.9 3.4 all-to-all-done.1
  932.0 5.5 reduce-scatter.27.cloned.1.call-done
  (400 shorter events, 106.3 us)
Async XLA Ops:
  7.2 86.9 %all-gather.15.cloned.1.call-start = ((), (), s32[]{:S(2)}) async-start(), calls=%async_computation.25 | async-start | bytes 1310720 | tf_op jit(solution)/shard_map/all_gather | solution.py:1115
  33.4 66.4 %all-gather.13.cloned.1.call-start = ((), (), s32[]{:S(2)}) async-start(), calls=%async_computation.24 | async-start | bytes 1966080 | tf_op jit(solution)/shard_map/all_gather | solution.py:1115
  33.6 68.0 %collective-permute-start = (bf16[1,6,30,32]{3,1,2,0:T(8,128)(2,1)S(1)}, bf16[1,6,30,32]{3,1,2,0:T(8,128)(2,1)S(1)}, u32[]{:S(2)}, u32[]{:S(2)}) collective-permute-start(bf16[1,6,30,32]{3,1,2,0:T(8,128)(2,1)S(1)} %maximum_bitcast_fusion.2), channel_id=1, source_target_pairs={{0,1},{1,0},{2,3},{3,2},{4,5},{5,4},{6,7},{7,6},{8,9},{9,8},{10,11... | collective-permute-start | bytes 34568 | tf_op jit(solution)/shard_map/ppermute | solution.py:61
  35.2 45.9 %collective-permute-start.2 = (bf16[1,5,2,32]{3,2,1,0:T(2,128)(2,1)S(1)}, bf16[1,5,2,32]{3,2,1,0:T(2,128)(2,1)S(1)}, u32[]{:S(2)}, u32[]{:S(2)}) collective-permute-start(bf16[1,5,2,32]{3,2,1,0:T(2,128)(2,1)S(1)} %maximum_bitcast_fusion.3), channel_id=1, source_target_pairs={{0,1},{1,0},{2,3},{3,2},{4,5},{5,4},{6,7},{7,6},{8,9},{9,8},{10,11... | collective-permute-start | bytes 1928 | tf_op jit(solution)/shard_map/ppermute | solution.py:61
  36.6 156.2 %all-gather.19.cloned.1.call-start = ((), (), s32[]{:S(2)}) async-start(), calls=%async_computation.27 | async-start | bytes 1310720 | tf_op jit(solution)/shard_map/all_gather | solution.py:1115
  81.2 5.4 collective-permute-start.3
  87.9 12.1 %collective-permute-start.5 = (bf16[8,5,2,32]{3,2,1,0:T(2,128)(2,1)S(1)}, bf16[8,5,2,32]{3,2,1,0:T(2,128)(2,1)S(1)}, u32[]{:S(2)}, u32[]{:S(2)}) collective-permute-start(bf16[8,5,2,32]{3,2,1,0:T(2,128)(2,1)S(1)} %broadcast_select_fusion.4), channel_id=1, source_target_pairs={{0,8},{4,12},{8,0},{12,4},{16,24},{20,28},{24,16},{28,20},{1,9},{5... | collective-permute-start | bytes 15368 | tf_op jit(solution)/shard_map/ppermute | solution.py:61
  99.9 92.9 %all-gather.17.cloned.1.call-start = ((), (), s32[]{:S(2)}) async-start(), calls=%async_computation.26 | async-start | bytes 2457600 | tf_op jit(solution)/shard_map/all_gather | solution.py:1115
  100.1 4.1 collective-permute-start.6
  101.7 8.0 collective-permute-start.1
  113.9 108.5 %all-gather.21.cloned.1.call-start = ((), (), s32[]{:S(2)}) async-start(), calls=%async_computation.28 | async-start | bytes 1474560 | tf_op jit(solution)/shard_map/all_gather | solution.py:1115
  192.9 183.9 %all-gather.23.cloned.1.call-start = ((), (), s32[]{:S(2)}) async-start(), calls=%async_computation.29 | async-start | bytes 1638400 | tf_op jit(solution)/shard_map/all_gather | solution.py:1115
  202.6 410.9 %reduce-scatter.13.cloned.1.call-start = ((), (), s32[]{:S(2)}) async-start(), calls=%async_computation.15 | async-start | bytes 1474560 | tf_op jit(solution)/shard_map/reduce_scatter | solution.py:1257
  516.2 97.4 %reduce-scatter.11.cloned.1.call-start = ((), (), s32[]{:S(2)}) async-start(), calls=%async_computation.14 | async-start | bytes 1638400 | tf_op jit(solution)/shard_map/reduce_scatter | solution.py:1257
  517.0 175.0 %reduce-scatter.15.cloned.1.call-start = ((), (), s32[]{:S(2)}) async-start(), calls=%async_computation.16 | async-start | bytes 327680 | tf_op jit(solution)/shard_map/reduce_scatter | solution.py:1257
  613.6 78.3 %reduce-scatter.17.cloned.1.call-start = ((), (), s32[]{:S(2)}) async-start(), calls=%async_computation.17 | async-start | bytes 983040 | tf_op jit(solution)/shard_map/reduce_scatter | solution.py:1257
  614.2 161.6 %reduce-scatter.19.cloned.1.call-start = ((), (), s32[]{:S(2)}) async-start(), calls=%async_computation.18 | async-start | bytes 327680 | tf_op jit(solution)/shard_map/reduce_scatter | solution.py:1257
  702.0 73.9 %reduce-scatter.21.cloned.1.call-start = ((), (), s32[]{:S(2)}) async-start(), calls=%async_computation.19 | async-start | bytes 983040 | tf_op jit(solution)/shard_map/reduce_scatter | solution.py:1257
  702.5 177.3 %reduce-scatter.25.cloned.1.call-start = ((), (), s32[]{:S(2)}) async-start(), calls=%async_computation.21 | async-start | bytes 1474560 | tf_op jit(solution)/shard_map/reduce_scatter | solution.py:1257
  789.1 84.7 %all-to-all-start.3 = ((bf16[8,32,1,896]{3,1,2,0:T(8,128)(2,1)}), bf16[8,32,1,896]{3,1,2,0:T(8,128)(2,1)}, u32[]{:S(2)}, u32[]{:S(2)}) async-start(bf16[8,32,1,896]{3,1,2,0:T(8,128)(2,1)} %maximum_bitcast_fusion.1), calls=%async_computation.13 | async-start | bytes 917504 | tf_op jit(solution)/shard_map/all_to_all | solution.py:1369
  793.3 86.6 %reduce-scatter.23.cloned.1.call-start = ((), (), s32[]{:S(2)}) async-start(), calls=%async_computation.20 | async-start | bytes 1638400 | tf_op jit(solution)/shard_map/reduce_scatter | solution.py:1257
  793.8 128.8 %reduce-scatter.29.cloned.1.call-start = ((), (), s32[]{:S(2)}) async-start(), calls=%async_computation.23 | async-start | bytes 327680 | tf_op jit(solution)/shard_map/reduce_scatter | solution.py:1257
  881.6 10.8 %collective-permute-start.9 = (f32[16,5,2,32]{3,2,1,0:T(2,128)S(1)}, f32[16,5,2,32]{3,2,1,0:T(2,128)S(1)}, u32[]{:S(2)}, u32[]{:S(2)}) collective-permute-start(f32[16,5,2,32]{3,2,1,0:T(2,128)S(1)} %broadcast_select_fusion.1), channel_id=1, source_target_pairs={{0,16},{4,20},{8,24},{12,28},{16,0},{20,4},{24,8},{28,12},{1,17},{... | collective-permute-start | bytes 61448 | tf_op jit(solution)/shard_map/ppermute | solution.py:76
  892.4 4.1 collective-permute-start.10
  896.5 1.3 collective-permute-start.11
  897.8 5.0 collective-permute-start.12
  902.8 6.0 collective-permute-start.13
  903.5 13.3 %collective-permute-start.7 = (f32[2,6,30,32]{3,1,2,0:T(8,128)S(1)}, f32[2,6,30,32]{3,1,2,0:T(8,128)S(1)}, u32[]{:S(2)}, u32[]{:S(2)}) collective-permute-start(f32[2,6,30,32]{3,1,2,0:T(8,128)S(1)} %slice_select_fusion), channel_id=1, source_target_pairs={{0,2},{1,3},{2,0},{3,1},{4,6},{5,7},{6,4},{7,5},{8,10},{9,11},{10,... | collective-permute-start | bytes 138248 | tf_op jit(solution)/shard_map/ppermute | solution.py:76
  904.8 17.8 %all-to-all-start.2 = ((bf16[8,32,1,640]{3,1,2,0:T(8,128)(2,1)}), bf16[8,32,1,640]{3,1,2,0:T(8,128)(2,1)S(1)}, u32[]{:S(2)}, u32[]{:S(2)}) async-start(bf16[8,32,1,640]{3,1,2,0:T(8,128)(2,1)} %bitcast.139), calls=%async_computation.12 | async-start | bytes 655360 | tf_op jit(solution)/shard_map/all_to_all | solution.py:1369
  908.3 29.3 %reduce-scatter.27.cloned.1.call-start = ((), (), s32[]{:S(2)}) async-start(), calls=%async_computation.22 | async-start | bytes 983040 | tf_op jit(solution)/shard_map/reduce_scatter | solution.py:1257
  917.0 4.9 collective-permute-start.8
  922.7 8.6 all-to-all-start.1
  (76 other events, 1279.6 us)
Sparse Core Ops, SparseCore 0:
  33.6 27.2 all-gather.14
  63.0 36.7 all-gather.12
  102.0 26.7 all-gather.18
  130.8 43.0 all-gather.16
  193.0 29.3 all-gather.20
  224.4 31.8 all-gather.22
  516.3 27.8 reduce-scatter.12
  546.6 29.9 reduce-scatter.10
  613.7 18.0 reduce-scatter.14
  634.1 21.5 reduce-scatter.16
  702.1 16.8 reduce-scatter.18
  721.7 21.5 reduce-scatter.20
  776.0 26.3 reduce-scatter.24
  804.6 29.9 reduce-scatter.22
  892.4 17.1 reduce-scatter.28
  912.5 25.0 reduce-scatter.26

commit v4 on v3

--- a/solution.py
+++ b/solution.py
@@ -360,43 +360,34 @@
     ]
 
 
-def merged(first, second):
-    steps = []
-    for index in range(max(len(first), len(second))):
-        steps += first[index : index + 1] + second[index : index + 1]
-    return steps
-
-
-def run_stage(micros, arrive, compute, leave):
-    for step in arrive(0):
-        step()
-    for micro in range(micros):
-        other = (leave(micro - 1) if micro > 0 else []) + (
-            arrive(micro + 1) if micro + 1 < micros else []
-        )
-        for step in merged(compute(micro), other):
-            step()
-    for step in leave(micros - 1):
-        step()
+NEAR_GAP, FAR_GAP, SHORT_GAP = 3.0, 6.0, 0.1
 
 
 def arrive_steps(gathers, micro):
     steps = []
-    for gather in gathers:
-        for phase in range(gather.phases()):
-            steps.append(functools.partial(gather.advance, micro, phase))
-    return steps + [functools.partial(gather.near, micro) for gather in gathers]
+    for phase in range(gathers[0].phases() if gathers else 0):
+        for index, gather in enumerate(gathers):
+            gap = SHORT_GAP if index else FAR_GAP
+            steps.append((functools.partial(gather.advance, micro, phase), gap))
+    for index, gather in enumerate(gathers):
+        gap = SHORT_GAP if index else NEAR_GAP
+        steps.append((functools.partial(gather.near, micro), gap))
+    return steps
 
 
 def leave_steps(scatters, finish, micro):
-    steps = [functools.partial(scatter.near_sum, micro) for scatter in scatters]
+    steps = []
+    for index, scatter in enumerate(scatters):
+        gap = SHORT_GAP if index else NEAR_GAP
+        steps.append((functools.partial(scatter.near_sum, micro), gap))
     for phase in range(scatters[0].phases()):
-        for scatter in scatters:
-            steps.append(functools.partial(scatter.far_sum, micro, phase))
-    return steps + [functools.partial(finish, micro)]
-
-
-def half_steps(scatter, micro, length, chunk):
+        for index, scatter in enumerate(scatters):
+            gap = SHORT_GAP if index else FAR_GAP
+            steps.append((functools.partial(scatter.far_sum, micro, phase), gap))
+    return steps + [(functools.partial(finish, micro), SHORT_GAP)]
+
+
+def half_steps(scatter, micro, length, chunk, cost):
     half = length // 2
     size = min(CHUNK, half)
 
@@ -418,81 +409,7 @@
 
         lax.fori_loop(0, half // size, body, 0)
 
-    return [odd, even]
-
-
-def ffn_kernel(
-    seq, own_ref, resid_ref, one_ref, two_ref, pair_ref, all_ref, before_ref, hidden_ref, sum_ref,
-    norm_ref, *scratch,
-):
-    links = Links(seq)
-    micros, rows, _ = own_ref.shape
-    length = all_ref.shape[1]
-    gather = Gather(links, own_ref, all_ref, *scratch[:3])
-    scatter = Scatter(links, rows, *scratch[3:8], scratch[8:])
-    links.enter()
-    for micro in range(micros):
-        gather.start(micro)
-
-    def compute(micro):
-        def chunk(start, size):
-            place = pl.ds(start, size)
-            before = dot(all_ref[micro, place], one_ref[...], 1, 1)
-            before_ref[micro, place] = before
-            after = gelu_exact(before).astype(low)
-            hidden_ref[micro, place] = after
-            return dot(after, two_ref[...], 1, 1)
-
-        return half_steps(scatter, micro, length, chunk)
-
-    def finish(micro):
-        total = resid_ref[micro] + scatter.total(micro)
-        sum_ref[micro] = total
-        norm_ref[micro] = layer_norm(total, (pair_ref[0:1], pair_ref[1:2]))
-
-    run_stage(
-        micros,
-        functools.partial(arrive_steps, [gather]),
-        compute,
-        functools.partial(leave_steps, [scatter], finish),
-    )
-    for micro in range(micros):
-        gather.drain(micro)
-        scatter.drain(micro)
-
-
-def stage_call(kernel, name_id, outs, scratch, args, micros):
-    return pl.pallas_call(
-        kernel,
-        out_shape=outs,
-        in_specs=[pl.BlockSpec(memory_space=pltpu.VMEM)] * len(args),
-        out_specs=tuple(pl.BlockSpec(memory_space=pltpu.VMEM) for _ in outs),
-        scratch_shapes=scratch,
-        compiler_params=pltpu.CompilerParams(
-            collective_id=name_id, has_side_effects=True, vmem_limit_bytes=VMEM_LIMIT
-        ),
-        cost_estimate=pl.CostEstimate(
-            flops=micros * 2_500_000_000, bytes_accessed=1 << 24, transcendentals=0
-        ),
-    )(*args)
-
-
-def ffn_stage(seq, name_id, own, resid, one, two, pair):
-    micros, rows, width = own.shape
-    hidden = one.shape[0]
-    length = rows * seq
-    outs = (
-        jax.ShapeDtypeStruct((micros, length, width), low),
-        jax.ShapeDtypeStruct((micros, length, hidden), wide),
-        jax.ShapeDtypeStruct((micros, length, hidden), low),
-        jax.ShapeDtypeStruct((micros, rows, width), wide),
-        jax.ShapeDtypeStruct((micros, rows, width), wide),
-    )
-    scratch = gather_scratch(seq, micros) + scatter_scratch(seq, micros, rows, width)
-    return stage_call(
-        functools.partial(ffn_kernel, seq), name_id, outs, scratch,
-        (own, resid, one, two, pair), 60,
-    )
+    return [(odd, cost), (even, cost)]
 
 
 def prologue(micro, up_ref, resid_ref, pair_ref, own_ref, kept_ref, pair_grad_ref):
@@ -508,9 +425,168 @@
         pair_grad_ref[1:2] += shift_grad
 
 
-def ffn_back_kernel(
-    seq, up_ref, resid_ref, pair_ref, before_ref, one_ref, two_ref, all_ref, slope_ref, out_ref,
-    pair_grad_ref, own_ref, kept_ref, *scratch,
+class Task:
+    def __init__(self, begin, arrive, compute, leave, drain, load=None, store=None):
+        self.begin, self.arrive, self.compute = begin, arrive, compute
+        self.leave, self.drain, self.load, self.store = leave, drain, load, store
+
+
+class Waits:
+    def __init__(self):
+        self.time, self.queues = 0.0, []
+
+    def add(self, steps):
+        if steps:
+            self.queues.append([list(steps), self.time + steps[0][1]])
+
+    def take(self, entry):
+        queue = entry[0]
+        queue.pop(0)[0]()
+        self.time += 0.4
+        if queue:
+            entry[1] = self.time + queue[0][1]
+        else:
+            self.queues.remove(entry)
+
+    def run(self, step, cost):
+        step()
+        self.time += cost
+        ready = [entry for entry in self.queues if entry[1] <= self.time]
+        while ready:
+            self.take(ready[0])
+            ready = [entry for entry in self.queues if entry[1] <= self.time]
+
+    def finish(self, steps):
+        while any(entry[0] and entry[0][-1] is steps[-1] for entry in self.queues):
+            entry = min(self.queues, key=lambda entry: entry[1])
+            self.time = max(self.time, entry[1])
+            self.take(entry)
+
+
+def run_tasks(tasks, io, fill=(), fill_load=None):
+    waits = Waits()
+    for task in tasks[:2]:
+        task.begin()
+        waits.add(task.arrive)
+    for index, task in enumerate(tasks):
+        if task.arrive:
+            waits.finish(task.arrive)
+        io.load(task.load)
+        for step, cost in task.compute:
+            waits.run(step, cost)
+        io.store(task.store)
+        waits.add(task.leave)
+        if index + 2 < len(tasks):
+            tasks[index + 2].begin()
+            waits.add(tasks[index + 2].arrive)
+    if fill:
+        io.load(fill_load)
+        for step, cost in fill:
+            waits.run(step, cost)
+    while waits.queues:
+        waits.take(min(waits.queues, key=lambda entry: entry[1]))
+    for task in tasks:
+        task.drain()
+    io.close()
+
+
+def make_task(micro, gathers, scatters, compute, finish, before=None, load=None, store=None):
+    def begin():
+        if before is not None:
+            before(micro)
+        for gather in gathers:
+            gather.start(micro)
+
+    def drain():
+        for item in gathers + scatters:
+            item.drain(micro)
+
+    arrive = arrive_steps(gathers, micro)
+    leave = leave_steps(scatters, finish, micro) if scatters else []
+    return Task(begin, arrive, compute(micro), leave, drain, load, store)
+
+
+class Operands:
+    def __init__(self, ins, outs, in_sems, out_sems):
+        self.ins, self.outs, self.in_sems, self.out_sems = ins, outs, in_sems, out_sems
+        self.open = []
+
+    def start(self):
+        for index, (_, source, target) in enumerate(self.ins):
+            pltpu.make_async_copy(source, target, self.in_sems.at[index]).start()
+
+    def load(self, key):
+        for index, (name, source, target) in enumerate(self.ins):
+            if key is not None and name == key:
+                pltpu.make_async_copy(source, target, self.in_sems.at[index]).wait()
+
+    def copy_out(self, index, micro):
+        _, source, target = self.outs[index]
+        return pltpu.make_async_copy(
+            source.at[micro], target.at[micro], self.out_sems.at[index, micro]
+        )
+
+    def store(self, key):
+        if key is None:
+            return
+        name, micro = key
+        for index, (group, _, _) in enumerate(self.outs):
+            if group == name:
+                self.copy_out(index, micro).start()
+                self.open.append((index, micro))
+
+    def close(self):
+        for index, micro in self.open:
+            self.copy_out(index, micro).wait()
+
+
+def stage_call(kernel, name_id, outs, scratch, args, micros, lazy=None, early=None):
+    lazy, early = lazy or {}, early or {}
+    count, given, own = len(args), len(outs), len(scratch)
+    lazy_places, early_places = sorted(lazy), sorted(early)
+    parts = max([outs[place].shape[0] for place in early_places] + [1])
+
+    def body(*refs):
+        ins, results = list(refs[:count]), list(refs[count : count + given])
+        own_scratch = refs[count + given : count + given + own]
+        extra = refs[count + given + own :]
+        loads, stores = [], []
+        for index, place in enumerate(lazy_places):
+            loads.append((lazy[place], ins[place], extra[index]))
+            ins[place] = extra[index]
+        for index, place in enumerate(early_places):
+            buffer = extra[len(lazy_places) + index]
+            stores.append((early[place], buffer, results[place]))
+            results[place] = buffer
+        io = Operands(loads, stores, extra[-2], extra[-1])
+        io.start()
+        kernel(io, *ins, *results, *own_scratch)
+
+    held = [pltpu.VMEM(args[place].shape, args[place].dtype) for place in lazy_places]
+    held += [pltpu.VMEM(outs[place].shape, outs[place].dtype) for place in early_places]
+    sems = [
+        pltpu.SemaphoreType.DMA((max(len(lazy_places), 1),)),
+        pltpu.SemaphoreType.DMA((max(len(early_places), 1), parts)),
+    ]
+    near, far = pl.BlockSpec(memory_space=pltpu.VMEM), pl.BlockSpec(memory_space=pl.ANY)
+    return pl.pallas_call(
+        body,
+        out_shape=tuple(outs),
+        in_specs=[far if place in lazy else near for place in range(count)],
+        out_specs=tuple(far if place in early else near for place in range(given)),
+        scratch_shapes=list(scratch) + held + sems,
+        compiler_params=pltpu.CompilerParams(
+            collective_id=name_id, has_side_effects=True, vmem_limit_bytes=VMEM_LIMIT
+        ),
+        cost_estimate=pl.CostEstimate(
+            flops=micros * 2_500_000_000, bytes_accessed=1 << 24, transcendentals=0
+        ),
+    )(*args)
+
+
+def ffn_kernel(
+    seq, io, own_ref, resid_ref, one_ref, two_ref, pair_ref, all_ref, before_ref, hidden_ref,
+    sum_ref, norm_ref, low_ref, *scratch,
 ):
     links = Links(seq)
     micros, rows, _ = own_ref.shape
@@ -518,9 +594,76 @@
     gather = Gather(links, own_ref, all_ref, *scratch[:3])
     scatter = Scatter(links, rows, *scratch[3:8], scratch[8:])
     links.enter()
+
+    def compute(micro):
+        def chunk(start, size):
+            place = pl.ds(start, size)
+            before = dot(all_ref[micro, place], one_ref[...], 1, 1)
+            before_ref[micro, place] = before
+            after = gelu_exact(before).astype(low)
+            hidden_ref[micro, place] = after
+            return dot(after, two_ref[...], 1, 1)
+
+        return half_steps(scatter, micro, length, chunk, 2.5)
+
+    def finish(micro):
+        total = resid_ref[micro] + scatter.total(micro)
+        sum_ref[micro] = total
+        value = layer_norm(total, (pair_ref[0:1], pair_ref[1:2]))
+        norm_ref[micro] = value
+        low_ref[micro] = value.astype(low)
+
+    tasks = [
+        make_task(
+            micro, [gather], [scatter], compute, finish, None, 0 if micro == 0 else None, (0, micro)
+        )
+        for micro in range(micros)
+    ]
+    run_tasks(tasks, io)
+
+
+def ffn_stage(seq, name_id, own, resid, one, two, pair):
+    micros, rows, width = own.shape
+    hidden = one.shape[0]
+    length = rows * seq
+    outs = (
+        jax.ShapeDtypeStruct((micros, length, width), low),
+        jax.ShapeDtypeStruct((micros, length, hidden), wide),
+        jax.ShapeDtypeStruct((micros, length, hidden), low),
+        jax.ShapeDtypeStruct((micros, rows, width), wide),
+        jax.ShapeDtypeStruct((micros, rows, width), wide),
+        jax.ShapeDtypeStruct((micros, rows, width), low),
+    )
+    scratch = gather_scratch(seq, micros) + scatter_scratch(seq, micros, rows, width)
+    return stage_call(
+        functools.partial(ffn_kernel, seq), name_id, outs, scratch,
+        (own, resid, one, two, pair), 60, {1: 0, 2: 0, 3: 0, 4: 0}, {0: 0, 1: 0, 2: 0},
+    )
+
+
+def token_sum(left_ref, lanes, right_ref, micros):
+    total = None
     for micro in range(micros):
+        value = dot(left_ref[micro, :, lanes], right_ref[micro], 0, 0)
+        total = value if total is None else total + value
+    return total
+
+
+def ffn_back_kernel(
+    seq, ranks, hidden, io, up_ref, resid_ref, pair_ref, before_ref, one_ref, two_ref, rows_ref,
+    hidden_ref, out_ref, pair_grad_ref, expand_ref, down_ref, two_terms_ref, all_ref, slope_ref,
+    own_ref, kept_ref, *scratch,
+):
+    links = Links(seq)
+    micros, rows, width = own_ref.shape
+    length = all_ref.shape[1]
+    adapt = down_ref.shape[0] * down_ref.shape[1]
+    gather = Gather(links, own_ref, all_ref, *scratch[:3])
+    scatter = Scatter(links, rows, *scratch[3:8], scratch[8:])
+    links.enter()
+
+    def before(micro):
         prologue(micro, up_ref, resid_ref, pair_ref, own_ref, kept_ref, pair_grad_ref)
-        gather.start(micro)
 
     def compute(micro):
         def chunk(start, size):
@@ -530,97 +673,67 @@
             slope_ref[micro, place] = slope
             return dot(slope, one_ref[...], 1, 0)
 
-        return half_steps(scatter, micro, length, chunk)
+        return half_steps(scatter, micro, length, chunk, 2.5)
 
     def finish(micro):
         out_ref[micro] = kept_ref[micro] + scatter.total(micro)
 
-    run_stage(
-        micros,
-        functools.partial(arrive_steps, [gather]),
-        compute,
-        functools.partial(leave_steps, [scatter], finish),
-    )
-    for micro in range(micros):
-        gather.drain(micro)
-        scatter.drain(micro)
-
-
-def ffn_back_stage(seq, name_id, up, resid, pair, before, one, two):
+    cut = hidden // ranks
+
+    def one_tile(start):
+        value = token_sum(slope_ref, slice(start, start + LANES), rows_ref, micros)
+        if start < hidden:
+            for part in range(0, LANES, cut):
+                rank = (start + part) // cut
+                expand_ref[rank] = value[part : part + cut].astype(low)
+        else:
+            down_ref[...] = value[:adapt].reshape(ranks, adapt // ranks, width).astype(low)
+
+    def two_tile(start):
+        value = token_sum(hidden_ref, slice(start, start + LANES), all_ref, micros).T
+        value = value.reshape(seq, ranks, width // (seq * ranks), LANES)
+        for rank in range(ranks):
+            two_terms_ref[rank, :, :, start : start + LANES] = value[:, rank].astype(low)
+
+    starts = range(0, slope_ref.shape[2], LANES)
+    fill = [
+        (functools.partial(tile, start), 1.2) for tile in (two_tile, one_tile) for start in starts
+    ]
+    tasks = [
+        make_task(
+            micro, [gather], [scatter], compute, finish, before, 0 if micro == 0 else None
+        )
+        for micro in range(micros)
+    ]
+    run_tasks(tasks, io, fill, 1)
+
+
+def ffn_back_stage(seq, ranks, hidden, adapt, name_id, up, resid, pair, before, one, two, rows_all,
+                   hidden_low):
     micros, rows, width = up.shape
-    hidden = one.shape[0]
+    padded = one.shape[0]
     length = rows * seq
     outs = (
-        jax.ShapeDtypeStruct((micros, length, width), low),
-        jax.ShapeDtypeStruct((micros, length, hidden), low),
         jax.ShapeDtypeStruct((micros, rows, width), wide),
         jax.ShapeDtypeStruct((2, width), wide),
+        jax.ShapeDtypeStruct((ranks, hidden // ranks, width), low),
+        jax.ShapeDtypeStruct((ranks, adapt // ranks, width), low),
+        jax.ShapeDtypeStruct((ranks, seq, width // (seq * ranks), padded), low),
     )
     scratch = (
-        [pltpu.VMEM((micros, rows, width), low), pltpu.VMEM((micros, rows, width), wide)]
+        [pltpu.VMEM((micros, length, width), low), pltpu.VMEM((micros, length, padded), low)]
+        + back_scratch(micros, rows, width)
         + gather_scratch(seq, micros)
         + scatter_scratch(seq, micros, rows, width)
     )
     return stage_call(
-        functools.partial(ffn_back_kernel, seq), name_id, outs, scratch,
-        (up, resid, pair, before, one, two), 60,
-    )
-
-
-class Task:
-    def __init__(self, begin, arrive, compute, leave, drain):
-        self.begin, self.arrive, self.compute = begin, arrive, compute
-        self.leave, self.drain = leave, drain
-
-
-def spread(first, second):
-    steps, done = [], 0
-    for index, step in enumerate(first):
-        steps.append(step)
-        upto = len(second) * (index + 1) // len(first)
-        steps += second[done:upto]
-        done = upto
-    return steps + second[done:]
-
-
-def run_tasks(tasks):
-    for task in tasks[:2]:
-        task.begin()
-    for step in tasks[0].arrive:
-        step()
-    for index, task in enumerate(tasks):
-        other = []
-        if index > 0:
-            other += tasks[index - 1].leave
-        if index + 1 < len(tasks):
-            other += tasks[index + 1].arrive
-        if index + 2 < len(tasks):
-            other.append(tasks[index + 2].begin)
-        for step in spread(task.compute, other):
-            step()
-    for step in tasks[-1].leave:
-        step()
-    for task in tasks:
-        task.drain()
-
-
-def make_task(micro, gathers, scatters, compute, finish, before=None):
-    def begin():
-        if before is not None:
-            before(micro)
-        for gather in gathers:
-            gather.start(micro)
-
-    def drain():
-        for item in gathers + scatters:
-            item.drain(micro)
-
-    arrive = arrive_steps(gathers, micro)
-    leave = leave_steps(scatters, finish, micro) if scatters else []
-    return Task(begin, arrive, compute(micro), leave, drain)
-
-
-def gather_kernel(seq, count, *refs):
+        functools.partial(ffn_back_kernel, seq, ranks, hidden), name_id, outs, scratch,
+        (up, resid, pair, before, one, two, rows_all, hidden_low), 65,
+        {3: 0, 4: 0, 5: 0, 6: 1, 7: 1},
+    )
+
+
+def gather_kernel(seq, count, io, *refs):
     links = Links(seq)
     owns, alls, scratch = refs[:count], refs[count : 2 * count], refs[2 * count :]
     gathers = [
@@ -635,7 +748,7 @@
         task.begin()
     for phase in range(len(tasks[0].arrive)):
         for task in tasks:
-            task.arrive[phase]()
+            task.arrive[phase][0]()
     for task in tasks:
         task.drain()
 
@@ -731,10 +844,10 @@
         place = pl.ds(start, size)
         out_ref[micro, place] = dot(rows_ref[micro, place], weight_ref[...], 1, 1).astype(low)
 
-    return [lambda: loop(0, length // size, size, body)]
-
-
-def self_kernel(seq, count, *refs):
+    return [(lambda: loop(0, length // size, size, body), 1.3)]
+
+
+def self_kernel(seq, count, io, *refs):
     kinds = 2
     scratch = refs[-kinds * 7 :]
     refs = refs[: -kinds * 7]
@@ -768,7 +881,7 @@
                 return dot(context_ref[micro, pl.ds(start, size)], out_ref[...], 1, 1)
 
             return project_steps(micro, all_ref, in_ref, qkv_ref) + half_steps(
-                scatter, micro, length, chunk
+                scatter, micro, length, chunk, 4.2
             )
 
         def finish(
@@ -782,8 +895,11 @@
             low_ref[micro] = value.astype(low)
 
         for micro in range(micros):
-            tasks.append(make_task(micro, [], [scatter], compute, finish))
-    run_tasks(tasks)
+            load = kind if micro == 0 else None
+            tasks.append(
+                make_task(micro, [], [scatter], compute, finish, None, load, (kind, micro))
+            )
+    run_tasks(tasks, io)
 
 
 def self_stage(seq, name_id, count, places, sides):
@@ -802,13 +918,14 @@
     scratch = scatter_scratch(seq, micros, rows, width) * 2
     args = tuple(places) + sides[0] + sides[1]
     outs = stage_call(
-        functools.partial(self_kernel, seq, count), name_id, side_outs * 2, scratch, args, 75
+        functools.partial(self_kernel, seq, count), name_id, side_outs * 2, scratch, args, 75,
+        {10: 1, 11: 1, 12: 1, 13: 1, 15: 1}, {0: 0, 1: 0, 6: 1, 7: 1},
     )
     return outs[:6], outs[6:]
 
 
 def cross_kernel(
-    seq, count, kpos_ref, qpos_ref, first_ref, first_low_ref, memory_ref, q_in_ref, kv_in_ref,
+    seq, count, io, kpos_ref, qpos_ref, first_ref, first_low_ref, memory_ref, q_in_ref, kv_in_ref,
     out_ref, prefix_ref, kid_ref, qid_ref, pair_ref, first_all, memory_all, q_ref, kv_ref,
     context_ref, logs_ref, sum_ref, norm_ref, low_ref, *scratch,
 ):
@@ -833,7 +950,7 @@
         return (
             project_steps(micro, memory_all, kv_in_ref, kv_ref)
             + project_steps(micro, first_all, q_in_ref, q_ref)
-            + half_steps(scatter, micro, length, chunk)
+            + half_steps(scatter, micro, length, chunk, 4.2)
         )
 
     def finish(micro):
@@ -843,9 +960,13 @@
         norm_ref[micro] = value
         low_ref[micro] = value.astype(low)
 
-    run_tasks(
-        [make_task(micro, gathers, [scatter], compute, finish) for micro in range(micros)]
-    )
+    tasks = [
+        make_task(
+            micro, gathers, [scatter], compute, finish, None, 0 if micro == 0 else None, (0, micro)
+        )
+        for micro in range(micros)
+    ]
+    run_tasks(tasks, io)
 
 
 def cross_stage(seq, name_id, count, places, args):
@@ -868,7 +989,8 @@
     scratch = gather_scratch(seq, micros) * 2 + scatter_scratch(seq, micros, rows, width)
     return stage_call(
         functools.partial(cross_kernel, seq, count), name_id, outs, scratch,
-        tuple(places) + args, 85,
+        tuple(places) + args, 85, {place: 0 for place in (2, 5, 6, 7, 8, 9, 10)},
+        {place: 0 for place in range(5)},
     )
 
 
@@ -902,13 +1024,41 @@
         grad_ref[micro, :, head_width : 2 * head_width] = k_sum[...].astype(low)
         grad_ref[micro, :, 2 * head_width : 3 * head_width] = v_sum[...].astype(low)
 
-    return [lambda: run(half, True), lambda: run(0, False), keys]
+    return [(lambda: run(half, True), 5.0), (lambda: run(0, False), 5.0), (keys, 0.5)]
+
+
+def term_steps(context_ref, up_all, grad_ref, sources, in_terms_ref, out_terms_ref):
+    micros = grad_ref.shape[0]
+    ranks, seq, cols, head_width = out_terms_ref.shape
+    width = up_all.shape[2]
+
+    def out_tile():
+        value = token_sum(context_ref, slice(0, head_width), up_all, micros).T
+        value = value.reshape(seq, ranks, cols, head_width)
+        for rank in range(ranks):
+            out_terms_ref[rank] = value[:, rank].astype(low)
+
+    def in_tile(part):
+        lanes = slice(part * head_width, (part + 1) * head_width)
+        value = token_sum(grad_ref, lanes, sources[part], micros)
+        in_terms_ref[:, part] = value.reshape(ranks, cols, width).astype(low)
+
+    return [(out_tile, 1.5)] + [(functools.partial(in_tile, part), 1.0) for part in range(3)]
+
+
+def term_shapes(seq, ranks, width, head_width):
+    cols = width // (seq * ranks)
+    return (
+        jax.ShapeDtypeStruct((ranks, 3, cols, width), low),
+        jax.ShapeDtypeStruct((ranks, seq, cols, head_width), low),
+    )
 
 
 def cross_back_kernel(
-    seq, count, kpos_ref, qpos_ref, up_ref, resid_ref, pair_ref, q_ref, kv_ref, logs_ref, q_in_ref,
-    kv_in_ref, out_ref, prefix_ref, kid_ref, qid_ref, up_all, grad_ref, pre_ref, first_out,
-    memory_out, pair_grad_ref, own_ref, kept_ref, k_sum, v_sum, up_chunk, *scratch,
+    seq, count, io, kpos_ref, qpos_ref, up_ref, resid_ref, pair_ref, q_ref, kv_ref, logs_ref,
+    q_in_ref, kv_in_ref, out_ref, prefix_ref, kid_ref, qid_ref, first_all, memory_all, context_ref,
+    pre_ref, first_out, memory_out, pair_grad_ref, in_terms_ref, out_terms_ref, up_all, grad_ref,
+    own_ref, kept_ref, k_sum, v_sum, up_chunk, *scratch,
 ):
     links = Links(seq)
     micros, rows, _ = own_ref.shape
@@ -942,46 +1092,56 @@
             attention, micro, length, up_all, out_ref, logs_ref, grad_ref, k_sum, v_sum, pre_ref,
             up_chunk,
         )
-        sums = half_steps(first_sum, micro, length, first_chunk)
+        sums = half_steps(first_sum, micro, length, first_chunk, 0.6)
         return (
             [attend[0], sums[0], attend[1], sums[1], attend[2]]
-            + half_steps(memory_sum, micro, length, memory_chunk)
+            + half_steps(memory_sum, micro, length, memory_chunk, 0.8)
         )
 
     def finish(micro):
         first_out[micro] = kept_ref[micro] + first_sum.total(micro)
         memory_out[micro] = memory_sum.total(micro)
 
-    run_tasks(
-        [
-            make_task(micro, [gather], [first_sum, memory_sum], compute, finish, before)
-            for micro in range(micros)
-        ]
-    )
-
-
-def cross_back_stage(seq, name_id, count, places, args):
+    tasks = [
+        make_task(
+            micro, [gather], [first_sum, memory_sum], compute, finish, before,
+            0 if micro == 0 else None,
+        )
+        for micro in range(micros)
+    ]
+    fill = term_steps(
+        context_ref, up_all, grad_ref, (first_all, memory_all, memory_all), in_terms_ref,
+        out_terms_ref,
+    )
+    run_tasks(tasks, io, fill, 1)
+
+
+def cross_back_stage(seq, ranks, name_id, count, places, args):
     micros, rows, width = args[0].shape
     length = rows * seq
     head_width = args[9].shape[2]
     own = jax.ShapeDtypeStruct((micros, rows, width), wide)
     outs = (
-        jax.ShapeDtypeStruct((micros, length, width), low),
-        jax.ShapeDtypeStruct((micros, length, 3 * head_width), low),
         jax.ShapeDtypeStruct((2, PAD_PREFIX, head_width), wide),
         own,
         own,
         jax.ShapeDtypeStruct((2, width), wide),
-    )
+    ) + term_shapes(seq, ranks, width, head_width)
     scratch = (
-        back_scratch(micros, rows, width)
+        [
+            pltpu.VMEM((micros, length, width), low),
+            pltpu.VMEM((micros, length, 3 * head_width), low),
+        ]
+        + back_scratch(micros, rows, width)
         + sum_scratch(length, head_width)
         + gather_scratch(seq, micros)
         + scatter_scratch(seq, micros, rows, width) * 2
     )
+    lazy = {place: 0 for place in range(5, 14)}
+    lazy.update({14: 1, 15: 1, 16: 1})
     return stage_call(
         functools.partial(cross_back_kernel, seq, count), name_id, outs, scratch,
-        tuple(places) + args, 85,
+        tuple(places) + args, 85, lazy,
     )
 
 
@@ -997,80 +1157,75 @@
     ]
 
 
-def self_back_kernel(seq, count, causals, *refs):
-    kinds = len(causals)
-    size = 2 + 3 + 7
-    scratch = refs[-(3 + kinds * size) :]
-    refs = refs[: -(3 + kinds * size)]
-    k_sum, v_sum, up_chunk = scratch[:3]
-    places = refs[:2]
+def self_back_kernel(
+    seq, count, causal, io, kpos_ref, qpos_ref, up_ref, resid_ref, pair_ref, qkv_ref, logs_ref,
+    in_ref, out_ref, prefix_ref, kid_ref, qid_ref, context_ref, rows_ref, pre_ref, grad_out,
+    pair_grad_ref, in_terms_ref, out_terms_ref, up_all, grad_ref, own_ref, kept_ref, k_sum, v_sum,
+    up_chunk, *scratch,
+):
     links = Links(seq)
+    micros, rows, _ = own_ref.shape
+    length = up_all.shape[1]
+    head_width = prefix_ref.shape[2]
+    gather = Gather(links, own_ref, up_all, *scratch[:3])
+    scatter = Scatter(links, rows, *scratch[3:8], scratch[8:10])
+    ids = (kid_ref, qid_ref, kpos_ref, qpos_ref)
+    attention = Attention(
+        qkv_ref, qkv_ref, (0, head_width, 2 * head_width), prefix_ref, ids, count, causal
+    )
     links.enter()
-    tasks = []
-    for kind in range(kinds):
-        (
-            up_ref, resid_ref, pair_ref, qkv_ref, logs_ref, in_ref, out_ref, prefix_ref, kid_ref,
-            qid_ref,
-        ) = refs[2 + 10 * kind : 12 + 10 * kind]
-        up_all, grad_ref, pre_ref, grad_out, pair_grad_ref = refs[
-            2 + 10 * kinds + 5 * kind : 7 + 10 * kinds + 5 * kind
-        ]
-        piece = scratch[3 + size * kind : 3 + size * kind + size]
-        own_ref, kept_ref = piece[:2]
-        micros, rows, _ = own_ref.shape
-        length = up_all.shape[1]
-        head_width = prefix_ref.shape[2]
-        gather = Gather(links, own_ref, up_all, *piece[2:5])
-        scatter = Scatter(links, rows, *piece[5:10], piece[10:12])
-        ids = (kid_ref, qid_ref) + tuple(places)
-        attention = Attention(
-            qkv_ref, qkv_ref, (0, head_width, 2 * head_width), prefix_ref, ids, count, causals[kind]
-        )
-
-        def before(
-            micro, args=(up_ref, resid_ref, pair_ref, own_ref, kept_ref, pair_grad_ref)
-        ):
-            prologue(micro, *args)
-
-        def compute(
-            micro, attention=attention, up_all=up_all, out_ref=out_ref, logs_ref=logs_ref,
-            grad_ref=grad_ref, pre_ref=pre_ref, in_ref=in_ref, scatter=scatter,
-        ):
-            def chunk(start, size):
-                return dot(grad_ref[micro, pl.ds(start, size)], in_ref[...], 1, 0)
-
-            return attend_back_steps(
-                attention, micro, length, up_all, out_ref, logs_ref, grad_ref, k_sum, v_sum,
-                pre_ref, up_chunk,
-            ) + half_steps(scatter, micro, length, chunk)
-
-        def finish(micro, grad_out=grad_out, kept_ref=kept_ref, scatter=scatter):
-            grad_out[micro] = kept_ref[micro] + scatter.total(micro)
-
-        for micro in range(micros):
-            tasks.append(make_task(micro, [gather], [scatter], compute, finish, before))
-    run_tasks(tasks)
-
-
-def self_back_stage(seq, name_id, count, places, causal, side):
+
+    def before(micro):
+        prologue(micro, up_ref, resid_ref, pair_ref, own_ref, kept_ref, pair_grad_ref)
+
+    def compute(micro):
+        def chunk(start, size):
+            return dot(grad_ref[micro, pl.ds(start, size)], in_ref[...], 1, 0)
+
+        return attend_back_steps(
+            attention, micro, length, up_all, out_ref, logs_ref, grad_ref, k_sum, v_sum,
+            pre_ref, up_chunk,
+        ) + half_steps(scatter, micro, length, chunk, 0.9)
+
+    def finish(micro):
+        grad_out[micro] = kept_ref[micro] + scatter.total(micro)
+
+    tasks = [
+        make_task(
+            micro, [gather], [scatter], compute, finish, before, 0 if micro == 0 else None
+        )
+        for micro in range(micros)
+    ]
+    fill = term_steps(
+        context_ref, up_all, grad_ref, (rows_ref,) * 3, in_terms_ref, out_terms_ref
+    )
+    run_tasks(tasks, io, fill, 1)
+
+
+def self_back_stage(seq, ranks, name_id, count, places, causal, side):
     micros, rows, width = side[0].shape
     length = rows * seq
     head_width = side[7].shape[2]
     outs = (
-        jax.ShapeDtypeStruct((micros, length, width), low),
-        jax.ShapeDtypeStruct((micros, length, 3 * head_width), low),
         jax.ShapeDtypeStruct((2, PAD_PREFIX, head_width), wide),
         jax.ShapeDtypeStruct((micros, rows, width), wide),
         jax.ShapeDtypeStruct((2, width), wide),
-    )
-    scratch = sum_scratch(length, head_width) + (
-        back_scratch(micros, rows, width)
+    ) + term_shapes(seq, ranks, width, head_width)
+    scratch = (
+        [
+            pltpu.VMEM((micros, length, width), low),
+            pltpu.VMEM((micros, length, 3 * head_width), low),
+        ]
+        + back_scratch(micros, rows, width)
+        + sum_scratch(length, head_width)
         + gather_scratch(seq, micros)
         + scatter_scratch(seq, micros, rows, width)
     )
+    lazy = {place: 0 for place in range(5, 12)}
+    lazy.update({12: 1, 13: 1})
     return stage_call(
-        functools.partial(self_back_kernel, seq, count, (causal,)), name_id, outs, scratch,
-        tuple(places) + side, 75,
+        functools.partial(self_back_kernel, seq, count, causal), name_id, outs, scratch,
+        tuple(places) + side, 75, lazy,
     )
 
 
@@ -1235,7 +1390,7 @@
     decoder_two = row_order(gather_rows(last[1]))
 
     decoder_qkvs, decoder_ctx, decoder_logs, resid_three, first, first_low = decoder_side
-    middle_all, encoder_before, encoder_hidden, resid_two, memory = ffn_stage(
+    middle_all, encoder_before, encoder_hidden, resid_two, _, memory_low = ffn_stage(
         seq, 3, middle_low, middle, encoder_one, encoder_two, scales[1]
     )
     (
@@ -1244,124 +1399,75 @@
     ) = cross_stage(
         seq, 4, count, places,
         (
-            first, first_low, memory.astype(low), cross_q_in, cross_kv_in, cross_out, cross_pre,
+            first, first_low, memory_low, cross_q_in, cross_kv_in, cross_out, cross_pre,
             source_keys, target_queries, scales[norm_count + 1],
         ),
     )
-    second_all, decoder_before, decoder_hidden, resid_five, third = ffn_stage(
+    second_all, decoder_before, decoder_hidden, resid_five, _, result = ffn_stage(
         seq, 5, second_low, second, decoder_one, decoder_two, scales[norm_count + 2]
     )
-    result = third.astype(low)
 
     def scatter_ranks(value):
         return lax.psum_scatter(value, "rows", scatter_dimension=0, tiled=False)
 
-    def laid(value):
-        return with_layout_constraint(value.astype(low), Layout(tuple(range(value.ndim))))
-
-    def column_terms(grad, parts):
-        value = grad.reshape(parts, ranks, slice_cols, width)
-        return laid(jnp.swapaxes(value, 0, 1))
-
-    def row_terms(grad):
-        value = grad.astype(low).T.reshape(seq, ranks, slice_cols, -1)
-        return laid(jnp.swapaxes(value, 0, 1))
-
-    def ffn_in_terms(grad):
-        return laid(
-            jnp.concatenate(
-                [
-                    grad[:hidden].reshape(ranks, -1, width),
-                    grad[hidden:both].reshape(ranks, -1, width),
-                ],
-                axis=1,
-            )
-        )
-
-    def flat(value):
-        return value.reshape(-1, value.shape[-1])
-
     norm_grads = {}
 
     def ffn_back(name_id, index, up, resid, before, hidden_low, rows_all, one, two):
-        up_all, slope, out, pair = ffn_back_stage(
-            seq, name_id, up, resid, scales[index], before, one, two
-        )
-        norm_grads[index] = (pair[0:1], pair[1:2])
-        two_terms = row_terms(dot(flat(hidden_low), flat(up_all), 0, 0))
-        one_terms = ffn_in_terms(dot(flat(slope), flat(rows_all), 0, 0))
-        return out, one_terms, two_terms
+        out, pair, expand, down, two_terms = ffn_back_stage(
+            seq, ranks, hidden, adapt, name_id, up, resid, scales[index], before, one, two,
+            rows_all, hidden_low,
+        )
+        keep_pair(index, pair)
+        return out, [two_terms, jnp.concatenate([expand, down], axis=1)]
 
     def hold(value, terms, sums):
         value, terms, sums = lax.optimization_barrier((value, terms, sums))
         return value, [scatter_ranks(term) for term in terms], sums
 
-    second_up, one_terms, two_terms = ffn_back(
+    def keep_pair(index, pair):
+        norm_grads[index] = (pair[0:1], pair[1:2])
+
+    second_up, terms = ffn_back(
         6, norm_count + 2, cotangent.reshape(stacked, block, width), resid_five, decoder_before,
         decoder_hidden, second_all, decoder_one, decoder_two,
     )
-    second_up, ffn_sums, _ = hold(second_up, [two_terms, one_terms], [])
-
-    def keep_pair(index, pair):
-        norm_grads[index] = (pair[0:1], pair[1:2])
-
-    second_grad_all, cross_grads, cross_pre_grad, first_up, memory_up, pair = cross_back_stage(
-        seq, 7, count, places,
+    second_up, ffn_sums, _ = hold(second_up, terms, [])
+
+    cross_pre_grad, first_up, memory_up, pair, in_terms, out_terms = cross_back_stage(
+        seq, ranks, 7, count, places,
         (
             second_up, resid_four, scales[norm_count + 1], cross_q, cross_kvs, cross_logs,
             cross_q_in, cross_kv_in, cross_out, cross_pre, source_keys, target_queries,
+            first_all, memory_all, cross_ctx,
         ),
     )
     keep_pair(norm_count + 1, pair)
-    cross_terms = [
-        row_terms(dot(flat(cross_ctx), flat(second_grad_all), 0, 0)),
-        column_terms(
-            jnp.concatenate(
-                [
-                    dot(flat(cross_grads[:, :, :head_width]), flat(first_all), 0, 0),
-                    dot(flat(cross_grads[:, :, head_width:]), flat(memory_all), 0, 0),
-                ]
-            ),
-            3,
-        ),
-    ]
-    first_up, cross_sums, ffn_sums = hold(first_up, cross_terms, ffn_sums)
+    first_up, cross_sums, ffn_sums = hold(first_up, [out_terms, in_terms], ffn_sums)
     decoder_two_grad, decoder_one_grad = ffn_sums
 
-    def self_back(name_id, index, causal, side, context, rows_all, sums):
-        grad_all, grads, pre_grad, out, pair = self_back_stage(
-            seq, name_id, count, places, causal, side
-        )
-        grad_all, grads, pre_grad, out, pair, sums = lax.optimization_barrier(
-            (grad_all, grads, pre_grad, out, pair, sums)
-        )
+    def self_back(name_id, index, causal, side, sums):
+        held = self_back_stage(seq, ranks, name_id, count, places, causal, side)
+        held, sums = lax.optimization_barrier((held, sums))
+        pre_grad, out, pair, in_terms, out_terms = held
         keep_pair(index, pair)
-        return (
-            out,
-            pre_grad,
-            sums,
-            [
-                row_terms(dot(flat(context), flat(grad_all), 0, 0)),
-                column_terms(dot(flat(grads), flat(rows_all), 0, 0), 3),
-            ],
-        )
+        return out, pre_grad, sums, [out_terms, in_terms]
 
     target_grad, decoder_pre_grad, cross_sums, self_terms = self_back(
         9, norm_count, True,
         (
             first_up, resid_three, scales[norm_count], decoder_qkvs, decoder_logs, decoder_in,
-            decoder_out, decoder_pre, target_keys, target_queries,
+            decoder_out, decoder_pre, target_keys, target_queries, decoder_ctx, target_all,
         ),
-        decoder_ctx, target_all, cross_sums,
+        cross_sums,
     )
     memory_up, self_sums, _ = hold(memory_up, self_terms, [])
     cross_out_grad, cross_in_grad = cross_sums
 
-    middle_up, one_terms, two_terms = ffn_back(
+    middle_up, terms = ffn_back(
         8, 1, memory_up, resid_two, encoder_before, encoder_hidden, middle_all,
         encoder_one, encoder_two,
     )
-    middle_up, ffn_sums, self_sums = hold(middle_up, [two_terms, one_terms], self_sums)
+    middle_up, ffn_sums, self_sums = hold(middle_up, terms, self_sums)
     decoder_out_grad, decoder_in_grad = self_sums
 
     def give_back(pieces):
@@ -1374,9 +1480,9 @@
         10, 0, False,
         (
             middle_up, resid_one, scales[0], encoder_qkvs, encoder_logs, encoder_in,
-            encoder_out, encoder_pre, source_keys, source_queries,
+            encoder_out, encoder_pre, source_keys, source_queries, encoder_ctx, source_all,
         ),
-        encoder_ctx, source_all, ffn_sums,
+        ffn_sums,
     )
     source_grad, self_sums, _ = hold(source_grad, self_terms, [])
     encoder_two_grad, encoder_one_grad = ffn_sums

time: 960 us -> 813 us (0.85)
  Pallas kernels: 699 us -> 609 us
  matrix products: 41.9 us -> 0 us
    pallas_call x10, Pallas kernels: 699 us -> 609 us  [stage_call(): pl.pallas_call(body, out_shape=tuple(outs), in_specs=[far if place in laz...]
    dot_general x11 -> x0, matrix products: 41.9 us -> none  [dot(): lax.dot_general(left, right, (((left_axis,), (right_axis,)), ((), ())), p...]
  transfers between devices with their start and end apart: 33 -> 33, of which waited for: 13 -> 14; matrix products, arithmetic and copies ran while one was open for 9% -> 7% of each run, Pallas kernels for 61% -> 63%
where the time goes in v4:
time: 813 us; the launch traced here: 807 us
  Pallas kernels  609 us (75%)
  waiting for transfers between devices  64.1 us (8%)
  local copies, waits for them, and re-layouts  51.3 us (6%)
  starting transfers between devices  25 us (3%)
  other arithmetic  23.5 us (3%)
  blocking collectives  18.4 us (2%)
  between operations  15.9 us (2%)
    pallas_call x10, Pallas kernels, stage_call(): pl.pallas_call(body, out_shape=tuple(outs), in_specs=[far if place in laz...  609 us
    all_gather x6, waiting for transfers between devices, gather_rows(): return lax.all_gather(value, 'rows', axis=0, tiled=False)  26.3 us
    ppermute x7, waiting for transfers between devices, small_scatter(): lax.ppermute(jnp.where(flip, lower, upper), name, swap_pairs(count, bit))  18.5 us
    all_to_all x1, blocking collectives, local(): lax.all_to_all(row_pieces, 'seq', 1, 0, tiled=False)  18.4 us
  transfers between devices with their start and end apart: 33, of which 14 were waited for; matrix products, arithmetic and copies ran while one was open for 7% of the time, Pallas kernels for 63%

profile of v4, /device:TPU:0, one launch (start us, length us, event | category | flops | bytes accessed | tf_op | source)
XLA Modules:
  0.0 807.4 jit_solution(10070695472998613299)
XLA Ops:
  13.4 18.4 %all_to_all.54 = bf16[1,32,8,1664]{3,1,0,2:T(8,128)(2,1)S(1)} all-to-all(bf16[1,32,8,1664]{3,1,0,2:T(8,128)(2,1)S(1)} %copy.227), channel_id=1, replica_groups=mesh['seq'=8,'rows'=4] {'seq'}, dimensions={2} | all-to-all | bytes 1703936 | tf_op jit(solution)/shard_map/all_to_all | solution.py:1305
  32.8 1.6 collective-permute-start
  36.4 42.9 %shard_map.416 = (bf16[2,1024,1024]{2,1,0:T(8,128)(2,1)}, bf16[2,1024,1024]{2,1,0:T(8,128)(2,1)}) custom-call(bf16[2,128,1024]{2,1,0:T(8,128)(2,1)} %bitcast.323, bf16[2,128,1024]{2,1,0:T(8,128)(2,1)} %bitcast.325), custom_call_target="tpu_custom_call" | custom-call | flops 112499998720 | bytes 16777216 | tf_op jit(solution)/shard_map/pallas_call | solution.py:572
  80.5 2.7 collective-permute-start.3
  83.9 2.0 collective-permute-done.3
  93.4 5.8 all-gather.13.cloned.1.call-done
  105.7 3.2 collective-permute-done.1
  113.9 70.3 %shard_map.417 = (bf16[2,1024,384]{2,1,0:T(8,128)(2,1)}, bf16[2,1024,128]{2,1,0:T(8,128)(2,1)}, f32[2,2,1024]{2,1,0:T(2,128)}, f32[2,128,1024]{2,1,0:T(8,128)}, ...) custom-call(s32[1024,1]{1,0:T(8,128)} %copy.251.refs_0_, ...), custom_call_target="tpu_custom_call" | custom-call | flops 187500003328 | bytes 16777216 | tf_op jit(solution)/shard_map/pallas_call | solution.py:572
  194.1 20.5 %all-gather.21.cloned.1.call-done = bf16[576,1024]{1,0:T(8,128)(2,1)} async-done(((bf16[144,1024]{1,0:T(8,128)(2,1)}), bf16[576,1024]{1,0:T(8,128)(2,1)}) %all-gather.21.cloned.1.call-update) | async-done | bytes 1179664 | tf_op jit(solution)/shard_map/all_gather | solution.py:1270
  216.8 2.0 maximum_maximum_fusion.1
  218.8 53.2 %shard_map.418 = (bf16[2,1024,1024]{2,1,0:T(8,128)(2,1)}, f32[2,1024,640]{2,1,0:T(8,128)}, bf16[2,1024,640]{2,1,0:T(8,128)(2,1)}, f32[2,128,1024]{2,1,0:T(8,128)...) custom-call(bf16[2,128,1024]{2,1,0:T(8,128)(2,1)} %get-tuple-element.139.refs_0_, ...), custom_call_target="tpu_custom_call" | custom-call | flops 149999992832 | bytes 16777216 | tf_op jit(solution)/shard_map/pallas_call | solution.py:572
  272.0 81.6 %shard_map.419 = (bf16[2,1024,1024]{2,1,0:T(8,128)(2,1)}, bf16[2,1024,1024]{2,1,0:T(8,128)(2,1)}, bf16[2,1024,128]{2,1,0:T(8,128)(2,1)}, bf16[2,1024,256]{2,1,0:...) custom-call(s32[1024,1]{1,0:T(8,128)} %copy.251.refs_0_, ...), custom_call_target="tpu_custom_call" | custom-call | flops 212500004864 | bytes 16777216 | tf_op jit(solution)/shard_map/pallas_call | solution.py:572
  353.7 2.5 copy.253
  356.3 52.0 %shard_map.420 = (bf16[2,1024,1024]{2,1,0:T(8,128)(2,1)}, f32[2,1024,640]{2,1,0:T(8,128)}, bf16[2,1024,640]{2,1,0:T(8,128)(2,1)}, f32[2,128,1024]{2,1,0:T(8,128)...) custom-call(bf16[2,128,1024]{2,1,0:T(8,128)(2,1)} %get-tuple-element.144.refs_0_, ...), custom_call_target="tpu_custom_call" | custom-call | flops 149999992832 | bytes 16777216 | tf_op jit(solution)/shard_map/pallas_call | solution.py:572
  408.3 51.7 %shard_map.421 = (f32[2,128,1024]{2,1,0:T(8,128)}, f32[2,1024]{1,0:T(2,128)}, bf16[4,128,1024]{2,1,0:T(8,128)(2,1)}, bf16[4,16,1024]{2,1,0:T(8,128)(2,1)}, bf16[4,8,32,640]{3,2,1,0:T(8,128)(2,1)}) custom-call(bf16[2,128,1024]{2,1,0:T(8,128)(2,1)} %bitcast.327, f32[2,128,1024]{2,1,0:T(8,128)} %get-tuple-element.149.refs_1_, ...), custom_call_target="tpu_custom_call" | custom-call | flops 162500001792 | bytes 16777216 | tf_op jit(solution)/shard_map/pallas_call | solution.py:572
  460.1 2.4 pad_maximum_fusion
  463.3 77.7 %shard_map.422 = (f32[2,32,128]{2,1,0:T(8,128)}, f32[2,128,1024]{2,1,0:T(8,128)}, f32[2,128,1024]{2,1,0:T(8,128)}, f32[2,1024]{1,0:T(2,128)}, bf16[4,3,32,1024]{...) custom-call(s32[1024,1]{1,0:T(8,128)} %copy.251.refs_0_, s32[1,1024]{1,0:T(1,128)} %bitcast.312, ...), custom_call_target="tpu_custom_call" | custom-call | flops 212500004864 | bytes 16777216 | tf_op jit(solution)/shard_map/pallas_call | solution.py:572
  541.7 62.0 %shard_map.423 = (f32[2,32,128]{2,1,0:T(8,128)}, f32[2,128,1024]{2,1,0:T(8,128)}, f32[2,1024]{1,0:T(2,128)}, bf16[4,3,32,1024]{3,2,1,0:T(8,128)(2,1)}, bf16[4,8,32,128]{3,2,1,0:T(8,128)(2,1)}) custom-call(s32[1024,1]{1,0:T(8,128)} %copy.251.refs_0_, s32[1,1024]{1,0:T(1,128)} %bitcast.313, f32[2,128,1024]{2,1,0:T(8,128)} %get-tuple-element.171.refs_2_, ...), custom_call_target="tpu_custom_call" | custom-call | flops 187500003328 | bytes 16777216 | tf_op jit(solution)/shard_map/pallas_call | solution.py:572
  604.4 51.4 %shard_map.424 = (f32[2,128,1024]{2,1,0:T(8,128)}, f32[2,1024]{1,0:T(2,128)}, bf16[4,128,1024]{2,1,0:T(8,128)(2,1)}, bf16[4,16,1024]{2,1,0:T(8,128)(2,1)}, bf16[4,8,32,640]{3,2,1,0:T(8,128)(2,1)}) custom-call(f32[2,128,1024]{2,1,0:T(8,128)} %get-tuple-element.185.refs_0_, f32[2,128,1024]{2,1,0:T(8,128)} %get-tuple-element.186.refs_1_, ...), custom_call_target="tpu_custom_call" | custom-call | flops 162500001792 | bytes 16777216 | tf_op jit(solution)/shard_map/pallas_call | solution.py:572
  655.8 2.4 pad_maximum_fusion.1
  670.7 4.3 all-to-all-start.3
  675.6 66.4 %shard_map.425 = (f32[2,32,128]{2,1,0:T(8,128)}, f32[2,128,1024]{2,1,0:T(8,128)}, f32[2,1024]{1,0:T(2,128)}, bf16[4,3,32,1024]{3,2,1,0:T(8,128)(2,1)}, bf16[4,8,32,128]{3,2,1,0:T(8,128)(2,1)}) custom-call(s32[1024,1]{1,0:T(8,128)} %copy.251.refs_0_, s32[1,1024]{1,0:T(1,128)} %bitcast.314, f32[2,128,1024]{2,1,0:T(8,128)} %get-tuple-element.196.refs_2_, ...), custom_call_target="tpu_custom_call" | custom-call | flops 187500003328 | bytes 16777216 | tf_op jit(solution)/shard_map/pallas_call | solution.py:572
  750.6 1.5 collective-permute-start.10
  752.2 2.5 collective-permute-done.10
  757.2 3.6 collective-permute-done.12
  764.4 3.4 all-to-all-start.2
  769.0 6.7 collective-permute-done.7
  776.4 4.3 collective-permute-done.8
  781.4 3.5 all-to-all-start.1
  786.6 3.3 all-to-all-done.1
  790.7 5.3 reduce-scatter.27.cloned.1.call-done
  796.0 1.7 convert_bitcast_fusion.4
  (347 shorter events, 78.5 us)
Async XLA Ops:
  7.2 86.2 %all-gather.15.cloned.1.call-start = ((), (), s32[]{:S(2)}) async-start(), calls=%async_computation.25 | async-start | bytes 1310720 | tf_op jit(solution)/shard_map/all_gather | solution.py:1270
  32.7 66.4 %all-gather.13.cloned.1.call-start = ((), (), s32[]{:S(2)}) async-start(), calls=%async_computation.24 | async-start | bytes 1966080 | tf_op jit(solution)/shard_map/all_gather | solution.py:1270
  32.8 68.0 %collective-permute-start = (bf16[1,6,30,32]{3,1,2,0:T(8,128)(2,1)S(1)}, bf16[1,6,30,32]{3,1,2,0:T(8,128)(2,1)S(1)}, u32[]{:S(2)}, u32[]{:S(2)}) collective-permute-start(bf16[1,6,30,32]{3,1,2,0:T(8,128)(2,1)S(1)} %maximum_bitcast_fusion.2), channel_id=1, source_target_pairs={{0,1},{1,0},{2,3},{3,2},{4,5},{5,4},{6,7},{7,6},{8,9},{9,8},{10,11... | collective-permute-start | bytes 34568 | tf_op jit(solution)/shard_map/ppermute | solution.py:61
  34.5 45.9 %collective-permute-start.2 = (bf16[1,5,2,32]{3,2,1,0:T(2,128)(2,1)S(1)}, bf16[1,5,2,32]{3,2,1,0:T(2,128)(2,1)S(1)}, u32[]{:S(2)}, u32[]{:S(2)}) collective-permute-start(bf16[1,5,2,32]{3,2,1,0:T(2,128)(2,1)S(1)} %maximum_bitcast_fusion.3), channel_id=1, source_target_pairs={{0,1},{1,0},{2,3},{3,2},{4,5},{5,4},{6,7},{7,6},{8,9},{9,8},{10,11... | collective-permute-start | bytes 1928 | tf_op jit(solution)/shard_map/ppermute | solution.py:61
  35.8 148.4 %all-gather.19.cloned.1.call-start = ((), (), s32[]{:S(2)}) async-start(), calls=%async_computation.27 | async-start | bytes 1310720 | tf_op jit(solution)/shard_map/all_gather | solution.py:1270
  80.5 5.4 collective-permute-start.3
  87.1 12.1 %collective-permute-start.5 = (bf16[8,5,2,32]{3,2,1,0:T(2,128)(2,1)S(1)}, bf16[8,5,2,32]{3,2,1,0:T(2,128)(2,1)S(1)}, u32[]{:S(2)}, u32[]{:S(2)}) collective-permute-start(bf16[8,5,2,32]{3,2,1,0:T(2,128)(2,1)S(1)} %broadcast_select_fusion.4), channel_id=1, source_target_pairs={{0,8},{4,12},{8,0},{12,4},{16,24},{20,28},{24,16},{28,20},{1,9},{5... | collective-permute-start | bytes 15368 | tf_op jit(solution)/shard_map/ppermute | solution.py:61
  99.1 85.1 %all-gather.17.cloned.1.call-start = ((), (), s32[]{:S(2)}) async-start(), calls=%async_computation.26 | async-start | bytes 2457600 | tf_op jit(solution)/shard_map/all_gather | solution.py:1270
  99.3 4.1 collective-permute-start.6
  100.9 8.0 collective-permute-start.1
  113.6 101.0 %all-gather.21.cloned.1.call-start = ((), (), s32[]{:S(2)}) async-start(), calls=%async_computation.28 | async-start | bytes 1474560 | tf_op jit(solution)/shard_map/all_gather | solution.py:1270
  184.3 169.4 %all-gather.23.cloned.1.call-start = ((), (), s32[]{:S(2)}) async-start(), calls=%async_computation.29 | async-start | bytes 1638400 | tf_op jit(solution)/shard_map/all_gather | solution.py:1270
  194.1 346.9 %reduce-scatter.13.cloned.1.call-start = ((), (), s32[]{:S(2)}) async-start(), calls=%async_computation.15 | async-start | bytes 1474560 | tf_op jit(solution)/shard_map/reduce_scatter | solution.py:1411
  462.5 78.5 %reduce-scatter.11.cloned.1.call-start = ((), (), s32[]{:S(2)}) async-start(), calls=%async_computation.14 | async-start | bytes 1638400 | tf_op jit(solution)/shard_map/reduce_scatter | solution.py:1411
  463.3 140.5 %reduce-scatter.15.cloned.1.call-start = ((), (), s32[]{:S(2)}) async-start(), calls=%async_computation.16 | async-start | bytes 327680 | tf_op jit(solution)/shard_map/reduce_scatter | solution.py:1411
  541.0 62.7 %reduce-scatter.17.cloned.1.call-start = ((), (), s32[]{:S(2)}) async-start(), calls=%async_computation.17 | async-start | bytes 983040 | tf_op jit(solution)/shard_map/reduce_scatter | solution.py:1411
  541.6 116.6 %reduce-scatter.19.cloned.1.call-start = ((), (), s32[]{:S(2)}) async-start(), calls=%async_computation.18 | async-start | bytes 327680 | tf_op jit(solution)/shard_map/reduce_scatter | solution.py:1411
  603.8 54.5 %reduce-scatter.21.cloned.1.call-start = ((), (), s32[]{:S(2)}) async-start(), calls=%async_computation.19 | async-start | bytes 983040 | tf_op jit(solution)/shard_map/reduce_scatter | solution.py:1411
  604.4 140.6 %reduce-scatter.25.cloned.1.call-start = ((), (), s32[]{:S(2)}) async-start(), calls=%async_computation.21 | async-start | bytes 1474560 | tf_op jit(solution)/shard_map/reduce_scatter | solution.py:1411
  670.7 72.4 %all-to-all-start.3 = ((bf16[8,32,1,896]{3,1,2,0:T(8,128)(2,1)}), bf16[8,32,1,896]{3,1,2,0:T(8,128)(2,1)}, u32[]{:S(2)}, u32[]{:S(2)}) async-start(bf16[8,32,1,896]{3,1,2,0:T(8,128)(2,1)} %maximum_bitcast_fusion.1), calls=%async_computation.13 | async-start | bytes 917504 | tf_op jit(solution)/shard_map/all_to_all | solution.py:1475
  675.0 70.0 %reduce-scatter.23.cloned.1.call-start = ((), (), s32[]{:S(2)}) async-start(), calls=%async_computation.20 | async-start | bytes 1638400 | tf_op jit(solution)/shard_map/reduce_scatter | solution.py:1411
  675.6 105.9 %reduce-scatter.29.cloned.1.call-start = ((), (), s32[]{:S(2)}) async-start(), calls=%async_computation.23 | async-start | bytes 327680 | tf_op jit(solution)/shard_map/reduce_scatter | solution.py:1411
  746.0 4.5 collective-permute-start.9
  750.6 4.1 collective-permute-start.10
  754.7 1.3 collective-permute-start.11
  756.0 4.8 collective-permute-start.12
  760.8 7.5 collective-permute-start.13
  761.9 13.7 %collective-permute-start.7 = (f32[2,6,30,32]{3,1,2,0:T(8,128)S(1)}, f32[2,6,30,32]{3,1,2,0:T(8,128)S(1)}, u32[]{:S(2)}, u32[]{:S(2)}) collective-permute-start(f32[2,6,30,32]{3,1,2,0:T(8,128)S(1)} %slice_select_fusion), channel_id=1, source_target_pairs={{0,2},{1,3},{2,0},{3,1},{4,6},{5,7},{6,4},{7,5},{8,10},{9,11},{10,... | collective-permute-start | bytes 138248 | tf_op jit(solution)/shard_map/ppermute | solution.py:76
  764.4 17.0 %all-to-all-start.2 = ((bf16[8,32,1,640]{3,1,2,0:T(8,128)(2,1)}), bf16[8,32,1,640]{3,1,2,0:T(8,128)(2,1)S(1)}, u32[]{:S(2)}, u32[]{:S(2)}) async-start(bf16[8,32,1,640]{3,1,2,0:T(8,128)(2,1)} %bitcast.101), calls=%async_computation.12 | async-start | bytes 655360 | tf_op jit(solution)/shard_map/all_to_all | solution.py:1475
  767.8 28.2 %reduce-scatter.27.cloned.1.call-start = ((), (), s32[]{:S(2)}) async-start(), calls=%async_computation.22 | async-start | bytes 983040 | tf_op jit(solution)/shard_map/reduce_scatter | solution.py:1411
  775.7 4.9 collective-permute-start.8
  781.4 8.4 %all-to-all-start.1 = ((bf16[8,32,1,128]{3,1,2,0:T(8,128)(2,1)}), bf16[8,32,1,128]{3,1,2,0:T(8,128)(2,1)S(1)}, u32[]{:S(2)}, u32[]{:S(2)}) async-start(bf16[8,32,1,128]{3,1,2,0:T(8,128)(2,1)} %bitcast.305), calls=%async_computation.11 | async-start | bytes 131072 | tf_op jit(solution)/shard_map/all_to_all | solution.py:1475
  (60 other events, 882.6 us)
Sparse Core Ops, SparseCore 0:
  32.8 27.2 all-gather.14
  62.3 36.7 all-gather.12
  101.3 26.7 all-gather.18
  130.0 43.0 all-gather.16
  184.4 30.1 all-gather.20
  216.6 31.8 all-gather.22
  462.6 27.1 reduce-scatter.12
  492.1 29.9 reduce-scatter.10
  541.2 17.6 reduce-scatter.14
  561.1 21.5 reduce-scatter.16
  603.9 17.6 reduce-scatter.18
  623.8 21.6 reduce-scatter.20
  658.4 27.1 reduce-scatter.24
  687.8 29.9 reduce-scatter.22
  750.1 18.6 reduce-scatter.28
  771.0 24.9 reduce-scatter.26

commit v5 on v4

--- a/solution.py
+++ b/solution.py
@@ -53,19 +53,6 @@
     return jnp.moveaxis(value, depth - 1, 0).reshape(-1)
 
 
-def small_gather(value, axes):
-    value = value[None]
-    for name, count in axes[::-1]:
-        me = lax.axis_index(name)
-        for bit in bit_list(count):
-            other = lax.ppermute(value, name, swap_pairs(count, bit))
-            flip = (me & bit) != 0
-            value = jnp.where(
-                flip, jnp.concatenate([other, value]), jnp.concatenate([value, other])
-            )
-    return value
-
-
 def small_scatter(value, axes):
     for name, count in axes:
         me = lax.axis_index(name)
@@ -128,14 +115,17 @@
     def device(self, bit):
         return {"seq": jnp.bitwise_xor(self.me, bit)}
 
-    def enter(self):
+    def enter(self, others=()):
         barrier = pltpu.get_barrier_semaphore()
         bits = bit_list(self.seq)
         for bit in bits:
             pl.semaphore_signal(
                 barrier, inc=1, device_id=self.device(bit), device_id_type=pl.DeviceIdType.MESH
             )
-        pl.semaphore_wait(barrier, len(bits))
+        count = len(bits)
+        for other in others:
+            count += other.greet(barrier)
+        pl.semaphore_wait(barrier, count)
 
     def copy(self, source, target, send_sem, recv_sem, bit):
         return pltpu.make_async_remote_copy(
@@ -733,32 +723,182 @@
     )
 
 
-def gather_kernel(seq, count, io, *refs):
+def opening_kernel(
+    seq, ranks, io, source_ref, target_ref, out_ref, ffn_ref, small_ref, source_all, target_all,
+    out_all, ffn_all, small_all, norm_all, *scratch,
+):
     links = Links(seq)
-    owns, alls, scratch = refs[:count], refs[count : 2 * count], refs[2 * count :]
+    me, row = lax.axis_index("seq"), lax.axis_index("rows")
     gathers = [
-        Gather(links, owns[k], alls[k], *scratch[3 * k : 3 * k + 3]) for k in range(count)
+        Gather(links, source_ref, source_all, *scratch[0:3]),
+        Gather(links, target_ref, target_all, *scratch[3:6]),
     ]
-    links.enter()
-    tasks = []
-    for gather in gathers:
-        for micro in range(owns[0].shape[0]):
-            tasks.append(make_task(micro, [gather], [], lambda micro: [], None))
+    out_sems, ffn_sems, norm_sems, out_row_sems, small_row_sems, local_sems = scratch[6:]
+    masks = range(1, seq)
+    row_bits = bit_list(ranks)
+    norm_rows = norm_all.shape[2]
+
+    def remote(source, target, sems, index, device):
+        return pltpu.make_async_remote_copy(
+            src_ref=source,
+            dst_ref=target,
+            send_sem=sems.at[0, index],
+            recv_sem=sems.at[1, index],
+            device_id=device,
+            device_id_type=pl.DeviceIdType.MESH,
+        )
+
+    def plane(mask):
+        return {"seq": jnp.bitwise_xor(me, mask)}
+
+    def other(mask):
+        return jnp.bitwise_xor(me, mask)
+
+    barrier = pltpu.get_barrier_semaphore()
+    for mask in masks:
+        pl.semaphore_signal(
+            barrier, inc=1, device_id=plane(mask), device_id_type=pl.DeviceIdType.MESH
+        )
+    for bit in row_bits:
+        pl.semaphore_signal(
+            barrier,
+            inc=1,
+            device_id={"rows": jnp.bitwise_xor(row, bit)},
+            device_id_type=pl.DeviceIdType.MESH,
+        )
+    pl.semaphore_wait(barrier, seq - 1 + len(row_bits))
+
+    locals_ = [
+        pltpu.make_async_copy(out_ref.at[me], out_all.at[row, me], local_sems.at[0]),
+        pltpu.make_async_copy(ffn_ref.at[me], ffn_all.at[me], local_sems.at[1]),
+        pltpu.make_async_copy(small_ref, small_all.at[row], local_sems.at[2]),
+    ]
+    for copy in locals_:
+        copy.start()
+
+    def out_send(mask):
+        return remote(
+            out_ref.at[other(mask)], out_all.at[row, me], out_sems, mask, plane(mask)
+        )
+
+    def out_wait(mask):
+        return remote(
+            out_ref.at[other(mask)], out_all.at[row, other(mask)], out_sems, mask, plane(mask)
+        )
+
+    def ffn_send(mask):
+        return remote(ffn_ref.at[other(mask)], ffn_all.at[me], ffn_sems, mask, plane(mask))
+
+    def ffn_wait(mask):
+        return remote(
+            ffn_ref.at[other(mask)], ffn_all.at[other(mask)], ffn_sems, mask, plane(mask)
+        )
+
+    def norm_send(mask):
+        return remote(
+            small_all.at[:, 0:norm_rows], norm_all.at[me], norm_sems, mask, plane(mask)
+        )
+
+    def norm_wait(mask):
+        return remote(
+            small_all.at[:, 0:norm_rows], norm_all.at[other(mask)], norm_sems, mask, plane(mask)
+        )
+
+    def row_copy(array, sems, mask, bit, there):
+        at = jnp.bitwise_xor(row, mask)
+        place = jnp.bitwise_xor(at, bit) if there else at
+        return remote(
+            array.at[at],
+            array.at[place],
+            sems,
+            mask | bit,
+            {"rows": jnp.bitwise_xor(row, bit)},
+        )
+
+    def row_phase(array, sems, phase):
+        bit = row_bits[phase]
+        for mask in span(row_bits[:phase]):
+            row_copy(array, sems, mask, bit, False).start()
+
+    def row_done(array, sems, phase):
+        bit = row_bits[phase]
+        for mask in span(row_bits[:phase]):
+            row_copy(array, sems, mask, bit, True).wait_recv()
+
+    for mask in masks:
+        out_send(mask).start()
+    tasks = [
+        make_task(micro, [gather], [], lambda micro: [], None)
+        for gather in gathers
+        for micro in range(source_ref.shape[0])
+    ]
+    locals_[2].wait()
+    row_phase(small_all, small_row_sems, 0)
     for task in tasks:
         task.begin()
-    for phase in range(len(tasks[0].arrive)):
-        for task in tasks:
-            task.arrive[phase][0]()
+    for mask in masks:
+        ffn_send(mask).start()
+    locals_[0].wait()
+    for mask in masks:
+        out_wait(mask).wait_recv()
+    row_phase(out_all, out_row_sems, 0)
+    steps = [
+        functools.partial(task.arrive[phase][0])
+        for phase in range(len(tasks[0].arrive))
+        for task in tasks
+    ]
+    for phase in range(len(row_bits)):
+        row_done(small_all, small_row_sems, phase)
+        if phase + 1 < len(row_bits):
+            row_phase(small_all, small_row_sems, phase + 1)
+    norm_all[me] = small_all[:, 0:norm_rows]
+    for mask in masks:
+        norm_send(mask).start()
+    cuts = [len(steps) * part // len(row_bits) for part in range(len(row_bits) + 1)]
+    for phase in range(len(row_bits)):
+        for step in steps[cuts[phase] : cuts[phase + 1]]:
+            step()
+        row_done(out_all, out_row_sems, phase)
+        if phase + 1 < len(row_bits):
+            row_phase(out_all, out_row_sems, phase + 1)
+    for mask in masks:
+        norm_wait(mask).wait_recv()
+        ffn_wait(mask).wait_recv()
+    locals_[1].wait()
+    for mask in masks:
+        out_send(mask).wait_send()
+        ffn_send(mask).wait_send()
+        norm_send(mask).wait_send()
+    for phase, bit in enumerate(row_bits):
+        for mask in span(row_bits[:phase]):
+            row_copy(out_all, out_row_sems, mask, bit, False).wait_send()
+            row_copy(small_all, small_row_sems, mask, bit, False).wait_send()
     for task in tasks:
         task.drain()
 
 
-def gather_stage(seq, name_id, owns):
-    micros, rows, width = owns[0].shape
-    outs = tuple(jax.ShapeDtypeStruct((micros, seq * rows, width), low) for _ in owns)
-    scratch = gather_scratch(seq, micros) * len(owns)
+def opening_stage(seq, ranks, name_id, norm_rows, args):
+    source, _, out_pieces, ffn_pieces, small = args
+    micros, rows, width = source.shape
+    whole = jax.ShapeDtypeStruct((micros, seq * rows, width), low)
+    outs = (
+        whole,
+        whole,
+        jax.ShapeDtypeStruct((ranks,) + out_pieces.shape, low),
+        jax.ShapeDtypeStruct(ffn_pieces.shape, low),
+        jax.ShapeDtypeStruct((ranks,) + small.shape, low),
+        jax.ShapeDtypeStruct((seq, ranks, norm_rows, small.shape[1]), low),
+    )
+    scratch = gather_scratch(seq, micros) * 2 + [
+        pltpu.SemaphoreType.DMA((2, seq)),
+        pltpu.SemaphoreType.DMA((2, seq)),
+        pltpu.SemaphoreType.DMA((2, seq)),
+        pltpu.SemaphoreType.DMA((2, ranks)),
+        pltpu.SemaphoreType.DMA((2, ranks)),
+        pltpu.SemaphoreType.DMA((3,)),
+    ]
     return stage_call(
-        functools.partial(gather_kernel, seq, len(owns)), name_id, outs, scratch, owns, 45
+        functools.partial(opening_kernel, seq, ranks), name_id, outs, scratch, args, 55
     )
 
 
@@ -1027,38 +1167,78 @@
     return [(lambda: run(half, True), 5.0), (lambda: run(0, False), 5.0), (keys, 0.5)]
 
 
-def term_steps(context_ref, up_all, grad_ref, sources, in_terms_ref, out_terms_ref):
+def term_steps(context_ref, up_all, grad_ref, sources, terms_ref, seq, send=None):
     micros = grad_ref.shape[0]
-    ranks, seq, cols, head_width = out_terms_ref.shape
-    width = up_all.shape[2]
-
-    def out_tile():
-        value = token_sum(context_ref, slice(0, head_width), up_all, micros).T
-        value = value.reshape(seq, ranks, cols, head_width)
-        for rank in range(ranks):
-            out_terms_ref[rank] = value[:, rank].astype(low)
-
-    def in_tile(part):
-        lanes = slice(part * head_width, (part + 1) * head_width)
-        value = token_sum(grad_ref, lanes, sources[part], micros)
-        in_terms_ref[:, part] = value.reshape(ranks, cols, width).astype(low)
-
-    return [(out_tile, 1.5)] + [(functools.partial(in_tile, part), 1.0) for part in range(3)]
-
-
-def term_shapes(seq, ranks, width, head_width):
-    cols = width // (seq * ranks)
-    return (
-        jax.ShapeDtypeStruct((ranks, 3, cols, width), low),
-        jax.ShapeDtypeStruct((ranks, seq, cols, head_width), low),
-    )
+    ranks, _, cols, width = terms_ref.shape
+    head_width = context_ref.shape[2]
+
+    def tile(part):
+        if part == 3:
+            value = token_sum(context_ref, slice(0, head_width), up_all, micros).T
+            value = value.reshape(seq, ranks, cols, head_width)
+            for owner in range(seq):
+                lanes = slice(owner * head_width, (owner + 1) * head_width)
+                terms_ref[:, 3, :, lanes] = value[owner].astype(low)
+        else:
+            lanes = slice(part * head_width, (part + 1) * head_width)
+            value = token_sum(grad_ref, lanes, sources[part], micros)
+            terms_ref[:, part] = value.reshape(ranks, cols, width).astype(low)
+        if send is not None:
+            send(part)
+
+    return [(functools.partial(tile, part), 1.2) for part in (3, 0, 1, 2)]
+
+
+def term_shape(seq, ranks, width):
+    return jax.ShapeDtypeStruct((ranks, 4, width // (seq * ranks), width), low)
+
+
+class RankSum:
+    def __init__(self, ranks, terms_ref, recv_ref, total_ref, sems):
+        self.ranks, self.terms, self.recv = ranks, terms_ref, recv_ref
+        self.total, self.sems, self.row = total_ref, sems, lax.axis_index("rows")
+
+    def greet(self, barrier):
+        for mask in range(1, self.ranks):
+            pl.semaphore_signal(
+                barrier,
+                inc=1,
+                device_id={"rows": jnp.bitwise_xor(self.row, mask)},
+                device_id_type=pl.DeviceIdType.MESH,
+            )
+        return self.ranks - 1
+
+    def copy(self, part, mask):
+        owner = jnp.bitwise_xor(self.row, mask)
+        return pltpu.make_async_remote_copy(
+            src_ref=self.terms.at[owner, part],
+            dst_ref=self.recv.at[mask, part],
+            send_sem=self.sems.at[0, mask, part],
+            recv_sem=self.sems.at[1, mask, part],
+            device_id={"rows": owner},
+            device_id_type=pl.DeviceIdType.MESH,
+        )
+
+    def send(self, part):
+        for mask in range(1, self.ranks):
+            self.copy(part, mask).start()
+
+    def finish(self):
+        for part in (3, 0, 1, 2):
+            value = self.terms[self.row, part].astype(wide)
+            for mask in range(1, self.ranks):
+                self.copy(part, mask).wait_recv()
+                value = value + self.recv[mask, part].astype(wide)
+            self.total[part] = value
+        for part in range(4):
+            for mask in range(1, self.ranks):
+                self.copy(part, mask).wait_send()
 
 
 def cross_back_kernel(
     seq, count, io, kpos_ref, qpos_ref, up_ref, resid_ref, pair_ref, q_ref, kv_ref, logs_ref,
     q_in_ref, kv_in_ref, out_ref, prefix_ref, kid_ref, qid_ref, first_all, memory_all, context_ref,
-    pre_ref, first_out, memory_out, pair_grad_ref, in_terms_ref, out_terms_ref, up_all, grad_ref,
-    own_ref, kept_ref, k_sum, v_sum, up_chunk, *scratch,
+    pre_ref, first_out, memory_out, pair_grad_ref, terms_ref, up_all, grad_ref, own_ref, kept_ref, k_sum, v_sum, up_chunk, *scratch,
 ):
     links = Links(seq)
     micros, rows, _ = own_ref.shape
@@ -1110,8 +1290,7 @@
         for micro in range(micros)
     ]
     fill = term_steps(
-        context_ref, up_all, grad_ref, (first_all, memory_all, memory_all), in_terms_ref,
-        out_terms_ref,
+        context_ref, up_all, grad_ref, (first_all, memory_all, memory_all), terms_ref, seq
     )
     run_tasks(tasks, io, fill, 1)
 
@@ -1126,7 +1305,8 @@
         own,
         own,
         jax.ShapeDtypeStruct((2, width), wide),
-    ) + term_shapes(seq, ranks, width, head_width)
+        term_shape(seq, ranks, width),
+    )
     scratch = (
         [
             pltpu.VMEM((micros, length, width), low),
@@ -1158,9 +1338,9 @@
 
 
 def self_back_kernel(
-    seq, count, causal, io, kpos_ref, qpos_ref, up_ref, resid_ref, pair_ref, qkv_ref, logs_ref,
-    in_ref, out_ref, prefix_ref, kid_ref, qid_ref, context_ref, rows_ref, pre_ref, grad_out,
-    pair_grad_ref, in_terms_ref, out_terms_ref, up_all, grad_ref, own_ref, kept_ref, k_sum, v_sum,
+    seq, count, causal, reduce, io, kpos_ref, qpos_ref, up_ref, resid_ref, pair_ref, qkv_ref,
+    logs_ref, in_ref, out_ref, prefix_ref, kid_ref, qid_ref, context_ref, rows_ref, pre_ref,
+    grad_out, pair_grad_ref, result_ref, up_all, grad_ref, own_ref, kept_ref, k_sum, v_sum,
     up_chunk, *scratch,
 ):
     links = Links(seq)
@@ -1169,11 +1349,15 @@
     head_width = prefix_ref.shape[2]
     gather = Gather(links, own_ref, up_all, *scratch[:3])
     scatter = Scatter(links, rows, *scratch[3:8], scratch[8:10])
+    terms_ref, rank_sum = result_ref, None
+    if reduce:
+        terms_ref, recv_ref, rank_sems = scratch[10:]
+        rank_sum = RankSum(terms_ref.shape[0], terms_ref, recv_ref, result_ref, rank_sems)
     ids = (kid_ref, qid_ref, kpos_ref, qpos_ref)
     attention = Attention(
         qkv_ref, qkv_ref, (0, head_width, 2 * head_width), prefix_ref, ids, count, causal
     )
-    links.enter()
+    links.enter([rank_sum] if reduce else [])
 
     def before(micro):
         prologue(micro, up_ref, resid_ref, pair_ref, own_ref, kept_ref, pair_grad_ref)
@@ -1197,12 +1381,15 @@
         for micro in range(micros)
     ]
     fill = term_steps(
-        context_ref, up_all, grad_ref, (rows_ref,) * 3, in_terms_ref, out_terms_ref
+        context_ref, up_all, grad_ref, (rows_ref,) * 3, terms_ref, seq,
+        rank_sum.send if reduce else None,
     )
     run_tasks(tasks, io, fill, 1)
-
-
-def self_back_stage(seq, ranks, name_id, count, places, causal, side):
+    if reduce:
+        rank_sum.finish()
+
+
+def self_back_stage(seq, ranks, name_id, count, places, causal, reduce, side):
     micros, rows, width = side[0].shape
     length = rows * seq
     head_width = side[7].shape[2]
@@ -1210,7 +1397,11 @@
         jax.ShapeDtypeStruct((2, PAD_PREFIX, head_width), wide),
         jax.ShapeDtypeStruct((micros, rows, width), wide),
         jax.ShapeDtypeStruct((2, width), wide),
-    ) + term_shapes(seq, ranks, width, head_width)
+        term_shape(seq, ranks, width),
+    )
+    terms = outs[3]
+    if reduce:
+        outs = outs[:3] + (jax.ShapeDtypeStruct(terms.shape[1:], wide),)
     scratch = (
         [
             pltpu.VMEM((micros, length, width), low),
@@ -1221,10 +1412,16 @@
         + gather_scratch(seq, micros)
         + scatter_scratch(seq, micros, rows, width)
     )
+    if reduce:
+        scratch += [
+            pltpu.VMEM(terms.shape, low),
+            pltpu.VMEM(terms.shape, low),
+            pltpu.SemaphoreType.DMA((2, ranks, 4)),
+        ]
     lazy = {place: 0 for place in range(5, 12)}
     lazy.update({12: 1, 13: 1})
     return stage_call(
-        functools.partial(self_back_kernel, seq, count, causal), name_id, outs, scratch,
+        functools.partial(self_back_kernel, seq, count, causal, reduce), name_id, outs, scratch,
         tuple(places) + side, 75, lazy,
     )
 
@@ -1284,11 +1481,7 @@
         return jnp.swapaxes(value, 0, 1).reshape(parts * ranks * slice_cols, width)
 
     def split_rows(weight):
-        value = columns(weight)
-        return value.reshape(slice_cols, seq, -1)
-
-    def exchange(value):
-        return lax.all_to_all(value, "seq", 1, 1, tiled=False)
+        return columns(weight).reshape(slice_cols, seq, -1)
 
     def ffn_rows(contract, up):
         pieces = [split_rows(contract), split_rows(up) * jnp.asarray(ADAPTER_SCALE, low)]
@@ -1296,14 +1489,15 @@
             pieces.append(jnp.zeros((slice_cols, seq, padded - both), low))
         return pieces
 
-    row_pieces = jnp.concatenate(
-        [split_rows(encoder_output), split_rows(decoder_output), split_rows(cross_output)]
+    def by_target(pieces):
+        return jnp.swapaxes(jnp.concatenate(pieces, axis=2), 0, 1)
+
+    out_pieces = by_target([split_rows(encoder_output), split_rows(decoder_output)])
+    ffn_pieces = by_target(
+        [split_rows(cross_output)]
         + ffn_rows(encoder_contract, encoder_up)
-        + ffn_rows(decoder_contract, decoder_up),
-        axis=2,
-    )
-    row_pieces = lax.all_to_all(row_pieces, "seq", 1, 0, tiled=False).reshape(seq, slice_cols, -1)
-
+        + ffn_rows(decoder_contract, decoder_up)
+    )
     qkv_parts = gather_rows(
         jnp.concatenate(
             [
@@ -1312,8 +1506,27 @@
             ]
         )
     )
-    lead = 512 if 3 * head_width < 512 else 3 * head_width
-    front = gather_rows(row_pieces[:, :, :lead])
+    norm_count = encoder_norms.shape[0]
+    norms = jnp.concatenate([encoder_norms, decoder_norms]).reshape(-1, slice_cols)
+    prefixes = jnp.concatenate([encoder_prefix, decoder_prefix, cross_prefix])
+    prefixes = prefixes.reshape(-1, slice_cols)
+    norm_rows = (norms.shape[0] + 15) // 16 * 16
+    small = jnp.concatenate(
+        [jnp.pad(norms, ((0, norm_rows - norms.shape[0]), (0, 0))), prefixes]
+    )
+    small = jnp.pad(small, ((0, -small.shape[0] % 16), (0, 0)))
+    source_all, target_all, front, row_pieces, small_all, norm_all = opening_stage(
+        seq, ranks, 1, norm_rows, (sources, targets, out_pieces, ffn_pieces, small)
+    )
+    scales = norm_all[:, :, : norms.shape[0]].reshape(seq * ranks, -1, slice_cols)
+    scales = jnp.moveaxis(scales, 0, 1).reshape(-1, 2, width).astype(wide)
+    prefixes = small_all[:, norm_rows : norm_rows + 6 * count]
+    prefixes = jnp.moveaxis(prefixes.reshape(ranks, 6, count, slice_cols), 0, 2)
+    prefixes = prefixes.reshape(6, count, head_width)
+    prefixes = jnp.pad(prefixes, ((0, 0), (0, PAD_PREFIX - count), (0, 0)))
+    encoder_pre, decoder_pre, cross_pre = prefixes[0:2], prefixes[2:4], prefixes[4:6]
+    norm_axes = [("seq", seq), ("rows", ranks)]
+
     late = [
         jnp.concatenate(
             [
@@ -1323,20 +1536,16 @@
                 columns(cross_kv).reshape(-1, width),
             ]
         ),
-        row_pieces[:, :, lead : 3 * head_width + padded],
+        row_pieces[:, :, : head_width + padded],
         jnp.concatenate([columns(decoder_expand), columns(decoder_down)]),
-        row_pieces[:, :, 3 * head_width + padded :],
+        row_pieces[:, :, head_width + padded :],
     ]
-    source_all, target_all = gather_stage(seq, 1, (sources, targets))
-    source_all, qkv_parts, front, late = lax.optimization_barrier(
-        (source_all, qkv_parts, front, late)
-    )
+    source_all, late = lax.optimization_barrier((source_all, late))
     encoder_in = flat_columns(qkv_parts[:, : 3 * slice_cols], 3)
     decoder_in = flat_columns(qkv_parts[:, 3 * slice_cols :], 3)
-    front_rows = jnp.swapaxes(front[..., : 3 * head_width], 0, 1).reshape(width, -1)
+    front_rows = jnp.swapaxes(front, 0, 1).reshape(width, -1)
     encoder_out = front_rows[:, :head_width]
-    decoder_out = front_rows[:, head_width : 2 * head_width]
-    cross_out = front_rows[:, 2 * head_width :]
+    decoder_out = front_rows[:, head_width:]
     cut = encoder_expand.shape[1]
 
     def ffn_in(gathered):
@@ -1350,20 +1559,6 @@
 
     second_parts = gather_rows(late[0])
     rest = gather_rows(late[1])
-    prefixes = small_gather(
-        jnp.concatenate([encoder_prefix, decoder_prefix, cross_prefix]), [("rows", ranks)]
-    )
-    prefixes = jnp.moveaxis(prefixes, 0, 2).reshape(6, count, head_width)
-    prefixes = jnp.pad(prefixes, ((0, 0), (0, PAD_PREFIX - count), (0, 0)))
-    encoder_pre, decoder_pre, cross_pre = prefixes[0:2], prefixes[2:4], prefixes[4:6]
-
-    norm_axes = [("seq", seq), ("rows", ranks)]
-    scales = small_gather(
-        jnp.concatenate([encoder_norms, decoder_norms]), norm_axes
-    )
-    scales = jnp.moveaxis(scales, 0, 2).reshape(-1, 2, width).astype(wide)
-    norm_count = encoder_norms.shape[0]
-
     encoder_side, decoder_side = self_stage(
         seq, 2, count, places,
         (
@@ -1381,18 +1576,20 @@
     middle_low, second_parts, rest, last = lax.optimization_barrier(
         (middle_low, second_parts, rest, late[2:])
     )
-    encoder_two = row_order(jnp.concatenate([front[..., 3 * head_width :], rest], axis=3))
+    rest = row_order(rest)
+    cross_out, encoder_two = rest[:, :head_width], rest[:, head_width:]
     ffn_cut = cut + encoder_down.shape[1]
     encoder_one = ffn_in(second_parts[:, :ffn_cut])
     cross_in = flat_columns(second_parts[:, ffn_cut:], 3)
     cross_q_in, cross_kv_in = cross_in[:head_width], cross_in[head_width:]
-    decoder_one = ffn_in(gather_rows(last[0]))
-    decoder_two = row_order(gather_rows(last[1]))
-
     decoder_qkvs, decoder_ctx, decoder_logs, resid_three, first, first_low = decoder_side
     middle_all, encoder_before, encoder_hidden, resid_two, _, memory_low = ffn_stage(
         seq, 3, middle_low, middle, encoder_one, encoder_two, scales[1]
     )
+    memory_low, last = lax.optimization_barrier(
+        (memory_low, [gather_rows(piece) for piece in last])
+    )
+    decoder_one, decoder_two = ffn_in(last[0]), row_order(last[1])
     (
         first_all, memory_all, cross_q, cross_kvs, cross_ctx, cross_logs, resid_four, second,
         second_low,
@@ -1433,7 +1630,7 @@
     )
     second_up, ffn_sums, _ = hold(second_up, terms, [])
 
-    cross_pre_grad, first_up, memory_up, pair, in_terms, out_terms = cross_back_stage(
+    cross_pre_grad, first_up, memory_up, pair, terms = cross_back_stage(
         seq, ranks, 7, count, places,
         (
             second_up, resid_four, scales[norm_count + 1], cross_q, cross_kvs, cross_logs,
@@ -1442,33 +1639,37 @@
         ),
     )
     keep_pair(norm_count + 1, pair)
-    first_up, cross_sums, ffn_sums = hold(first_up, [out_terms, in_terms], ffn_sums)
+    first_up, cross_sums, ffn_sums = hold(first_up, [terms], ffn_sums)
     decoder_two_grad, decoder_one_grad = ffn_sums
 
-    def self_back(name_id, index, causal, side, sums):
-        held = self_back_stage(seq, ranks, name_id, count, places, causal, side)
+    def self_back(name_id, index, causal, reduce, side, sums):
+        held = self_back_stage(seq, ranks, name_id, count, places, causal, reduce, side)
         held, sums = lax.optimization_barrier((held, sums))
-        pre_grad, out, pair, in_terms, out_terms = held
+        pre_grad, out, pair, terms = held
         keep_pair(index, pair)
-        return out, pre_grad, sums, [out_terms, in_terms]
+        return out, pre_grad, sums, terms
+
+    def owner_parts(value):
+        out_part = value[3].reshape(slice_cols, seq, head_width)
+        return jnp.swapaxes(out_part, 0, 1), value[:3]
 
     target_grad, decoder_pre_grad, cross_sums, self_terms = self_back(
-        9, norm_count, True,
+        9, norm_count, True, False,
         (
             first_up, resid_three, scales[norm_count], decoder_qkvs, decoder_logs, decoder_in,
             decoder_out, decoder_pre, target_keys, target_queries, decoder_ctx, target_all,
         ),
         cross_sums,
     )
-    memory_up, self_sums, _ = hold(memory_up, self_terms, [])
-    cross_out_grad, cross_in_grad = cross_sums
+    memory_up, self_sums, _ = hold(memory_up, [self_terms], [])
+    cross_out_grad, cross_in_grad = owner_parts(cross_sums[0])
 
     middle_up, terms = ffn_back(
         8, 1, memory_up, resid_two, encoder_before, encoder_hidden, middle_all,
         encoder_one, encoder_two,
     )
     middle_up, ffn_sums, self_sums = hold(middle_up, terms, self_sums)
-    decoder_out_grad, decoder_in_grad = self_sums
+    decoder_out_grad, decoder_in_grad = owner_parts(self_sums[0])
 
     def give_back(pieces):
         value = jnp.concatenate(pieces, axis=2) if len(pieces) > 1 else pieces[0]
@@ -1477,18 +1678,17 @@
     decoder_rows = give_back([decoder_two_grad, cross_out_grad, decoder_out_grad])
 
     source_grad, encoder_pre_grad, ffn_sums, self_terms = self_back(
-        10, 0, False,
+        10, 0, False, True,
         (
             middle_up, resid_one, scales[0], encoder_qkvs, encoder_logs, encoder_in,
             encoder_out, encoder_pre, source_keys, source_queries, encoder_ctx, source_all,
         ),
         ffn_sums,
     )
-    source_grad, self_sums, _ = hold(source_grad, self_terms, [])
     encoder_two_grad, encoder_one_grad = ffn_sums
-    encoder_out_grad, encoder_in_grad = self_sums
+    encoder_out_grad, encoder_in_grad = owner_parts(self_terms)
     encoder_rows = give_back([encoder_two_grad])
-    encoder_out_rows = give_back([encoder_out_grad])
+    encoder_out_rows = give_back([encoder_out_grad.astype(low)])
 
     def row_grad(value, start, size, scale=None):
         piece = value[:, :, start : start + size].astype(wide)

time: 813 us -> 782 us (0.962)
  waiting for transfers between devices: 64.1 us -> 27.8 us
  Pallas kernels: 609 us -> 637 us
  blocking collectives: 18.4 us -> 0 us
    pallas_call x10, Pallas kernels: 609 us -> 637 us  [stage_call(): pl.pallas_call(body, out_shape=tuple(outs), in_specs=[far if place in laz...]
    all_gather x6 -> x5, waiting for transfers between devices: 26.3 us -> 0.04 us  [gather_rows(): return lax.all_gather(value, 'rows', axis=0, tiled=False)]
    all_to_all x1 -> x0, blocking collectives: 18.4 us -> none  [local(): lax.all_to_all(row_pieces, 'seq', 1, 0, tiled=False)]
    ppermute x7 -> x0, starting transfers between devices: 8.19 us -> none  [small_gather(): other = lax.ppermute(value, name, swap_pairs(count, bit))]
  transfers between devices with their start and end apart: 33 -> 21, of which waited for: 14 -> 7; matrix products, arithmetic and copies ran while one was open for 7% -> 8% of each run, Pallas kernels for 63% -> 58%
where the time goes in v5:
time: 782 us; the launch traced here: 777 us
  Pallas kernels  637 us (81%)
  local copies, waits for them, and re-layouts  54.6 us (7%)
  waiting for transfers between devices  27.8 us (4%)
  other arithmetic  23.6 us (3%)
  starting transfers between devices  17.9 us (2%)
  between operations  15.7 us (2%)
    pallas_call x10, Pallas kernels, stage_call(): pl.pallas_call(body, out_shape=tuple(outs), in_specs=[far if place in laz...  637 us
    ppermute x7, waiting for transfers between devices, small_scatter(): lax.ppermute(jnp.where(flip, lower, upper), name, swap_pairs(count, bit))  19.7 us
  transfers between devices with their start and end apart: 21, of which 7 were waited for; matrix products, arithmetic and copies ran while one was open for 8% of the time, Pallas kernels for 58%

profile of v5, /device:TPU:0, one launch (start us, length us, event | category | flops | bytes accessed | tf_op | source)
XLA Modules:
  0.0 776.8 jit_solution(15548856321854187680)
XLA Ops:
  7.3 1.9 pad_maximum_fusion.3
  13.9 60.3 %shard_map.416 = (bf16[2,1024,1024]{2,1,0:T(8,128)(2,1)}, bf16[2,1024,1024]{2,1,0:T(8,128)(2,1)}, bf16[4,8,32,256]{3,2,1,0:T(8,128)(2,1)}, bf16[8,32,1408]{2,1,0...) custom-call(bf16[2,128,1024]{2,1,0:T(8,128)(2,1)} %bitcast.333, ...), custom_call_target="tpu_custom_call" | custom-call | flops 137500000256 | bytes 16777216 | tf_op jit(solution)/shard_map/pallas_call | solution.py:562
  74.4 1.8 slice.258
  76.2 1.7 slice.259
  84.0 1.3 copy.276.refs_7_.refs_9_.refs_12_.refs_10_
  87.5 1.3 copy.277.refs_15_.refs_10_
  90.1 1.5 fusion.15
  93.5 71.9 %shard_map.417 = (bf16[2,1024,384]{2,1,0:T(8,128)(2,1)}, bf16[2,1024,128]{2,1,0:T(8,128)(2,1)}, f32[2,2,1024]{2,1,0:T(2,128)}, f32[2,128,1024]{2,1,0:T(8,128)}, ...) custom-call(s32[1024,1]{1,0:T(8,128)} %copy.280.refs_0_, ...), custom_call_target="tpu_custom_call" | custom-call | flops 187500003328 | bytes 16777216 | tf_op jit(solution)/shard_map/pallas_call | solution.py:562
  172.4 1.4 maximum_maximum_fusion.refs_2_.refs_4_
  173.8 52.8 %shard_map.418 = (bf16[2,1024,1024]{2,1,0:T(8,128)(2,1)}, f32[2,1024,640]{2,1,0:T(8,128)}, bf16[2,1024,640]{2,1,0:T(8,128)(2,1)}, f32[2,128,1024]{2,1,0:T(8,128)...) custom-call(bf16[2,128,1024]{2,1,0:T(8,128)(2,1)} %get-tuple-element.134.refs_0_, ...), custom_call_target="tpu_custom_call" | custom-call | flops 149999992832 | bytes 16777216 | tf_op jit(solution)/shard_map/pallas_call | solution.py:562
  228.6 1.7 slice.347.refs_7_.refs_10_
  234.7 1.3 maximum_maximum_fusion.1.refs_2_.refs_4_
  236.0 81.8 %shard_map.419 = (bf16[2,1024,1024]{2,1,0:T(8,128)(2,1)}, bf16[2,1024,1024]{2,1,0:T(8,128)(2,1)}, bf16[2,1024,128]{2,1,0:T(8,128)(2,1)}, bf16[2,1024,256]{2,1,0:...) custom-call(s32[1024,1]{1,0:T(8,128)} %copy.280.refs_0_, ...), custom_call_target="tpu_custom_call" | custom-call | flops 212500004864 | bytes 16777216 | tf_op jit(solution)/shard_map/pallas_call | solution.py:562
  317.8 52.0 %shard_map.420 = (bf16[2,1024,1024]{2,1,0:T(8,128)(2,1)}, f32[2,1024,640]{2,1,0:T(8,128)}, bf16[2,1024,640]{2,1,0:T(8,128)(2,1)}, f32[2,128,1024]{2,1,0:T(8,128)...) custom-call(bf16[2,128,1024]{2,1,0:T(8,128)(2,1)} %get-tuple-element.142.refs_0_, ...), custom_call_target="tpu_custom_call" | custom-call | flops 149999992832 | bytes 16777216 | tf_op jit(solution)/shard_map/pallas_call | solution.py:562
  369.8 51.2 %shard_map.421 = (f32[2,128,1024]{2,1,0:T(8,128)}, f32[2,1024]{1,0:T(2,128)}, bf16[4,128,1024]{2,1,0:T(8,128)(2,1)}, bf16[4,16,1024]{2,1,0:T(8,128)(2,1)}, bf16[4,8,32,640]{3,2,1,0:T(8,128)(2,1)}) custom-call(bf16[2,128,1024]{2,1,0:T(8,128)(2,1)} %bitcast.337, f32[2,128,1024]{2,1,0:T(8,128)} %get-tuple-element.147.refs_1_, ...), custom_call_target="tpu_custom_call" | custom-call | flops 162500001792 | bytes 16777216 | tf_op jit(solution)/shard_map/pallas_call | solution.py:562
  421.0 2.4 pad_maximum_fusion
  424.3 77.5 %shard_map.422 = (f32[2,32,128]{2,1,0:T(8,128)}, f32[2,128,1024]{2,1,0:T(8,128)}, f32[2,128,1024]{2,1,0:T(8,128)}, f32[2,1024]{1,0:T(2,128)}, bf16[4,4,32,1024]{3,2,1,0:T(8,128)(2,1)}) custom-call(s32[1024,1]{1,0:T(8,128)} %copy.280.refs_0_, s32[1,1024]{1,0:T(1,128)} %bitcast.322, f32[2,128,1024]{2,1,0:T(8,128)} %get-tuple-element.155.refs_2_, ...), custom_call_target="tpu_custom_call" | custom-call | flops 212500004864 | bytes 16777216 | tf_op jit(solution)/shard_map/pallas_call | solution.py:562
  501.9 62.1 %shard_map.423 = (f32[2,32,128]{2,1,0:T(8,128)}, f32[2,128,1024]{2,1,0:T(8,128)}, f32[2,1024]{1,0:T(2,128)}, bf16[4,4,32,1024]{3,2,1,0:T(8,128)(2,1)}) custom-call(s32[1024,1]{1,0:T(8,128)} %copy.280.refs_0_, s32[1,1024]{1,0:T(1,128)} %bitcast.323, f32[2,128,1024]{2,1,0:T(8,128)} %get-tuple-element.168.refs_2_, f32[2,128,1024]{2,1,0:T(8,128)} %get-tuple-element.169.refs_3_, ...), custom_call_target="tpu_custom_call" | custom-call | flops 187500003328 | bytes 16777216 | tf_op jit(solution)/shard_map/pallas_call | solution.py:562
  564.2 51.4 %shard_map.424 = (f32[2,128,1024]{2,1,0:T(8,128)}, f32[2,1024]{1,0:T(2,128)}, bf16[4,128,1024]{2,1,0:T(8,128)(2,1)}, bf16[4,16,1024]{2,1,0:T(8,128)(2,1)}, bf16[4,8,32,640]{3,2,1,0:T(8,128)(2,1)}) custom-call(f32[2,128,1024]{2,1,0:T(8,128)} %get-tuple-element.179.refs_0_, f32[2,128,1024]{2,1,0:T(8,128)} %get-tuple-element.180.refs_1_, ...), custom_call_target="tpu_custom_call" | custom-call | flops 162500001792 | bytes 16777216 | tf_op jit(solution)/shard_map/pallas_call | solution.py:562
  615.6 2.4 pad_maximum_fusion.1
  631.2 4.3 all-to-all-start.2
  636.3 76.2 %shard_map.425 = (f32[2,32,128]{2,1,0:T(8,128)}, f32[2,128,1024]{2,1,0:T(8,128)}, f32[2,1024]{1,0:T(2,128)}, f32[4,32,1024]{2,1,0:T(8,128)}) custom-call(s32[1024,1]{1,0:T(8,128)} %copy.280.refs_0_, s32[1,1024]{1,0:T(1,128)} %bitcast.324, f32[2,128,1024]{2,1,0:T(8,128)} %get-tuple-element.189.refs_2_, f32[2,128,1024]{2,1,0:T(8,128)} %get-tuple-element.190.refs_3_, ...), custom_call_target="tpu_custom_call" | custom-call | flops 187500003328 | bytes 16777216 | tf_op jit(solution)/shard_map/pallas_call | solution.py:562
  721.0 1.9 collective-permute-start.2
  723.0 2.6 collective-permute-done.2
  725.6 1.8 collective-permute-start.3
  727.4 2.3 collective-permute-done.3
  731.1 3.4 all-to-all-start
  735.5 3.6 collective-permute-done.5
  739.2 1.3 collective-permute-start.6
  744.1 9.6 %collective-permute-done = f32[2,6,30,32]{3,1,2,0:T(8,128)S(1)} collective-permute-done((f32[2,6,30,32]{3,1,2,0:T(8,128)S(1)}, f32[2,6,30,32]{3,1,2,0:T(8,128)S(1)}, u32[]{:S(2)}, u32[]{:S(2)}) %collective-permute-start) | collective-permute-done | bytes 46112 | tf_op jit(solution)/shard_map/ppermute | solution.py:63
  753.8 3.8 all-to-all-start.1
  759.5 5.8 all-to-all-done.1
  (336 shorter events, 64.6 us)
Async XLA Ops:
  7.3 82.8 %all-gather.11.cloned.1.call-start = ((), (), s32[]{:S(2)}) async-start(), calls=%async_computation.15 | async-start | bytes 1966080 | tf_op jit(solution)/shard_map/all_gather | solution.py:1467
  9.3 156.1 %all-gather.15.cloned.1.call-start = ((), (), s32[]{:S(2)}) async-start(), calls=%async_computation.17 | async-start | bytes 1966080 | tf_op jit(solution)/shard_map/all_gather | solution.py:1467
  79.8 85.6 %all-gather.13.cloned.1.call-start = ((), (), s32[]{:S(2)}) async-start(), calls=%async_computation.16 | async-start | bytes 2457600 | tf_op jit(solution)/shard_map/all_gather | solution.py:1467
  80.6 150.5 %all-gather.17.cloned.1.call-start = ((), (), s32[]{:S(2)}) async-start(), calls=%async_computation.18 | async-start | bytes 1474560 | tf_op jit(solution)/shard_map/all_gather | solution.py:1467
  93.5 72.0 %copy-start.24 = (f32[2,32,32]{2,1,0:T(8,128)S(1)}, f32[2,32,32]{2,1,0:T(8,128)}, u32[]{:S(2)}) copy-start(f32[2,32,32]{2,1,0:T(8,128)} %get-tuple-element.352) | copy-start | bytes 24580
  93.5 72.7 %copy-start.23 = (f32[2,32,32]{2,1,0:T(8,128)S(1)}, f32[2,32,32]{2,1,0:T(8,128)}, u32[]{:S(2)}) copy-start(f32[2,32,32]{2,1,0:T(8,128)} %get-tuple-element.351) | copy-start | bytes 24580
  93.5 73.4 %copy-start.22 = (f32[2,32,32]{2,1,0:T(8,128)S(1)}, f32[2,32,32]{2,1,0:T(8,128)}, u32[]{:S(2)}) copy-start(f32[2,32,32]{2,1,0:T(8,128)} %get-tuple-element.350) | copy-start | bytes 24580
  165.4 65.6 %all-gather.19.cloned.1.call-start = ((), (), s32[]{:S(2)}) async-start(), calls=%async_computation.19 | async-start | bytes 1638400 | tf_op jit(solution)/shard_map/all_gather | solution.py:1467
  172.4 329.5 %reduce-scatter.9.cloned.1.call-start = ((), (), s32[]{:S(2)}) async-start(), calls=%async_computation.10 | async-start | bytes 1474560 | tf_op jit(solution)/shard_map/reduce_scatter | solution.py:1608
  423.5 78.4 %reduce-scatter.7.cloned.1.call-start = ((), (), s32[]{:S(2)}) async-start(), calls=%async_computation.9 | async-start | bytes 1638400 | tf_op jit(solution)/shard_map/reduce_scatter | solution.py:1608
  424.2 139.8 %reduce-scatter.11.cloned.1.call-start = ((), (), s32[]{:S(2)}) async-start(), calls=%async_computation.11 | async-start | bytes 1310720 | tf_op jit(solution)/shard_map/reduce_scatter | solution.py:1608
  501.9 116.1 %reduce-scatter.13.cloned.1.call-start = ((), (), s32[]{:S(2)}) async-start(), calls=%async_computation.12 | async-start | bytes 1310720 | tf_op jit(solution)/shard_map/reduce_scatter | solution.py:1608
  564.1 155.2 %reduce-scatter.17.cloned.1.call-start = ((), (), s32[]{:S(2)}) async-start(), calls=%async_computation.14 | async-start | bytes 1474560 | tf_op jit(solution)/shard_map/reduce_scatter | solution.py:1608
  615.6 8.1 %copy-start.12 = (bf16[1,144,1024]{2,1,0:T(8,128)(2,1)S(1)}, bf16[1,144,1024]{2,1,0:T(8,128)(2,1)}, u32[]{:S(2)}) copy-start(bf16[1,144,1024]{2,1,0:T(8,128)(2,1)} %reduce-scatter.9.cloned.1.call-done) | copy-start | bytes 884740
  618.0 8.7 %copy-start.52 = (f32[2,1024]{1,0:T(2,128)S(1)}, f32[2,1024]{1,0:T(2,128)}, u32[]{:S(2)}) copy-start(f32[2,1024]{1,0:T(2,128)} %get-tuple-element.209) | copy-start | bytes 24580
  618.0 10.1 %copy-start.13 = (bf16[1,4,32,1024]{3,2,1,0:T(8,128)(2,1)S(1)}, bf16[1,4,32,1024]{3,2,1,0:T(8,128)(2,1)}, u32[]{:S(2)}) copy-start(bf16[1,4,32,1024]{3,2,1,0:T(8,128)(2,1)} %reduce-scatter.11.cloned.1.call-done) | copy-start | bytes 786436
  631.2 82.1 %all-to-all-start.2 = ((bf16[8,32,1,896]{3,1,2,0:T(8,128)(2,1)}), bf16[8,32,1,896]{3,1,2,0:T(8,128)(2,1)}, u32[]{:S(2)}, u32[]{:S(2)}) async-start(bf16[8,32,1,896]{3,1,2,0:T(8,128)(2,1)} %maximum_bitcast_fusion), calls=%async_computation.8 | async-start | bytes 917504 | tf_op jit(solution)/shard_map/all_to_all | solution.py:1676
  635.6 83.7 %reduce-scatter.15.cloned.1.call-start = ((), (), s32[]{:S(2)}) async-start(), calls=%async_computation.13 | async-start | bytes 1638400 | tf_op jit(solution)/shard_map/reduce_scatter | solution.py:1608
  636.3 76.2 %copy-start.16 = (bf16[1,4,32,1024]{3,2,1,0:T(8,128)(2,1)S(1)}, bf16[1,4,32,1024]{3,2,1,0:T(8,128)(2,1)}, u32[]{:S(2)}) copy-start(bf16[1,4,32,1024]{3,2,1,0:T(8,128)(2,1)} %reduce-scatter.13.cloned.1.call-done) | copy-start | bytes 786436
  720.1 15.1 %copy-start.38 = (f32[2,32,128]{2,1,0:T(8,128)S(1)}, f32[2,32,128]{2,1,0:T(8,128)}, u32[]{:S(2)}) copy-start(f32[2,32,128]{2,1,0:T(8,128)} %get-tuple-element.205) | copy-start | bytes 98308
  720.1 15.1 %copy-start.39 = (f32[2,32,128]{2,1,0:T(8,128)S(1)}, f32[2,32,128]{2,1,0:T(8,128)}, u32[]{:S(2)}) copy-start(f32[2,32,128]{2,1,0:T(8,128)} %get-tuple-element.204) | copy-start | bytes 98308
  720.1 15.1 %copy-start.40 = (f32[2,32,128]{2,1,0:T(8,128)S(1)}, f32[2,32,128]{2,1,0:T(8,128)}, u32[]{:S(2)}) copy-start(f32[2,32,128]{2,1,0:T(8,128)} %get-tuple-element.203) | copy-start | bytes 98308
  721.0 4.5 collective-permute-start.2
  725.6 4.1 collective-permute-start.3
  729.8 4.7 collective-permute-start.4
  731.1 22.7 %all-to-all-start = ((bf16[8,32,1,128]{3,1,2,0:T(8,128)(2,1)}), bf16[8,32,1,128]{3,1,2,0:T(8,128)(2,1)S(1)}, u32[]{:S(2)}, u32[]{:S(2)}) async-start(bf16[8,32,1,128]{3,1,2,0:T(8,128)(2,1)} %bitcast.244), calls=%async_computation.6 | async-start | bytes 131072 | tf_op jit(solution)/shard_map/all_to_all | solution.py:1676
  734.5 4.6 collective-permute-start.5
  739.2 3.7 collective-permute-start.6
  740.6 13.1 %collective-permute-start = (f32[2,6,30,32]{3,1,2,0:T(8,128)S(1)}, f32[2,6,30,32]{3,1,2,0:T(8,128)S(1)}, u32[]{:S(2)}, u32[]{:S(2)}) collective-permute-start(f32[2,6,30,32]{3,1,2,0:T(8,128)S(1)} %slice_select_fusion), channel_id=1, source_target_pairs={{0,2},{1,3},{2,0},{3,1},{4,6},{5,7},{6,4},{7,5},{8,10},{9,11},{10,... | collective-permute-start | bytes 138248 | tf_op jit(solution)/shard_map/ppermute | solution.py:63
  753.7 5.1 collective-permute-start.1
  753.8 11.5 %all-to-all-start.1 = ((bf16[8,32,1,640]{3,1,2,0:T(8,128)(2,1)}), bf16[8,32,1,640]{3,1,2,0:T(8,128)(2,1)S(1)}, u32[]{:S(2)}, u32[]{:S(2)}) async-start(bf16[8,32,1,640]{3,1,2,0:T(8,128)(2,1)} %bitcast.95), calls=%async_computation.7 | async-start | bytes 655360 | tf_op jit(solution)/shard_map/all_to_all | solution.py:1676
  758.5 8.6 %copy-start.7 = (bf16[2,128,1024]{2,1,0:T(8,128)(2,1)S(1)}, bf16[2,128,1024]{2,1,0:T(8,128)(2,1)}, u32[]{:S(2)}) copy-start(bf16[2,128,1024]{2,1,0:T(8,128)(2,1)} %get-tuple-element.146) | copy-start | bytes 1572868
  (55 other events, 230.3 us)
Sparse Core Ops, SparseCore 0:
  10.3 43.7 all-gather.10
  79.9 35.6 all-gather.14
  117.7 42.4 all-gather.12
  165.6 28.1 all-gather.16
  195.8 31.8 all-gather.18
  423.6 27.2 reduce-scatter.8
  453.2 29.9 reduce-scatter.6
  502.0 25.4 reduce-scatter.10
  564.2 25.4 reduce-scatter.12
  618.2 27.4 reduce-scatter.16
  648.0 29.9 reduce-scatter.14

commit v6 on v5

--- a/solution.py
+++ b/solution.py
@@ -51,18 +51,6 @@
         bit = 1 << (depth - 1 - axis)
         value = jnp.where((me & bit) != 0, jnp.flip(value, axis), value)
     return jnp.moveaxis(value, depth - 1, 0).reshape(-1)
-
-
-def small_scatter(value, axes):
-    for name, count in axes:
-        me = lax.axis_index(name)
-        for bit in bit_list(count)[::-1]:
-            half = value.shape[0] // 2
-            flip = (me & bit) != 0
-            lower, upper = value[:half], value[half:]
-            sent = lax.ppermute(jnp.where(flip, lower, upper), name, swap_pairs(count, bit))
-            value = jnp.where(flip, upper, lower) + sent
-    return value[0]
 
 
 def normalized(tensor):
@@ -453,11 +441,13 @@
             self.take(entry)
 
 
-def run_tasks(tasks, io, fill=(), fill_load=None):
+def run_tasks(tasks, io, fill=(), fill_load=None, opening=None, closing=None):
     waits = Waits()
     for task in tasks[:2]:
         task.begin()
         waits.add(task.arrive)
+    if opening is not None and len(tasks) <= 2:
+        waits.add(opening())
     for index, task in enumerate(tasks):
         if task.arrive:
             waits.finish(task.arrive)
@@ -469,6 +459,10 @@
         if index + 2 < len(tasks):
             tasks[index + 2].begin()
             waits.add(tasks[index + 2].arrive)
+    if opening is not None and len(tasks) > 2:
+        waits.add(opening())
+    if closing is not None:
+        waits.add(closing())
     if fill:
         io.load(fill_load)
         for step, cost in fill:
@@ -1235,6 +1229,47 @@
                 self.copy(part, mask).wait_send()
 
 
+class SmallSum:
+    def __init__(self, hops, held_ref, recv_ref, sems):
+        self.hops, self.held, self.recv, self.sems = hops, held_ref, recv_ref, sems
+
+    def copy(self, hop):
+        name, bit = self.hops[hop]
+        return pltpu.make_async_remote_copy(
+            src_ref=self.held.at[hop],
+            dst_ref=self.recv.at[hop],
+            send_sem=self.sems.at[0, hop],
+            recv_sem=self.sems.at[1, hop],
+            device_id={name: jnp.bitwise_xor(lax.axis_index(name), bit)},
+            device_id_type=pl.DeviceIdType.MESH,
+        )
+
+    def step(self, hop):
+        self.copy(hop).wait_recv()
+        self.held[hop + 1] = self.held[hop] + self.recv[hop]
+        if hop + 1 < len(self.hops):
+            self.copy(hop + 1).start()
+
+    def start(self, gap):
+        self.copy(0).start()
+        return [(functools.partial(self.step, hop), gap) for hop in range(len(self.hops))]
+
+    def total(self):
+        return self.held[len(self.hops)]
+
+    def drain(self):
+        for hop in range(len(self.hops)):
+            self.copy(hop).wait_send()
+
+
+def small_scratch(hops, shape):
+    return [
+        pltpu.VMEM((hops + 1,) + shape, wide),
+        pltpu.VMEM((hops,) + shape, wide),
+        pltpu.SemaphoreType.DMA((2, hops)),
+    ]
+
+
 def cross_back_kernel(
     seq, count, io, kpos_ref, qpos_ref, up_ref, resid_ref, pair_ref, q_ref, kv_ref, logs_ref,
     q_in_ref, kv_in_ref, out_ref, prefix_ref, kid_ref, qid_ref, first_all, memory_all, context_ref,
@@ -1339,10 +1374,13 @@
 
 def self_back_kernel(
     seq, count, causal, reduce, io, kpos_ref, qpos_ref, up_ref, resid_ref, pair_ref, qkv_ref,
-    logs_ref, in_ref, out_ref, prefix_ref, kid_ref, qid_ref, context_ref, rows_ref, pre_ref,
-    grad_out, pair_grad_ref, result_ref, up_all, grad_ref, own_ref, kept_ref, k_sum, v_sum,
-    up_chunk, *scratch,
+    logs_ref, in_ref, out_ref, prefix_ref, kid_ref, qid_ref, context_ref, rows_ref, *rest,
 ):
+    if reduce:
+        norm_in_ref, pre_in_ref, norm_out_ref, pre_out_ref, *rest = rest
+    else:
+        pre_ref, pair_grad_ref, *rest = rest
+    grad_out, result_ref, up_all, grad_ref, own_ref, kept_ref, k_sum, v_sum, up_chunk, *scratch = rest
     links = Links(seq)
     micros, rows, _ = own_ref.shape
     length = up_all.shape[1]
@@ -1351,7 +1389,12 @@
     scatter = Scatter(links, rows, *scratch[3:8], scratch[8:10])
     terms_ref, rank_sum = result_ref, None
     if reduce:
-        terms_ref, recv_ref, rank_sems = scratch[10:]
+        terms_ref, recv_ref, rank_sems, pre_ref, pair_grad_ref = scratch[10:15]
+        row_hops = [("rows", bit) for bit in bit_list(terms_ref.shape[0])]
+        norm_sum = SmallSum(
+            [("seq", bit) for bit in bit_list(seq)] + row_hops, *scratch[15:18]
+        )
+        pre_sum = SmallSum(row_hops, *scratch[18:21])
         rank_sum = RankSum(terms_ref.shape[0], terms_ref, recv_ref, result_ref, rank_sems)
     ids = (kid_ref, qid_ref, kpos_ref, qpos_ref)
     attention = Attention(
@@ -1384,24 +1427,42 @@
         context_ref, up_all, grad_ref, (rows_ref,) * 3, terms_ref, seq,
         rank_sum.send if reduce else None,
     )
-    run_tasks(tasks, io, fill, 1)
+    def opening():
+        norm_sum.held[0] = norm_in_ref[...]
+        norm_sum.held[0, 0:2] = pair_grad_ref[...]
+        return norm_sum.start(9.0)
+
+    def closing():
+        pre_sum.held[0, 0:2] = pre_ref[...]
+        pre_sum.held[0, 2:6] = pre_in_ref[...]
+        return pre_sum.start(15.0)
+
     if reduce:
+        run_tasks(tasks, io, fill, 1, opening, closing)
         rank_sum.finish()
+        norm_out_ref[...] = norm_sum.total()
+        pre_out_ref[...] = pre_sum.total()
+        norm_sum.drain()
+        pre_sum.drain()
+    else:
+        run_tasks(tasks, io, fill, 1)
 
 
 def self_back_stage(seq, ranks, name_id, count, places, causal, reduce, side):
     micros, rows, width = side[0].shape
     length = rows * seq
     head_width = side[7].shape[2]
-    outs = (
-        jax.ShapeDtypeStruct((2, PAD_PREFIX, head_width), wide),
-        jax.ShapeDtypeStruct((micros, rows, width), wide),
-        jax.ShapeDtypeStruct((2, width), wide),
-        term_shape(seq, ranks, width),
-    )
-    terms = outs[3]
+    terms = term_shape(seq, ranks, width)
+    pre = jax.ShapeDtypeStruct((2, PAD_PREFIX, head_width), wide)
+    outs = (pre, jax.ShapeDtypeStruct((2, width), wide))
+    total = terms
     if reduce:
-        outs = outs[:3] + (jax.ShapeDtypeStruct(terms.shape[1:], wide),)
+        outs = tuple(
+            jax.ShapeDtypeStruct(shape, wide)
+            for shape in (side[12].shape, (6, PAD_PREFIX, head_width))
+        )
+        total = jax.ShapeDtypeStruct(terms.shape[1:], wide)
+    outs += (jax.ShapeDtypeStruct((micros, rows, width), wide), total)
     scratch = (
         [
             pltpu.VMEM((micros, length, width), low),
@@ -1417,7 +1478,12 @@
             pltpu.VMEM(terms.shape, low),
             pltpu.VMEM(terms.shape, low),
             pltpu.SemaphoreType.DMA((2, ranks, 4)),
+            pltpu.VMEM(pre.shape, wide),
+            pltpu.VMEM((2, width), wide),
         ]
+        row_hops, hops = len(bit_list(ranks)), len(bit_list(ranks)) + len(bit_list(seq))
+        scratch += small_scratch(hops, side[12].shape)
+        scratch += small_scratch(row_hops, (6, PAD_PREFIX, head_width))
     lazy = {place: 0 for place in range(5, 12)}
     lazy.update({12: 1, 13: 1})
     return stage_call(
@@ -1525,7 +1591,6 @@
     prefixes = prefixes.reshape(6, count, head_width)
     prefixes = jnp.pad(prefixes, ((0, 0), (0, PAD_PREFIX - count), (0, 0)))
     encoder_pre, decoder_pre, cross_pre = prefixes[0:2], prefixes[2:4], prefixes[4:6]
-    norm_axes = [("seq", seq), ("rows", ranks)]
 
     late = [
         jnp.concatenate(
@@ -1622,7 +1687,7 @@
         return value, [scatter_ranks(term) for term in terms], sums
 
     def keep_pair(index, pair):
-        norm_grads[index] = (pair[0:1], pair[1:2])
+        norm_grads[index] = pair
 
     second_up, terms = ffn_back(
         6, norm_count + 2, cotangent.reshape(stacked, block, width), resid_five, decoder_before,
@@ -1644,16 +1709,14 @@
 
     def self_back(name_id, index, causal, reduce, side, sums):
         held = self_back_stage(seq, ranks, name_id, count, places, causal, reduce, side)
-        held, sums = lax.optimization_barrier((held, sums))
-        pre_grad, out, pair, terms = held
-        keep_pair(index, pair)
-        return out, pre_grad, sums, terms
+        held, sums = lax.optimization_barrier((tuple(held), sums))
+        return held + (sums,)
 
     def owner_parts(value):
         out_part = value[3].reshape(slice_cols, seq, head_width)
         return jnp.swapaxes(out_part, 0, 1), value[:3]
 
-    target_grad, decoder_pre_grad, cross_sums, self_terms = self_back(
+    decoder_pre_grad, pair, target_grad, self_terms, cross_sums = self_back(
         9, norm_count, True, False,
         (
             first_up, resid_three, scales[norm_count], decoder_qkvs, decoder_logs, decoder_in,
@@ -1661,6 +1724,7 @@
         ),
         cross_sums,
     )
+    keep_pair(norm_count, pair)
     memory_up, self_sums, _ = hold(memory_up, [self_terms], [])
     cross_out_grad, cross_in_grad = owner_parts(cross_sums[0])
 
@@ -1677,18 +1741,21 @@
 
     decoder_rows = give_back([decoder_two_grad, cross_out_grad, decoder_out_grad])
 
-    source_grad, encoder_pre_grad, ffn_sums, self_terms = self_back(
+    pairs = [jnp.zeros((2, width), wide)] + [norm_grads[index] for index in sorted(norm_grads)]
+    norm_in = jnp.concatenate(pairs)
+    norm_in = jnp.pad(norm_in, ((0, -norm_in.shape[0] % 16), (0, 0)))
+    norm_total, prefix_total, source_grad, self_terms, ffn_sums = self_back(
         10, 0, False, True,
         (
             middle_up, resid_one, scales[0], encoder_qkvs, encoder_logs, encoder_in,
             encoder_out, encoder_pre, source_keys, source_queries, encoder_ctx, source_all,
+            norm_in, jnp.concatenate([decoder_pre_grad, cross_pre_grad]),
         ),
         ffn_sums,
     )
     encoder_two_grad, encoder_one_grad = ffn_sums
     encoder_out_grad, encoder_in_grad = owner_parts(self_terms)
-    encoder_rows = give_back([encoder_two_grad])
-    encoder_out_rows = give_back([encoder_out_grad.astype(low)])
+    encoder_rows = give_back([encoder_two_grad, encoder_out_grad.astype(low)])
 
     def row_grad(value, start, size, scale=None):
         piece = value[:, :, start : start + size].astype(wide)
@@ -1699,14 +1766,14 @@
     def column_grad(value):
         return jnp.swapaxes(value.astype(wide), -1, -2)
 
-    prefix_total = jnp.concatenate([encoder_pre_grad, decoder_pre_grad, cross_pre_grad])[:, :count]
-    prefix_total = jnp.moveaxis(prefix_total.reshape(6, count, ranks, slice_cols), 2, 0)
-    prefix_total = small_scatter(prefix_total, [("rows", ranks)])
-    norm_rows = [row for index in sorted(norm_grads) for row in norm_grads[index]]
-    which = lax.broadcasted_iota(jnp.int32, (len(norm_rows), width), 0)
-    norm_total = sum(jnp.where(which == k, row, 0.0) for k, row in enumerate(norm_rows))
-    norm_total = jnp.moveaxis(norm_total.reshape(-1, 2, seq * ranks, slice_cols), 2, 0)
-    norm_total = small_scatter(norm_total, norm_axes)
+    row = lax.axis_index("rows")
+    prefix_total = lax.dynamic_slice_in_dim(
+        prefix_total[:, :count], row * slice_cols, slice_cols, 2
+    )
+    norm_total = lax.dynamic_slice_in_dim(
+        norm_total[: 2 * len(pairs)], (me * ranks + row) * slice_cols, slice_cols, 1
+    )
+    norm_total = norm_total.reshape(-1, 2, slice_cols)
 
     shape_out = source.shape
     return (
@@ -1714,7 +1781,7 @@
         source_grad.reshape(shape_out),
         target_grad.reshape(shape_out),
         column_grad(encoder_in_grad),
-        row_grad(encoder_out_rows, 0, head_width),
+        row_grad(encoder_rows, padded, head_width),
         prefix_total[0:2],
         column_grad(encoder_one_grad[:cut]),
         row_grad(encoder_rows, 0, hidden),

time: 782 us -> 753 us (0.963)
  waiting for transfers between devices: 27.8 us -> 3.88 us
  starting transfers between devices: 17.9 us -> 8.24 us
  Pallas kernels: 637 us -> 645 us
    ppermute x7 -> x0, waiting for transfers between devices: 19.7 us -> none  [small_scatter(): lax.ppermute(jnp.where(flip, lower, upper), name, swap_pairs(count, bit))]
  transfers between devices with their start and end apart: 21 -> 13, of which waited for: 7 -> 1; matrix products, arithmetic and copies ran while one was open for 8% -> 7% of each run, Pallas kernels for 58% -> 61%
where the time goes in v6:
time: 753 us; the launch traced here: 748 us
  Pallas kernels  645 us (86%)
  local copies, waits for them, and re-layouts  50.7 us (7%)
  other arithmetic  24.7 us (3%)
  between operations  15.4 us (2%)
  starting transfers between devices  8.24 us (1%)
    pallas_call x10, Pallas kernels, stage_call(): pl.pallas_call(body, out_shape=tuple(outs), in_specs=[far if place in laz...  645 us
  transfers between devices with their start and end apart: 13, of which 1 were waited for; matrix products, arithmetic and copies ran while one was open for 7% of the time, Pallas kernels for 61%

profile of v6, /device:TPU:0, one launch (start us, length us, event | category | flops | bytes accessed | tf_op | source)
XLA Modules:
  0.0 747.7 jit_solution(2396432349243315887)
XLA Ops:
  7.3 1.9 pad_maximum_fusion.3
  13.9 60.4 %shard_map.416 = (bf16[2,1024,1024]{2,1,0:T(8,128)(2,1)}, bf16[2,1024,1024]{2,1,0:T(8,128)(2,1)}, bf16[4,8,32,256]{3,2,1,0:T(8,128)(2,1)}, bf16[8,32,1408]{2,1,0...) custom-call(bf16[2,128,1024]{2,1,0:T(8,128)(2,1)} %bitcast.318, ...), custom_call_target="tpu_custom_call" | custom-call | flops 137500000256 | bytes 16777216 | tf_op jit(solution)/shard_map/pallas_call | solution.py:556
  74.4 1.8 slice.183
  76.2 1.7 slice.184
  84.0 1.3 copy.288.refs_7_.refs_9_.refs_12_.refs_10_
  87.6 1.3 copy.289.refs_15_.refs_10_
  90.2 1.5 fusion.5
  93.6 71.9 %shard_map.417 = (bf16[2,1024,384]{2,1,0:T(8,128)(2,1)}, bf16[2,1024,128]{2,1,0:T(8,128)(2,1)}, f32[2,2,1024]{2,1,0:T(2,128)}, f32[2,128,1024]{2,1,0:T(8,128)}, ...) custom-call(s32[1024,1]{1,0:T(8,128)} %copy.292.refs_0_, ...), custom_call_target="tpu_custom_call" | custom-call | flops 187500003328 | bytes 16777216 | tf_op jit(solution)/shard_map/pallas_call | solution.py:556
  168.7 1.3 slice.195
  171.3 1.2 slice.243.refs_3_.refs_5_
  172.6 1.4 maximum_maximum_fusion.refs_2_.refs_4_
  173.9 52.8 %shard_map.418 = (bf16[2,1024,1024]{2,1,0:T(8,128)(2,1)}, f32[2,1024,640]{2,1,0:T(8,128)}, bf16[2,1024,640]{2,1,0:T(8,128)(2,1)}, f32[2,128,1024]{2,1,0:T(8,128)...) custom-call(bf16[2,128,1024]{2,1,0:T(8,128)(2,1)} %get-tuple-element.134.refs_0_, ...), custom_call_target="tpu_custom_call" | custom-call | flops 149999992832 | bytes 16777216 | tf_op jit(solution)/shard_map/pallas_call | solution.py:556
  226.7 1.2 slice.199
  228.7 1.7 slice.247.refs_7_.refs_10_
  232.3 1.3 slice.207
  233.6 1.2 copy.294
  234.8 1.3 maximum_maximum_fusion.1.refs_2_.refs_4_
  236.2 81.8 %shard_map.419 = (bf16[2,1024,1024]{2,1,0:T(8,128)(2,1)}, bf16[2,1024,1024]{2,1,0:T(8,128)(2,1)}, bf16[2,1024,128]{2,1,0:T(8,128)(2,1)}, bf16[2,1024,256]{2,1,0:...) custom-call(s32[1024,1]{1,0:T(8,128)} %copy.292.refs_0_, ...), custom_call_target="tpu_custom_call" | custom-call | flops 212500004864 | bytes 16777216 | tf_op jit(solution)/shard_map/pallas_call | solution.py:556
  318.0 52.0 %shard_map.420 = (bf16[2,1024,1024]{2,1,0:T(8,128)(2,1)}, f32[2,1024,640]{2,1,0:T(8,128)}, bf16[2,1024,640]{2,1,0:T(8,128)(2,1)}, f32[2,128,1024]{2,1,0:T(8,128)...) custom-call(bf16[2,128,1024]{2,1,0:T(8,128)(2,1)} %get-tuple-element.142.refs_0_, ...), custom_call_target="tpu_custom_call" | custom-call | flops 149999992832 | bytes 16777216 | tf_op jit(solution)/shard_map/pallas_call | solution.py:556
  370.0 51.2 %shard_map.421 = (f32[2,128,1024]{2,1,0:T(8,128)}, f32[2,1024]{1,0:T(2,128)}, bf16[4,128,1024]{2,1,0:T(8,128)(2,1)}, bf16[4,16,1024]{2,1,0:T(8,128)(2,1)}, bf16[4,8,32,640]{3,2,1,0:T(8,128)(2,1)}) custom-call(bf16[2,128,1024]{2,1,0:T(8,128)(2,1)} %bitcast.322, f32[2,128,1024]{2,1,0:T(8,128)} %get-tuple-element.147.refs_1_, ...), custom_call_target="tpu_custom_call" | custom-call | flops 162500001792 | bytes 16777216 | tf_op jit(solution)/shard_map/pallas_call | solution.py:556
  421.2 2.4 pad_maximum_fusion
  424.4 77.5 %shard_map.422 = (f32[2,32,128]{2,1,0:T(8,128)}, f32[2,128,1024]{2,1,0:T(8,128)}, f32[2,128,1024]{2,1,0:T(8,128)}, f32[2,1024]{1,0:T(2,128)}, bf16[4,4,32,1024]{3,2,1,0:T(8,128)(2,1)}) custom-call(s32[1024,1]{1,0:T(8,128)} %copy.292.refs_0_, s32[1,1024]{1,0:T(1,128)} %bitcast.304, f32[2,128,1024]{2,1,0:T(8,128)} %get-tuple-element.155.refs_2_, ...), custom_call_target="tpu_custom_call" | custom-call | flops 212500004864 | bytes 16777216 | tf_op jit(solution)/shard_map/pallas_call | solution.py:556
  502.1 62.1 %shard_map.423 = (f32[2,32,128]{2,1,0:T(8,128)}, f32[2,1024]{1,0:T(2,128)}, f32[2,128,1024]{2,1,0:T(8,128)}, bf16[4,4,32,1024]{3,2,1,0:T(8,128)(2,1)}) custom-call(s32[1024,1]{1,0:T(8,128)} %copy.292.refs_0_, s32[1,1024]{1,0:T(1,128)} %bitcast.305, f32[2,128,1024]{2,1,0:T(8,128)} %get-tuple-element.168.refs_2_, f32[2,128,1024]{2,1,0:T(8,128)} %get-tuple-element.169.refs_3_, ...), custom_call_target="tpu_custom_call" | custom-call | flops 187500003328 | bytes 16777216 | tf_op jit(solution)/shard_map/pallas_call | solution.py:556
  564.3 51.4 %shard_map.424 = (f32[2,128,1024]{2,1,0:T(8,128)}, f32[2,1024]{1,0:T(2,128)}, bf16[4,128,1024]{2,1,0:T(8,128)(2,1)}, bf16[4,16,1024]{2,1,0:T(8,128)(2,1)}, bf16[4,8,32,640]{3,2,1,0:T(8,128)(2,1)}) custom-call(f32[2,128,1024]{2,1,0:T(8,128)} %get-tuple-element.179.refs_0_, f32[2,128,1024]{2,1,0:T(8,128)} %get-tuple-element.180.refs_1_, ...), custom_call_target="tpu_custom_call" | custom-call | flops 162500001792 | bytes 16777216 | tf_op jit(solution)/shard_map/pallas_call | solution.py:556
  615.7 2.4 pad_maximum_fusion.1
  624.5 4.1 all-to-all-start.1
  629.4 83.6 %shard_map.425 = (f32[16,1024]{1,0:T(8,128)}, f32[6,32,128]{2,1,0:T(8,128)}, f32[2,128,1024]{2,1,0:T(8,128)}, f32[4,32,1024]{2,1,0:T(8,128)}) custom-call(s32[1024,1]{1,0:T(8,128)} %copy.292.refs_0_, s32[1,1024]{1,0:T(1,128)} %bitcast.306, f32[2,128,1024]{2,1,0:T(8,128)} %get-tuple-element.189.refs_2_, f32[2,128,1024]{2,1,0:T(8,128)} %get-tuple-element.190.refs_3_, ...), custom_call_target="tpu_custom_call" | custom-call | flops 187500003328 | bytes 16777216 | tf_op jit(solution)/shard_map/pallas_call | solution.py:556
  720.6 1.4 convert_bitcast_fusion.11
  722.1 1.8 maximum_bitcast_fusion.1
  723.8 3.5 all-to-all-start
  731.6 1.3 constant_dynamic-slice_fusion
  733.7 1.8 all-to-all-done
  (249 shorter events, 48.5 us)
Async XLA Ops:
  7.2 4.2 copy-start
  7.3 4.2 copy-start.25
  7.3 4.9 copy-start.16
  7.3 4.9 copy-start.17
  7.3 82.9 %all-gather.11.cloned.1.call-start = ((), (), s32[]{:S(2)}) async-start(), calls=%async_computation.14 | async-start | bytes 1966080 | tf_op jit(solution)/shard_map/all_gather | solution.py:1533
  9.3 156.2 %all-gather.15.cloned.1.call-start = ((), (), s32[]{:S(2)}) async-start(), calls=%async_computation.16 | async-start | bytes 1966080 | tf_op jit(solution)/shard_map/all_gather | solution.py:1533
  74.4 4.7 copy-start.19
  74.4 4.6 copy-start.26
  74.4 4.6 copy-start.28
  79.9 85.6 %all-gather.13.cloned.1.call-start = ((), (), s32[]{:S(2)}) async-start(), calls=%async_computation.15 | async-start | bytes 2457600 | tf_op jit(solution)/shard_map/all_gather | solution.py:1533
  80.6 150.6 %all-gather.17.cloned.1.call-start = ((), (), s32[]{:S(2)}) async-start(), calls=%async_computation.17 | async-start | bytes 1474560 | tf_op jit(solution)/shard_map/all_gather | solution.py:1533
  81.9 4.1 copy-start.20
  82.8 4.6 copy-start.39
  93.6 72.0 %copy-start.23 = (f32[2,32,32]{2,1,0:T(8,128)S(1)}, f32[2,32,32]{2,1,0:T(8,128)}, u32[]{:S(2)}) copy-start(f32[2,32,32]{2,1,0:T(8,128)} %get-tuple-element.342) | copy-start | bytes 24580
  93.6 72.7 %copy-start.22 = (f32[2,32,32]{2,1,0:T(8,128)S(1)}, f32[2,32,32]{2,1,0:T(8,128)}, u32[]{:S(2)}) copy-start(f32[2,32,32]{2,1,0:T(8,128)} %get-tuple-element.341) | copy-start | bytes 24580
  93.6 73.4 %copy-start.21 = (f32[2,32,32]{2,1,0:T(8,128)S(1)}, f32[2,32,32]{2,1,0:T(8,128)}, u32[]{:S(2)}) copy-start(f32[2,32,32]{2,1,0:T(8,128)} %get-tuple-element.340) | copy-start | bytes 24580
  165.5 4.5 copy-start.3
  165.6 65.7 %all-gather.19.cloned.1.call-start = ((), (), s32[]{:S(2)}) async-start(), calls=%async_computation.18 | async-start | bytes 1638400 | tf_op jit(solution)/shard_map/all_gather | solution.py:1533
  167.8 4.8 copy-start.32
  172.5 329.5 %reduce-scatter.9.cloned.1.call-start = ((), (), s32[]{:S(2)}) async-start(), calls=%async_computation.9 | async-start | bytes 1474560 | tf_op jit(solution)/shard_map/reduce_scatter | solution.py:1673
  423.6 78.4 %reduce-scatter.7.cloned.1.call-start = ((), (), s32[]{:S(2)}) async-start(), calls=%async_computation.8 | async-start | bytes 1638400 | tf_op jit(solution)/shard_map/reduce_scatter | solution.py:1673
  424.4 139.8 %reduce-scatter.11.cloned.1.call-start = ((), (), s32[]{:S(2)}) async-start(), calls=%async_computation.10 | async-start | bytes 1310720 | tf_op jit(solution)/shard_map/reduce_scatter | solution.py:1673
  502.1 116.1 %reduce-scatter.13.cloned.1.call-start = ((), (), s32[]{:S(2)}) async-start(), calls=%async_computation.11 | async-start | bytes 1310720 | tf_op jit(solution)/shard_map/reduce_scatter | solution.py:1673
  564.3 155.3 %reduce-scatter.17.cloned.1.call-start = ((), (), s32[]{:S(2)}) async-start(), calls=%async_computation.13 | async-start | bytes 1474560 | tf_op jit(solution)/shard_map/reduce_scatter | solution.py:1673
  618.3 5.3 copy-start.10
  624.5 89.3 %all-to-all-start.1 = ((bf16[8,32,1,896]{3,1,2,0:T(8,128)(2,1)}), bf16[8,32,1,896]{3,1,2,0:T(8,128)(2,1)}, u32[]{:S(2)}, u32[]{:S(2)}) async-start(bf16[8,32,1,896]{3,1,2,0:T(8,128)(2,1)} %maximum_bitcast_fusion), calls=%async_computation.7 | async-start | bytes 917504 | tf_op jit(solution)/shard_map/all_to_all | solution.py:1740
  628.6 91.0 %reduce-scatter.15.cloned.1.call-start = ((), (), s32[]{:S(2)}) async-start(), calls=%async_computation.12 | async-start | bytes 1638400 | tf_op jit(solution)/shard_map/reduce_scatter | solution.py:1673
  629.4 83.6 %copy-start.15 = (bf16[1,4,32,1024]{3,2,1,0:T(8,128)(2,1)S(1)}, bf16[1,4,32,1024]{3,2,1,0:T(8,128)(2,1)}, u32[]{:S(2)}) copy-start(bf16[1,4,32,1024]{3,2,1,0:T(8,128)(2,1)} %reduce-scatter.13.cloned.1.call-done) | copy-start | bytes 786436
  716.0 6.0 copy-start.9
  718.9 8.4 %copy-start.24 = (f32[6,32,128]{2,1,0:T(8,128)S(1)}, f32[6,32,128]{2,1,0:T(8,128)}, u32[]{:S(2)}) copy-start(f32[6,32,128]{2,1,0:T(8,128)} %get-tuple-element.210) | copy-start | bytes 294916
  723.8 11.7 %all-to-all-start = ((bf16[8,32,1,768]{3,1,2,0:T(8,128)(2,1)}), bf16[8,32,1,768]{3,1,2,0:T(8,128)(2,1)S(1)}, u32[]{:S(2)}, u32[]{:S(2)}) async-start(bf16[8,32,1,768]{3,1,2,0:T(8,128)(2,1)} %maximum_bitcast_fusion.1), calls=%async_computation.6 | async-start | bytes 786432 | tf_op jit(solution)/shard_map/all_to_all | solution.py:1740
  733.0 5.0 copy-start.7
  (27 other events, 75.3 us)
Sparse Core Ops, SparseCore 0:
  10.3 43.7 all-gather.10
  80.0 35.6 all-gather.14
  117.8 42.4 all-gather.12
  165.7 28.1 all-gather.16
  195.9 31.7 all-gather.18
  423.8 27.2 reduce-scatter.8
  453.3 29.9 reduce-scatter.6
  502.2 25.3 reduce-scatter.10
  564.4 25.3 reduce-scatter.12
  618.4 27.3 reduce-scatter.16
  648.1 31.3 reduce-scatter.14

commit v7 on v6

--- a/solution.py
+++ b/solution.py
@@ -441,9 +441,9 @@
             self.take(entry)
 
 
-def run_tasks(tasks, io, fill=(), fill_load=None, opening=None, closing=None):
+def run_tasks(tasks, io, fill=(), fill_load=None, opening=None, closing=None, ahead=2):
     waits = Waits()
-    for task in tasks[:2]:
+    for task in tasks[:ahead]:
         task.begin()
         waits.add(task.arrive)
     if opening is not None and len(tasks) <= 2:
@@ -456,9 +456,9 @@
             waits.run(step, cost)
         io.store(task.store)
         waits.add(task.leave)
-        if index + 2 < len(tasks):
-            tasks[index + 2].begin()
-            waits.add(tasks[index + 2].arrive)
+        if index + ahead < len(tasks):
+            tasks[index + ahead].begin()
+            waits.add(tasks[index + ahead].arrive)
     if opening is not None and len(tasks) > 2:
         waits.add(opening())
     if closing is not None:
@@ -718,16 +718,13 @@
 
 
 def opening_kernel(
-    seq, ranks, io, source_ref, target_ref, out_ref, ffn_ref, small_ref, source_all, target_all,
-    out_all, ffn_all, small_all, norm_all, *scratch,
+    seq, ranks, io, source_ref, out_ref, ffn_ref, small_ref, source_all, out_all, ffn_all,
+    small_all, norm_all, *scratch,
 ):
     links = Links(seq)
     me, row = lax.axis_index("seq"), lax.axis_index("rows")
-    gathers = [
-        Gather(links, source_ref, source_all, *scratch[0:3]),
-        Gather(links, target_ref, target_all, *scratch[3:6]),
-    ]
-    out_sems, ffn_sems, norm_sems, out_row_sems, small_row_sems, local_sems = scratch[6:]
+    gathers = [Gather(links, source_ref, source_all, *scratch[0:3])]
+    out_sems, ffn_sems, norm_sems, out_row_sems, small_row_sems, local_sems = scratch[3:]
     masks = range(1, seq)
     row_bits = bit_list(ranks)
     norm_rows = norm_all.shape[2]
@@ -872,18 +869,17 @@
 
 
 def opening_stage(seq, ranks, name_id, norm_rows, args):
-    source, _, out_pieces, ffn_pieces, small = args
+    source, out_pieces, ffn_pieces, small = args
     micros, rows, width = source.shape
     whole = jax.ShapeDtypeStruct((micros, seq * rows, width), low)
     outs = (
-        whole,
         whole,
         jax.ShapeDtypeStruct((ranks,) + out_pieces.shape, low),
         jax.ShapeDtypeStruct(ffn_pieces.shape, low),
         jax.ShapeDtypeStruct((ranks,) + small.shape, low),
         jax.ShapeDtypeStruct((seq, ranks, norm_rows, small.shape[1]), low),
     )
-    scratch = gather_scratch(seq, micros) * 2 + [
+    scratch = gather_scratch(seq, micros) + [
         pltpu.SemaphoreType.DMA((2, seq)),
         pltpu.SemaphoreType.DMA((2, seq)),
         pltpu.SemaphoreType.DMA((2, seq)),
@@ -892,7 +888,7 @@
         pltpu.SemaphoreType.DMA((3,)),
     ]
     return stage_call(
-        functools.partial(opening_kernel, seq, ranks), name_id, outs, scratch, args, 55
+        functools.partial(opening_kernel, seq, ranks), name_id, outs, scratch, args, 40
     )
 
 
@@ -983,19 +979,22 @@
 
 def self_kernel(seq, count, io, *refs):
     kinds = 2
-    scratch = refs[-kinds * 7 :]
-    refs = refs[: -kinds * 7]
+    scratch = refs[-kinds * 7 - 3 :]
+    refs = refs[: -kinds * 7 - 3]
+    target_all = refs[-1]
     places = refs[:2]
     links = Links(seq)
     links.enter()
     tasks = []
     for kind in range(kinds):
-        (all_ref, own_ref, in_ref, out_ref, prefix_ref, kid_ref, qid_ref, pair_ref) = refs[
-            2 + 8 * kind : 10 + 8 * kind
+        own_ref, in_ref, out_ref, prefix_ref, kid_ref, qid_ref, pair_ref = refs[
+            3 + 7 * kind : 10 + 7 * kind
         ]
         (qkv_ref, context_ref, logs_ref, sum_ref, norm_ref, low_ref) = refs[
-            2 + 8 * kinds + 6 * kind : 8 + 8 * kinds + 6 * kind
+            3 + 7 * kinds + 6 * kind : 9 + 7 * kinds + 6 * kind
         ]
+        all_ref = target_all if kind else refs[2]
+        gathers = [Gather(links, own_ref, all_ref, *scratch[-3:])] if kind else []
         micros, rows, _ = own_ref.shape
         length = all_ref.shape[1]
         head_width = prefix_ref.shape[2]
@@ -1031,15 +1030,15 @@
         for micro in range(micros):
             load = kind if micro == 0 else None
             tasks.append(
-                make_task(micro, [], [scatter], compute, finish, None, load, (kind, micro))
+                make_task(micro, gathers, [scatter], compute, finish, None, load, (kind, micro))
             )
-    run_tasks(tasks, io)
-
-
-def self_stage(seq, name_id, count, places, sides):
-    micros, rows, width = sides[0][1].shape
+    run_tasks(tasks, io, ahead=len(tasks))
+
+
+def self_stage(seq, name_id, count, places, source_all, sides):
+    micros, rows, width = sides[0][0].shape
     length = rows * seq
-    head_width = sides[0][4].shape[2]
+    head_width = sides[0][3].shape[2]
     heads = head_width // HEAD_DIM
     side_outs = (
         jax.ShapeDtypeStruct((micros, length, 3 * head_width), low),
@@ -1049,13 +1048,15 @@
         jax.ShapeDtypeStruct((micros, rows, width), wide),
         jax.ShapeDtypeStruct((micros, rows, width), low),
     )
-    scratch = scatter_scratch(seq, micros, rows, width) * 2
-    args = tuple(places) + sides[0] + sides[1]
+    scratch = scatter_scratch(seq, micros, rows, width) * 2 + gather_scratch(seq, micros)
+    args = tuple(places) + (source_all,) + sides[0] + sides[1]
+    gathered = jax.ShapeDtypeStruct((micros, length, width), low)
     outs = stage_call(
-        functools.partial(self_kernel, seq, count), name_id, side_outs * 2, scratch, args, 75,
-        {10: 1, 11: 1, 12: 1, 13: 1, 15: 1}, {0: 0, 1: 0, 6: 1, 7: 1},
-    )
-    return outs[:6], outs[6:]
+        functools.partial(self_kernel, seq, count), name_id, side_outs * 2 + (gathered,), scratch,
+        args, 75,
+        {11: 1, 12: 1, 14: 1}, {0: 0, 1: 0, 6: 1, 7: 1, 12: 1},
+    )
+    return outs[:6], outs[6:12], outs[12]
 
 
 def cross_kernel(
@@ -1438,7 +1439,8 @@
         return pre_sum.start(15.0)
 
     if reduce:
-        run_tasks(tasks, io, fill, 1, opening, closing)
+        tasks[-1].compute = [(lambda: io.load(1), 0.1), fill[0]] + tasks[-1].compute
+        run_tasks(tasks, io, fill[1:], None, opening, closing)
         rank_sum.finish()
         norm_out_ref[...] = norm_sum.total()
         pre_out_ref[...] = pre_sum.total()
@@ -1581,8 +1583,8 @@
         [jnp.pad(norms, ((0, norm_rows - norms.shape[0]), (0, 0))), prefixes]
     )
     small = jnp.pad(small, ((0, -small.shape[0] % 16), (0, 0)))
-    source_all, target_all, front, row_pieces, small_all, norm_all = opening_stage(
-        seq, ranks, 1, norm_rows, (sources, targets, out_pieces, ffn_pieces, small)
+    source_all, front, row_pieces, small_all, norm_all = opening_stage(
+        seq, ranks, 1, norm_rows, (sources, out_pieces, ffn_pieces, small)
     )
     scales = norm_all[:, :, : norms.shape[0]].reshape(seq * ranks, -1, slice_cols)
     scales = jnp.moveaxis(scales, 0, 1).reshape(-1, 2, width).astype(wide)
@@ -1624,16 +1626,16 @@
 
     second_parts = gather_rows(late[0])
     rest = gather_rows(late[1])
-    encoder_side, decoder_side = self_stage(
-        seq, 2, count, places,
+    encoder_side, decoder_side, target_all = self_stage(
+        seq, 2, count, places, source_all,
         (
             (
-                source_all, sources, encoder_in, encoder_out, encoder_pre, source_keys,
-                source_queries, scales[0],
+                sources, encoder_in, encoder_out, encoder_pre, source_keys, source_queries,
+                scales[0],
             ),
             (
-                target_all, targets, decoder_in, decoder_out, decoder_pre, target_keys,
-                target_queries, scales[norm_count],
+                targets, decoder_in, decoder_out, decoder_pre, target_keys, target_queries,
+                scales[norm_count],
             ),
         ),
     )

time: 753 us -> 747 us (level)
  no operation moved by 1% of the time
where the time goes in v7:
time: 747 us; the launch traced here: 742 us
  Pallas kernels  639 us (86%)
  local copies, waits for them, and re-layouts  50.7 us (7%)
  other arithmetic  24.7 us (3%)
  between operations  15.4 us (2%)
  starting transfers between devices  8.23 us (1%)
    pallas_call x10, Pallas kernels, stage_call(): pl.pallas_call(body, out_shape=tuple(outs), in_specs=[far if place in laz...  639 us
  transfers between devices with their start and end apart: 13, of which 1 were waited for; matrix products, arithmetic and copies ran while one was open for 7% of the time, Pallas kernels for 61%

profile of v7, /device:TPU:0, one launch (start us, length us, event | category | flops | bytes accessed | tf_op | source)
XLA Modules:
  0.0 742.5 jit_solution(3291904305182507253)
XLA Ops:
  7.3 1.9 pad_maximum_fusion.3
  13.9 55.4 %shard_map.416 = (bf16[2,1024,1024]{2,1,0:T(8,128)(2,1)}, bf16[4,8,32,256]{3,2,1,0:T(8,128)(2,1)}, bf16[8,32,1408]{2,1,0:T(8,128)(2,1)}, bf16[4,208,32]{2,1,0:T(8,128)(2,1)}, bf16[8,4,16,32]{3,2,1,0:T(8,128)(2,1)}) custom-call(bf16[2,128,1024]{2,1,0:T(8,128)(2,1)} %bitcast.318, bf16[8,32,256]{2,1,0:T(8,128)(2,1)} %maximum_bitcast_fusion.2.refs_1_, ...), custom_call_target="tpu_custom_call" | custom-call | flops 99999997952 | bytes 16777216 | tf_op jit(solution)/shard_map/pallas_call | solution.py:556
  69.4 1.8 slice.183
  71.3 1.7 slice.184
  79.1 1.3 copy.288.refs_7_.refs_9_.refs_12_.refs_10_
  82.6 1.3 copy.289.refs_14_.refs_10_
  85.2 1.5 fusion.5
  88.6 74.6 %shard_map.417 = (bf16[2,1024,384]{2,1,0:T(8,128)(2,1)}, bf16[2,1024,128]{2,1,0:T(8,128)(2,1)}, f32[2,2,1024]{2,1,0:T(2,128)}, f32[2,128,1024]{2,1,0:T(8,128)}, ...) custom-call(s32[1024,1]{1,0:T(8,128)} %copy.292.refs_0_, ...), custom_call_target="tpu_custom_call" | custom-call | flops 187500003328 | bytes 16777216 | tf_op jit(solution)/shard_map/pallas_call | solution.py:556
  166.4 1.3 slice.195
  169.0 1.2 slice.243.refs_3_.refs_5_
  170.3 1.4 maximum_maximum_fusion.refs_2_.refs_4_
  171.6 52.7 %shard_map.418 = (bf16[2,1024,1024]{2,1,0:T(8,128)(2,1)}, f32[2,1024,640]{2,1,0:T(8,128)}, bf16[2,1024,640]{2,1,0:T(8,128)(2,1)}, f32[2,128,1024]{2,1,0:T(8,128)...) custom-call(bf16[2,128,1024]{2,1,0:T(8,128)(2,1)} %get-tuple-element.133.refs_0_, ...), custom_call_target="tpu_custom_call" | custom-call | flops 149999992832 | bytes 16777216 | tf_op jit(solution)/shard_map/pallas_call | solution.py:556
  224.3 1.2 slice.199
  226.3 1.7 slice.247.refs_7_.refs_10_
  229.8 1.3 slice.207
  231.1 1.2 copy.294
  232.4 1.3 maximum_maximum_fusion.1.refs_2_.refs_4_
  233.7 82.0 %shard_map.419 = (bf16[2,1024,1024]{2,1,0:T(8,128)(2,1)}, bf16[2,1024,1024]{2,1,0:T(8,128)(2,1)}, bf16[2,1024,128]{2,1,0:T(8,128)(2,1)}, bf16[2,1024,256]{2,1,0:...) custom-call(s32[1024,1]{1,0:T(8,128)} %copy.292.refs_0_, ...), custom_call_target="tpu_custom_call" | custom-call | flops 212500004864 | bytes 16777216 | tf_op jit(solution)/shard_map/pallas_call | solution.py:556
  315.7 52.4 %shard_map.420 = (bf16[2,1024,1024]{2,1,0:T(8,128)(2,1)}, f32[2,1024,640]{2,1,0:T(8,128)}, bf16[2,1024,640]{2,1,0:T(8,128)(2,1)}, f32[2,128,1024]{2,1,0:T(8,128)...) custom-call(bf16[2,128,1024]{2,1,0:T(8,128)(2,1)} %get-tuple-element.141.refs_0_, ...), custom_call_target="tpu_custom_call" | custom-call | flops 149999992832 | bytes 16777216 | tf_op jit(solution)/shard_map/pallas_call | solution.py:556
  368.2 51.3 %shard_map.421 = (f32[2,128,1024]{2,1,0:T(8,128)}, f32[2,1024]{1,0:T(2,128)}, bf16[4,128,1024]{2,1,0:T(8,128)(2,1)}, bf16[4,16,1024]{2,1,0:T(8,128)(2,1)}, bf16[4,8,32,640]{3,2,1,0:T(8,128)(2,1)}) custom-call(bf16[2,128,1024]{2,1,0:T(8,128)(2,1)} %bitcast.321, f32[2,128,1024]{2,1,0:T(8,128)} %get-tuple-element.146.refs_1_, ...), custom_call_target="tpu_custom_call" | custom-call | flops 162500001792 | bytes 16777216 | tf_op jit(solution)/shard_map/pallas_call | solution.py:556
  419.5 2.4 pad_maximum_fusion
  422.7 77.7 %shard_map.422 = (f32[2,32,128]{2,1,0:T(8,128)}, f32[2,128,1024]{2,1,0:T(8,128)}, f32[2,128,1024]{2,1,0:T(8,128)}, f32[2,1024]{1,0:T(2,128)}, bf16[4,4,32,1024]{3,2,1,0:T(8,128)(2,1)}) custom-call(s32[1024,1]{1,0:T(8,128)} %copy.292.refs_0_, s32[1,1024]{1,0:T(1,128)} %bitcast.304, f32[2,128,1024]{2,1,0:T(8,128)} %get-tuple-element.154.refs_2_, ...), custom_call_target="tpu_custom_call" | custom-call | flops 212500004864 | bytes 16777216 | tf_op jit(solution)/shard_map/pallas_call | solution.py:556
  500.6 62.1 %shard_map.423 = (f32[2,32,128]{2,1,0:T(8,128)}, f32[2,1024]{1,0:T(2,128)}, f32[2,128,1024]{2,1,0:T(8,128)}, bf16[4,4,32,1024]{3,2,1,0:T(8,128)(2,1)}) custom-call(s32[1024,1]{1,0:T(8,128)} %copy.292.refs_0_, s32[1,1024]{1,0:T(1,128)} %bitcast.305, f32[2,128,1024]{2,1,0:T(8,128)} %get-tuple-element.167.refs_2_, f32[2,128,1024]{2,1,0:T(8,128)} %get-tuple-element.168.refs_3_, ...), custom_call_target="tpu_custom_call" | custom-call | flops 187500003328 | bytes 16777216 | tf_op jit(solution)/shard_map/pallas_call | solution.py:556
  562.8 51.4 %shard_map.424 = (f32[2,128,1024]{2,1,0:T(8,128)}, f32[2,1024]{1,0:T(2,128)}, bf16[4,128,1024]{2,1,0:T(8,128)(2,1)}, bf16[4,16,1024]{2,1,0:T(8,128)(2,1)}, bf16[4,8,32,640]{3,2,1,0:T(8,128)(2,1)}) custom-call(f32[2,128,1024]{2,1,0:T(8,128)} %get-tuple-element.179.refs_0_, f32[2,128,1024]{2,1,0:T(8,128)} %get-tuple-element.180.refs_1_, ...), custom_call_target="tpu_custom_call" | custom-call | flops 162500001792 | bytes 16777216 | tf_op jit(solution)/shard_map/pallas_call | solution.py:556
  614.2 2.4 pad_maximum_fusion.1
  622.9 4.1 all-to-all-start.1
  627.8 79.7 %shard_map.425 = (f32[16,1024]{1,0:T(8,128)}, f32[6,32,128]{2,1,0:T(8,128)}, f32[2,128,1024]{2,1,0:T(8,128)}, f32[4,32,1024]{2,1,0:T(8,128)}) custom-call(s32[1024,1]{1,0:T(8,128)} %copy.292.refs_0_, s32[1,1024]{1,0:T(1,128)} %bitcast.306, f32[2,128,1024]{2,1,0:T(8,128)} %get-tuple-element.189.refs_2_, f32[2,128,1024]{2,1,0:T(8,128)} %get-tuple-element.190.refs_3_, ...), custom_call_target="tpu_custom_call" | custom-call | flops 187500003328 | bytes 16777216 | tf_op jit(solution)/shard_map/pallas_call | solution.py:556
  715.1 1.4 convert_bitcast_fusion.11
  716.6 1.8 maximum_bitcast_fusion.1
  718.4 3.7 all-to-all-start
  726.4 1.3 constant_dynamic-slice_fusion
  728.5 1.9 all-to-all-done
  (249 shorter events, 48.5 us)
Async XLA Ops:
  7.2 4.2 copy-start
  7.3 4.2 copy-start.25
  7.3 4.9 copy-start.16
  7.3 4.9 copy-start.17
  7.3 77.9 %all-gather.11.cloned.1.call-start = ((), (), s32[]{:S(2)}) async-start(), calls=%async_computation.14 | async-start | bytes 1966080 | tf_op jit(solution)/shard_map/all_gather | solution.py:1535
  9.3 153.9 %all-gather.15.cloned.1.call-start = ((), (), s32[]{:S(2)}) async-start(), calls=%async_computation.16 | async-start | bytes 1966080 | tf_op jit(solution)/shard_map/all_gather | solution.py:1535
  69.4 4.7 copy-start.19
  69.4 4.6 copy-start.26
  69.4 4.6 copy-start.28
  74.9 88.3 %all-gather.13.cloned.1.call-start = ((), (), s32[]{:S(2)}) async-start(), calls=%async_computation.15 | async-start | bytes 2457600 | tf_op jit(solution)/shard_map/all_gather | solution.py:1535
  75.7 153.1 %all-gather.17.cloned.1.call-start = ((), (), s32[]{:S(2)}) async-start(), calls=%async_computation.17 | async-start | bytes 1474560 | tf_op jit(solution)/shard_map/all_gather | solution.py:1535
  76.9 4.1 copy-start.20
  77.9 4.6 copy-start.39
  88.6 74.7 %copy-start.23 = (f32[2,32,32]{2,1,0:T(8,128)S(1)}, f32[2,32,32]{2,1,0:T(8,128)}, u32[]{:S(2)}) copy-start(f32[2,32,32]{2,1,0:T(8,128)} %get-tuple-element.342) | copy-start | bytes 24580
  88.6 75.4 %copy-start.22 = (f32[2,32,32]{2,1,0:T(8,128)S(1)}, f32[2,32,32]{2,1,0:T(8,128)}, u32[]{:S(2)}) copy-start(f32[2,32,32]{2,1,0:T(8,128)} %get-tuple-element.341) | copy-start | bytes 24580
  88.6 76.1 %copy-start.21 = (f32[2,32,32]{2,1,0:T(8,128)S(1)}, f32[2,32,32]{2,1,0:T(8,128)}, u32[]{:S(2)}) copy-start(f32[2,32,32]{2,1,0:T(8,128)} %get-tuple-element.340) | copy-start | bytes 24580
  163.2 4.5 copy-start.3
  163.3 65.5 %all-gather.19.cloned.1.call-start = ((), (), s32[]{:S(2)}) async-start(), calls=%async_computation.18 | async-start | bytes 1638400 | tf_op jit(solution)/shard_map/all_gather | solution.py:1535
  165.5 4.8 copy-start.32
  170.2 330.3 %reduce-scatter.9.cloned.1.call-start = ((), (), s32[]{:S(2)}) async-start(), calls=%async_computation.9 | async-start | bytes 1474560 | tf_op jit(solution)/shard_map/reduce_scatter | solution.py:1675
  421.9 78.6 %reduce-scatter.7.cloned.1.call-start = ((), (), s32[]{:S(2)}) async-start(), calls=%async_computation.8 | async-start | bytes 1638400 | tf_op jit(solution)/shard_map/reduce_scatter | solution.py:1675
  422.7 140.0 %reduce-scatter.11.cloned.1.call-start = ((), (), s32[]{:S(2)}) async-start(), calls=%async_computation.10 | async-start | bytes 1310720 | tf_op jit(solution)/shard_map/reduce_scatter | solution.py:1675
  500.5 116.1 %reduce-scatter.13.cloned.1.call-start = ((), (), s32[]{:S(2)}) async-start(), calls=%async_computation.11 | async-start | bytes 1310720 | tf_op jit(solution)/shard_map/reduce_scatter | solution.py:1675
  562.7 151.4 %reduce-scatter.17.cloned.1.call-start = ((), (), s32[]{:S(2)}) async-start(), calls=%async_computation.13 | async-start | bytes 1474560 | tf_op jit(solution)/shard_map/reduce_scatter | solution.py:1675
  616.8 5.3 copy-start.10
  622.9 85.4 %all-to-all-start.1 = ((bf16[8,32,1,896]{3,1,2,0:T(8,128)(2,1)}), bf16[8,32,1,896]{3,1,2,0:T(8,128)(2,1)}, u32[]{:S(2)}, u32[]{:S(2)}) async-start(bf16[8,32,1,896]{3,1,2,0:T(8,128)(2,1)} %maximum_bitcast_fusion), calls=%async_computation.7 | async-start | bytes 917504 | tf_op jit(solution)/shard_map/all_to_all | solution.py:1742
  627.1 87.1 %reduce-scatter.15.cloned.1.call-start = ((), (), s32[]{:S(2)}) async-start(), calls=%async_computation.12 | async-start | bytes 1638400 | tf_op jit(solution)/shard_map/reduce_scatter | solution.py:1675
  627.8 79.7 %copy-start.15 = (bf16[1,4,32,1024]{3,2,1,0:T(8,128)(2,1)S(1)}, bf16[1,4,32,1024]{3,2,1,0:T(8,128)(2,1)}, u32[]{:S(2)}) copy-start(bf16[1,4,32,1024]{3,2,1,0:T(8,128)(2,1)} %reduce-scatter.13.cloned.1.call-done) | copy-start | bytes 786436
  710.6 6.0 copy-start.9
  713.4 8.6 %copy-start.24 = (f32[6,32,128]{2,1,0:T(8,128)S(1)}, f32[6,32,128]{2,1,0:T(8,128)}, u32[]{:S(2)}) copy-start(f32[6,32,128]{2,1,0:T(8,128)} %get-tuple-element.210) | copy-start | bytes 294916
  718.4 12.0 %all-to-all-start = ((bf16[8,32,1,768]{3,1,2,0:T(8,128)(2,1)}), bf16[8,32,1,768]{3,1,2,0:T(8,128)(2,1)S(1)}, u32[]{:S(2)}, u32[]{:S(2)}) async-start(bf16[8,32,1,768]{3,1,2,0:T(8,128)(2,1)} %maximum_bitcast_fusion.1), calls=%async_computation.6 | async-start | bytes 786432 | tf_op jit(solution)/shard_map/all_to_all | solution.py:1742
  727.7 5.0 copy-start.7
  (27 other events, 75.3 us)
Sparse Core Ops, SparseCore 0:
  10.3 53.0 all-gather.10
  75.0 35.8 all-gather.14
  113.1 42.4 all-gather.12
  163.4 28.6 all-gather.16
  194.1 31.7 all-gather.18
  422.1 27.0 reduce-scatter.8
  451.5 29.9 reduce-scatter.6
  500.7 25.0 reduce-scatter.10
  562.9 25.0 reduce-scatter.12
  616.8 27.0 reduce-scatter.16
  646.3 35.7 reduce-scatter.14

commit v8 on v7

--- a/solution.py
+++ b/solution.py
@@ -338,7 +338,7 @@
     ]
 
 
-NEAR_GAP, FAR_GAP, SHORT_GAP = 3.0, 6.0, 0.1
+NEAR_GAP, FAR_GAP, SHORT_GAP = 2.5, 4.5, 0.1
 
 
 def arrive_steps(gathers, micro):

time: 747 us -> 751 us (level)
  transfers between devices with their start and end apart: 13 -> 13, of which waited for: 1 -> 1; matrix products, arithmetic and copies ran while one was open for 7% -> 7% of each run, Pallas kernels for 61% -> 62%
where the time goes in v8:
time: 751 us; the launch traced here: 746 us
  Pallas kernels  643 us (86%)
  local copies, waits for them, and re-layouts  50.7 us (7%)
  other arithmetic  24.7 us (3%)
  between operations  15.2 us (2%)
  starting transfers between devices  8.03 us (1%)
    pallas_call x10, Pallas kernels, stage_call(): pl.pallas_call(body, out_shape=tuple(outs), in_specs=[far if place in laz...  643 us
  transfers between devices with their start and end apart: 13, of which 1 were waited for; matrix products, arithmetic and copies ran while one was open for 7% of the time, Pallas kernels for 62%

profile of v8, /device:TPU:0, one launch (start us, length us, event | category | flops | bytes accessed | tf_op | source)
XLA Modules:
  0.0 745.8 jit_solution(6248740180325219802)
XLA Ops:
  7.3 1.9 pad_maximum_fusion.3
  13.9 55.4 %shard_map.416 = (bf16[2,1024,1024]{2,1,0:T(8,128)(2,1)}, bf16[4,8,32,256]{3,2,1,0:T(8,128)(2,1)}, bf16[8,32,1408]{2,1,0:T(8,128)(2,1)}, bf16[4,208,32]{2,1,0:T(8,128)(2,1)}, bf16[8,4,16,32]{3,2,1,0:T(8,128)(2,1)}) custom-call(bf16[2,128,1024]{2,1,0:T(8,128)(2,1)} %bitcast.318, bf16[8,32,256]{2,1,0:T(8,128)(2,1)} %maximum_bitcast_fusion.2.refs_1_, ...), custom_call_target="tpu_custom_call" | custom-call | flops 99999997952 | bytes 16777216 | tf_op jit(solution)/shard_map/pallas_call | solution.py:556
  69.4 1.8 slice.183
  71.3 1.7 slice.184
  79.1 1.3 copy.288.refs_7_.refs_9_.refs_12_.refs_10_
  82.6 1.3 copy.289.refs_14_.refs_10_
  85.2 1.5 fusion.5
  88.6 78.7 %shard_map.417 = (bf16[2,1024,384]{2,1,0:T(8,128)(2,1)}, bf16[2,1024,128]{2,1,0:T(8,128)(2,1)}, f32[2,2,1024]{2,1,0:T(2,128)}, f32[2,128,1024]{2,1,0:T(8,128)}, ...) custom-call(s32[1024,1]{1,0:T(8,128)} %copy.292.refs_0_, ...), custom_call_target="tpu_custom_call" | custom-call | flops 187500003328 | bytes 16777216 | tf_op jit(solution)/shard_map/pallas_call | solution.py:556
  170.5 1.3 slice.195
  173.1 1.2 slice.243.refs_3_.refs_5_
  174.4 1.4 maximum_maximum_fusion.refs_2_.refs_4_
  175.8 51.2 %shard_map.418 = (bf16[2,1024,1024]{2,1,0:T(8,128)(2,1)}, f32[2,1024,640]{2,1,0:T(8,128)}, bf16[2,1024,640]{2,1,0:T(8,128)(2,1)}, f32[2,128,1024]{2,1,0:T(8,128)...) custom-call(bf16[2,128,1024]{2,1,0:T(8,128)(2,1)} %get-tuple-element.133.refs_0_, ...), custom_call_target="tpu_custom_call" | custom-call | flops 149999992832 | bytes 16777216 | tf_op jit(solution)/shard_map/pallas_call | solution.py:556
  227.0 1.2 slice.199
  228.9 1.7 slice.247.refs_7_.refs_10_
  232.5 1.3 slice.207
  233.8 1.2 copy.294
  235.1 1.3 maximum_maximum_fusion.1.refs_2_.refs_4_
  236.4 79.3 %shard_map.419 = (bf16[2,1024,1024]{2,1,0:T(8,128)(2,1)}, bf16[2,1024,1024]{2,1,0:T(8,128)(2,1)}, bf16[2,1024,128]{2,1,0:T(8,128)(2,1)}, bf16[2,1024,256]{2,1,0:...) custom-call(s32[1024,1]{1,0:T(8,128)} %copy.292.refs_0_, ...), custom_call_target="tpu_custom_call" | custom-call | flops 212500004864 | bytes 16777216 | tf_op jit(solution)/shard_map/pallas_call | solution.py:556
  315.7 51.0 %shard_map.420 = (bf16[2,1024,1024]{2,1,0:T(8,128)(2,1)}, f32[2,1024,640]{2,1,0:T(8,128)}, bf16[2,1024,640]{2,1,0:T(8,128)(2,1)}, f32[2,128,1024]{2,1,0:T(8,128)...) custom-call(bf16[2,128,1024]{2,1,0:T(8,128)(2,1)} %get-tuple-element.141.refs_0_, ...), custom_call_target="tpu_custom_call" | custom-call | flops 149999992832 | bytes 16777216 | tf_op jit(solution)/shard_map/pallas_call | solution.py:556
  366.8 51.3 %shard_map.421 = (f32[2,128,1024]{2,1,0:T(8,128)}, f32[2,1024]{1,0:T(2,128)}, bf16[4,128,1024]{2,1,0:T(8,128)(2,1)}, bf16[4,16,1024]{2,1,0:T(8,128)(2,1)}, bf16[4,8,32,640]{3,2,1,0:T(8,128)(2,1)}) custom-call(bf16[2,128,1024]{2,1,0:T(8,128)(2,1)} %bitcast.321, f32[2,128,1024]{2,1,0:T(8,128)} %get-tuple-element.146.refs_1_, ...), custom_call_target="tpu_custom_call" | custom-call | flops 162500001792 | bytes 16777216 | tf_op jit(solution)/shard_map/pallas_call | solution.py:556
  418.1 2.4 pad_maximum_fusion
  421.3 78.9 %shard_map.422 = (f32[2,32,128]{2,1,0:T(8,128)}, f32[2,128,1024]{2,1,0:T(8,128)}, f32[2,128,1024]{2,1,0:T(8,128)}, f32[2,1024]{1,0:T(2,128)}, bf16[4,4,32,1024]{3,2,1,0:T(8,128)(2,1)}) custom-call(s32[1024,1]{1,0:T(8,128)} %copy.292.refs_0_, s32[1,1024]{1,0:T(1,128)} %bitcast.304, f32[2,128,1024]{2,1,0:T(8,128)} %get-tuple-element.154.refs_2_, ...), custom_call_target="tpu_custom_call" | custom-call | flops 212500004864 | bytes 16777216 | tf_op jit(solution)/shard_map/pallas_call | solution.py:556
  500.4 64.6 %shard_map.423 = (f32[2,32,128]{2,1,0:T(8,128)}, f32[2,1024]{1,0:T(2,128)}, f32[2,128,1024]{2,1,0:T(8,128)}, bf16[4,4,32,1024]{3,2,1,0:T(8,128)(2,1)}) custom-call(s32[1024,1]{1,0:T(8,128)} %copy.292.refs_0_, s32[1,1024]{1,0:T(1,128)} %bitcast.305, f32[2,128,1024]{2,1,0:T(8,128)} %get-tuple-element.167.refs_2_, f32[2,128,1024]{2,1,0:T(8,128)} %get-tuple-element.168.refs_3_, ...), custom_call_target="tpu_custom_call" | custom-call | flops 187500003328 | bytes 16777216 | tf_op jit(solution)/shard_map/pallas_call | solution.py:556
  565.1 51.5 %shard_map.424 = (f32[2,128,1024]{2,1,0:T(8,128)}, f32[2,1024]{1,0:T(2,128)}, bf16[4,128,1024]{2,1,0:T(8,128)(2,1)}, bf16[4,16,1024]{2,1,0:T(8,128)(2,1)}, bf16[4,8,32,640]{3,2,1,0:T(8,128)(2,1)}) custom-call(f32[2,128,1024]{2,1,0:T(8,128)} %get-tuple-element.179.refs_0_, f32[2,128,1024]{2,1,0:T(8,128)} %get-tuple-element.180.refs_1_, ...), custom_call_target="tpu_custom_call" | custom-call | flops 162500001792 | bytes 16777216 | tf_op jit(solution)/shard_map/pallas_call | solution.py:556
  616.6 2.4 pad_maximum_fusion.1
  625.3 4.1 all-to-all-start.1
  630.2 81.1 %shard_map.425 = (f32[16,1024]{1,0:T(8,128)}, f32[6,32,128]{2,1,0:T(8,128)}, f32[2,128,1024]{2,1,0:T(8,128)}, f32[4,32,1024]{2,1,0:T(8,128)}) custom-call(s32[1024,1]{1,0:T(8,128)} %copy.292.refs_0_, s32[1,1024]{1,0:T(1,128)} %bitcast.306, f32[2,128,1024]{2,1,0:T(8,128)} %get-tuple-element.189.refs_2_, f32[2,128,1024]{2,1,0:T(8,128)} %get-tuple-element.190.refs_3_, ...), custom_call_target="tpu_custom_call" | custom-call | flops 187500003328 | bytes 16777216 | tf_op jit(solution)/shard_map/pallas_call | solution.py:556
  719.0 1.4 convert_bitcast_fusion.11
  720.4 1.8 maximum_bitcast_fusion.1
  722.2 3.5 all-to-all-start
  730.0 1.3 constant_dynamic-slice_fusion
  732.1 1.8 all-to-all-done
  (249 shorter events, 48.5 us)
Async XLA Ops:
  7.2 4.2 copy-start
  7.3 4.2 copy-start.25
  7.3 4.9 copy-start.16
  7.3 4.9 copy-start.17
  7.3 77.9 %all-gather.11.cloned.1.call-start = ((), (), s32[]{:S(2)}) async-start(), calls=%async_computation.14 | async-start | bytes 1966080 | tf_op jit(solution)/shard_map/all_gather | solution.py:1535
  9.3 158.1 %all-gather.15.cloned.1.call-start = ((), (), s32[]{:S(2)}) async-start(), calls=%async_computation.16 | async-start | bytes 1966080 | tf_op jit(solution)/shard_map/all_gather | solution.py:1535
  69.4 4.7 copy-start.19
  69.4 4.6 copy-start.26
  69.4 4.6 copy-start.28
  74.9 92.5 %all-gather.13.cloned.1.call-start = ((), (), s32[]{:S(2)}) async-start(), calls=%async_computation.15 | async-start | bytes 2457600 | tf_op jit(solution)/shard_map/all_gather | solution.py:1535
  75.7 155.8 %all-gather.17.cloned.1.call-start = ((), (), s32[]{:S(2)}) async-start(), calls=%async_computation.17 | async-start | bytes 1474560 | tf_op jit(solution)/shard_map/all_gather | solution.py:1535
  76.9 4.1 copy-start.20
  77.9 4.6 copy-start.39
  88.6 78.9 %copy-start.23 = (f32[2,32,32]{2,1,0:T(8,128)S(1)}, f32[2,32,32]{2,1,0:T(8,128)}, u32[]{:S(2)}) copy-start(f32[2,32,32]{2,1,0:T(8,128)} %get-tuple-element.342) | copy-start | bytes 24580
  88.6 79.6 %copy-start.22 = (f32[2,32,32]{2,1,0:T(8,128)S(1)}, f32[2,32,32]{2,1,0:T(8,128)}, u32[]{:S(2)}) copy-start(f32[2,32,32]{2,1,0:T(8,128)} %get-tuple-element.341) | copy-start | bytes 24580
  88.6 80.2 %copy-start.21 = (f32[2,32,32]{2,1,0:T(8,128)S(1)}, f32[2,32,32]{2,1,0:T(8,128)}, u32[]{:S(2)}) copy-start(f32[2,32,32]{2,1,0:T(8,128)} %get-tuple-element.340) | copy-start | bytes 24580
  167.4 4.5 copy-start.3
  167.4 64.1 %all-gather.19.cloned.1.call-start = ((), (), s32[]{:S(2)}) async-start(), calls=%async_computation.18 | async-start | bytes 1638400 | tf_op jit(solution)/shard_map/all_gather | solution.py:1535
  169.6 4.8 copy-start.32
  174.4 325.9 %reduce-scatter.9.cloned.1.call-start = ((), (), s32[]{:S(2)}) async-start(), calls=%async_computation.9 | async-start | bytes 1474560 | tf_op jit(solution)/shard_map/reduce_scatter | solution.py:1675
  420.5 79.8 %reduce-scatter.7.cloned.1.call-start = ((), (), s32[]{:S(2)}) async-start(), calls=%async_computation.8 | async-start | bytes 1638400 | tf_op jit(solution)/shard_map/reduce_scatter | solution.py:1675
  421.3 143.7 %reduce-scatter.11.cloned.1.call-start = ((), (), s32[]{:S(2)}) async-start(), calls=%async_computation.10 | async-start | bytes 1310720 | tf_op jit(solution)/shard_map/reduce_scatter | solution.py:1675
  500.3 118.7 %reduce-scatter.13.cloned.1.call-start = ((), (), s32[]{:S(2)}) async-start(), calls=%async_computation.11 | async-start | bytes 1310720 | tf_op jit(solution)/shard_map/reduce_scatter | solution.py:1675
  565.0 152.9 %reduce-scatter.17.cloned.1.call-start = ((), (), s32[]{:S(2)}) async-start(), calls=%async_computation.13 | async-start | bytes 1474560 | tf_op jit(solution)/shard_map/reduce_scatter | solution.py:1675
  619.2 5.3 copy-start.10
  625.3 86.8 %all-to-all-start.1 = ((bf16[8,32,1,896]{3,1,2,0:T(8,128)(2,1)}), bf16[8,32,1,896]{3,1,2,0:T(8,128)(2,1)}, u32[]{:S(2)}, u32[]{:S(2)}) async-start(bf16[8,32,1,896]{3,1,2,0:T(8,128)(2,1)} %maximum_bitcast_fusion), calls=%async_computation.7 | async-start | bytes 917504 | tf_op jit(solution)/shard_map/all_to_all | solution.py:1742
  629.5 88.5 %reduce-scatter.15.cloned.1.call-start = ((), (), s32[]{:S(2)}) async-start(), calls=%async_computation.12 | async-start | bytes 1638400 | tf_op jit(solution)/shard_map/reduce_scatter | solution.py:1675
  630.2 81.1 %copy-start.15 = (bf16[1,4,32,1024]{3,2,1,0:T(8,128)(2,1)S(1)}, bf16[1,4,32,1024]{3,2,1,0:T(8,128)(2,1)}, u32[]{:S(2)}) copy-start(bf16[1,4,32,1024]{3,2,1,0:T(8,128)(2,1)} %reduce-scatter.13.cloned.1.call-done) | copy-start | bytes 786436
  714.4 6.0 copy-start.9
  717.2 8.4 %copy-start.24 = (f32[6,32,128]{2,1,0:T(8,128)S(1)}, f32[6,32,128]{2,1,0:T(8,128)}, u32[]{:S(2)}) copy-start(f32[6,32,128]{2,1,0:T(8,128)} %get-tuple-element.210) | copy-start | bytes 294916
  722.2 11.7 %all-to-all-start = ((bf16[8,32,1,768]{3,1,2,0:T(8,128)(2,1)}), bf16[8,32,1,768]{3,1,2,0:T(8,128)(2,1)S(1)}, u32[]{:S(2)}, u32[]{:S(2)}) async-start(bf16[8,32,1,768]{3,1,2,0:T(8,128)(2,1)} %maximum_bitcast_fusion.1), calls=%async_computation.6 | async-start | bytes 786432 | tf_op jit(solution)/shard_map/all_to_all | solution.py:1742
  731.3 5.0 copy-start.7
  (27 other events, 75.3 us)
Sparse Core Ops, SparseCore 0:
  10.3 53.0 all-gather.10
  75.0 35.8 all-gather.14
  113.1 42.4 all-gather.12
  167.5 28.1 all-gather.16
  197.7 31.8 all-gather.18
  420.6 28.7 reduce-scatter.8
  451.7 29.9 reduce-scatter.6
  500.4 25.5 reduce-scatter.10
  565.1 25.2 reduce-scatter.12
  619.2 28.6 reduce-scatter.16
  650.2 35.4 reduce-scatter.14
